TPU v7x, 32 devices: a whole 2x2x4 slice. The times are simulated.
32 devices in a mesh: section: 2 (over core), ctx: 4 (over y, x), fsdp: 4 (over z).
Axes of the slice: x: 2, y: 2, z: 4, core: 2. Of those that a mesh axis runs over, the one named last changes fastest.
Arguments:
- tokens: bfloat16 [8, 1024, 1024], P('fsdp', 'ctx'), may hold values from -6 to 6
- cotangent: bfloat16 [8, 1024, 1024], P('fsdp', 'ctx'), may hold values from -6 to 6
- segment_ids: int32 [8, 1024], P('fsdp'), may hold values from 0 to 3, never falling along the last dimension, each value on 1 to 512 neighbouring positions
- w_qkv: float32 [2, 1024, 3072], P('section', 'fsdp'), may hold values from -0.1875 to 0.1875
- w_out: float32 [2, 1024, 1024], P('section', 'fsdp'), may hold values from -1 to 1
- w_up: float32 [2, 1024, 4096], P('section', 'fsdp'), may hold values from -0.1875 to 0.1875
- w_down: float32 [2, 4096, 1024], P('section', 'fsdp'), may hold values from -0.09375 to 0.09375
- gain_attn: float32 [2, 1024], P('section', 'fsdp'), may hold values from 0.5 to 1.5
- gain_mlp: float32 [2, 1024], P('section', 'fsdp'), may hold values from 0.5 to 1.5
- row_qkv: float32 [2, 1024], P('section', 'fsdp'), may hold values from 29.4912 to 4259.84
- col_qkv: float32 [2, 3072], P('section'), may hold values from 106.496 to 983.04
- row_out: float32 [2, 1024], P('section', 'fsdp'), may hold values from 2.21184 to 319.488
- col_out: float32 [2, 1024], P('section'), may hold values from 8.192 to 81.92
- row_up: float32 [2, 1024], P('section', 'fsdp'), may hold values from 32.768 to 4751.36
- col_up: float32 [2, 4096], P('section'), may hold values from 122.88 to 1105.92
- row_down: float32 [2, 4096], P('section', 'fsdp'), may hold values from 110.592 to 15728.64
- col_down: float32 [2, 1024], P('section'), may hold values from 409.6 to 3686.4
- var_attn: float32 [2, 1024], P('section', 'fsdp'), may hold values from 819.2 to 8192
- var_mlp: float32 [2, 1024], P('section', 'fsdp'), may hold values from 819.2 to 8192
Outputs:
- hidden: bfloat16 [2, 8, 1024, 1024], P('section', 'fsdp', 'ctx')
- input_grads: bfloat16 [2, 8, 1024, 1024], P('section', 'fsdp', 'ctx')
- grad_qkv: float32 [2, 1024, 3072], P('section', 'fsdp')
- grad_out: float32 [2, 1024, 1024], P('section', 'fsdp')
- grad_up: float32 [2, 1024, 4096], P('section', 'fsdp')
- grad_down: float32 [2, 4096, 1024], P('section', 'fsdp')
- grad_gain_attn: float32 [2, 1024], P('section', 'fsdp')
- grad_gain_mlp: float32 [2, 1024], P('section', 'fsdp')
- new_qkv: float32 [2, 1024, 3072], P('section', 'fsdp')
- new_out: float32 [2, 1024, 1024], P('section', 'fsdp')
- new_up: float32 [2, 1024, 4096], P('section', 'fsdp')
- new_down: float32 [2, 4096, 1024], P('section', 'fsdp')
- new_gain_attn: float32 [2, 1024], P('section', 'fsdp')
- new_gain_mlp: float32 [2, 1024], P('section', 'fsdp')
- new_row_qkv: float32 [2, 1024], P('section', 'fsdp')
- new_col_qkv: float32 [2, 3072], P('section')
- new_row_out: float32 [2, 1024], P('section', 'fsdp')
- new_col_out: float32 [2, 1024], P('section')
- new_row_up: float32 [2, 1024], P('section', 'fsdp')
- new_col_up: float32 [2, 4096], P('section')
- new_row_down: float32 [2, 4096], P('section', 'fsdp')
- new_col_down: float32 [2, 1024], P('section')
- new_var_attn: float32 [2, 1024], P('section', 'fsdp')
- new_var_mlp: float32 [2, 1024], P('section', 'fsdp')
- clip_ratio: float32 [2, 6], P('section')
Inputs may be any that keep to these rules, and one draw needn't show every extreme that they name: `segment_ids`: within a sequence the ids never fall; each id covers 1 to 512 positions of its sequence and one covers exactly 512.
All inputs are finite; a program needn't handle non-finite values.
Results may differ from a plain program's by a relative error of at most 0.025.
Values may be sent and summed in bfloat16 or wider, within the bound.
No kernel may reach another device: no remote copies, remote signals or barrier semaphores. Data moves between devices by JAX's collectives and lax.ppermute only.
A program may use at most 384 MiB of HBM per device.

v0:
```python
import jax
import jax.numpy as jnp
from jax import lax
from jax.sharding import PartitionSpec as P

HEADS = 16


decay_rate = 0.5
clip_level = 0.5
step_rate = 1.0
norm_eps = 1e-05
weight_eps = 1e-06
mask_fill = -1e30


def shifted(value, axis, steps):
    count = lax.axis_size(axis)
    leading, last = (max(0, -steps), min(count, count - steps))
    return lax.ppermute(value, axis, [(source, source + steps) for source in range(leading, last)])


def layer_norm(values, gain):
    center = values - jnp.mean(values, axis=-1, keepdims=True)
    spread = jnp.mean(center * center, axis=-1, keepdims=True)
    return center * lax.rsqrt(spread + norm_eps) * gain


def gelu_exact(values):
    return jax.nn.gelu(values, approximate=False)


def times_transposed(left, right):
    return lax.dot_general(
        left, right, (((1,), (1,)), ((), ())), preferred_element_type=jnp.float32
    )


def rows_product(left, right):
    return lax.dot_general(
        left, right, (((0,), (0,)), ((), ())), preferred_element_type=jnp.float32
    )


def take_slot(buffers, slot_index):
    return jax.tree.map(
        lambda buffer: lax.dynamic_index_in_dim(buffer, slot_index, 0, keepdims=False), buffers
    )


def put_slot(buffers, entries, slot_index, slot_live):

    def update_one(buffer, entry):
        current = lax.dynamic_index_in_dim(buffer, slot_index, 0, keepdims=False)
        return lax.dynamic_update_index_in_dim(
            buffer, jnp.where(slot_live, entry, current), slot_index, 0
        )

    return jax.tree.map(update_one, buffers, entries)


def masked_scores(queries, key_heads, doc_mask, scale_factor):
    scores = (
        jnp.einsum("qhd,khd->hqk", queries, key_heads, preferred_element_type=jnp.float32)
        * scale_factor
    )
    return jnp.where(doc_mask[None], scores, mask_fill)


def per_device(
    tokens,
    cotangent,
    segment_ids,
    w_qkv,
    w_out,
    w_up,
    w_down,
    gain_attn,
    gain_mlp,
    row_qkv,
    col_qkv,
    row_out,
    col_out,
    row_up,
    col_up,
    row_down,
    col_down,
    var_attn,
    var_mlp,
):
    section_index = lax.axis_index("section")
    ctx_index = lax.axis_index("ctx")
    fsdp_count = lax.axis_size("fsdp")
    micro_count, row_count, model_width = tokens.shape
    seq_len = segment_ids.shape[1]
    head_dim = model_width // HEADS
    scale_factor = head_dim ** (-0.5)
    hidden_width = w_up.shape[2]
    full_qkv, full_out, full_up, full_down, attn_gain_low, mlp_gain_low = (
        lax.all_gather(w_qkv[0].astype(jnp.bfloat16), "fsdp", axis=0, tiled=True),
        lax.all_gather(w_out[0].astype(jnp.bfloat16), "fsdp", axis=0, tiled=True),
        lax.all_gather(w_up[0].astype(jnp.bfloat16), "fsdp", axis=0, tiled=True),
        lax.all_gather(w_down[0].astype(jnp.bfloat16), "fsdp", axis=0, tiled=True),
        lax.all_gather(gain_attn[0].astype(jnp.bfloat16), "fsdp", axis=0, tiled=True),
        lax.all_gather(gain_mlp[0].astype(jnp.bfloat16), "fsdp", axis=0, tiled=True),
    )
    attn_gain = attn_gain_low.astype(jnp.float32)
    mlp_gain = mlp_gain_low.astype(jnp.float32)

    def doc_mask_at(slot_index):
        doc_ids = lax.dynamic_index_in_dim(segment_ids, slot_index, 0, keepdims=False)
        query_ids = lax.dynamic_slice_in_dim(doc_ids, ctx_index * row_count, row_count)
        return query_ids[:, None] == doc_ids[None, :]

    def project(layer_in):
        return jnp.dot(layer_in, full_qkv, preferred_element_type=jnp.float32).astype(jnp.bfloat16)

    def skip_project(layer_in):
        return jnp.zeros((row_count, 3 * model_width), jnp.bfloat16)

    def forward_rest(layer_in, projected, key_rows, value_rows, doc_mask):
        queries = projected[:, :model_width].reshape(row_count, HEADS, head_dim)
        scores = masked_scores(
            queries, key_rows.reshape(seq_len, HEADS, head_dim), doc_mask, scale_factor
        )
        row_peak = jnp.max(scores, axis=-1, keepdims=True)
        exponent = jnp.exp(scores - row_peak)
        row_total = jnp.sum(exponent, axis=-1, keepdims=True)
        log_total = row_peak + jnp.log(row_total)
        attn_low = (exponent / row_total).astype(jnp.bfloat16)
        context = jnp.einsum(
            "hqk,khd->qhd",
            attn_low,
            value_rows.reshape(seq_len, HEADS, head_dim),
            preferred_element_type=jnp.float32,
        )
        context = context.reshape(row_count, model_width).astype(jnp.bfloat16)
        pre_attn = layer_in.astype(jnp.float32) + jnp.dot(
            context, full_out, preferred_element_type=jnp.float32
        )
        normed = layer_norm(pre_attn, attn_gain)
        normed_low = normed.astype(jnp.bfloat16)
        upward = jnp.dot(normed_low, full_up, preferred_element_type=jnp.float32)
        activated = gelu_exact(upward).astype(jnp.bfloat16)
        pre_mlp = normed + jnp.dot(activated, full_down, preferred_element_type=jnp.float32)
        layer_out = layer_norm(pre_mlp, mlp_gain).astype(jnp.bfloat16)
        return (layer_out, (log_total, context, pre_attn, normed_low, upward, activated, pre_mlp))

    def skip_rest(layer_in, projected, key_rows, value_rows, doc_mask):
        blank_rows = jnp.zeros((row_count, model_width), jnp.float32)
        blank_wide = jnp.zeros((row_count, hidden_width), jnp.float32)
        return (
            blank_rows.astype(jnp.bfloat16),
            (
                jnp.zeros((HEADS, row_count, 1), jnp.float32),
                blank_rows.astype(jnp.bfloat16),
                blank_rows,
                blank_rows.astype(jnp.bfloat16),
                blank_wide,
                blank_wide.astype(jnp.bfloat16),
                blank_rows,
            ),
        )

    forward_store = (
        jnp.zeros((micro_count, row_count, model_width), jnp.bfloat16),
        jnp.zeros((micro_count, row_count, 3 * model_width), jnp.bfloat16),
        jnp.zeros((micro_count, seq_len, model_width), jnp.bfloat16),
        jnp.zeros((micro_count, seq_len, model_width), jnp.bfloat16),
        jnp.zeros((micro_count, HEADS, row_count, 1), jnp.float32),
        jnp.zeros((micro_count, row_count, model_width), jnp.bfloat16),
        jnp.zeros((micro_count, row_count, model_width), jnp.float32),
        jnp.zeros((micro_count, row_count, model_width), jnp.bfloat16),
        jnp.zeros((micro_count, row_count, hidden_width), jnp.float32),
        jnp.zeros((micro_count, row_count, hidden_width), jnp.bfloat16),
        jnp.zeros((micro_count, row_count, model_width), jnp.float32),
    )
    outputs_store = jnp.zeros((micro_count, row_count, model_width), jnp.bfloat16)
    arriving = jnp.zeros((row_count, model_width), jnp.bfloat16)
    for time_step in range(micro_count + 1):
        slot_raw = time_step - section_index
        slot_live = (slot_raw >= 0) & (slot_raw < micro_count)
        slot_index = jnp.clip(slot_raw, 0, micro_count - 1)
        layer_in = jnp.where(section_index == 0, take_slot(tokens, slot_index), arriving)
        projected = lax.cond(slot_live, project, skip_project, layer_in)
        key_rows, value_rows = (
            lax.all_gather(projected[:, model_width : 2 * model_width], "ctx", axis=0, tiled=True),
            lax.all_gather(projected[:, 2 * model_width :], "ctx", axis=0, tiled=True),
        )
        doc_mask = doc_mask_at(slot_index)
        layer_out, kept = lax.cond(
            slot_live, forward_rest, skip_rest, layer_in, projected, key_rows, value_rows, doc_mask
        )
        forward_store = put_slot(
            forward_store, (layer_in, projected, key_rows, value_rows) + kept, slot_index, slot_live
        )
        outputs_store = put_slot(outputs_store, layer_out, slot_index, slot_live)
        arriving = shifted(layer_out, "section", 1)

    def backward_local(grad_out, doc_mask, kept):
        (
            layer_in,
            projected,
            key_rows,
            value_rows,
            log_total,
            context,
            pre_attn,
            normed_low,
            upward,
            activated,
            pre_mlp,
        ) = kept
        mlp_back = jax.vjp(layer_norm, pre_mlp, mlp_gain)[1]
        mlp_in_grad, mlp_gain_grad = mlp_back(grad_out)
        down_grad = mlp_in_grad.astype(jnp.bfloat16)
        gelu_back = jax.vjp(gelu_exact, upward)[1]
        upward_grad = gelu_back(times_transposed(down_grad, full_down))[0].astype(jnp.bfloat16)
        normed_grad = mlp_in_grad + times_transposed(upward_grad, full_up)
        attn_back = jax.vjp(layer_norm, pre_attn, attn_gain)[1]
        attn_in_grad, attn_gain_grad = attn_back(normed_grad)
        branch_grad = attn_in_grad.astype(jnp.bfloat16)
        context_grad = (
            times_transposed(branch_grad, full_out)
            .astype(jnp.bfloat16)
            .reshape(row_count, HEADS, head_dim)
        )
        queries = projected[:, :model_width].reshape(row_count, HEADS, head_dim)
        key_heads = key_rows.reshape(seq_len, HEADS, head_dim)
        value_heads = value_rows.reshape(seq_len, HEADS, head_dim)
        attn_weights = jnp.exp(
            masked_scores(queries, key_heads, doc_mask, scale_factor) - log_total
        )
        prob_grad = jnp.einsum(
            "qhd,khd->hqk", context_grad, value_heads, preferred_element_type=jnp.float32
        )
        row_dot = jnp.sum(attn_weights * prob_grad, axis=-1, keepdims=True)
        score_grad = (attn_weights * (prob_grad - row_dot)).astype(jnp.bfloat16)
        query_grad = (
            jnp.einsum("hqk,khd->qhd", score_grad, key_heads, preferred_element_type=jnp.float32)
            * scale_factor
        )
        key_grad = (
            jnp.einsum("hqk,qhd->khd", score_grad, queries, preferred_element_type=jnp.float32)
            * scale_factor
        )
        value_grad = jnp.einsum(
            "hqk,qhd->khd",
            attn_weights.astype(jnp.bfloat16),
            context_grad,
            preferred_element_type=jnp.float32,
        )
        return (
            query_grad.reshape(row_count, model_width),
            key_grad.reshape(seq_len, model_width),
            value_grad.reshape(seq_len, model_width),
            attn_in_grad,
            attn_gain_grad,
            mlp_gain_grad,
            branch_grad,
            upward_grad,
            down_grad,
        )

    def skip_backward(grad_out, doc_mask, kept):
        blank_rows = jnp.zeros((row_count, model_width), jnp.float32)
        blank_keys = jnp.zeros((seq_len, model_width), jnp.float32)
        blank_gain = jnp.zeros((model_width,), jnp.float32)
        return (
            blank_rows,
            blank_keys,
            blank_keys,
            blank_rows,
            blank_gain,
            blank_gain,
            blank_rows.astype(jnp.bfloat16),
            jnp.zeros((row_count, hidden_width), jnp.bfloat16),
            blank_rows.astype(jnp.bfloat16),
        )

    def finish(query_grad, key_part, value_part, attn_in_grad):
        stacked = jnp.concatenate([query_grad, key_part, value_part], axis=1).astype(jnp.bfloat16)
        return (stacked, (attn_in_grad + times_transposed(stacked, full_qkv)).astype(jnp.bfloat16))

    def skip_finish(query_grad, key_part, value_part, attn_in_grad):
        return (
            jnp.zeros((row_count, 3 * model_width), jnp.bfloat16),
            jnp.zeros((row_count, model_width), jnp.bfloat16),
        )

    grad_store = (
        jnp.zeros((micro_count, row_count, 3 * model_width), jnp.bfloat16),
        jnp.zeros((micro_count, row_count, model_width), jnp.bfloat16),
        jnp.zeros((micro_count, row_count, hidden_width), jnp.bfloat16),
        jnp.zeros((micro_count, row_count, model_width), jnp.bfloat16),
        jnp.zeros((micro_count, model_width), jnp.float32),
        jnp.zeros((micro_count, model_width), jnp.float32),
    )
    in_grad_store = jnp.zeros((micro_count, row_count, model_width), jnp.bfloat16)
    arriving_grad = jnp.zeros((row_count, model_width), jnp.bfloat16)
    for time_step in range(micro_count + 1):
        slot_raw = time_step - 1 + section_index
        slot_live = (slot_raw >= 0) & (slot_raw < micro_count)
        slot_index = jnp.clip(slot_raw, 0, micro_count - 1)
        grad_out = jnp.where(
            section_index == 1, take_slot(cotangent, slot_index), arriving_grad
        ).astype(jnp.float32)
        kept = take_slot(forward_store, slot_index)
        doc_mask = doc_mask_at(slot_index)
        (
            query_grad,
            key_grad,
            value_grad,
            attn_in_grad,
            attn_gain_grad,
            mlp_gain_grad,
            branch_grad,
            upward_grad,
            down_grad,
        ) = lax.cond(slot_live, backward_local, skip_backward, grad_out, doc_mask, kept)
        key_part, value_part = (
            lax.psum_scatter(
                key_grad.astype(jnp.bfloat16), "ctx", scatter_dimension=0, tiled=True
            ).astype(jnp.float32),
            lax.psum_scatter(
                value_grad.astype(jnp.bfloat16), "ctx", scatter_dimension=0, tiled=True
            ).astype(jnp.float32),
        )
        stacked, input_grad = lax.cond(
            slot_live, finish, skip_finish, query_grad, key_part, value_part, attn_in_grad
        )
        grad_store = put_slot(
            grad_store,
            (stacked, branch_grad, upward_grad, down_grad, attn_gain_grad, mlp_gain_grad),
            slot_index,
            slot_live,
        )
        in_grad_store = put_slot(in_grad_store, input_grad, slot_index, slot_live)
        arriving_grad = shifted(input_grad, "section", -1)
    grad_qkv_sum = jnp.zeros((model_width, 3 * model_width), jnp.float32)
    grad_out_sum = jnp.zeros((model_width, model_width), jnp.float32)
    grad_up_sum = jnp.zeros((model_width, hidden_width), jnp.float32)
    grad_down_sum = jnp.zeros((hidden_width, model_width), jnp.float32)
    gain_attn_sum = jnp.zeros((model_width,), jnp.float32)
    gain_mlp_sum = jnp.zeros((model_width,), jnp.float32)
    for slot_index in range(micro_count):
        grad_qkv_sum = grad_qkv_sum + rows_product(
            forward_store[0][slot_index], grad_store[0][slot_index]
        )
        grad_out_sum = grad_out_sum + rows_product(
            forward_store[5][slot_index], grad_store[1][slot_index]
        )
        grad_up_sum = grad_up_sum + rows_product(
            forward_store[7][slot_index], grad_store[2][slot_index]
        )
        grad_down_sum = grad_down_sum + rows_product(
            forward_store[9][slot_index], grad_store[3][slot_index]
        )
        gain_attn_sum = gain_attn_sum + grad_store[4][slot_index]
        gain_mlp_sum = gain_mlp_sum + grad_store[5][slot_index]
    shard_qkv, shard_out, shard_up, shard_down, shard_attn, shard_mlp = (
        lax.psum_scatter(
            grad_qkv_sum.astype(jnp.bfloat16), "fsdp", scatter_dimension=0, tiled=True
        ).astype(jnp.float32),
        lax.psum_scatter(
            grad_out_sum.astype(jnp.bfloat16), "fsdp", scatter_dimension=0, tiled=True
        ).astype(jnp.float32),
        lax.psum_scatter(
            grad_up_sum.astype(jnp.bfloat16), "fsdp", scatter_dimension=0, tiled=True
        ).astype(jnp.float32),
        lax.psum_scatter(
            grad_down_sum.astype(jnp.bfloat16), "fsdp", scatter_dimension=0, tiled=True
        ).astype(jnp.float32),
        lax.psum_scatter(
            gain_attn_sum.astype(jnp.bfloat16), "fsdp", scatter_dimension=0, tiled=True
        ).astype(jnp.float32),
        lax.psum_scatter(
            gain_mlp_sum.astype(jnp.bfloat16), "fsdp", scatter_dimension=0, tiled=True
        ).astype(jnp.float32),
    )
    shard_qkv, shard_out, shard_up, shard_down, shard_attn, shard_mlp = (
        lax.psum(shard_qkv.astype(jnp.bfloat16), "ctx").astype(jnp.float32),
        lax.psum(shard_out.astype(jnp.bfloat16), "ctx").astype(jnp.float32),
        lax.psum(shard_up.astype(jnp.bfloat16), "ctx").astype(jnp.float32),
        lax.psum(shard_down.astype(jnp.bfloat16), "ctx").astype(jnp.float32),
        lax.psum(shard_attn.astype(jnp.bfloat16), "ctx").astype(jnp.float32),
        lax.psum(shard_mlp.astype(jnp.bfloat16), "ctx").astype(jnp.float32),
    )
    masters = (w_qkv[0], w_out[0], w_up[0], w_down[0])
    gradients = (shard_qkv, shard_out, shard_up, shard_down)
    rows_old = (row_qkv[0], row_out[0], row_up[0], row_down[0])
    cols_old = (col_qkv[0], col_out[0], col_up[0], col_down[0])
    squares = [gradient * gradient for gradient in gradients]
    rows_new = [
        decay_rate * old_row + (1.0 - decay_rate) * jnp.mean(square, axis=1)
        for old_row, square in zip(rows_old, squares)
    ]
    row_counts = [gradient.shape[0] * fsdp_count for gradient in gradients]
    col_partial = [jnp.sum(square, axis=0) for square in squares]
    row_totals = jnp.stack([jnp.sum(row_value) for row_value in rows_new])
    weight_totals = jnp.stack(
        [jnp.sum(master * master) for master in masters]
        + [jnp.sum(gain_attn[0] * gain_attn[0]), jnp.sum(gain_mlp[0] * gain_mlp[0])]
    )
    moment_attn = decay_rate * var_attn[0] + (1.0 - decay_rate) * shard_attn * shard_attn
    moment_mlp = decay_rate * var_mlp[0] + (1.0 - decay_rate) * shard_mlp * shard_mlp
    gain_updates = (shard_attn * lax.rsqrt(moment_attn), shard_mlp * lax.rsqrt(moment_mlp))
    vector_totals = jnp.stack([jnp.sum(gain_step * gain_step) for gain_step in gain_updates])
    col_sum_qkv, col_sum_out, col_sum_up, col_sum_down, row_all, weight_all, vector_all = (
        lax.psum(col_partial[0].astype(jnp.bfloat16), "fsdp").astype(jnp.float32),
        lax.psum(col_partial[1].astype(jnp.bfloat16), "fsdp").astype(jnp.float32),
        lax.psum(col_partial[2].astype(jnp.bfloat16), "fsdp").astype(jnp.float32),
        lax.psum(col_partial[3].astype(jnp.bfloat16), "fsdp").astype(jnp.float32),
        lax.psum(row_totals.astype(jnp.bfloat16), "fsdp").astype(jnp.float32),
        lax.psum(weight_totals.astype(jnp.bfloat16), "fsdp").astype(jnp.float32),
        lax.psum(vector_totals.astype(jnp.bfloat16), "fsdp").astype(jnp.float32),
    )
    col_sums = (col_sum_qkv, col_sum_out, col_sum_up, col_sum_down)
    cols_new = [
        decay_rate * cols_old[matrix_pos]
        + (1.0 - decay_rate) * col_sums[matrix_pos] / row_counts[matrix_pos]
        for matrix_pos in range(4)
    ]
    updates = [
        gradients[matrix_pos]
        * lax.rsqrt(
            rows_new[matrix_pos][:, None]
            * cols_new[matrix_pos][None, :]
            / (row_all[matrix_pos] / row_counts[matrix_pos])
        )
        for matrix_pos in range(4)
    ]
    update_all = lax.psum(jnp.stack([jnp.sum(update * update) for update in updates]), "fsdp")
    fresh_masters = []
    ratios = []
    for matrix_pos in range(4):
        entry_count = row_counts[matrix_pos] * gradients[matrix_pos].shape[1]
        clip_ratio = jnp.sqrt(update_all[matrix_pos] / entry_count)
        weight_scale = jnp.sqrt(weight_all[matrix_pos] / entry_count + weight_eps)
        fresh_masters.append(
            masters[matrix_pos]
            - step_rate
            * weight_scale
            * updates[matrix_pos]
            / jnp.maximum(1.0, clip_ratio / clip_level)
        )
        ratios.append(clip_ratio)
    gain_masters = (gain_attn[0], gain_mlp[0])
    gain_count = shard_attn.shape[0] * fsdp_count
    for gain_pos in range(2):
        clip_ratio = jnp.sqrt(vector_all[gain_pos] / gain_count)
        weight_scale = jnp.sqrt(weight_all[4 + gain_pos] / gain_count + weight_eps)
        fresh_masters.append(
            gain_masters[gain_pos]
            - step_rate
            * weight_scale
            * gain_updates[gain_pos]
            / jnp.maximum(1.0, clip_ratio / clip_level)
        )
        ratios.append(clip_ratio)
    return (
        outputs_store[None],
        in_grad_store[None],
        shard_qkv[None],
        shard_out[None],
        shard_up[None],
        shard_down[None],
        shard_attn[None],
        shard_mlp[None],
        fresh_masters[0][None],
        fresh_masters[1][None],
        fresh_masters[2][None],
        fresh_masters[3][None],
        fresh_masters[4][None],
        fresh_masters[5][None],
        rows_new[0][None],
        cols_new[0][None],
        rows_new[1][None],
        cols_new[1][None],
        rows_new[2][None],
        cols_new[2][None],
        rows_new[3][None],
        cols_new[3][None],
        moment_attn[None],
        moment_mlp[None],
        jnp.stack(ratios)[None],
    )


def solution(mesh):
    in_specs = (
        P("fsdp", "ctx", None),
        P("fsdp", "ctx", None),
        P("fsdp", None),
        P("section", "fsdp", None),
        P("section", "fsdp", None),
        P("section", "fsdp", None),
        P("section", "fsdp", None),
        P("section", "fsdp"),
        P("section", "fsdp"),
        P("section", "fsdp"),
        P("section", None),
        P("section", "fsdp"),
        P("section", None),
        P("section", "fsdp"),
        P("section", None),
        P("section", "fsdp"),
        P("section", None),
        P("section", "fsdp"),
        P("section", "fsdp"),
    )
    out_specs = (
        P("section", "fsdp", "ctx", None),
        P("section", "fsdp", "ctx", None),
        P("section", "fsdp", None),
        P("section", "fsdp", None),
        P("section", "fsdp", None),
        P("section", "fsdp", None),
        P("section", "fsdp"),
        P("section", "fsdp"),
        P("section", "fsdp", None),
        P("section", "fsdp", None),
        P("section", "fsdp", None),
        P("section", "fsdp", None),
        P("section", "fsdp"),
        P("section", "fsdp"),
        P("section", "fsdp"),
        P("section", None),
        P("section", "fsdp"),
        P("section", None),
        P("section", "fsdp"),
        P("section", None),
        P("section", "fsdp"),
        P("section", None),
        P("section", "fsdp"),
        P("section", "fsdp"),
        P("section", None),
    )
    return jax.shard_map(
        per_device, mesh=mesh, in_specs=in_specs, out_specs=out_specs, check_vma=False
    )
```

profile of v0, /device:TPU:0, one launch (start us, length us, event | category | flops | bytes accessed | tf_op | source)
XLA Modules:
  0.0 2109.2 jit_solution(9699494622801378961)
XLA Ops:
  14.0 114.9 %all-gather.13.cloned.1.call-done = bf16[1024,3072]{1,0:T(8,128)(2,1)} async-done(((bf16[256,3072]{1,0:T(8,128)(2,1)}), bf16[1024,3072]{1,0:T(8,128)(2,1)}) %all-gather.13.cloned.1.call-update) | async-done | bytes 6291472 | tf_op jit(solution)/shard_map/all_gather | solution.py:100
  128.9 4.8 conditional.12
  128.9 4.8 convolution_convert_fusion
  144.2 8.0 all-gather
  152.3 9.4 all-gather.1
  161.6 13.7 all-gather.19.cloned.1.call-done
  175.3 36.4 %all-gather.15.cloned.1.call-done = bf16[1024,1024]{0,1:T(8,128)(2,1)} async-done(((bf16[256,1024]{0,1:T(8,128)(2,1)}), bf16[1024,1024]{0,1:T(8,128)(2,1)}) %all-gather.15.cloned.1.call-update) | async-done | bytes 2097168 | tf_op jit(solution)/shard_map/all_gather | solution.py:187
  211.7 37.5 %all-gather.17.cloned.1.call-done = bf16[1024,1024]{0,1:T(8,128)(2,1)} async-done(((bf16[256,1024]{0,1:T(8,128)(2,1)}), bf16[1024,1024]{0,1:T(8,128)(2,1)}) %all-gather.17.cloned.1.call-update) | async-done | bytes 2097168 | tf_op jit(solution)/shard_map/all_gather | solution.py:188
  249.1 151.7 %all-gather.21.cloned.1.call-done = bf16[1024,4096]{1,0:T(8,128)(2,1)} async-done(((bf16[256,4096]{1,0:T(8,128)(2,1)}), bf16[1024,4096]{1,0:T(8,128)(2,1)}) %all-gather.21.cloned.1.call-update) | async-done | bytes 8388624 | tf_op jit(solution)/shard_map/all_gather | solution.py:102
  400.8 149.9 %all-gather.23.cloned.1.call-done = bf16[4096,1024]{1,0:T(8,128)(2,1)} async-done(((bf16[1024,1024]{1,0:T(8,128)(2,1)}), bf16[4096,1024]{1,0:T(8,128)(2,1)}) %all-gather.23.cloned.1.call-update) | async-done | bytes 8388624 | tf_op jit(solution)/shard_map/all_gather | solution.py:103
  550.7 47.9 %conditional.13 = (bf16[256,1024]{1,0:T(8,128)(2,1)}, f32[16,256,1]{1,0,2:T(8,128)S(1)}, f32[256,1024]{1,0:T(8,128)}, bf16[256,1024]{1,0:T(8,128)(2,1)}, f32[256...) conditional(s32[]{:T(128)} %convert_element_type.432, ...), branch_computations={%region_2.3_spmd, %region_3.10_spmd} | conditional | flops 6030356992 | bytes 141212864 | solution.py:191
  560.9 5.1 fusion.13
  572.7 15.5 fusion.5
  588.2 5.2 fusion.204
  644.3 37.0 %all-gather.25.cloned.1.call-done = bf16[1024,1024]{0,1:T(8,128)(2,1)} async-done(((bf16[256,1024]{0,1:T(8,128)(2,1)}), bf16[1024,1024]{0,1:T(8,128)(2,1)}) %all-gather.25.cloned.1.call-update) | async-done | bytes 2097168 | tf_op jit(solution)/shard_map/all_gather | solution.py:187
  681.3 51.0 %conditional.15 = (bf16[256,1024]{1,0:T(8,128)(2,1)}, f32[16,256,1]{1,0,2:T(8,128)S(1)}, f32[256,1024]{1,0:T(8,128)}, bf16[256,1024]{1,0:T(8,128)(2,1)}, f32[256...) conditional(s32[]{:T(128)} %convert_element_type.441, ...), branch_computations={%region_12.13_spmd, %region_13.20_spmd} | conditional | flops 6030356992 | bytes 134921408 | solution.py:191
  694.3 6.4 fusion.30
  706.6 15.7 fusion.22
  722.4 5.2 fusion.206
  744.8 4.8 constant_dynamic-slice_fusion.38
  769.9 4.9 bitcast_dynamic-update-slice_fusion.1
  774.8 4.8 constant_dynamic-slice_fusion.37
  783.5 36.9 %all-gather.29.cloned.1.call-done = bf16[1024,1024]{0,1:T(8,128)(2,1)} async-done(((bf16[256,1024]{0,1:T(8,128)(2,1)}), bf16[1024,1024]{0,1:T(8,128)(2,1)}) %all-gather.29.cloned.1.call-update) | async-done | bytes 2097168 | tf_op jit(solution)/shard_map/all_gather | solution.py:187
  820.3 16.9 conditional.17
  838.3 5.1 bitcast_dynamic-update-slice_fusion
  851.4 16.3 conditional.18
  875.7 134.6 %reduce-scatter.11.cloned.1.call-done = bf16[256,1024]{1,0:T(8,128)(2,1)} async-done(((bf16[1024,1024]{1,0:T(8,128)(2,1)}), bf16[256,1024]{1,0:T(8,128)(2,1)}) %reduce-scatter.11.cloned.1.call-update) | async-done | bytes 524304 | tf_op jit(solution)/shard_map/reduce_scatter | solution.py:322
  1010.3 38.9 %reduce-scatter.13.cloned.1.call-done = bf16[256,1024]{1,0:T(8,128)(2,1)} async-done(((bf16[1024,1024]{1,0:T(8,128)(2,1)}), bf16[256,1024]{1,0:T(8,128)(2,1)}) %reduce-scatter.13.cloned.1.call-update) | async-done | bytes 524304 | tf_op jit(solution)/shard_map/reduce_scatter | solution.py:325
  1051.8 11.5 collective-permute-done.2
  1064.6 88.9 %conditional.20 = (bf16[256,1024]{0,1:T(8,128)(2,1)}, bf16[1024,1024]{0,1:T(8,128)(2,1)}, bf16[1024,1024]{0,1:T(8,128)(2,1)}, f32[256,1024]{1,0:T(8,128)}, f32[1...) conditional(s32[]{:T(128)} %convert_element_type.450, ...), branch_computations={%region_47.48_spmd, %region_48.60_spmd} | conditional | flops 7643592192 | bytes 302678400 | solution.py:320
  1069.5 16.3 fusion.58
  1097.9 8.1 fusion.216
  1108.1 13.2 multiply_reduce_fusion.6
  1121.3 15.2 multiply_convert_fusion.3
  1136.5 7.2 convolution_multiply_fusion
  1146.7 6.8 convolution_multiply_fusion.1
  1161.6 31.3 %reduce-scatter.15.cloned.1.call-done = bf16[256,1024]{1,0:T(8,128)(2,1)} async-done(((bf16[1024,1024]{1,0:T(8,128)(2,1)}), bf16[256,1024]{1,0:T(8,128)(2,1)}) %reduce-scatter.15.cloned.1.call-update) | async-done | bytes 524304 | tf_op jit(solution)/shard_map/reduce_scatter | solution.py:322
  1192.8 38.9 %reduce-scatter.17.cloned.1.call-done = bf16[256,1024]{1,0:T(8,128)(2,1)} async-done(((bf16[1024,1024]{1,0:T(8,128)(2,1)}), bf16[256,1024]{1,0:T(8,128)(2,1)}) %reduce-scatter.17.cloned.1.call-update) | async-done | bytes 524304 | tf_op jit(solution)/shard_map/reduce_scatter | solution.py:325
  1231.7 11.5 conditional.21
  1238.0 5.2 fusion.80
  1248.4 86.8 %conditional.22 = (bf16[256,1024]{0,1:T(8,128)(2,1)}, bf16[1024,1024]{0,1:T(8,128)(2,1)}, bf16[1024,1024]{0,1:T(8,128)(2,1)}, f32[256,1024]{1,0:T(8,128)}, f32[1...) conditional(s32[]{:T(128)} %convert_element_type.456, ...), branch_computations={%region_64.65_spmd, %region_65.77_spmd} | conditional | flops 7643592192 | bytes 327844192 | solution.py:320
  1253.8 15.2 fusion.87
  1279.8 8.1 fusion.217
  1289.8 13.2 multiply_reduce_fusion.13
  1303.0 15.0 multiply_convert_fusion.4
  1318.1 7.2 convolution_multiply_fusion.2
  1328.2 6.8 convolution_multiply_fusion.3
  1360.1 14.5 reduce-scatter.19.cloned.1.call-done
  1374.6 38.9 %reduce-scatter.21.cloned.1.call-done = bf16[256,1024]{1,0:T(8,128)(2,1)} async-done(((bf16[1024,1024]{1,0:T(8,128)(2,1)}), bf16[256,1024]{1,0:T(8,128)(2,1)}) %reduce-scatter.21.cloned.1.call-update) | async-done | bytes 524304 | tf_op jit(solution)/shard_map/reduce_scatter | solution.py:325
  1413.4 11.1 conditional.23
  1418.1 6.1 fusion.109
  1434.8 5.6 add_convert_fusion.5
  1449.5 8.1 fusion.154
  1457.6 12.3 add_convert_fusion.3
  1477.6 8.2 fusion.155
  1485.7 11.6 add_convert_fusion.4
  1506.1 66.3 %reduce-scatter.23.cloned.1.call-done = bf16[256,3072]{1,0:T(8,128)(2,1)} async-done(((bf16[1024,3072]{1,0:T(8,128)(2,1)}), bf16[256,3072]{1,0:T(8,128)(2,1)}) %reduce-scatter.23.cloned.1.call-update) | async-done | bytes 1572880 | tf_op jit(solution)/shard_map/reduce_scatter | solution.py:362
  1572.4 147.5 %reduce-scatter.29.cloned.1.call-done = bf16[1024,1024]{1,0:T(8,128)(2,1)} async-done(((bf16[4096,1024]{1,0:T(8,128)(2,1)}), bf16[1024,1024]{1,0:T(8,128)(2,1)}) %reduce-scatter.29.cloned.1.call-update) | async-done | bytes 2097168 | tf_op jit(solution)/shard_map/reduce_scatter | solution.py:371
  1719.9 147.5 %reduce-scatter.27.cloned.1.call-done = bf16[256,4096]{1,0:T(8,128)(2,1)} async-done(((bf16[1024,4096]{1,0:T(8,128)(2,1)}), bf16[256,4096]{1,0:T(8,128)(2,1)}) %reduce-scatter.27.cloned.1.call-update) | async-done | bytes 2097168 | tf_op jit(solution)/shard_map/reduce_scatter | solution.py:368
  1880.3 11.2 all-reduce.3
  1891.6 10.5 all-reduce.4
  1906.4 105.7 %all-reduce.8.cloned.1.call-done = (bf16[256,3072]{1,0:T(8,128)(2,1)}, bf16[256,1024]{1,0:T(8,128)(2,1)}, bf16[256,4096]{1,0:T(8,128)(2,1)}, bf16[1024,1024]{1,0:T(8,128)(2,1)}) async-done(((bf16[256,3072]{1,0:T(8,128)(2,1)}, bf16[256,1024]{1,0:T(8,128)(2,1)}, bf16[256,4096]{1,0:T(8,128)(2,1)}, bf16[1024,1024]{1,0:T(8,128)(2,1)}), (bf16[256,3072]{1,0:T(8,128)(2,1)}, bf16[256,1024]{1,0:T(8,128)(2,1)}, ...) | async-done | bytes 6291472 | tf_op jit(solution)/shard_map/psum | solution.py:382
  2025.8 19.0 all-reduce.2
  2063.5 8.3 psum.110
  (588 shorter events, 384.6 us)
Async XLA Ops:
  7.2 121.7 %all-gather.13.cloned.1.call-start = ((), (), s32[]{:S(2)}) async-start(), calls=%async_computation.10 | async-start | bytes 7864320 | tf_op jit(solution)/shard_map/all_gather | solution.py:100
  10.7 164.6 %all-gather.19.cloned.1.call-start = ((), (), s32[]{:S(2)}) async-start(), calls=%async_computation.13 | async-start | bytes 2621440 | tf_op jit(solution)/shard_map/all_gather | solution.py:101
  11.6 200.0 %all-gather.15.cloned.1.call-start = ((), (), s32[]{:S(2)}) async-start(), calls=%async_computation.11 | async-start | bytes 2621440 | tf_op jit(solution)/shard_map/all_gather | solution.py:187
  135.5 113.7 %all-gather.17.cloned.1.call-start = ((), (), s32[]{:S(2)}) async-start(), calls=%async_computation.12 | async-start | bytes 2621440 | tf_op jit(solution)/shard_map/all_gather | solution.py:188
  136.1 264.7 %all-gather.21.cloned.1.call-start = ((), (), s32[]{:S(2)}) async-start(), calls=%async_computation.14 | async-start | bytes 10485760 | tf_op jit(solution)/shard_map/all_gather | solution.py:102
  140.2 12.1 copy-start.84
  140.2 410.5 %copy-start.62 = (s32[2,1024]{1,0:T(2,128)S(1)}, s32[2,1024]{1,0:T(2,128)}, u32[]{:S(2)}) copy-start(s32[2,1024]{1,0:T(2,128)} %param.45) | copy-start | bytes 24580
  140.2 410.5 %all-gather.23.cloned.1.call-start = ((), (), s32[]{:S(2)}) async-start(), calls=%async_computation.15 | async-start | bytes 10485760 | tf_op jit(solution)/shard_map/all_gather | solution.py:103
  144.1 500.1 %all-gather.27.cloned.1.call-start = ((), (), s32[]{:S(2)}) async-start(), calls=%async_computation.17 | async-start | bytes 2621440 | tf_op jit(solution)/shard_map/all_gather | solution.py:188
  568.8 19.4 slice-start.16
  572.7 15.5 slice-start.17
  598.7 3.0 collective-permute-start
  610.7 70.6 %all-gather.25.cloned.1.call-start = ((), (), s32[]{:S(2)}) async-start(), calls=%async_computation.16 | async-start | bytes 2621440 | tf_op jit(solution)/shard_map/all_gather | solution.py:187
  611.4 172.0 %all-gather.31.cloned.1.call-start = ((), (), s32[]{:S(2)}) async-start(), calls=%async_computation.19 | async-start | bytes 2621440 | tf_op jit(solution)/shard_map/all_gather | solution.py:188
  634.7 99.5 %copy-start = (f32[2,256,1024]{2,1,0:T(8,128)}, f32[2,256,1024]{2,1,0:T(8,128)S(1)}, u32[]{:S(2)}) copy-start(f32[2,256,1024]{2,1,0:T(8,128)S(1)} %bitcast_dynamic-update-slice_fusion.22) | copy-start | bytes 6291460
  703.6 18.8 slice-start.18
  706.6 15.7 copy-start.57
  706.6 15.7 slice-start.19
  732.3 4.7 collective-permute-start.1
  744.6 75.7 %all-gather.29.cloned.1.call-start = ((), (), s32[]{:S(2)}) async-start(), calls=%async_computation.18 | async-start | bytes 2621440 | tf_op jit(solution)/shard_map/all_gather | solution.py:187
  762.4 247.9 %reduce-scatter.11.cloned.1.call-start = ((), (), s32[]{:S(2)}) async-start(), calls=%async_computation.20 | async-start | bytes 2621440 | tf_op jit(solution)/shard_map/reduce_scatter | solution.py:322
  838.3 12.2 copy-start.88
  871.6 177.5 %reduce-scatter.13.cloned.1.call-start = ((), (), s32[]{:S(2)}) async-start(), calls=%async_computation.21 | async-start | bytes 2621440 | tf_op jit(solution)/shard_map/reduce_scatter | solution.py:325
  875.7 317.2 %reduce-scatter.15.cloned.1.call-start = ((), (), s32[]{:S(2)}) async-start(), calls=%async_computation.22 | async-start | bytes 2621440 | tf_op jit(solution)/shard_map/reduce_scatter | solution.py:322
  1050.5 12.8 collective-permute-start.2
  1068.5 17.3 slice-start.12
  1069.5 16.4 copy-start.4
  1069.5 16.4 slice-start.13
  1121.3 22.4 %slice-start.4 = ((s8[16777216]{0:T(1024)(128)(4,1)}), s8[4194304]{0:T(1024)(128)(4,1)S(1)}, s32[]{:S(2)}) async-start(s8[16777216]{0:T(1024)(128)(4,1)} %bitcast.912), calls=%async_computation.35 | async-start | bytes 8388608 | tf_op jit(solution)/shard_map/cond
  1121.3 22.4 %slice-start.5 = ((s8[16777216]{0:T(1024)(128)(4,1)}), s8[4194304]{0:T(1024)(128)(4,1)S(1)}, s32[]{:S(2)}) async-start(s8[16777216]{0:T(1024)(128)(4,1)} %bitcast.912), calls=%async_computation.36 | async-start | bytes 8388608 | tf_op jit(solution)/shard_map/cond
  1121.3 22.4 %slice-start.6 = ((s8[16777216]{0:T(1024)(128)(4,1)}), s8[4194304]{0:T(1024)(128)(4,1)S(1)}, s32[]{:S(2)}) async-start(s8[16777216]{0:T(1024)(128)(4,1)} %bitcast.912), calls=%async_computation.37 | async-start | bytes 8388608 | tf_op jit(solution)/shard_map/cond
  1157.5 74.2 %reduce-scatter.17.cloned.1.call-start = ((), (), s32[]{:S(2)}) async-start(), calls=%async_computation.23 | async-start | bytes 2621440 | tf_op jit(solution)/shard_map/reduce_scatter | solution.py:325
  1161.5 213.0 %reduce-scatter.19.cloned.1.call-start = ((), (), s32[]{:S(2)}) async-start(), calls=%async_computation.24 | async-start | bytes 2621440 | tf_op jit(solution)/shard_map/reduce_scatter | solution.py:322
  1243.2 3.9 collective-permute-start.3
  1252.8 16.1 slice-start.14
  1253.8 15.2 copy-start.5
  1253.8 15.2 slice-start.15
  1303.0 22.2 %slice-start.8 = ((s8[16777216]{0:T(1024)(128)(4,1)}), s8[4194304]{0:T(1024)(128)(4,1)S(1)}, s32[]{:S(2)}) async-start(s8[16777216]{0:T(1024)(128)(4,1)} %bitcast.914), calls=%async_computation.39 | async-start | bytes 8388608 | tf_op jit(solution)/shard_map/cond
  1303.0 22.2 %slice-start.9 = ((s8[16777216]{0:T(1024)(128)(4,1)}), s8[4194304]{0:T(1024)(128)(4,1)S(1)}, s32[]{:S(2)}) async-start(s8[16777216]{0:T(1024)(128)(4,1)} %bitcast.914), calls=%async_computation.40 | async-start | bytes 8388608 | tf_op jit(solution)/shard_map/cond
  1303.0 22.2 %slice-start.10 = ((s8[16777216]{0:T(1024)(128)(4,1)}), s8[4194304]{0:T(1024)(128)(4,1)S(1)}, s32[]{:S(2)}) async-start(s8[16777216]{0:T(1024)(128)(4,1)} %bitcast.914), calls=%async_computation.41 | async-start | bytes 8388608 | tf_op jit(solution)/shard_map/cond
  1339.2 74.2 %reduce-scatter.21.cloned.1.call-start = ((), (), s32[]{:S(2)}) async-start(), calls=%async_computation.25 | async-start | bytes 2621440 | tf_op jit(solution)/shard_map/reduce_scatter | solution.py:325
  1343.2 162.9 %reduce-scatter.25.cloned.1.call-start = ((), (), s32[]{:S(2)}) async-start(), calls=%async_computation.27 | async-start | bytes 2621440 | tf_op jit(solution)/shard_map/reduce_scatter | solution.py:365
  1353.5 219.0 %reduce-scatter.23.cloned.1.call-start = ((), (), s32[]{:S(2)}) async-start(), calls=%async_computation.26 | async-start | bytes 7864320 | tf_op jit(solution)/shard_map/reduce_scatter | solution.py:362
  1440.5 279.4 %reduce-scatter.29.cloned.1.call-start = ((), (), s32[]{:S(2)}) async-start(), calls=%async_computation.29 | async-start | bytes 10485760 | tf_op jit(solution)/shard_map/reduce_scatter | solution.py:371
  1469.9 397.6 %reduce-scatter.27.cloned.1.call-start = ((), (), s32[]{:S(2)}) async-start(), calls=%async_computation.28 | async-start | bytes 10485760 | tf_op jit(solution)/shard_map/reduce_scatter | solution.py:368
  1497.4 514.7 %all-reduce.8.cloned.1.call-start = ((), (), s32[]{:S(2)}) async-start(), calls=%async_computation.30 | async-start | bytes 12582912 | tf_op jit(solution)/shard_map/psum | solution.py:382
  1506.0 361.4 %copy-start.85 = (f32[1,256]{1,0:T(1,128)S(1)}, f32[1,256]{1,0:T(1,128)}, u32[]{:S(2)}) copy-start(f32[1,256]{1,0:T(1,128)} %param.51) | copy-start | bytes 3076
  1506.0 362.1 %copy-start.90 = (u32[32]{0:T(128)S(1)}, u32[32]{0:T(128)}, u32[]{:S(2)}) copy-start(u32[32]{0:T(128)} %constant.1619) | copy-start | bytes 388
  1506.0 367.3 %copy-start.80 = (f32[1,256]{1,0:T(1,128)S(1)}, f32[1,256]{1,0:T(1,128)}, u32[]{:S(2)}) copy-start(f32[1,256]{1,0:T(1,128)} %param.60) | copy-start | bytes 3076
  1506.1 367.3 %copy-start.76 = (f32[1,1024]{1,0:T(1,128)S(1)}, f32[1,1024]{1,0:T(1,128)}, u32[]{:S(2)}) copy-start(f32[1,1024]{1,0:T(1,128)} %param.55) | copy-start | bytes 12292
  1506.1 367.3 %copy-start.77 = (f32[1,1024]{1,0:T(1,128)S(1)}, f32[1,1024]{1,0:T(1,128)}, u32[]{:S(2)}) copy-start(f32[1,1024]{1,0:T(1,128)} %param.59) | copy-start | bytes 12292
  1506.1 367.3 %copy-start.75 = (f32[1,3072]{1,0:T(1,128)S(1)}, f32[1,3072]{1,0:T(1,128)}, u32[]{:S(2)}) copy-start(f32[1,3072]{1,0:T(1,128)} %param.53) | copy-start | bytes 36868
  1506.1 367.4 %copy-start.70 = (f32[1,4096]{1,0:T(1,128)S(1)}, f32[1,4096]{1,0:T(1,128)}, u32[]{:S(2)}) copy-start(f32[1,4096]{1,0:T(1,128)} %param.57) | copy-start | bytes 49156
  1867.5 9.7 copy-start.74
  1867.5 9.7 copy-start.72
  1878.4 135.8 %copy-start.81 = (f32[1,256]{1,0:T(1,128)S(1)}, f32[1,256]{1,0:T(1,128)}, u32[]{:S(2)}) copy-start(f32[1,256]{1,0:T(1,128)} %param.52) | copy-start | bytes 3076
  1878.5 138.1 %copy-start.82 = (f32[1,256]{1,0:T(1,128)S(1)}, f32[1,256]{1,0:T(1,128)}, u32[]{:S(2)}) copy-start(f32[1,256]{1,0:T(1,128)} %param.54) | copy-start | bytes 3076
  1878.7 141.4 %copy-start.83 = (f32[1,256]{1,0:T(1,128)S(1)}, f32[1,256]{1,0:T(1,128)}, u32[]{:S(2)}) copy-start(f32[1,256]{1,0:T(1,128)} %param.56) | copy-start | bytes 3076
  1879.1 142.8 %copy-start.78 = (f32[1,1024]{1,0:T(1,128)S(1)}, f32[1,1024]{1,0:T(1,128)}, u32[]{:S(2)}) copy-start(f32[1,1024]{1,0:T(1,128)} %param.58) | copy-start | bytes 12292
  2012.1 9.2 copy-start.11
  2047.3 52.3 %copy-start.63 = (f32[3072]{0:T(1024)}, f32[3072]{0:T(1024)S(1)}, u32[]{:S(2)}) copy-start(f32[3072]{0:T(1024)S(1)} %multiply_add_fusion.7) | copy-start | bytes 36868
  2047.3 50.9 %copy-start.64 = (f32[1024]{0:T(1024)}, f32[1024]{0:T(1024)S(1)}, u32[]{:S(2)}) copy-start(f32[1024]{0:T(1024)S(1)} %multiply_add_fusion.9) | copy-start | bytes 12292
  2047.4 47.2 %copy-start.61 = (f32[4096]{0:T(1024)}, f32[4096]{0:T(1024)S(1)}, u32[]{:S(2)}) copy-start(f32[4096]{0:T(1024)S(1)} %multiply_add_fusion.6) | copy-start | bytes 49156
  2047.4 44.3 %copy-start.65 = (f32[1024]{0:T(1024)}, f32[1024]{0:T(1024)S(1)}, u32[]{:S(2)}) copy-start(f32[1024]{0:T(1024)S(1)} %multiply_add_fusion.8) | copy-start | bytes 12292
  (63 other events, 267.9 us)
Sparse Core Ops, SparseCore 0:
  10.8 118.0 all-gather.12
  131.0 44.2 all-gather.18
  177.7 33.9 all-gather.14
  213.9 35.1 all-gather.16
  251.1 149.6 all-gather.20
  402.8 147.8 all-gather.22
  610.8 33.4 all-gather.26
  646.1 35.1 all-gather.24
  744.7 38.6 all-gather.30
  785.1 35.1 all-gather.28
  871.8 138.4 reduce-scatter.10
  1014.0 35.1 reduce-scatter.12
  1157.6 35.1 reduce-scatter.14
  1196.5 35.1 reduce-scatter.16
  1339.3 35.1 reduce-scatter.18
  1378.2 35.1 reduce-scatter.20
  1416.2 43.8 reduce-scatter.24
  1462.3 110.0 reduce-scatter.22
  1574.9 144.9 reduce-scatter.28
  1722.2 145.1 reduce-scatter.26
  1871.7 140.3 all-reduce.7
where the time goes:
time: 2120 us; the launch traced here: 2110 us
  waiting for transfers between devices  1360 us (64%)
  matrix products  260 us (12%)
  other arithmetic  221 us (10%)
  local copies, waits for them, and re-layouts  148 us (7%)
  blocking collectives  66.4 us (3%)
  between operations  27.6 us (1%)
    reduce_scatter x3, waiting for transfers between devices, per_device(): lax.psum_scatter(key_grad.astype(jnp.bfloat16), 'ctx', scatter_dimension=...  180 us
    all_gather x1, waiting for transfers between devices, per_device(): lax.all_gather(w_up[0].astype(jnp.bfloat16), 'fsdp', axis=0, tiled=True)  152 us
    all_gather x1, waiting for transfers between devices, per_device(): lax.all_gather(w_down[0].astype(jnp.bfloat16), 'fsdp', axis=0, tiled=True)  150 us
    reduce_scatter x1, waiting for transfers between devices, per_device(): lax.psum_scatter(grad_up_sum.astype(jnp.bfloat16), 'fsdp', scatter_dimens...  148 us
    reduce_scatter x1, waiting for transfers between devices, per_device(): lax.psum_scatter(grad_down_sum.astype(jnp.bfloat16), 'fsdp', scatter_dime...  148 us
    reduce_scatter x3, waiting for transfers between devices, per_device(): lax.psum_scatter(value_grad.astype(jnp.bfloat16), 'ctx', scatter_dimensio...  117 us
    all_gather x1, waiting for transfers between devices, per_device(): lax.all_gather(w_qkv[0].astype(jnp.bfloat16), 'fsdp', axis=0, tiled=True)  115 us
    all_gather x3, waiting for transfers between devices, per_device(): lax.all_gather(projected[:, model_width:2 * model_width], 'ctx', axis=0,...  110 us
  transfers between devices with their start and end apart: 25, of which 23 were waited for; matrix products, arithmetic and copies ran while one was open for 11% of the time, Pallas kernels for 0%

commit v1 on v0

v1 whole, which is shorter than its diff:
```python
import functools

import jax
import jax.numpy as jnp
from jax import lax
from jax.experimental import pallas as pl
from jax.experimental.pallas import tpu as pltpu
from jax.sharding import PartitionSpec as P

HEADS = 16


decay_rate = 0.5
clip_level = 0.5
step_rate = 1.0
norm_eps = 1e-05
weight_eps = 1e-06
mask_fill = -1e30

bf16 = jnp.bfloat16
f32 = jnp.float32
LANES = 128


def swap_core(value):
    return lax.ppermute(value, "section", [(0, 1), (1, 0)])


def swap_x(value):
    return lax.ppermute(value, "ctx", [(i, i ^ 1) for i in range(4)])


def swap_y(value):
    return lax.ppermute(value, "ctx", [(i, i ^ 2) for i in range(4)])


def dot(left, right):
    return jnp.dot(left, right, preferred_element_type=f32)


def times_transposed(left, right):
    return lax.dot_general(left, right, (((1,), (1,)), ((), ())), preferred_element_type=f32)


def rows_product(left, right):
    return lax.dot_general(left, right, (((0,), (0,)), ((), ())), preferred_element_type=f32)


def gather4(value):
    pair = jnp.concatenate([value, swap_x(value)], axis=0)
    return jnp.concatenate([pair, swap_core(pair)], axis=0)


def scatter4(partial):
    half = partial.shape[0] // 2
    rows = half // 2
    partial = partial.astype(bf16)
    mine, theirs = partial[:half], swap_core(partial[half:])
    across = (mine[rows:].astype(f32) + theirs[rows:].astype(f32)).astype(bf16)
    return mine[:rows].astype(f32) + theirs[:rows].astype(f32) + swap_x(across).astype(f32)


def norm_parts(values):
    center = values - jnp.mean(values, axis=-1, keepdims=True)
    spread = jnp.mean(center * center, axis=-1, keepdims=True)
    scale = lax.rsqrt(spread + norm_eps)
    return center * scale, scale


def norm_back(out_grad, unit, scale, gain):
    scaled = out_grad * gain
    mean_scaled = jnp.mean(scaled, axis=-1, keepdims=True)
    mean_unit = jnp.mean(scaled * unit, axis=-1, keepdims=True)
    return scale * (scaled - mean_scaled - unit * mean_unit), jnp.sum(out_grad * unit, axis=0)


def nt(left, right):
    return lax.dot_general(left, right, (((1,), (1,)), ((), ())), preferred_element_type=f32)


def attention_kernel(q_ref, k_ref, v_ref, qid_ref, kid_ref, out_ref, lse_ref, *, scale):
    queries = q_ref[...] * jnp.asarray(scale, bf16)
    keys, values_t = k_ref[...], v_ref[...].T
    same = kid_ref[...] == qid_ref[...]
    first = lax.broadcasted_iota(jnp.int32, queries.shape, 1) < queries.shape[1] // 2
    parts = []
    for head in range(2):
        own = jnp.where(first if head == 0 else ~first, queries, jnp.zeros_like(queries))
        scores = jnp.where(same, nt(keys, own), mask_fill)
        peak = jnp.max(scores, axis=0, keepdims=True)
        weights = jnp.exp(scores - peak)
        total = jnp.sum(weights, axis=0, keepdims=True)
        lse_ref[0, head : head + 1, :] = peak + jnp.log(total)
        parts.append(dot(values_t, weights.astype(bf16)) * (1.0 / total))
    width = values_t.shape[0] // 2
    stacked = jnp.concatenate([parts[0][:width], parts[1][width:]], axis=0)
    out_ref[...] = stacked.T.astype(bf16)


def attention_forward(projected, keys_values, query_ids, key_ids, scale):
    rows, seq_len = projected.shape[0], keys_values.shape[0]
    tile = min(256, rows)
    elems = 4 * rows * seq_len
    return pl.pallas_call(
        functools.partial(attention_kernel, scale=scale),
        grid=(2, rows // tile),
        in_specs=[
            pl.BlockSpec((tile, LANES), lambda p, i: (i, 3 * p)),
            pl.BlockSpec((seq_len, LANES), lambda p, i: (0, 3 * p + 1)),
            pl.BlockSpec((seq_len, LANES), lambda p, i: (0, 3 * p + 2)),
            pl.BlockSpec((1, tile), lambda p, i: (0, i)),
            pl.BlockSpec((seq_len, 1), lambda p, i: (0, 0)),
        ],
        out_specs=[
            pl.BlockSpec((tile, LANES), lambda p, i: (i, p)),
            pl.BlockSpec((1, 2, tile), lambda p, i: (p, 0, i)),
        ],
        out_shape=[
            jax.ShapeDtypeStruct((rows, 2 * LANES), bf16),
            jax.ShapeDtypeStruct((2, 2, rows), f32),
        ],
        compiler_params=pltpu.CompilerParams(vmem_limit_bytes=32 << 20),
        cost_estimate=pl.CostEstimate(
            flops=elems * 4 * 128, bytes_accessed=4 << 20, transcendentals=elems
        ),
        name="attention_forward",
    )(projected, keys_values, keys_values, query_ids, key_ids)


def attention_back_kernel(
    q_ref, k_ref, v_ref, g_ref, lse_ref, qid_ref, kid_ref, dq_ref, dk_ref, dv_ref, *, scale
):
    queries = q_ref[...] * jnp.asarray(scale, bf16)
    keys, values, grads = k_ref[...], v_ref[...], g_ref[...]
    keys_t = keys.T
    same = kid_ref[...] == qid_ref[...]
    first = lax.broadcasted_iota(jnp.int32, queries.shape, 1) < queries.shape[1] // 2

    @pl.when(pl.program_id(1) == 0)
    def _():
        dk_ref[...] = jnp.zeros_like(dk_ref)
        dv_ref[...] = jnp.zeros_like(dv_ref)

    parts = []
    for head in range(2):
        mine = first if head == 0 else ~first
        own = jnp.where(mine, queries, jnp.zeros_like(queries))
        own_grads = jnp.where(mine, grads, jnp.zeros_like(grads))
        scores = jnp.where(same, nt(keys, own), mask_fill)
        weights = jnp.exp(scores - lse_ref[0, head : head + 1, :])
        prob_grad = nt(values, own_grads)
        row_dot = jnp.sum(weights * prob_grad, axis=0, keepdims=True)
        score_grad = (weights * (prob_grad - row_dot)).astype(bf16)
        dv_ref[...] += dot(weights.astype(bf16), own_grads)
        dk_ref[...] += dot(score_grad, own)
        parts.append(dot(keys_t, score_grad))
    width = keys_t.shape[0] // 2
    stacked = jnp.concatenate([parts[0][:width], parts[1][width:]], axis=0)
    dq_ref[...] = (stacked.T * scale).astype(bf16)


def attention_backward(projected, keys_values, grads, lse, query_ids, key_ids, scale):
    rows, seq_len = projected.shape[0], keys_values.shape[0]
    tile = min(256, rows)
    elems = 4 * rows * seq_len
    return pl.pallas_call(
        functools.partial(attention_back_kernel, scale=scale),
        grid=(2, rows // tile),
        in_specs=[
            pl.BlockSpec((tile, LANES), lambda p, i: (i, 3 * p)),
            pl.BlockSpec((seq_len, LANES), lambda p, i: (0, 3 * p + 1)),
            pl.BlockSpec((seq_len, LANES), lambda p, i: (0, 3 * p + 2)),
            pl.BlockSpec((tile, LANES), lambda p, i: (i, p)),
            pl.BlockSpec((1, 2, tile), lambda p, i: (p, 0, i)),
            pl.BlockSpec((1, tile), lambda p, i: (0, i)),
            pl.BlockSpec((seq_len, 1), lambda p, i: (0, 0)),
        ],
        out_specs=[
            pl.BlockSpec((tile, LANES), lambda p, i: (i, p)),
            pl.BlockSpec((seq_len, LANES), lambda p, i: (0, p)),
            pl.BlockSpec((seq_len, LANES), lambda p, i: (0, p)),
        ],
        out_shape=[
            jax.ShapeDtypeStruct((rows, 2 * LANES), bf16),
            jax.ShapeDtypeStruct((seq_len, 2 * LANES), f32),
            jax.ShapeDtypeStruct((seq_len, 2 * LANES), f32),
        ],
        compiler_params=pltpu.CompilerParams(vmem_limit_bytes=32 << 20),
        cost_estimate=pl.CostEstimate(
            flops=elems * 10 * 128, bytes_accessed=6 << 20, transcendentals=elems
        ),
        name="attention_backward",
    )(projected, keys_values, keys_values, grads, lse, query_ids, key_ids)


def per_device(
    tokens,
    cotangent,
    segment_ids,
    w_qkv,
    w_out,
    w_up,
    w_down,
    gain_attn,
    gain_mlp,
    row_qkv,
    col_qkv,
    row_out,
    col_out,
    row_up,
    col_up,
    row_down,
    col_down,
    var_attn,
    var_mlp,
):
    core = lax.axis_index("section")
    chip = lax.axis_index("ctx")
    depth = lax.axis_index("fsdp")
    y, x = chip // 2, chip % 2
    fsdp_count = lax.axis_size("fsdp")
    assert lax.axis_size("section") == 2 and lax.axis_size("ctx") == 4
    _, block, width = tokens.shape
    half = block // 2
    rows = w_qkv.shape[1]
    hidden_width = w_up.shape[2]
    unit = hidden_width // fsdp_count // 8
    scale = (width // HEADS) ** (-0.5)
    wide = 2 * LANES
    even_out = width // fsdp_count == wide
    first_core, first_y, first_x = core == 0, y == 0, x == 0

    def flipped(when, value, axis=0):
        low, high = jnp.split(value, 2, axis)
        return jnp.where(when, jnp.concatenate([high, low], axis), value)

    def eighth(e, of_core):
        qkv = lax.dynamic_index_in_dim(w_qkv[0].reshape(rows, 3, 8, LANES), e, 2, keepdims=False)
        up = lax.dynamic_index_in_dim(
            w_up[0].reshape(rows, fsdp_count, 8, unit), e, 2, keepdims=False
        )
        down = lax.dynamic_slice_in_dim(w_down[0], e * unit, unit, 0)
        parts = [qkv.reshape(rows, 3 * LANES), up.reshape(rows, fsdp_count * unit), down]
        if even_out:
            parts.append(
                lax.dynamic_slice(w_out[0], (of_core * LANES, chip * wide), (LANES, wide))
            )
        return [part.astype(bf16) for part in parts]

    mine_parts = eighth(2 * chip + core, core)
    other_parts = [swap_core(part) for part in eighth(2 * chip + 1 - core, 1 - core)]
    layer_parts = [
        [jnp.where(first_core, a, b) for a, b in zip(mine_parts, other_parts)],
        [jnp.where(first_core, b, a) for a, b in zip(mine_parts, other_parts)],
    ]
    if not even_out:
        whole_out = lax.all_gather(w_out[0].astype(bf16), "fsdp", axis=0, tiled=True)
        other_out = swap_core(whole_out)
        outs = (
            jnp.where(first_core, whole_out, other_out),
            jnp.where(first_core, other_out, whole_out),
        )

    gains_own = lax.all_gather(
        jnp.concatenate([gain_attn, gain_mlp], axis=0).astype(bf16), "fsdp", axis=1, tiled=True
    )
    gains_other = swap_core(gains_own)
    gains = (
        jnp.where(first_core, gains_own, gains_other).astype(f32),
        jnp.where(first_core, gains_other, gains_own).astype(f32),
    )

    def gather_rows(value):
        return lax.all_gather(value, "fsdp", axis=0, tiled=True)

    def layer_weights(layer):
        parts = layer_parts[layer]
        qkv = gather_rows(parts[0])
        qkv = jnp.concatenate([qkv, swap_y(qkv)], axis=1)
        if even_out:
            cols = gather_rows(parts[3]).reshape(fsdp_count, LANES, wide)

            def pick(index):
                return lax.dynamic_index_in_dim(cols, index, 0, keepdims=False)

            keep = jnp.stack([pick(chip), pick(chip ^ 2)])
            give = jnp.stack([pick(chip ^ 1), pick(chip ^ 3)])
            pair = jnp.concatenate([keep, swap_x(give)], axis=2)
            pair = flipped(~first_x, pair, 2)
            far = swap_y(pair[::-1])
            out = flipped(~first_y, jnp.concatenate([pair, far], axis=2), 2).reshape(wide, width)
        else:
            blocks = outs[layer].reshape(4, 2, LANES, width)
            blocks = lax.dynamic_index_in_dim(blocks, core, 1, keepdims=False)
            out = jnp.concatenate(
                [
                    lax.dynamic_index_in_dim(blocks, chip, 0, keepdims=False),
                    lax.dynamic_index_in_dim(blocks, chip ^ 2, 0, keepdims=False),
                ],
                axis=0,
            )
        up = gather_rows(parts[1])
        up = jnp.concatenate([up, swap_y(up)], axis=1)
        down = gather_rows(parts[2])
        down = jnp.concatenate([down, swap_y(down)], axis=0)
        return qkv, out, up, down

    weights = [layer_weights(0), layer_weights(1)]

    def own_rows(value):
        near = lax.dynamic_slice(value, (y, core * half, 0), (1, half, width))[0]
        away = lax.dynamic_slice(value, (1 - y, core * half, 0), (1, half, width))[0]
        return [near, swap_y(away)]

    ids = lax.dynamic_index_in_dim(segment_ids, y, 0, keepdims=False).reshape(2, 2, 2, half)
    ids = flipped(~first_y, flipped(~first_x, flipped(~first_core, ids, 2), 1), 0)
    ids = ids.transpose(0, 2, 1, 3)
    key_ids = ids.reshape(8 * half, 1)
    query_ids = [ids[k].reshape(1, 4 * half) for k in range(2)]

    def forward(inputs, layer):
        qkv_w, out_w, up_w, down_w = weights[layer]
        attn_gain, mlp_gain = gains[layer][0], gains[layer][1]
        inputs_all = [gather4(value) for value in inputs]
        projected = [dot(value, qkv_w).astype(bf16) for value in inputs_all]
        keys_values = jnp.concatenate(projected, axis=0)
        kept, outputs = [], []
        for k in range(2):
            context, lse = attention_forward(
                projected[k], keys_values, query_ids[k], key_ids, scale
            )
            pre_attn = inputs[k].astype(f32) + scatter4(dot(context, out_w))
            unit_attn, scale_attn = norm_parts(pre_attn)
            normed = unit_attn * attn_gain
            normed_all = gather4(normed.astype(bf16))
            upward = dot(normed_all, up_w)
            phi_whole = 0.5 * (1.0 + lax.erf(upward * (0.5**0.5)))
            activated = (upward * phi_whole).astype(bf16)
            density = jnp.exp(-0.5 * upward * upward) * 0.3989422804014327
            slope = (phi_whole + upward * density).astype(bf16)
            pre_mlp = normed + scatter4(dot(activated, down_w))
            unit_mlp, scale_mlp = norm_parts(pre_mlp)
            outputs.append((unit_mlp * mlp_gain).astype(bf16))
            kept.append(
                (context, lse, unit_attn, scale_attn, normed_all, activated, slope, unit_mlp, scale_mlp)
            )
        return outputs, (inputs_all, projected, keys_values, kept)

    def backward(out_grads, saved, layer):
        qkv_w, out_w, up_w, down_w = weights[layer]
        attn_gain, mlp_gain = gains[layer][0], gains[layer][1]
        inputs_all, projected, keys_values, kept = saved
        attn_gain_grad, mlp_gain_grad, attn_in, query_grads = 0.0, 0.0, [], []
        key_grad, value_grad = 0.0, 0.0
        grad_out, grad_up, grad_down = 0.0, 0.0, 0.0
        for k in range(2):
            context, lse, unit_attn, scale_attn, normed_all, activated, slope, unit_mlp, scale_mlp = kept[k]
            mlp_in, gain_part = norm_back(out_grads[k].astype(f32), unit_mlp, scale_mlp, mlp_gain)
            mlp_gain_grad += gain_part
            down_all = gather4(mlp_in.astype(bf16))
            upward_grad = (times_transposed(down_all, down_w) * slope.astype(f32)).astype(bf16)
            normed_grad = mlp_in + scatter4(times_transposed(upward_grad, up_w))
            attn_grad, gain_part = norm_back(normed_grad, unit_attn, scale_attn, attn_gain)
            attn_gain_grad += gain_part
            attn_in.append(attn_grad)
            branch_all = gather4(attn_grad.astype(bf16))
            context_grad = times_transposed(branch_all, out_w).astype(bf16)
            dq, dk, dv = attention_backward(
                projected[k], keys_values, context_grad, lse, query_ids[k], key_ids, scale
            )
            query_grads.append(dq)
            key_grad += dk
            value_grad += dv
            grad_down += rows_product(activated, down_all)
            grad_up += rows_product(normed_all, upward_grad)
            grad_out += rows_product(context, branch_all)
        key_grad, value_grad = key_grad.astype(bf16), value_grad.astype(bf16)
        in_grads, grad_qkv = [], 0.0
        for k in range(2):
            part = slice(4 * half * k, 4 * half * (k + 1))
            stacked = jnp.concatenate(
                [
                    piece[:, LANES * p : LANES * (p + 1)]
                    for p in range(2)
                    for piece in (query_grads[k], key_grad[part], value_grad[part])
                ],
                axis=1,
            )
            in_grads.append(
                (attn_in[k] + scatter4(times_transposed(stacked, qkv_w))).astype(bf16)
            )
            grad_qkv += rows_product(inputs_all[k], stacked)
        whole = tuple(g.astype(bf16) for g in (grad_qkv, grad_out, grad_up, grad_down))
        return in_grads, whole, jnp.stack([attn_gain_grad, mlp_gain_grad])

    def fold_y(keep, give):
        return (keep.astype(f32) + swap_y(give).astype(f32)).astype(bf16)

    def scatter_rows(value):
        return lax.psum_scatter(value, "fsdp", scatter_dimension=0, tiled=True)

    def spread(value, y_first):
        if y_first:
            pair = jnp.stack([value, swap_y(value)])
            far = swap_x(pair)
            return jnp.stack([pair[0], far[0], pair[1], far[1]])
        pair = jnp.stack([value, swap_x(value)])
        return jnp.concatenate([pair, swap_y(pair)], axis=0)

    def reduce_gradients(whole):
        grad_qkv, grad_out, grad_up, grad_down = whole
        wide_qkv = grad_qkv.shape[1] // 2
        down = scatter_rows(fold_y(grad_down[: fsdp_count * unit], grad_down[fsdp_count * unit :]))
        up = scatter_rows(fold_y(grad_up[:, : fsdp_count * unit], grad_up[:, fsdp_count * unit :]))
        if even_out:
            blocks = grad_out.reshape(2, LANES, width)
            near_cols = flipped(~first_y, blocks, 2)
            pair = fold_y(near_cols[:, :, : width // 2], near_cols[::-1, :, width // 2 :])
            pair = flipped(~first_x, pair, 2)
            cross = swap_x(pair[:, :, wide:])
            keep = pair[:, :, :wide]
            four = jnp.stack([keep[0], keep[1], cross[0], cross[1]])
            order = jnp.stack([chip, chip ^ 2, chip ^ 1, chip ^ 3])
            placed = jnp.where(
                (order[None, :] == jnp.arange(4)[:, None])[:, :, None, None], four[None], 0
            ).sum(axis=1, dtype=bf16)
            out = scatter_rows(placed.reshape(4 * LANES, wide))
        else:
            blocks = grad_out.reshape(2, LANES, width)
            place = jnp.zeros((4, 2, LANES, width), bf16)
            place = lax.dynamic_update_slice(place, blocks[:1, None], (chip, core, 0, 0))
            place = lax.dynamic_update_slice(place, blocks[1:, None], (chip ^ 2, core, 0, 0))
            out = scatter_rows(lax.psum(place.reshape(width, width), ("section", "ctx")))
        qkv = scatter_rows(fold_y(grad_qkv[:, :wide_qkv], grad_qkv[:, wide_qkv:]))
        spread_out = spread(out, True) if even_out else out
        return [spread(qkv, False), spread_out, spread(up, False), spread(down, True)]

    inputs = own_rows(tokens)
    out_grads = own_rows(cotangent)
    hidden0, saved0 = forward(inputs, 0)
    hidden1, saved1 = forward(hidden0, 1)
    in_grads1, whole1, gain_grads1 = backward(out_grads, saved1, 1)
    pieces1 = reduce_gradients(whole1)
    in_grads0, whole0, gain_grads0 = backward(in_grads1, saved0, 0)
    pieces0 = reduce_gradients(whole0)

    def to_owner(layer0, layer1):
        pairs = [jnp.stack([runs[0], swap_y(runs[1])]) for runs in (layer0, layer1)]
        keep = jnp.where(first_core, pairs[0], pairs[1])
        take = swap_core(jnp.where(first_core, pairs[1], pairs[0]))
        both = flipped(~first_core, jnp.stack([keep, take], axis=1), 1)
        return flipped(~first_y, both, 0).reshape(2, block, width)

    hidden_out = to_owner(hidden0, hidden1)
    in_grads_out = to_owner(in_grads0, in_grads1)

    def own_layer(piece0, piece1):
        keep = jnp.where(first_core, piece0, piece1)
        take = swap_core(jnp.where(first_core, piece1, piece0))
        both = jnp.stack([keep, take], axis=1)
        shape = both.shape
        both = both.reshape((2, 2, 2) + shape[2:])
        both = flipped(~first_y, flipped(~first_x, flipped(~first_core, both, 2), 1), 0)
        return both.reshape((8,) + shape[2:])

    natural = own_layer(pieces0[0], pieces1[0]).reshape(8, rows, 3, LANES)
    shard_qkv = natural.transpose(1, 2, 0, 3).reshape(rows, 3 * width).astype(f32)
    if even_out:
        natural = own_layer(pieces0[1], pieces1[1]).reshape(4, 2, LANES, wide)
        shard_out = natural.transpose(1, 2, 0, 3).reshape(2 * LANES, width).astype(f32)
    else:
        shard_out = jnp.where(first_core, pieces0[1], pieces1[1]).astype(f32)
    natural = own_layer(pieces0[2], pieces1[2]).reshape(8, rows, fsdp_count, unit)
    shard_up = natural.transpose(1, 2, 0, 3).reshape(rows, hidden_width).astype(f32)
    shard_down = own_layer(pieces0[3], pieces1[3]).reshape(8 * unit, width).astype(f32)

    gain_all = lax.psum(jnp.stack([gain_grads0, gain_grads1]), ("section", "ctx", "fsdp"))
    gain_own = jnp.where(first_core, gain_all[0], gain_all[1])
    gain_shard = lax.dynamic_slice(gain_own, (0, depth * rows), (2, rows))
    shard_attn, shard_mlp = gain_shard[0], gain_shard[1]
    masters = (w_qkv[0], w_out[0], w_up[0], w_down[0])
    gradients = (shard_qkv, shard_out, shard_up, shard_down)
    rows_old = (row_qkv[0], row_out[0], row_up[0], row_down[0])
    cols_old = (col_qkv[0], col_out[0], col_up[0], col_down[0])
    squares = [gradient * gradient for gradient in gradients]
    rows_new = [
        decay_rate * old_row + (1.0 - decay_rate) * jnp.mean(square, axis=1)
        for old_row, square in zip(rows_old, squares)
    ]
    row_counts = [gradient.shape[0] * fsdp_count for gradient in gradients]
    col_partial = [jnp.sum(square, axis=0) for square in squares]
    row_totals = jnp.stack([jnp.sum(row_value) for row_value in rows_new])
    weight_totals = jnp.stack(
        [jnp.sum(master * master) for master in masters]
        + [jnp.sum(gain_attn[0] * gain_attn[0]), jnp.sum(gain_mlp[0] * gain_mlp[0])]
    )
    moment_attn = decay_rate * var_attn[0] + (1.0 - decay_rate) * shard_attn * shard_attn
    moment_mlp = decay_rate * var_mlp[0] + (1.0 - decay_rate) * shard_mlp * shard_mlp
    gain_updates = (shard_attn * lax.rsqrt(moment_attn), shard_mlp * lax.rsqrt(moment_mlp))
    vector_totals = jnp.stack([jnp.sum(gain_step * gain_step) for gain_step in gain_updates])
    totals = lax.psum(
        jnp.concatenate(col_partial + [row_totals, weight_totals, vector_totals]), "fsdp"
    )
    col_sums, start = [], 0
    for partial in col_partial:
        col_sums.append(totals[start : start + partial.shape[0]])
        start += partial.shape[0]
    row_all, weight_all, vector_all = (
        totals[start : start + 4],
        totals[start + 4 : start + 10],
        totals[start + 10 :],
    )
    cols_new = [
        decay_rate * cols_old[matrix_pos]
        + (1.0 - decay_rate) * col_sums[matrix_pos] / row_counts[matrix_pos]
        for matrix_pos in range(4)
    ]
    updates = [
        gradients[matrix_pos]
        * lax.rsqrt(
            rows_new[matrix_pos][:, None]
            * cols_new[matrix_pos][None, :]
            / (row_all[matrix_pos] / row_counts[matrix_pos])
        )
        for matrix_pos in range(4)
    ]
    update_all = lax.psum(jnp.stack([jnp.sum(update * update) for update in updates]), "fsdp")
    fresh_masters = []
    ratios = []
    for matrix_pos in range(4):
        entry_count = row_counts[matrix_pos] * gradients[matrix_pos].shape[1]
        clip_ratio = jnp.sqrt(update_all[matrix_pos] / entry_count)
        weight_scale = jnp.sqrt(weight_all[matrix_pos] / entry_count + weight_eps)
        fresh_masters.append(
            masters[matrix_pos]
            - step_rate
            * weight_scale
            * updates[matrix_pos]
            / jnp.maximum(1.0, clip_ratio / clip_level)
        )
        ratios.append(clip_ratio)
    gain_masters = (gain_attn[0], gain_mlp[0])
    gain_count = shard_attn.shape[0] * fsdp_count
    for gain_pos in range(2):
        clip_ratio = jnp.sqrt(vector_all[gain_pos] / gain_count)
        weight_scale = jnp.sqrt(weight_all[4 + gain_pos] / gain_count + weight_eps)
        fresh_masters.append(
            gain_masters[gain_pos]
            - step_rate
            * weight_scale
            * gain_updates[gain_pos]
            / jnp.maximum(1.0, clip_ratio / clip_level)
        )
        ratios.append(clip_ratio)
    return (
        hidden_out[None],
        in_grads_out[None],
        shard_qkv[None],
        shard_out[None],
        shard_up[None],
        shard_down[None],
        shard_attn[None],
        shard_mlp[None],
        fresh_masters[0][None],
        fresh_masters[1][None],
        fresh_masters[2][None],
        fresh_masters[3][None],
        fresh_masters[4][None],
        fresh_masters[5][None],
        rows_new[0][None],
        cols_new[0][None],
        rows_new[1][None],
        cols_new[1][None],
        rows_new[2][None],
        cols_new[2][None],
        rows_new[3][None],
        cols_new[3][None],
        moment_attn[None],
        moment_mlp[None],
        jnp.stack(ratios)[None],
    )


def solution(mesh):
    in_specs = (
        P("fsdp", "ctx", None),
        P("fsdp", "ctx", None),
        P("fsdp", None),
        P("section", "fsdp", None),
        P("section", "fsdp", None),
        P("section", "fsdp", None),
        P("section", "fsdp", None),
        P("section", "fsdp"),
        P("section", "fsdp"),
        P("section", "fsdp"),
        P("section", None),
        P("section", "fsdp"),
        P("section", None),
        P("section", "fsdp"),
        P("section", None),
        P("section", "fsdp"),
        P("section", None),
        P("section", "fsdp"),
        P("section", "fsdp"),
    )
    out_specs = (
        P("section", "fsdp", "ctx", None),
        P("section", "fsdp", "ctx", None),
        P("section", "fsdp", None),
        P("section", "fsdp", None),
        P("section", "fsdp", None),
        P("section", "fsdp", None),
        P("section", "fsdp"),
        P("section", "fsdp"),
        P("section", "fsdp", None),
        P("section", "fsdp", None),
        P("section", "fsdp", None),
        P("section", "fsdp", None),
        P("section", "fsdp"),
        P("section", "fsdp"),
        P("section", "fsdp"),
        P("section", None),
        P("section", "fsdp"),
        P("section", None),
        P("section", "fsdp"),
        P("section", None),
        P("section", "fsdp"),
        P("section", None),
        P("section", "fsdp"),
        P("section", "fsdp"),
        P("section", None),
    )
    return jax.shard_map(
        per_device, mesh=mesh, in_specs=in_specs, out_specs=out_specs, check_vma=False
    )
```

time: 2120 us -> 980 us (0.46)
  waiting for transfers between devices: 1360 us -> 268 us
  matrix products: 260 us -> 90.8 us
  starting transfers between devices: 6.85 us -> 102 us
  blocking collectives: 66.4 us -> 156 us
  Pallas kernels: 0 us -> 66.3 us
  other arithmetic: 221 us -> 157 us
  local copies, waits for them, and re-layouts: 148 us -> 102 us
    reduce_scatter x10 -> x8, waiting for transfers between devices: 658 us -> 0.09 us  [scatter_rows(): return lax.psum_scatter(value, 'fsdp', scatter_dimension=0, tiled=True)]
    all_gather x10 -> x4, waiting for transfers between devices: 581 us -> 11 us  [gather_rows(): return lax.all_gather(value, 'fsdp', axis=0, tiled=True)]
    ppermute x4 -> x117, waiting for transfers between devices: 14.7 us -> 257 us  [the longest x30 138 us: swap_y(): return lax.ppermute(value, 'ctx', [(i, i ^ 2) for i in range(4)])]
    dot_general x22 -> x16, matrix products: 154 us -> 27.6 us  [dot(): return jnp.dot(left, right, preferred_element_type=f32)]
    psum x1 -> x0, waiting for transfers between devices: 106 us -> none  [per_device(): lax.psum(shard_qkv.astype(jnp.bfloat16), 'ctx').astype(jnp.float32)]
    ppermute x4 -> x117, starting transfers between devices: 5.81 us -> 100 us  [the longest x44 56.3 us: swap_x(): return lax.ppermute(value, 'ctx', [(i, i ^ 1) for i in range(4)])]
    dynamic_update_slice x48 -> x0, other arithmetic: 71.2 us -> none  [update_one(): lax.dynamic_update_index_in_dim(buffer, jnp.where(slot_live, entry, curre...]
    pallas_call x0 -> x8, Pallas kernels: none -> 66.3 us  [the longest x4 39.3 us: attention_backward(): pl.pallas_call(functools.partial(attention_back_kernel, scale=scale), gri...]
  transfers between devices with their start and end apart: 25 -> 129, of which waited for: 23 -> 54; matrix products, arithmetic and copies ran while one was open for 11% -> 27% of each run, Pallas kernels for 0% -> 7%
where the time goes in v1:
time: 980 us; the launch traced here: 971 us
  waiting for transfers between devices  268 us (27%)
  other arithmetic  157 us (16%)
  blocking collectives  156 us (16%)
  local copies, waits for them, and re-layouts  102 us (10%)
  starting transfers between devices  102 us (10%)
  matrix products  90.8 us (9%)
  Pallas kernels  66.3 us (7%)
  between operations  29.8 us (3%)
    ppermute x30, waiting for transfers between devices, swap_y(): return lax.ppermute(value, 'ctx', [(i, i ^ 2) for i in range(4)])  138 us
    ppermute x44, waiting for transfers between devices, swap_x(): return lax.ppermute(value, 'ctx', [(i, i ^ 1) for i in range(4)])  111 us
    all_gather x4, blocking collectives, gather_rows(): return lax.all_gather(value, 'fsdp', axis=0, tiled=True)  72.4 us
    ppermute x44, starting transfers between devices, swap_x(): return lax.ppermute(value, 'ctx', [(i, i ^ 1) for i in range(4)])  56.3 us
    unnamed x467, local copies, waits for them, and re-layouts  45.9 us
    psum x1, blocking collectives, per_device(): lax.psum(jnp.stack([gain_grads0, gain_grads1]), ('section', 'ctx', 'fsdp'))  44.7 us
    pallas_call x4, Pallas kernels, attention_backward(): pl.pallas_call(functools.partial(attention_back_kernel, scale=scale), gri...  39.3 us
    ppermute x30, starting transfers between devices, swap_y(): return lax.ppermute(value, 'ctx', [(i, i ^ 2) for i in range(4)])  38.6 us
  transfers between devices with their start and end apart: 129, of which 54 were waited for; matrix products, arithmetic and copies ran while one was open for 27% of the time, Pallas kernels for 7%

profile of v1, /device:TPU:0, one launch (start us, length us, event | category | flops | bytes accessed | tf_op | source)
XLA Modules:
  0.0 971.5 jit_solution(13328607477223219731)
XLA Ops:
  11.4 3.6 copy.237
  20.7 11.2 %all_gather.29 = bf16[2,1024]{1,0:T(2,128)(2,1)S(1)} all-gather(bf16[2,256]{1,0:T(2,128)(2,1)S(1)} %pad_maximum_fusion.80), channel_id=1, replica_groups=mesh['section'=2,'ctx'=4,'fsdp'=4] {'fsdp'}, dimensions={1}, use_global_device_ids=true | all-gather | bytes 5120 | tf_op jit(solution)/shard_map/all_gather | solution.py:264
  32.0 5.6 copy.241
  39.8 14.3 %all_gather.28 = bf16[512,256]{1,0:T(8,128)(2,1)S(1)} all-gather(bf16[128,256]{1,0:T(8,128)(2,1)S(1)} %get-tuple-element.265), channel_id=1, replica_groups=mesh['section'=2,'ctx'=4,'fsdp'=4] {'fsdp'}, dimensions={0}, use_global_device_ids=true | all-gather | bytes 327680 | tf_op jit(solution)/shard_map/all_gather | solution.py:274
  61.6 17.9 %all_gather.27 = bf16[1024,384]{0,1:T(8,128)(2,1)S(1)} all-gather(bf16[256,384]{0,1:T(8,128)(2,1)S(1)} %get-tuple-element.311), channel_id=1, replica_groups=mesh['section'=2,'ctx'=4,'fsdp'=4] {'fsdp'}, dimensions={0}, use_global_device_ids=true | all-gather | bytes 983040 | tf_op jit(solution)/shard_map/all_gather | solution.py:274
  84.8 5.9 collective-permute-done.5
  90.8 7.4 collective-permute-done.3
  106.1 6.8 attention_forward.4
  119.5 6.8 attention_forward.5
  132.8 10.7 %all-gather.7.cloned.1.call-done = bf16[512,1024]{1,0:T(8,128)(2,1)} async-done(((bf16[128,1024]{1,0:T(8,128)(2,1)}), bf16[512,1024]{1,0:T(8,128)(2,1)}) %all-gather.7.cloned.1.call-update) | async-done | bytes 1048592 | tf_op jit(solution)/shard_map/all_gather | solution.py:274
  147.8 8.0 collective-permute-done.16
  160.5 17.0 %collective-permute-done.18 = bf16[512,1024]{1,0:T(8,128)(2,1)S(1)} collective-permute-done((bf16[512,1024]{1,0:T(8,128)(2,1)}, bf16[512,1024]{1,0:T(8,128)(2,1)S(1)}, u32[]{:S(2)}, u32[]{:S(2)}) %collective-permute-start.18) | collective-permute-done | bytes 1048608 | tf_op jit(solution)/shard_map/ppermute | solution.py:34
  182.7 6.6 collective-permute-done.20
  191.3 6.0 collective-permute-done.26
  205.0 14.1 %all_gather.33 = bf16[512,256]{1,0:T(8,128)(2,1)S(1)} all-gather(bf16[128,256]{1,0:T(8,128)(2,1)S(1)} %get-tuple-element.264), channel_id=1, replica_groups=mesh['section'=2,'ctx'=4,'fsdp'=4] {'fsdp'}, dimensions={0}, use_global_device_ids=true | all-gather | bytes 327680 | tf_op jit(solution)/shard_map/all_gather | solution.py:274
  222.7 4.6 collective-permute-done.29
  231.3 26.1 %all_gather.32 = bf16[1024,384]{0,1:T(8,128)(2,1)S(1)} all-gather(bf16[256,384]{0,1:T(8,128)(2,1)S(1)} %copy-done.133), channel_id=1, replica_groups=mesh['section'=2,'ctx'=4,'fsdp'=4] {'fsdp'}, dimensions={0}, use_global_device_ids=true | all-gather | bytes 983040 | tf_op jit(solution)/shard_map/all_gather | solution.py:274
  271.9 3.6 collective-permute-done.23
  283.9 6.7 attention_forward.6
  300.4 3.5 collective-permute-done.35
  307.5 5.9 collective-permute-done.36
  313.7 9.8 %collective-permute-done.38 = bf16[1024,512]{0,1:T(8,128)(2,1)} collective-permute-done((bf16[1024,512]{0,1:T(8,128)(2,1)}, bf16[1024,512]{0,1:T(8,128)(2,1)}, u32[]{:S(2)}, u32[]{:S(2)}) %collective-permute-start.38) | collective-permute-done | bytes 1048608 | tf_op jit(solution)/shard_map/ppermute | solution.py:34
  324.8 19.9 %collective-permute-done.39 = bf16[512,1024]{1,0:T(8,128)(2,1)S(1)} collective-permute-done((bf16[512,1024]{1,0:T(8,128)(2,1)}, bf16[512,1024]{1,0:T(8,128)(2,1)S(1)}, u32[]{:S(2)}, u32[]{:S(2)}) %collective-permute-start.39) | collective-permute-done | bytes 1048608 | tf_op jit(solution)/shard_map/ppermute | solution.py:34
  350.1 6.7 attention_forward.7
  362.1 4.8 collective-permute-done.51
  379.0 6.0 collective-permute-done.54
  390.8 3.7 collective-permute-done.44
  404.6 5.2 collective-permute-done.47
  414.7 4.1 collective-permute-done.58
  436.4 5.0 fusion.56
  444.4 6.9 collective-permute-done.110
  454.1 4.1 add_convert_fusion.3
  466.5 9.8 %attention_backward.4 = (bf16[512,256]{1,0:T(8,128)(2,1)S(1)}, f32[1024,256]{1,0:T(8,128)S(1)}, f32[1024,256]{1,0:T(8,128)S(1)}) custom-call(bf16[512,768]{1,0:T(8,128)(2,1)S(1)} %copy-done.16, bf16[1024,768]{1,0:T(8,128)(2,1)S(1)} %pad_maximum_fusion.1.k_ref.v_ref, bf16[1024,768]{1,0:T(8,128)(2,1)S(1)} %pad_maximum_fusion.1.k_ref.v_ref, ...), custom_call_target="tpu_custom_call" | custom-call | flops 2684354560 | bytes 6291456 | tf_op jit(solution)/shard_map/attention_backward/pallas_call | solution.py:166
  485.6 9.9 %attention_backward.5 = (bf16[512,256]{1,0:T(8,128)(2,1)S(1)}, f32[1024,256]{1,0:T(8,128)S(1)}, f32[1024,256]{1,0:T(8,128)S(1)}) custom-call(bf16[512,768]{1,0:T(8,128)(2,1)S(1)} %copy-done.14, bf16[1024,768]{1,0:T(8,128)(2,1)S(1)} %pad_maximum_fusion.1.k_ref.v_ref, bf16[1024,768]{1,0:T(8,128)(2,1)S(1)} %pad_maximum_fusion.1.k_ref.v_ref, ...), custom_call_target="tpu_custom_call" | custom-call | flops 2684354560 | bytes 6291456 | tf_op jit(solution)/shard_map/attention_backward/pallas_call | solution.py:166
  526.5 4.9 collective-permute-done.75
  548.6 6.4 collective-permute-done.78
  555.6 4.3 collective-permute-done.72
  567.0 4.0 collective-permute-done.79
  588.1 5.0 collective-permute-done.98
  601.6 4.0 multiply_reduce_fusion.2
  612.5 13.2 %collective-permute-done.113 = bf16[512,1024]{1,0:T(8,128)(2,1)} collective-permute-done((bf16[512,1024]{1,0:T(8,128)(2,1)}, bf16[512,1024]{1,0:T(8,128)(2,1)}, u32[]{:S(2)}, u32[]{:S(2)}) %collective-permute-start.113) | collective-permute-done | bytes 1048608 | tf_op jit(solution)/shard_map/ppermute | solution.py:34
  631.7 3.6 collective-permute-done.111
  641.8 6.2 collective-permute-done.112
  650.1 44.7 %psum.21 = f32[2,2,1024]{2,1,0:T(2,128)S(1)} all-reduce(f32[2,2,1024]{2,1,0:T(2,128)S(1)} %pad_maximum_fusion.79), channel_id=1, replica_groups=mesh['section'=2,'ctx'=4,'fsdp'=4] {'section','ctx','fsdp'}, use_global_device_ids=true, to_apply=%region_50.51 | all-reduce | flops 4096 | bytes 32768 | tf_op jit(solution)/shard_map/psum | solution.py:477
  699.5 9.7 %attention_backward.7 = (bf16[512,256]{1,0:T(8,128)(2,1)S(1)}, f32[1024,256]{1,0:T(8,128)S(1)}, f32[1024,256]{1,0:T(8,128)S(1)}) custom-call(bf16[512,768]{1,0:T(8,128)(2,1)S(1)} %copy-done.11, bf16[1024,768]{1,0:T(8,128)(2,1)S(1)} %pad_maximum_fusion.k_ref.v_ref, bf16[1024,768]{1,0:T(8,128)(2,1)S(1)} %pad_maximum_fusion.k_ref.v_ref, ...), custom_call_target="tpu_custom_call" | custom-call | flops 2684354560 | bytes 6291456 | tf_op jit(solution)/shard_map/attention_backward/pallas_call | solution.py:166
  711.0 9.9 %attention_backward.6 = (bf16[512,256]{1,0:T(8,128)(2,1)S(1)}, f32[1024,256]{1,0:T(8,128)S(1)}, f32[1024,256]{1,0:T(8,128)S(1)}) custom-call(bf16[512,768]{1,0:T(8,128)(2,1)S(1)} %copy-done.9, bf16[1024,768]{1,0:T(8,128)(2,1)S(1)} %pad_maximum_fusion.k_ref.v_ref, bf16[1024,768]{1,0:T(8,128)(2,1)S(1)} %pad_maximum_fusion.k_ref.v_ref, ...), custom_call_target="tpu_custom_call" | custom-call | flops 2684354560 | bytes 6291456 | tf_op jit(solution)/shard_map/attention_backward/pallas_call | solution.py:166
  737.2 9.4 collective-permute-done.90
  752.2 13.2 %collective-permute-done.100 = bf16[128,256]{1,0:T(8,128)(2,1)S(1)} collective-permute-done((bf16[128,256]{1,0:T(8,128)(2,1)}, bf16[128,256]{1,0:T(8,128)(2,1)S(1)}, u32[]{:S(2)}, u32[]{:S(2)}) %collective-permute-start.100) | collective-permute-done | bytes 65568 | tf_op jit(solution)/shard_map/ppermute | solution.py:34
  774.9 4.0 collective-permute-done.97
  790.3 5.0 collective-permute-done.114
  800.0 10.0 %collective-permute-done.108 = bf16[2,256,512]{2,1,0:T(8,128)(2,1)S(1)} collective-permute-done((bf16[2,256,512]{2,1,0:T(8,128)(2,1)S(1)}, bf16[2,256,512]{2,1,0:T(8,128)(2,1)S(1)}, u32[]{:S(2)}, u32[]{:S(2)}) %collective-permute-start.108) | collective-permute-done | bytes 524320 | tf_op jit(solution)/shard_map/ppermute | solution.py:34
  815.6 4.5 collective-permute-done.91
  828.8 4.1 collective-permute-done.92
  855.8 5.6 copy.284
  868.4 7.8 concatenate.518
  876.2 19.1 %psum.22 = f32[9228]{0:T(1024)S(1)} all-reduce(f32[9228]{0:T(1024)S(1)} %concatenate.518), channel_id=1, replica_groups=mesh['section'=2,'ctx'=4,'fsdp'=4] {'fsdp'}, use_global_device_ids=true, to_apply=%region_71.72 | all-reduce | flops 9228 | bytes 73824 | tf_op jit(solution)/shard_map/psum | solution.py:501
  912.2 8.3 psum.23
  927.3 5.4 divide_subtract_fusion.1
  932.6 5.6 copy.286
  939.6 3.9 copy.258
  943.5 3.5 copy.283
  947.0 4.7 divide_subtract_fusion.2
  951.7 3.5 copy.285
  956.7 5.6 divide_subtract_fusion
  (1065 shorter events, 414.3 us)
Async XLA Ops:
  7.2 122.2 %all-gather.5.cloned.1.call-start = ((), (), s32[]{:S(2)}) async-start(), calls=%async_computation.8 | async-start | bytes 1310720 | tf_op jit(solution)/shard_map/all_gather | solution.py:274
  8.4 73.6 %collective-permute-start.4 = (bf16[128,1024]{1,0:T(8,128)(2,1)S(1)}, bf16[128,1024]{1,0:T(8,128)(2,1)S(1)}, u32[]{:S(2)}, u32[]{:S(2)}) collective-permute-start(bf16[128,1024]{1,0:T(8,128)(2,1)S(1)} %get-tuple-element.271), channel_id=1, source_target_pairs={{0,8},{4,12},{8,0},{12,4},{1,9},{5,13},{9,1},{13,5},{2,10},{6,14},... | collective-permute-start | bytes 786440 | tf_op jit(solution)/shard_map/ppermute | solution.py:34
  16.8 44.1 %collective-permute-start.2 = (bf16[256,384]{0,1:T(8,128)(2,1)}, bf16[256,384]{0,1:T(8,128)(2,1)S(1)}, u32[]{:S(2)}, u32[]{:S(2)}) collective-permute-start(bf16[256,384]{0,1:T(8,128)(2,1)} %bitcast.3), channel_id=1, source_target_pairs={{0,16},{16,0},{1,17},{17,1},{2,18},{18,2},{3,19},{19,3},{4,20},{20... | collective-permute-start | bytes 589832 | tf_op jit(solution)/shard_map/ppermute | solution.py:26
  16.8 64.3 %collective-permute-start = (bf16[128,1024]{1,0:T(8,128)(2,1)S(1)}, bf16[128,1024]{1,0:T(8,128)(2,1)S(1)}, u32[]{:S(2)}, u32[]{:S(2)}) collective-permute-start(bf16[128,1024]{1,0:T(8,128)(2,1)S(1)} %get-tuple-element.270), channel_id=1, source_target_pairs={{0,4},{4,0},{8,12},{12,8},{1,5},{5,1},{9,13},{13,9},{2,6},{6,2},{1... | collective-permute-start | bytes 786440 | tf_op jit(solution)/shard_map/ppermute | solution.py:30
  19.2 19.7 %collective-permute-start.7 = (bf16[128,256]{1,0:T(8,128)(2,1)S(1)}, bf16[128,256]{1,0:T(8,128)(2,1)S(1)}, u32[]{:S(2)}, u32[]{:S(2)}) collective-permute-start(bf16[128,256]{1,0:T(8,128)(2,1)S(1)} %fusion.66), channel_id=1, source_target_pairs={{0,16},{16,0},{1,17},{17,1},{2,18},{18,2},{3,19},{19,3},{4,20},{20... | collective-permute-start | bytes 196616 | tf_op jit(solution)/shard_map/ppermute | solution.py:26
  31.9 83.3 %collective-permute-start.12 = (bf16[2,1024]{1,0:T(2,128)(2,1)S(1)}, bf16[2,1024]{1,0:T(2,128)(2,1)S(1)}, u32[]{:S(2)}, u32[]{:S(2)}) collective-permute-start(bf16[2,1024]{1,0:T(2,128)(2,1)S(1)} %all_gather.29), channel_id=1, source_target_pairs={{0,16},{16,0},{1,17},{17,1},{2,18},{18,2},{3,19},{19,3},{4,20},{20... | collective-permute-start | bytes 12296 | tf_op jit(solution)/shard_map/ppermute | solution.py:26
  59.2 23.2 %collective-permute-start.15 = (bf16[256,512]{0,1:T(8,128)(2,1)S(1)}, bf16[256,512]{0,1:T(8,128)(2,1)}, u32[]{:S(2)}, u32[]{:S(2)}) collective-permute-start(bf16[256,512]{0,1:T(8,128)(2,1)S(1)} %bitcast.468), channel_id=1, source_target_pairs={{0,16},{16,0},{1,17},{17,1},{2,18},{18,2},{3,19},{19,3},{4,20},{20... | collective-permute-start | bytes 786440 | tf_op jit(solution)/shard_map/ppermute | solution.py:26
  79.6 18.7 %collective-permute-start.3 = (bf16[1024,384]{0,1:T(8,128)(2,1)S(1)}, bf16[1024,384]{0,1:T(8,128)(2,1)}, u32[]{:S(2)}, u32[]{:S(2)}) collective-permute-start(bf16[1024,384]{0,1:T(8,128)(2,1)S(1)} %all_gather.27), channel_id=1, source_target_pairs={{0,8},{4,12},{8,0},{12,4},{1,9},{5,13},{9,1},{13,5},{2,10},{6,14},... | collective-permute-start | bytes 2359304 | tf_op jit(solution)/shard_map/ppermute | solution.py:34
  81.1 34.1 %collective-permute-start.17 = (bf16[128,1024]{1,0:T(8,128)(2,1)}, bf16[128,1024]{1,0:T(8,128)(2,1)}, u32[]{:S(2)}, u32[]{:S(2)}) collective-permute-start(bf16[128,1024]{1,0:T(8,128)(2,1)} %fusion.64), channel_id=1, source_target_pairs={{0,16},{16,0},{1,17},{17,1},{2,18},{18,2},{3,19},{19,3},{4,20},{20... | collective-permute-start | bytes 786440 | tf_op jit(solution)/shard_map/ppermute | solution.py:26
  82.0 19.0 %collective-permute-start.1 = (bf16[256,1024]{1,0:T(8,128)(2,1)}, bf16[256,1024]{1,0:T(8,128)(2,1)}, u32[]{:S(2)}, u32[]{:S(2)}) collective-permute-start(bf16[256,1024]{1,0:T(8,128)(2,1)} %pad_maximum_fusion.17), channel_id=1, source_target_pairs={{0,16},{16,0},{1,17},{17,1},{2,18},{18,2},{3,19},{19,3},{4,20},{20... | collective-permute-start | bytes 1572872 | tf_op jit(solution)/shard_map/ppermute | solution.py:26
  84.8 58.7 %all-gather.7.cloned.1.call-start = ((), (), s32[]{:S(2)}) async-start(), calls=%async_computation.9 | async-start | bytes 1310720 | tf_op jit(solution)/shard_map/all_gather | solution.py:274
  98.3 14.6 %collective-permute-start.9 = (bf16[2,128,512]{2,1,0:T(8,128)(2,1)}, bf16[2,128,512]{2,1,0:T(8,128)(2,1)S(1)}, u32[]{:S(2)}, u32[]{:S(2)}) collective-permute-start(bf16[2,128,512]{2,1,0:T(8,128)(2,1)} %rev.12), channel_id=1, source_target_pairs={{0,8},{4,12},{8,0},{12,4},{1,9},{5,13},{9,1},{13,5},{2,10},{6,14},... | collective-permute-start | bytes 786440 | tf_op jit(solution)/shard_map/ppermute | solution.py:34
  117.3 179.8 %all-gather.9.cloned.1.call-start = ((), (), s32[]{:S(2)}) async-start(), calls=%async_computation.10 | async-start | bytes 1310720 | tf_op jit(solution)/shard_map/all_gather | solution.py:274
  127.7 17.3 %collective-permute-start.24 = (bf16[256,1024]{1,0:T(8,128)(2,1)}, bf16[256,1024]{1,0:T(8,128)(2,1)}, u32[]{:S(2)}, u32[]{:S(2)}) collective-permute-start(bf16[256,1024]{1,0:T(8,128)(2,1)} %slice.786), channel_id=1, source_target_pairs={{0,16},{16,0},{1,17},{17,1},{2,18},{18,2},{3,19},{19,3},{4,20},{20... | collective-permute-start | bytes 1572872 | tf_op jit(solution)/shard_map/ppermute | solution.py:26
  129.4 26.4 %collective-permute-start.16 = (bf16[1024,512]{0,1:T(8,128)(2,1)}, bf16[1024,512]{0,1:T(8,128)(2,1)}, u32[]{:S(2)}, u32[]{:S(2)}) collective-permute-start(bf16[1024,512]{0,1:T(8,128)(2,1)} %all-gather.5.cloned.1.call-done), channel_id=1, source_target_pairs={{0,8},{4,12},{8,0},{12,4},{1,9},{5,13},{9,1},{13,5},{2,10},{6,14},... | collective-permute-start | bytes 3145736 | tf_op jit(solution)/shard_map/ppermute | solution.py:34
  131.2 13.7 %collective-permute-start.13 = (bf16[128,1024]{1,0:T(8,128)(2,1)S(1)}, bf16[128,1024]{1,0:T(8,128)(2,1)S(1)}, u32[]{:S(2)}, u32[]{:S(2)}) collective-permute-start(bf16[128,1024]{1,0:T(8,128)(2,1)S(1)} %multiply_convert_fusion.15), channel_id=1, source_target_pairs={{0,4},{4,0},{8,12},{12,8},{1,5},{5,1},{9,13},{13,9},{2,6},{6,2},{1... | collective-permute-start | bytes 786440 | tf_op jit(solution)/shard_map/ppermute | solution.py:30
  143.4 34.1 %collective-permute-start.18 = (bf16[512,1024]{1,0:T(8,128)(2,1)}, bf16[512,1024]{1,0:T(8,128)(2,1)S(1)}, u32[]{:S(2)}, u32[]{:S(2)}) collective-permute-start(bf16[512,1024]{1,0:T(8,128)(2,1)} %all-gather.7.cloned.1.call-done), channel_id=1, source_target_pairs={{0,8},{4,12},{8,0},{12,4},{1,9},{5,13},{9,1},{13,5},{2,10},{6,14},... | collective-permute-start | bytes 3145736 | tf_op jit(solution)/shard_map/ppermute | solution.py:34
  146.1 32.9 %collective-permute-start.25 = (bf16[128,1024]{1,0:T(8,128)(2,1)S(1)}, bf16[128,1024]{1,0:T(8,128)(2,1)S(1)}, u32[]{:S(2)}, u32[]{:S(2)}) collective-permute-start(bf16[128,1024]{1,0:T(8,128)(2,1)S(1)} %add_convert_fusion.35), channel_id=1, source_target_pairs={{0,4},{4,0},{8,12},{12,8},{1,5},{5,1},{9,13},{13,9},{2,6},{6,2},{1... | collective-permute-start | bytes 786440 | tf_op jit(solution)/shard_map/ppermute | solution.py:30
  204.8 15.0 %collective-permute-start.28 = (bf16[256,1024]{1,0:T(8,128)(2,1)}, bf16[256,1024]{1,0:T(8,128)(2,1)}, u32[]{:S(2)}, u32[]{:S(2)}) collective-permute-start(bf16[256,1024]{1,0:T(8,128)(2,1)} %slice.791), channel_id=1, source_target_pairs={{0,16},{16,0},{1,17},{17,1},{2,18},{18,2},{3,19},{19,3},{4,20},{20... | collective-permute-start | bytes 1572872 | tf_op jit(solution)/shard_map/ppermute | solution.py:26
  219.8 79.2 %all-gather.11.cloned.1.call-start = ((), (), s32[]{:S(2)}) async-start(), calls=%async_computation.11 | async-start | bytes 1310720 | tf_op jit(solution)/shard_map/all_gather | solution.py:274
  229.8 33.1 %collective-permute-start.21 = (bf16[128,1024]{1,0:T(8,128)(2,1)S(1)}, bf16[128,1024]{1,0:T(8,128)(2,1)S(1)}, u32[]{:S(2)}, u32[]{:S(2)}) collective-permute-start(bf16[128,1024]{1,0:T(8,128)(2,1)S(1)} %get-tuple-element.367), channel_id=1, source_target_pairs={{0,4},{4,0},{8,12},{12,8},{1,5},{5,1},{9,13},{13,9},{2,6},{6,2},{1... | collective-permute-start | bytes 786440 | tf_op jit(solution)/shard_map/ppermute | solution.py:30
  257.4 18.1 %collective-permute-start.23 = (bf16[1024,384]{0,1:T(8,128)(2,1)S(1)}, bf16[1024,384]{0,1:T(8,128)(2,1)}, u32[]{:S(2)}, u32[]{:S(2)}) collective-permute-start(bf16[1024,384]{0,1:T(8,128)(2,1)S(1)} %all_gather.32), channel_id=1, source_target_pairs={{0,8},{4,12},{8,0},{12,4},{1,9},{5,13},{9,1},{13,5},{2,10},{6,14},... | collective-permute-start | bytes 2359304 | tf_op jit(solution)/shard_map/ppermute | solution.py:34
  263.8 13.8 %collective-permute-start.22 = (bf16[256,1024]{1,0:T(8,128)(2,1)}, bf16[256,1024]{1,0:T(8,128)(2,1)}, u32[]{:S(2)}, u32[]{:S(2)}) collective-permute-start(bf16[256,1024]{1,0:T(8,128)(2,1)} %pad_maximum_fusion.20), channel_id=1, source_target_pairs={{0,16},{16,0},{1,17},{17,1},{2,18},{18,2},{3,19},{19,3},{4,20},{20... | collective-permute-start | bytes 1572872 | tf_op jit(solution)/shard_map/ppermute | solution.py:26
  266.6 24.0 %collective-permute-start.33 = (bf16[2,128,512]{2,1,0:T(8,128)(2,1)}, bf16[2,128,512]{2,1,0:T(8,128)(2,1)}, u32[]{:S(2)}, u32[]{:S(2)}) collective-permute-start(bf16[2,128,512]{2,1,0:T(8,128)(2,1)} %rev.13), channel_id=1, source_target_pairs={{0,8},{4,12},{8,0},{12,4},{1,9},{5,13},{9,1},{13,5},{2,10},{6,14},... | collective-permute-start | bytes 786440 | tf_op jit(solution)/shard_map/ppermute | solution.py:34
  271.7 338.9 %reduce-scatter.21.cloned.1.call-start = ((), (), s32[]{:S(2)}) async-start(), calls=%async_computation.18 | async-start | bytes 1310720 | tf_op jit(solution)/shard_map/reduce_scatter | solution.py:400
  297.1 26.4 %collective-permute-start.38 = (bf16[1024,512]{0,1:T(8,128)(2,1)}, bf16[1024,512]{0,1:T(8,128)(2,1)}, u32[]{:S(2)}, u32[]{:S(2)}) collective-permute-start(bf16[1024,512]{0,1:T(8,128)(2,1)} %all-gather.9.cloned.1.call-done), channel_id=1, source_target_pairs={{0,8},{4,12},{8,0},{12,4},{1,9},{5,13},{9,1},{13,5},{2,10},{6,14},... | collective-permute-start | bytes 3145736 | tf_op jit(solution)/shard_map/ppermute | solution.py:34
  298.9 45.8 %collective-permute-start.39 = (bf16[512,1024]{1,0:T(8,128)(2,1)}, bf16[512,1024]{1,0:T(8,128)(2,1)S(1)}, u32[]{:S(2)}, u32[]{:S(2)}) collective-permute-start(bf16[512,1024]{1,0:T(8,128)(2,1)} %all-gather.11.cloned.1.call-done), channel_id=1, source_target_pairs={{0,8},{4,12},{8,0},{12,4},{1,9},{5,13},{9,1},{13,5},{2,10},{6,14},... | collective-permute-start | bytes 3145736 | tf_op jit(solution)/shard_map/ppermute | solution.py:34
  313.5 31.4 %collective-permute-start.37 = (bf16[256,1024]{1,0:T(8,128)(2,1)S(1)}, bf16[256,1024]{1,0:T(8,128)(2,1)S(1)}, u32[]{:S(2)}, u32[]{:S(2)}) collective-permute-start(bf16[256,1024]{1,0:T(8,128)(2,1)S(1)} %pad_maximum_fusion.23), channel_id=1, source_target_pairs={{0,16},{16,0},{1,17},{17,1},{2,18},{18,2},{3,19},{19,3},{4,20},{20... | collective-permute-start | bytes 1572872 | tf_op jit(solution)/shard_map/ppermute | solution.py:26
  389.2 21.2 %collective-permute-start.57 = (bf16[128,1024]{1,0:T(8,128)(2,1)S(1)}, bf16[128,1024]{1,0:T(8,128)(2,1)S(1)}, u32[]{:S(2)}, u32[]{:S(2)}) collective-permute-start(bf16[128,1024]{1,0:T(8,128)(2,1)S(1)} %dynamic-slice_bitcast_fusion), channel_id=1, source_target_pairs={{0,8},{4,12},{8,0},{12,4},{1,9},{5,13},{9,1},{13,5},{2,10},{6,14},... | collective-permute-start | bytes 786440 | tf_op jit(solution)/shard_map/ppermute | solution.py:34
  419.5 14.7 %collective-permute-start.55 = (bf16[128,1024]{1,0:T(8,128)(2,1)}, bf16[128,1024]{1,0:T(8,128)(2,1)}, u32[]{:S(2)}, u32[]{:S(2)}) collective-permute-start(bf16[128,1024]{1,0:T(8,128)(2,1)} %get-tuple-element.224), channel_id=1, source_target_pairs={{0,4},{4,0},{8,12},{12,8},{1,5},{5,1},{9,13},{13,9},{2,6},{6,2},{1... | collective-permute-start | bytes 786440 | tf_op jit(solution)/shard_map/ppermute | solution.py:30
  425.1 26.3 %collective-permute-start.110 = (bf16[512,1024]{1,0:T(8,128)(2,1)}, bf16[512,1024]{1,0:T(8,128)(2,1)}, u32[]{:S(2)}, u32[]{:S(2)}) collective-permute-start(bf16[512,1024]{1,0:T(8,128)(2,1)} %slice.894), channel_id=1, source_target_pairs={{0,8},{4,12},{8,0},{12,4},{1,9},{5,13},{9,1},{13,5},{2,10},{6,14},... | collective-permute-start | bytes 3145736 | tf_op jit(solution)/shard_map/ppermute | solution.py:34
  433.8 130.2 %collective-permute-start.49 = (bf16[128,1024]{1,0:T(8,128)(2,1)}, bf16[128,1024]{1,0:T(8,128)(2,1)}, u32[]{:S(2)}, u32[]{:S(2)}) collective-permute-start(bf16[128,1024]{1,0:T(8,128)(2,1)} %get-tuple-element.368), channel_id=1, source_target_pairs={{0,8},{4,12},{8,0},{12,4},{1,9},{5,13},{9,1},{13,5},{2,10},{6,14},... | collective-permute-start | bytes 786440 | tf_op jit(solution)/shard_map/ppermute | solution.py:34
  436.2 28.5 %collective-permute-start.56 = (bf16[256,1024]{1,0:T(8,128)(2,1)}, bf16[256,1024]{1,0:T(8,128)(2,1)}, u32[]{:S(2)}, u32[]{:S(2)}) collective-permute-start(bf16[256,1024]{1,0:T(8,128)(2,1)} %pad_maximum_fusion.26), channel_id=1, source_target_pairs={{0,16},{16,0},{1,17},{17,1},{2,18},{18,2},{3,19},{19,3},{4,20},{20... | collective-permute-start | bytes 1572872 | tf_op jit(solution)/shard_map/ppermute | solution.py:26
  443.2 16.7 %collective-permute-start.61 = (bf16[128,1024]{1,0:T(8,128)(2,1)}, bf16[128,1024]{1,0:T(8,128)(2,1)}, u32[]{:S(2)}, u32[]{:S(2)}) collective-permute-start(bf16[128,1024]{1,0:T(8,128)(2,1)} %add_convert_fusion.28), channel_id=1, source_target_pairs={{0,4},{4,0},{8,12},{12,8},{1,5},{5,1},{9,13},{13,9},{2,6},{6,2},{1... | collective-permute-start | bytes 786440 | tf_op jit(solution)/shard_map/ppermute | solution.py:30
  454.0 157.6 %reduce-scatter.17.cloned.1.call-start = ((), (), s32[]{:S(2)}) async-start(), calls=%async_computation.16 | async-start | bytes 1310720 | tf_op jit(solution)/shard_map/reduce_scatter | solution.py:400
  458.3 23.8 %collective-permute-start.103 = (bf16[1024,512]{1,0:T(8,128)(2,1)S(1)}, bf16[1024,512]{1,0:T(8,128)(2,1)S(1)}, u32[]{:S(2)}, u32[]{:S(2)}) collective-permute-start(bf16[1024,512]{1,0:T(8,128)(2,1)S(1)} %slice.890), channel_id=1, source_target_pairs={{0,8},{4,12},{8,0},{12,4},{1,9},{5,13},{9,1},{13,5},{2,10},{6,14},... | collective-permute-start | bytes 3145736 | tf_op jit(solution)/shard_map/ppermute | solution.py:34
  463.3 14.9 %collective-permute-start.62 = (bf16[128,1024]{1,0:T(8,128)(2,1)S(1)}, bf16[128,1024]{1,0:T(8,128)(2,1)S(1)}, u32[]{:S(2)}, u32[]{:S(2)}) collective-permute-start(bf16[128,1024]{1,0:T(8,128)(2,1)S(1)} %get-tuple-element.227), channel_id=1, source_target_pairs={{0,4},{4,0},{8,12},{12,8},{1,5},{5,1},{9,13},{13,9},{2,6},{6,2},{1... | collective-permute-start | bytes 786440 | tf_op jit(solution)/shard_map/ppermute | solution.py:30
  479.8 85.3 %collective-permute-start.48 = (bf16[128,1024]{1,0:T(8,128)(2,1)}, bf16[128,1024]{1,0:T(8,128)(2,1)}, u32[]{:S(2)}, u32[]{:S(2)}) collective-permute-start(bf16[128,1024]{1,0:T(8,128)(2,1)} %get-tuple-element.273), channel_id=1, source_target_pairs={{0,8},{4,12},{8,0},{12,4},{1,9},{5,13},{9,1},{13,5},{2,10},{6,14},... | collective-permute-start | bytes 786440 | tf_op jit(solution)/shard_map/ppermute | solution.py:34
  483.4 165.6 %reduce-scatter.9.cloned.1.call-start = ((), (), s32[]{:S(2)}) async-start(), calls=%async_computation.12 | async-start | bytes 983040 | tf_op jit(solution)/shard_map/reduce_scatter | solution.py:400
  508.7 25.3 %collective-permute-start.94 = (bf16[2,128,512]{2,1,0:T(8,128)(2,1)}, bf16[2,128,512]{2,1,0:T(8,128)(2,1)S(1)}, u32[]{:S(2)}, u32[]{:S(2)}) collective-permute-start(bf16[2,128,512]{2,1,0:T(8,128)(2,1)} %rev.14), channel_id=1, source_target_pairs={{0,8},{4,12},{8,0},{12,4},{1,9},{5,13},{9,1},{13,5},{2,10},{6,14},... | collective-permute-start | bytes 786440 | tf_op jit(solution)/shard_map/ppermute | solution.py:34
  534.0 44.8 %collective-permute-start.87 = (bf16[1024,384]{1,0:T(8,128)(2,1)S(1)}, bf16[1024,384]{1,0:T(8,128)(2,1)S(1)}, u32[]{:S(2)}, u32[]{:S(2)}) collective-permute-start(bf16[1024,384]{1,0:T(8,128)(2,1)S(1)} %slice.874), channel_id=1, source_target_pairs={{0,8},{4,12},{8,0},{12,4},{1,9},{5,13},{9,1},{13,5},{2,10},{6,14},... | collective-permute-start | bytes 2359304 | tf_op jit(solution)/shard_map/ppermute | solution.py:34
  564.0 13.9 %collective-permute-start.73 = (bf16[128,1024]{1,0:T(8,128)(2,1)S(1)}, bf16[128,1024]{1,0:T(8,128)(2,1)S(1)}, u32[]{:S(2)}, u32[]{:S(2)}) collective-permute-start(bf16[128,1024]{1,0:T(8,128)(2,1)S(1)} %get-tuple-element.216), channel_id=1, source_target_pairs={{0,4},{4,0},{8,12},{12,8},{1,5},{5,1},{9,13},{13,9},{2,6},{6,2},{1... | collective-permute-start | bytes 786440 | tf_op jit(solution)/shard_map/ppermute | solution.py:30
  567.0 39.6 %collective-permute-start.50 = (bf16[2,128,1024]{2,1,0:T(8,128)(2,1)}, bf16[2,128,1024]{2,1,0:T(8,128)(2,1)}, u32[]{:S(2)}, u32[]{:S(2)}) collective-permute-start(bf16[2,128,1024]{2,1,0:T(8,128)(2,1)} %maximum_select_fusion.21), channel_id=1, source_target_pairs={{0,16},{16,0},{1,17},{17,1},{2,18},{18,2},{3,19},{19,3},{4,20},{20... | collective-permute-start | bytes 1572872 | tf_op jit(solution)/shard_map/ppermute | solution.py:26
  579.9 169.9 %reduce-scatter.15.cloned.1.call-start = ((), (), s32[]{:S(2)}) async-start(), calls=%async_computation.15 | async-start | bytes 327680 | tf_op jit(solution)/shard_map/reduce_scatter | solution.py:400
  599.3 26.4 %collective-permute-start.113 = (bf16[512,1024]{1,0:T(8,128)(2,1)}, bf16[512,1024]{1,0:T(8,128)(2,1)}, u32[]{:S(2)}, u32[]{:S(2)}) collective-permute-start(bf16[512,1024]{1,0:T(8,128)(2,1)} %slice.898), channel_id=1, source_target_pairs={{0,8},{4,12},{8,0},{12,4},{1,9},{5,13},{9,1},{13,5},{2,10},{6,14},... | collective-permute-start | bytes 3145736 | tf_op jit(solution)/shard_map/ppermute | solution.py:34
  601.5 150.7 %reduce-scatter.13.cloned.1.call-start = ((), (), s32[]{:S(2)}) async-start(), calls=%async_computation.14 | async-start | bytes 327680 | tf_op jit(solution)/shard_map/reduce_scatter | solution.py:400
  608.1 178.8 %reduce-scatter.23.cloned.1.call-start = ((), (), s32[]{:S(2)}) async-start(), calls=%async_computation.19 | async-start | bytes 1310720 | tf_op jit(solution)/shard_map/reduce_scatter | solution.py:400
  609.6 169.4 %collective-permute-start.68 = (bf16[128,1024]{1,0:T(8,128)(2,1)S(1)}, bf16[128,1024]{1,0:T(8,128)(2,1)}, u32[]{:S(2)}, u32[]{:S(2)}) collective-permute-start(bf16[128,1024]{1,0:T(8,128)(2,1)S(1)} %get-tuple-element.223), channel_id=1, source_target_pairs={{0,8},{4,12},{8,0},{12,4},{1,9},{5,13},{9,1},{13,5},{2,10},{6,14},... | collective-permute-start | bytes 786440 | tf_op jit(solution)/shard_map/ppermute | solution.py:34
  610.6 24.7 %collective-permute-start.111 = (bf16[128,1024]{1,0:T(8,128)(2,1)}, bf16[128,1024]{1,0:T(8,128)(2,1)S(1)}, u32[]{:S(2)}, u32[]{:S(2)}) collective-permute-start(bf16[128,1024]{1,0:T(8,128)(2,1)} %reduce-scatter.21.cloned.1.call-done), channel_id=1, source_target_pairs={{0,8},{4,12},{8,0},{12,4},{1,9},{5,13},{9,1},{13,5},{2,10},{6,14},... | collective-permute-start | bytes 786440 | tf_op jit(solution)/shard_map/ppermute | solution.py:34
  611.6 28.3 %collective-permute-start.104 = (bf16[256,512]{1,0:T(8,128)(2,1)}, bf16[256,512]{1,0:T(8,128)(2,1)}, u32[]{:S(2)}, u32[]{:S(2)}) collective-permute-start(bf16[256,512]{1,0:T(8,128)(2,1)} %reduce-scatter.17.cloned.1.call-done), channel_id=1, source_target_pairs={{0,4},{4,0},{8,12},{12,8},{1,5},{5,1},{9,13},{13,9},{2,6},{6,2},{1... | collective-permute-start | bytes 786440 | tf_op jit(solution)/shard_map/ppermute | solution.py:30
  628.7 158.2 %reduce-scatter.19.cloned.1.call-start = ((), (), s32[]{:S(2)}) async-start(), calls=%async_computation.17 | async-start | bytes 1310720 | tf_op jit(solution)/shard_map/reduce_scatter | solution.py:400
  638.9 55.9 %collective-permute-start.106 = (bf16[1024,512]{1,0:T(8,128)(2,1)}, bf16[1024,512]{1,0:T(8,128)(2,1)S(1)}, u32[]{:S(2)}, u32[]{:S(2)}) collective-permute-start(bf16[1024,512]{1,0:T(8,128)(2,1)} %slice.892), channel_id=1, source_target_pairs={{0,8},{4,12},{8,0},{12,4},{1,9},{5,13},{9,1},{13,5},{2,10},{6,14},... | collective-permute-start | bytes 3145736 | tf_op jit(solution)/shard_map/ppermute | solution.py:34
  649.0 83.2 %collective-permute-start.88 = (bf16[256,384]{1,0:T(8,128)(2,1)}, bf16[256,384]{1,0:T(8,128)(2,1)}, u32[]{:S(2)}, u32[]{:S(2)}) collective-permute-start(bf16[256,384]{1,0:T(8,128)(2,1)} %reduce-scatter.9.cloned.1.call-done), channel_id=1, source_target_pairs={{0,4},{4,0},{8,12},{12,8},{1,5},{5,1},{9,13},{13,9},{2,6},{6,2},{1... | collective-permute-start | bytes 589832 | tf_op jit(solution)/shard_map/ppermute | solution.py:30
  697.3 115.2 %reduce-scatter.11.cloned.1.call-start = ((), (), s32[]{:S(2)}) async-start(), calls=%async_computation.13 | async-start | bytes 983040 | tf_op jit(solution)/shard_map/reduce_scatter | solution.py:400
  725.8 20.9 %collective-permute-start.90 = (bf16[1024,384]{1,0:T(8,128)(2,1)S(1)}, bf16[1024,384]{1,0:T(8,128)(2,1)S(1)}, u32[]{:S(2)}, u32[]{:S(2)}) collective-permute-start(bf16[1024,384]{1,0:T(8,128)(2,1)S(1)} %slice.876), channel_id=1, source_target_pairs={{0,8},{4,12},{8,0},{12,4},{1,9},{5,13},{9,1},{13,5},{2,10},{6,14},... | collective-permute-start | bytes 2359304 | tf_op jit(solution)/shard_map/ppermute | solution.py:34
  732.2 67.8 %collective-permute-start.105 = (bf16[2,256,512]{2,1,0:T(8,128)(2,1)}, bf16[2,256,512]{2,1,0:T(8,128)(2,1)}, u32[]{:S(2)}, u32[]{:S(2)}) collective-permute-start(bf16[2,256,512]{2,1,0:T(8,128)(2,1)} %pad_maximum_fusion.35), channel_id=1, source_target_pairs={{0,8},{4,12},{8,0},{12,4},{1,9},{5,13},{9,1},{13,5},{2,10},{6,14},... | collective-permute-start | bytes 1572872 | tf_op jit(solution)/shard_map/ppermute | solution.py:34
  733.9 94.8 %collective-permute-start.89 = (bf16[2,256,384]{2,1,0:T(8,128)(2,1)}, bf16[2,256,384]{2,1,0:T(8,128)(2,1)}, u32[]{:S(2)}, u32[]{:S(2)}) collective-permute-start(bf16[2,256,384]{2,1,0:T(8,128)(2,1)} %pad_maximum_fusion.69), channel_id=1, source_target_pairs={{0,8},{4,12},{8,0},{12,4},{1,9},{5,13},{9,1},{13,5},{2,10},{6,14},... | collective-permute-start | bytes 1179656 | tf_op jit(solution)/shard_map/ppermute | solution.py:34
  736.1 13.7 %collective-permute-start.82 = (bf16[128,1024]{1,0:T(8,128)(2,1)S(1)}, bf16[128,1024]{1,0:T(8,128)(2,1)}, u32[]{:S(2)}, u32[]{:S(2)}) collective-permute-start(bf16[128,1024]{1,0:T(8,128)(2,1)S(1)} %add_convert_fusion.21), channel_id=1, source_target_pairs={{0,4},{4,0},{8,12},{12,8},{1,5},{5,1},{9,13},{13,9},{2,6},{6,2},{1... | collective-permute-start | bytes 786440 | tf_op jit(solution)/shard_map/ppermute | solution.py:30
  746.6 21.4 %collective-permute-start.84 = (bf16[128,1024]{1,0:T(8,128)(2,1)S(1)}, bf16[128,1024]{1,0:T(8,128)(2,1)}, u32[]{:S(2)}, u32[]{:S(2)}) collective-permute-start(bf16[128,1024]{1,0:T(8,128)(2,1)S(1)} %add_convert_fusion.19), channel_id=1, source_target_pairs={{0,4},{4,0},{8,12},{12,8},{1,5},{5,1},{9,13},{13,9},{2,6},{6,2},{1... | collective-permute-start | bytes 786440 | tf_op jit(solution)/shard_map/ppermute | solution.py:30
  749.8 15.7 %collective-permute-start.100 = (bf16[128,256]{1,0:T(8,128)(2,1)}, bf16[128,256]{1,0:T(8,128)(2,1)S(1)}, u32[]{:S(2)}, u32[]{:S(2)}) collective-permute-start(bf16[128,256]{1,0:T(8,128)(2,1)} %reduce-scatter.15.cloned.1.call-done), channel_id=1, source_target_pairs={{0,8},{4,12},{8,0},{12,4},{1,9},{5,13},{9,1},{13,5},{2,10},{6,14},... | collective-permute-start | bytes 196616 | tf_op jit(solution)/shard_map/ppermute | solution.py:34
  796.2 17.5 %collective-permute-start.115 = (bf16[2,128,1024]{2,1,0:T(8,128)(2,1)}, bf16[2,128,1024]{2,1,0:T(8,128)(2,1)}, u32[]{:S(2)}, u32[]{:S(2)}) collective-permute-start(bf16[2,128,1024]{2,1,0:T(8,128)(2,1)} %pad_maximum_fusion.38), channel_id=1, source_target_pairs={{0,4},{4,0},{8,12},{12,8},{1,5},{5,1},{9,13},{13,9},{2,6},{6,2},{1... | collective-permute-start | bytes 1572872 | tf_op jit(solution)/shard_map/ppermute | solution.py:30
  812.5 24.2 %collective-permute-start.109 = (bf16[4,256,512]{2,1,0:T(8,128)(2,1)}, bf16[4,256,512]{2,1,0:T(8,128)(2,1)}, u32[]{:S(2)}, u32[]{:S(2)}) collective-permute-start(bf16[4,256,512]{2,1,0:T(8,128)(2,1)} %maximum_select_fusion.13), channel_id=1, source_target_pairs={{0,16},{16,0},{1,17},{17,1},{2,18},{18,2},{3,19},{19,3},{4,20},{20... | collective-permute-start | bytes 3145736 | tf_op jit(solution)/shard_map/ppermute | solution.py:26
  824.1 17.5 %collective-permute-start.116 = (bf16[4,128,1024]{2,1,0:T(8,128)(2,1)}, bf16[4,128,1024]{2,1,0:T(8,128)(2,1)}, u32[]{:S(2)}, u32[]{:S(2)}) collective-permute-start(bf16[4,128,1024]{2,1,0:T(8,128)(2,1)} %maximum_select_fusion.15), channel_id=1, source_target_pairs={{0,16},{16,0},{1,17},{17,1},{2,18},{18,2},{3,19},{19,3},{4,20},{20... | collective-permute-start | bytes 3145736 | tf_op jit(solution)/shard_map/ppermute | solution.py:26
  835.1 28.7 %collective-permute-start.93 = (bf16[4,256,384]{2,1,0:T(8,128)(2,1)}, bf16[4,256,384]{2,1,0:T(8,128)(2,1)}, u32[]{:S(2)}, u32[]{:S(2)}) collective-permute-start(bf16[4,256,384]{2,1,0:T(8,128)(2,1)} %maximum_select_fusion.17), channel_id=1, source_target_pairs={{0,16},{16,0},{1,17},{17,1},{2,18},{18,2},{3,19},{19,3},{4,20},{20... | collective-permute-start | bytes 2359304 | tf_op jit(solution)/shard_map/ppermute | solution.py:26
  (284 other events, 2711.9 us)
Sparse Core Ops, SparseCore 0:
  84.9 29.6 all-gather.4
  117.4 25.9 all-gather.6
  219.9 39.7 all-gather.8
  271.8 27.0 all-gather.10
  454.1 27.0 reduce-scatter.20
  484.0 26.3 reduce-scatter.16
  580.0 22.6 reduce-scatter.8
  605.0 18.8 reduce-scatter.14
  626.2 18.0 reduce-scatter.12
  647.0 25.3 reduce-scatter.22
  697.4 27.4 reduce-scatter.18
  749.8 22.5 reduce-scatter.10

commit v2 on v1

v2 whole, which is shorter than its diff:
```python
import functools

import jax
import jax.numpy as jnp
from jax import lax
from jax.experimental import pallas as pl
from jax.experimental.pallas import tpu as pltpu
from jax.sharding import PartitionSpec as P

HEADS = 16


decay_rate = 0.5
clip_level = 0.5
step_rate = 1.0
norm_eps = 1e-05
weight_eps = 1e-06
mask_fill = -1e30

bf16 = jnp.bfloat16
f32 = jnp.float32
LANES = 128


def swap_core(value):
    return lax.ppermute(value, "section", [(0, 1), (1, 0)])


def swap_x(value):
    return lax.ppermute(value, "ctx", [(i, i ^ 1) for i in range(4)])


def swap_y(value):
    return lax.ppermute(value, "ctx", [(i, i ^ 2) for i in range(4)])


def dot(left, right):
    return jnp.dot(left, right, preferred_element_type=f32)


def times_transposed(left, right):
    return lax.dot_general(left, right, (((1,), (1,)), ((), ())), preferred_element_type=f32)


def rows_product(left, right):
    return lax.dot_general(left, right, (((0,), (0,)), ((), ())), preferred_element_type=f32)


def after(value, *tokens):
    return lax.optimization_barrier((value, *tokens))[0]


def gather4(value):
    pair = jnp.concatenate([value, swap_x(value)], axis=0)
    return jnp.concatenate([pair, swap_core(pair)], axis=0)


def fold_core(partial):
    half = partial.shape[0] // 2
    rows = half // 2
    partial = partial.astype(bf16)
    mine, theirs = partial[:half], swap_core(partial[half:])
    keep = mine[:rows].astype(f32) + theirs[:rows].astype(f32)
    return keep, (mine[rows:].astype(f32) + theirs[rows:].astype(f32)).astype(bf16)


def norm_parts(values):
    center = values - jnp.mean(values, axis=-1, keepdims=True)
    spread = jnp.mean(center * center, axis=-1, keepdims=True)
    scale = lax.rsqrt(spread + norm_eps)
    return center * scale, scale


def norm_back(out_grad, unit, scale, gain):
    scaled = out_grad * gain
    mean_scaled = jnp.mean(scaled, axis=-1, keepdims=True)
    mean_unit = jnp.mean(scaled * unit, axis=-1, keepdims=True)
    return scale * (scaled - mean_scaled - unit * mean_unit), jnp.sum(out_grad * unit, axis=0)


def nt(left, right):
    return lax.dot_general(left, right, (((1,), (1,)), ((), ())), preferred_element_type=f32)


def attention_kernel(q_ref, k_ref, v_ref, qid_ref, kid_ref, out_ref, lse_ref, *, scale):
    queries = q_ref[...] * jnp.asarray(scale, bf16)
    keys, values_t = k_ref[...], v_ref[...].T
    same = kid_ref[...] == qid_ref[...]
    first = lax.broadcasted_iota(jnp.int32, queries.shape, 1) < queries.shape[1] // 2
    parts = []
    for head in range(2):
        own = jnp.where(first if head == 0 else ~first, queries, jnp.zeros_like(queries))
        scores = jnp.where(same, nt(keys, own), mask_fill)
        peak = jnp.max(scores, axis=0, keepdims=True)
        weights = jnp.exp(scores - peak)
        total = jnp.sum(weights, axis=0, keepdims=True)
        lse_ref[0, head : head + 1, :] = peak + jnp.log(total)
        parts.append(dot(values_t, weights.astype(bf16)) * (1.0 / total))
    width = values_t.shape[0] // 2
    stacked = jnp.concatenate([parts[0][:width], parts[1][width:]], axis=0)
    out_ref[...] = stacked.T.astype(bf16)


def attention_forward(projected, keys_values, query_ids, key_ids, scale):
    rows, seq_len = projected.shape[0], keys_values.shape[0]
    tile = min(256, rows)
    elems = 4 * rows * seq_len
    return pl.pallas_call(
        functools.partial(attention_kernel, scale=scale),
        grid=(2, rows // tile),
        in_specs=[
            pl.BlockSpec((tile, LANES), lambda p, i: (i, 3 * p)),
            pl.BlockSpec((seq_len, LANES), lambda p, i: (0, 3 * p + 1)),
            pl.BlockSpec((seq_len, LANES), lambda p, i: (0, 3 * p + 2)),
            pl.BlockSpec((1, tile), lambda p, i: (0, i)),
            pl.BlockSpec((seq_len, 1), lambda p, i: (0, 0)),
        ],
        out_specs=[
            pl.BlockSpec((tile, LANES), lambda p, i: (i, p)),
            pl.BlockSpec((1, 2, tile), lambda p, i: (p, 0, i)),
        ],
        out_shape=[
            jax.ShapeDtypeStruct((rows, 2 * LANES), bf16),
            jax.ShapeDtypeStruct((2, 2, rows), f32),
        ],
        compiler_params=pltpu.CompilerParams(vmem_limit_bytes=32 << 20),
        cost_estimate=pl.CostEstimate(
            flops=elems * 4 * 128, bytes_accessed=4 << 20, transcendentals=elems
        ),
        name="attention_forward",
    )(projected, keys_values, keys_values, query_ids, key_ids)


def attention_back_kernel(
    q_ref, k_ref, v_ref, g_ref, lse_ref, qid_ref, kid_ref, dq_ref, dk_ref, dv_ref, *, scale
):
    queries = q_ref[...] * jnp.asarray(scale, bf16)
    keys, values, grads = k_ref[...], v_ref[...], g_ref[...]
    keys_t = keys.T
    same = kid_ref[...] == qid_ref[...]
    first = lax.broadcasted_iota(jnp.int32, queries.shape, 1) < queries.shape[1] // 2

    @pl.when(pl.program_id(1) == 0)
    def _():
        dk_ref[...] = jnp.zeros_like(dk_ref)
        dv_ref[...] = jnp.zeros_like(dv_ref)

    parts = []
    for head in range(2):
        mine = first if head == 0 else ~first
        own = jnp.where(mine, queries, jnp.zeros_like(queries))
        own_grads = jnp.where(mine, grads, jnp.zeros_like(grads))
        scores = jnp.where(same, nt(keys, own), mask_fill)
        weights = jnp.exp(scores - lse_ref[0, head : head + 1, :])
        prob_grad = nt(values, own_grads)
        row_dot = jnp.sum(weights * prob_grad, axis=0, keepdims=True)
        score_grad = (weights * (prob_grad - row_dot)).astype(bf16)
        dv_ref[...] += dot(weights.astype(bf16), own_grads)
        dk_ref[...] += dot(score_grad, own)
        parts.append(dot(keys_t, score_grad))
    width = keys_t.shape[0] // 2
    stacked = jnp.concatenate([parts[0][:width], parts[1][width:]], axis=0)
    dq_ref[...] = (stacked.T * scale).astype(bf16)


def attention_backward(projected, keys_values, grads, lse, query_ids, key_ids, scale):
    rows, seq_len = projected.shape[0], keys_values.shape[0]
    tile = min(256, rows)
    elems = 4 * rows * seq_len
    return pl.pallas_call(
        functools.partial(attention_back_kernel, scale=scale),
        grid=(2, rows // tile),
        in_specs=[
            pl.BlockSpec((tile, LANES), lambda p, i: (i, 3 * p)),
            pl.BlockSpec((seq_len, LANES), lambda p, i: (0, 3 * p + 1)),
            pl.BlockSpec((seq_len, LANES), lambda p, i: (0, 3 * p + 2)),
            pl.BlockSpec((tile, LANES), lambda p, i: (i, p)),
            pl.BlockSpec((1, 2, tile), lambda p, i: (p, 0, i)),
            pl.BlockSpec((1, tile), lambda p, i: (0, i)),
            pl.BlockSpec((seq_len, 1), lambda p, i: (0, 0)),
        ],
        out_specs=[
            pl.BlockSpec((tile, LANES), lambda p, i: (i, p)),
            pl.BlockSpec((seq_len, LANES), lambda p, i: (0, p)),
            pl.BlockSpec((seq_len, LANES), lambda p, i: (0, p)),
        ],
        out_shape=[
            jax.ShapeDtypeStruct((rows, 2 * LANES), bf16),
            jax.ShapeDtypeStruct((seq_len, 2 * LANES), f32),
            jax.ShapeDtypeStruct((seq_len, 2 * LANES), f32),
        ],
        compiler_params=pltpu.CompilerParams(vmem_limit_bytes=32 << 20),
        cost_estimate=pl.CostEstimate(
            flops=elems * 10 * 128, bytes_accessed=6 << 20, transcendentals=elems
        ),
        name="attention_backward",
    )(projected, keys_values, keys_values, grads, lse, query_ids, key_ids)


def whole(shape):
    return pl.BlockSpec(shape, lambda *_: (0,) * len(shape))


def cut_kernel(_, *refs, width):
    first, up, down = refs[:16], refs[16:24], refs[24:26]
    packed, far, ups, downs = refs[26:28], refs[28:30], refs[30:32], refs[32:34]
    rows = first[0].shape[1]
    for core in range(2):
        for i in range(3):
            lanes = slice(LANES * i, LANES * (i + 1))
            packed[core][:rows, lanes] = first[3 * core + i][0].astype(bf16)
            far[core][:, lanes] = first[6 + 3 * core + i][0].astype(bf16)
        out = first[12 + core][0].astype(bf16)
        packed[core][:LANES, 3 * LANES :] = out[:, :LANES]
        packed[core][LANES:rows, 3 * LANES :] = out[:, LANES:]
        gains = jnp.concatenate([first[14][...], first[15][...]], axis=1)
        top = lax.broadcasted_iota(jnp.int32, (16, 2 * rows), 0) == 0
        gains = jnp.where(top, jnp.broadcast_to(gains, (16, 2 * rows)), 0.0)
        packed[core][rows:, :] = gains.astype(bf16)
        for i in range(4):
            ups[core][:, LANES * i : LANES * (i + 1)] = up[4 * core + i][0].astype(bf16)
        downs[core][...] = down[core][0].astype(bf16)


def cut_weights(w_qkv, w_out, w_up, w_down, gain_attn, gain_mlp, at_eighth):
    rows, width = w_qkv.shape[1], w_out.shape[2]

    def column(i, flip):
        return pl.BlockSpec((1, rows, LANES), lambda g, at: (0, 0, 8 * i + (at[0] ^ flip)))

    specs = [column(i, flip) for flip in (0, 1, 4, 5) for i in range(3)]
    specs += [
        pl.BlockSpec(
            (1, LANES, 2 * LANES), lambda g, at, c=core: (0, (at[0] & 1) ^ c, at[0] >> 1)
        )
        for core in range(2)
    ]
    specs += [whole(gain_attn.shape), whole(gain_mlp.shape)]
    specs += [column(i, core) for core in range(2) for i in range(4)]
    specs += [
        pl.BlockSpec((1, LANES, width), lambda g, at, c=core: (0, at[0] ^ c, 0))
        for core in range(2)
    ]
    outs = [
        jax.ShapeDtypeStruct(shape, bf16)
        for shape in (
            (rows + 16, 4 * LANES),
            (rows, 3 * LANES),
            (rows, 4 * LANES),
            (LANES, width),
        )
        for _ in range(2)
    ]
    operands = [w_qkv] * 12 + [w_out] * 2 + [gain_attn, gain_mlp] + [w_up] * 8 + [w_down] * 2
    return pl.pallas_call(
        functools.partial(cut_kernel, width=width),
        grid_spec=pltpu.PrefetchScalarGridSpec(
            num_scalar_prefetch=1,
            grid=(1,),
            in_specs=specs,
            out_specs=[whole(out.shape) for out in outs],
        ),
        out_shape=outs,
        compiler_params=pltpu.CompilerParams(vmem_limit_bytes=56 << 20),
        name="cut_weights",
    )(at_eighth, *operands)


def place_kernel(at, *refs, fixed):
    qkv_ref, out_ref, gain_ref = refs[-3:]
    count = (len(refs) - 3) // 2
    rows, cols = refs[count].shape
    for k in range(count):
        slot = k if fixed else lax.rem(at[0] + count - k, count)
        packed, far = refs[k], refs[count + k]
        part = pl.ds(pl.multiple_of(slot * rows, rows), rows)
        qkv_ref[part, :cols] = packed[:rows, :cols]
        qkv_ref[part, cols:] = far[...]
        away = slot ^ at[1]
        away = 2 * (away & 1) + (away >> 1)
        out_ref[away, :, :LANES] = packed[:LANES, cols:]
        out_ref[away, :, LANES:] = packed[LANES:rows, cols:]
        part = pl.ds(pl.multiple_of(slot * rows, rows), rows)
        gains = packed[rows:, :].astype(f32)
        gain_ref[0:1, part] = gains[0:1, :rows]
        gain_ref[1:2, part] = gains[0:1, rows:]


def place(packed, far, depth, fixed):
    count = 4
    rows, cols = far[0].shape
    if fixed:
        rows = rows // count
    shapes = ((rows + 16, cols + LANES), (rows, cols))
    specs = [
        pl.BlockSpec(shape, (lambda g, at, k=k: (k, 0)) if fixed else (lambda g, at: (0, 0)))
        for shape in shapes
        for k in range(count)
    ]
    outs = [
        jax.ShapeDtypeStruct((rows * count, 2 * cols), bf16),
        jax.ShapeDtypeStruct((count, LANES, 2 * LANES), bf16),
        jax.ShapeDtypeStruct((2, rows * count), f32),
    ]
    return pl.pallas_call(
        functools.partial(place_kernel, fixed=fixed),
        grid_spec=pltpu.PrefetchScalarGridSpec(
            num_scalar_prefetch=1,
            grid=(1,),
            in_specs=specs,
            out_specs=[whole(out.shape) for out in outs],
        ),
        out_shape=outs,
        compiler_params=pltpu.CompilerParams(vmem_limit_bytes=24 << 20),
        name="place_rows",
    )(depth, *(list(packed) * (count if fixed else 1)), *(list(far) * (count if fixed else 1)))


def small_call(kernel, at, operands, outs, name):
    return pl.pallas_call(
        kernel,
        grid_spec=pltpu.PrefetchScalarGridSpec(
            num_scalar_prefetch=1,
            grid=(1,),
            in_specs=[whole(value.shape) for value in operands],
            out_specs=[whole(out.shape) for out in outs],
        ),
        out_shape=outs,
        compiler_params=pltpu.CompilerParams(vmem_limit_bytes=40 << 20),
        name=name,
    )(at, *operands)


def join_out_kernel(at, keep, came, far_keep, far_came, out_ref):
    for b in range(2):
        rows = slice(LANES * b, LANES * (b + 1))
        for away, value in enumerate((keep[b], came[b], far_keep[1 - b], far_came[1 - b])):
            size = value.shape[1]
            start = pl.multiple_of((at[0] ^ away) * size, size)
            out_ref[rows, pl.ds(start, size)] = value


def fold_out_kernel(at, keep, came, near_ref, give_ref):
    size = near_ref.shape[2]
    first_x = (at[0] & 1) == 0
    for b in range(2):
        value = keep[b].astype(f32) + came[1 - b].astype(f32)
        low, high = value[:, :size], value[:, size:]
        near_ref[b] = jnp.where(first_x, low, high).astype(bf16)
        give_ref[b] = jnp.where(first_x, high, low).astype(bf16)


def pack_kernel(at, keep, came, near, cross, gains, out_ref):
    cols = keep.shape[1]
    rows = keep.shape[0] // 4
    top = lax.broadcasted_iota(jnp.int32, (16, 2 * rows), 0) == 0
    for f in range(4):
        base = f * (rows + 16)
        part = slice(rows * f, rows * (f + 1))
        out_ref[base : base + rows, :cols] = (
            keep[part, :].astype(f32) + came[part, :].astype(f32)
        ).astype(bf16)
        gain = jnp.concatenate([gains[0:1, part], gains[1:2, part]], axis=1)
        gain = jnp.where(top, jnp.broadcast_to(gain, (16, 2 * rows)), 0.0)
        out_ref[base + rows : base + rows + 16, :] = gain.astype(bf16)
    for away, value in enumerate((near[0], cross[0], near[1], cross[1])):
        base = (at[0] ^ away) * (rows + 16)
        for half in range(2):
            start = pl.multiple_of(base + LANES * half, 16)
            out_ref[pl.ds(start, LANES), cols:] = value[:, LANES * half : LANES * (half + 1)]


def assemble_kernel(at, *refs, kind, shapes):
    groups = [refs[4 * i : 4 * i + 4] for i in range(4)]
    rows_old = refs[16 : 16 + len(shapes)]
    outs = refs[16 + len(shapes) :]
    grads, rows_new, sums_ref = outs[: len(shapes)], outs[len(shapes) : 2 * len(shapes)], outs[-1]
    first_core = at[1] == 0
    gain = 0.0
    for core in range(2):
        for chip in range(4):
            eighth = (2 * chip + core) ^ at[0]
            value = jnp.where(first_core, groups[core][chip][...], groups[2 + core][chip][...])
            value = value.astype(f32)
            if kind == "rows":
                rows = value.shape[0]
                grads[0][pl.ds(pl.multiple_of(eighth * rows, rows), rows), :] = value
            elif kind == "columns":
                for i in range(value.shape[1] // LANES):
                    start = pl.multiple_of((8 * i + eighth) * LANES, LANES)
                    grads[0][:, pl.ds(start, LANES)] = value[:, LANES * i : LANES * (i + 1)]
            else:
                rows = shapes[0][0]
                for i in range(3):
                    start = pl.multiple_of((8 * i + eighth) * LANES, LANES)
                    grads[0][:, pl.ds(start, LANES)] = value[:rows, LANES * i : LANES * (i + 1)]
                part = pl.ds(pl.multiple_of((eighth & 1) * LANES, LANES), LANES)
                for half in range(2):
                    start = pl.multiple_of((2 * (eighth >> 1) + half) * LANES, LANES)
                    block = value[half * LANES : (half + 1) * LANES, 3 * LANES :]
                    grads[1][part, pl.ds(start, LANES)] = block
                gain = gain + value[rows : rows + 1, :]
    if kind == "packed":
        outs[-2][...] = gain
    sums_ref[...] = jnp.zeros_like(sums_ref)
    lane = lax.broadcasted_iota(jnp.int32, (1, LANES), 1)
    begin = LANES
    for index, (total_rows, cols) in enumerate(shapes):
        grad_ref, row_ref, new_ref = grads[index], rows_old[index], rows_new[index]
        col_part = slice(begin, begin + cols)
        ratio_part = slice(begin + cols, begin + 2 * cols)
        begin += 2 * cols

        def body(i, total):
            part = pl.ds(pl.multiple_of(i * 64, 64), 64)
            values = grad_ref[part, :]
            square = values * values
            row_new = decay_rate * row_ref[part, :] + (1.0 - decay_rate) * (
                jnp.sum(square, axis=1, keepdims=True) / cols
            )
            new_ref[part, :] = row_new
            sums_ref[:, col_part] += jnp.sum(square, axis=0, keepdims=True)
            sums_ref[:, ratio_part] += jnp.sum(square * (1.0 / row_new), axis=0, keepdims=True)
            return total + jnp.sum(row_new, axis=0, keepdims=True)

        total = lax.fori_loop(0, total_rows // 64, body, jnp.zeros((1, 1), f32))
        sums_ref[:, :LANES] += jnp.where(lane == index, total, 0.0)


def assemble(near0, near1, far0, far1, rows_old, where, kind, shapes):
    outs = [jax.ShapeDtypeStruct(shape, f32) for shape in shapes]
    outs += [jax.ShapeDtypeStruct((shape[0], 1), f32) for shape in shapes]
    if kind == "packed":
        outs.append(jax.ShapeDtypeStruct((1, near0[0].shape[1]), f32))
    outs.append(
        jax.ShapeDtypeStruct((1, LANES + 2 * sum(shape[1] for shape in shapes)), f32)
    )
    return small_call(
        functools.partial(assemble_kernel, kind=kind, shapes=shapes),
        where,
        [*near0, *far0, *near1, *far1, *rows_old],
        outs,
        "assemble_" + kind,
    )


def per_device(
    tokens,
    cotangent,
    segment_ids,
    w_qkv,
    w_out,
    w_up,
    w_down,
    gain_attn,
    gain_mlp,
    row_qkv,
    col_qkv,
    row_out,
    col_out,
    row_up,
    col_up,
    row_down,
    col_down,
    var_attn,
    var_mlp,
):
    core = lax.axis_index("section")
    chip = lax.axis_index("ctx")
    depth = lax.axis_index("fsdp")
    y, x = chip // 2, chip % 2
    fsdp_count = lax.axis_size("fsdp")
    assert lax.axis_size("section") == 2 and lax.axis_size("ctx") == 4
    _, block, width = tokens.shape
    half = block // 2
    rows = w_qkv.shape[1]
    hidden_width = w_up.shape[2]
    unit = hidden_width // fsdp_count // 8
    scale = (width // HEADS) ** (-0.5)
    even = fsdp_count == 4 and rows == 2 * LANES and unit == LANES
    first_core, first_y, first_x = core == 0, y == 0, x == 0

    def flipped(when, value, axis=0):
        low, high = jnp.split(value, 2, axis)
        return jnp.where(when, jnp.concatenate([high, low], axis), value)

    at_eighth = 2 * chip + core

    def eighth(e):
        qkv = lax.dynamic_index_in_dim(w_qkv[0].reshape(rows, 3, 8, LANES), e, 2, keepdims=False)
        up = lax.dynamic_index_in_dim(
            w_up[0].reshape(rows, fsdp_count, 8, unit), e, 2, keepdims=False
        )
        down = lax.dynamic_slice_in_dim(w_down[0], e * unit, unit, 0)
        return [
            part.astype(bf16)
            for part in (qkv.reshape(rows, 3 * LANES), up.reshape(rows, fsdp_count * unit), down)
        ]

    def by_layer(mine, other):
        taken = swap_core(other)
        return jnp.where(first_core, mine, taken), jnp.where(first_core, taken, mine)

    def gather_rows(value):
        return lax.all_gather(value, "fsdp", axis=0, tiled=True)

    def rotations(value):
        return [value] + [
            lax.ppermute(
                value, "fsdp", [(i, (i + k) % fsdp_count) for i in range(fsdp_count)]
            )
            for k in range(1, fsdp_count)
        ]

    def with_far(value):
        return value, swap_y(value)

    chip_array = chip.reshape(1).astype(jnp.int32)

    def out_from_columns(columns):
        keep, came = columns[:2], swap_x(columns[2:])
        out = jax.ShapeDtypeStruct((2 * LANES, width), bf16)
        operands = [keep, came, swap_y(keep), swap_y(came)]
        return small_call(join_out_kernel, chip_array, operands, [out], "join_out")[0]

    weights, gains = [{}, {}], [None, None]
    depth_array = jnp.stack([depth, chip]).astype(jnp.int32)
    if even:
        cuts = cut_weights(
            w_qkv, w_out, w_up, w_down, gain_attn, gain_mlp, at_eighth.reshape(1).astype(jnp.int32)
        )
        packed_parts = by_layer(*cuts[:2])
        far_parts = by_layer(*cuts[2:4])
        up_parts = by_layer(*cuts[4:6])
        down_parts = by_layer(*cuts[6:])
        turns = rotations(packed_parts[0])
        fars = [swap_y(value[:rows, : 3 * LANES]) for value in turns[1:]]
        qkv, columns, gains[0] = place(turns, [far_parts[0]] + fars, depth_array, False)
        weights[0]["qkv"] = qkv
        weights[0]["out"] = out_from_columns(columns)
        up_gathered = [gather_rows(after(up_parts[0], *turns[1:])), gather_rows(up_parts[1])]
        down_gathered = [gather_rows(after(down_parts[0], *turns[1:])), gather_rows(down_parts[1])]
        packed_gathered = gather_rows(packed_parts[1])
    else:
        mine_parts, other_parts = eighth(at_eighth), eighth(at_eighth ^ 1)
        qkv_parts, up_parts, down_parts = [by_layer(a, b) for a, b in zip(mine_parts, other_parts)]
        whole_out = gather_rows(w_out[0].astype(bf16))
        out_parts = by_layer(whole_out, whole_out)
        gains_own = lax.all_gather(
            jnp.concatenate([gain_attn, gain_mlp], axis=0).astype(bf16), "fsdp", axis=1, tiled=True
        )
        gains = [part.astype(f32) for part in by_layer(gains_own, gains_own)]
        for layer in range(2):
            blocks = out_parts[layer].reshape(4, 2, LANES, width)
            blocks = lax.dynamic_index_in_dim(blocks, core, 1, keepdims=False)
            weights[layer] = dict(
                qkv=jnp.concatenate(with_far(gather_rows(qkv_parts[layer])), axis=1),
                out=jnp.concatenate(
                    [
                        lax.dynamic_index_in_dim(blocks, chip, 0, keepdims=False),
                        lax.dynamic_index_in_dim(blocks, chip ^ 2, 0, keepdims=False),
                    ],
                    axis=0,
                ),
                up=with_far(gather_rows(up_parts[layer])),
                down=with_far(gather_rows(down_parts[layer])),
            )

    def own_rows(value):
        near = lax.dynamic_slice(value, (y, core * half, 0), (1, half, width))[0]
        away = lax.dynamic_slice(value, (1 - y, core * half, 0), (1, half, width))[0]
        return [near, swap_y(away)]

    ids = lax.dynamic_index_in_dim(segment_ids, y, 0, keepdims=False).reshape(2, 2, 2, half)
    ids = flipped(~first_y, flipped(~first_x, flipped(~first_core, ids, 2), 1), 0)
    ids = ids.transpose(0, 2, 1, 3)
    key_ids = ids.reshape(8 * half, 1)
    query_ids = [ids[k].reshape(1, 4 * half) for k in range(2)]

    def forward(inputs, layer, hook):
        held = weights[layer]
        attn_gain, mlp_gain = gains[layer][0], gains[layer][1]
        inputs_all = [gather4(value) for value in inputs]
        first_in = hook("project", inputs_all[0])
        projected = [dot(value, held["qkv"]).astype(bf16) for value in (first_in, inputs_all[1])]
        keys_values = jnp.concatenate(projected, axis=0)

        def attend(k, queries):
            context, lse = attention_forward(queries, keys_values, query_ids[k], key_ids, scale)
            return context, lse, *fold_core(dot(context, held["out"]))

        context0, lse0, keep0, across0 = attend(0, hook("attend0", projected[0]))
        context1, lse1, keep1, across1 = attend(1, hook("attend1", after(projected[1], across0)))
        came0 = hook("norm0", after(swap_x(across0), across1))
        came1 = hook("norm1", swap_x(across1))
        unit_attn, scale_attn, normed, normed_all = [], [], [], []
        for k, (keep, came) in enumerate(((keep0, came0), (keep1, came1))):
            pre_attn = inputs[k].astype(f32) + keep + came.astype(f32)
            unit, factor = norm_parts(pre_attn)
            unit_attn.append(unit)
            scale_attn.append(factor)
            normed.append(unit * attn_gain)
        low = [value.astype(bf16) for value in normed]
        normed_all = [gather4(value) for value in low]

        def feed(value):
            activated, slope, partial = [], [], 0.0
            for half_up, half_down in zip(held["up"], held["down"]):
                upward = dot(value, half_up)
                phi_whole = 0.5 * (1.0 + lax.erf(upward * (0.5**0.5)))
                activated.append((upward * phi_whole).astype(bf16))
                density = jnp.exp(-0.5 * upward * upward) * 0.3989422804014327
                slope.append((phi_whole + upward * density).astype(bf16))
                partial += dot(activated[-1], half_down)
            return activated, slope, *fold_core(partial)

        activated0, slope0, keep0, across0 = feed(hook("feed0", after(normed_all[0], low[1])))
        activated1, slope1, keep1, across1 = feed(hook("feed1", after(normed_all[1], across0)))
        came0 = hook("last0", after(swap_x(across0), across1))
        came1 = swap_x(across1)
        unit_mlp, scale_mlp, outputs = [], [], []
        for k, (keep, came) in enumerate(((keep0, came0), (keep1, came1))):
            unit, factor = norm_parts(normed[k] + keep + came.astype(f32))
            unit_mlp.append(unit)
            scale_mlp.append(factor)
            outputs.append((unit * mlp_gain).astype(bf16))
        return outputs, dict(
            inputs_all=inputs_all,
            projected=projected,
            keys_values=keys_values,
            context=(context0, context1),
            lse=(lse0, lse1),
            unit_attn=unit_attn,
            scale_attn=scale_attn,
            normed_all=normed_all,
            activated=(activated0, activated1),
            slope=(slope0, slope1),
            unit_mlp=unit_mlp,
            scale_mlp=scale_mlp,
        )

    def backward(out_grads, kept, layer, hook):
        held = weights[layer]

        def over_tokens(left, right):
            return (rows_product(left[0], right[0]) + rows_product(left[1], right[1])).astype(bf16)

        def by_half(left, right):
            size = right[0].shape[1] // 2
            return [
                over_tokens(left, [value[:, at : at + size] for value in right])
                for at in (0, size)
            ]

        attn_gain, mlp_gain = gains[layer][0], gains[layer][1]
        mlp_in, mlp_gain_grad = [], 0.0
        for k in range(2):
            grad, gain_part = norm_back(
                out_grads[k].astype(f32), kept["unit_mlp"][k], kept["scale_mlp"][k], mlp_gain
            )
            mlp_in.append(grad)
            mlp_gain_grad += gain_part
        low = [value.astype(bf16) for value in mlp_in]
        down_all = [gather4(value) for value in low]

        def feed_back(k, value):
            grads, partial = [], 0.0
            for half_up, half_down, slope in zip(held["up"], held["down"], kept["slope"][k]):
                grad = times_transposed(value, half_down) * slope.astype(f32)
                grads.append(grad.astype(bf16))
                partial += times_transposed(grads[-1], half_up)
            return grads, *fold_core(partial)

        upward0, keep0, across0 = feed_back(0, hook("feed0", after(down_all[0], low[1])))
        upward1, keep1, across1 = feed_back(1, hook("feed1", after(down_all[1], across0)))
        came0 = hook(
            "norm0",
            after(swap_x(across0), across1),
            down=[over_tokens(left, down_all) for left in zip(*kept["activated"])],
        )
        came1 = swap_x(across1)
        upward_grad = (upward0, upward1)
        attn_in, attn_gain_grad = [], 0.0
        for k, (keep, came) in enumerate(((keep0, came0), (keep1, came1))):
            grad, gain_part = norm_back(
                mlp_in[k] + keep + came.astype(f32),
                kept["unit_attn"][k],
                kept["scale_attn"][k],
                attn_gain,
            )
            attn_in.append(grad)
            attn_gain_grad += gain_part
        low = [value.astype(bf16) for value in attn_in]
        branch_all = [gather4(value) for value in low]

        def attend_back(k, value):
            grads = times_transposed(value, held["out"]).astype(bf16)
            return attention_backward(
                kept["projected"][k],
                kept["keys_values"],
                grads,
                kept["lse"][k],
                query_ids[k],
                key_ids,
                scale,
            )

        grad_up = [over_tokens(kept["normed_all"], right) for right in zip(*upward_grad)]
        query0, key0, value0 = attend_back(
            0, hook("attend0", after(branch_all[0], low[1]), up=grad_up)
        )
        grad_out = over_tokens(kept["context"], branch_all)
        gain_grads = jnp.stack([attn_gain_grad, mlp_gain_grad])
        query1, key1, value1 = attend_back(
            1, hook("attend1", after(branch_all[1], query0), out=grad_out, gains=gain_grads)
        )
        key_grad, value_grad = (key0 + key1).astype(bf16), (value0 + value1).astype(bf16)
        stacked = []
        for k, query_grad in enumerate((query0, query1)):
            part = slice(4 * half * k, 4 * half * (k + 1))
            stacked.append(
                jnp.concatenate(
                    [
                        piece[:, LANES * p : LANES * (p + 1)]
                        for p in range(2)
                        for piece in (query_grad, key_grad[part], value_grad[part])
                    ],
                    axis=1,
                )
            )
        stacked[0] = hook("stacked", stacked[0])
        keep0, across0 = fold_core(times_transposed(stacked[0], held["qkv"]))
        stacked[1] = hook("stacked1", stacked[1])
        keep1, across1 = fold_core(times_transposed(stacked[1], held["qkv"]))
        came = (hook("last0", after(swap_x(across0), across1)), swap_x(across1))
        grad_qkv = by_half(kept["inputs_all"], stacked)
        in_grads = [
            (attn_in[k] + keep + came[k].astype(f32)).astype(bf16)
            for k, keep in enumerate((keep0, keep1))
        ]
        return in_grads, grad_qkv

    def scatter_rows(value):
        return lax.psum_scatter(value, "fsdp", scatter_dimension=0, tiled=True)

    def sync(value, *others):
        return lax.optimization_barrier((value, *others))

    def fold(keep, came):
        return (keep.astype(f32) + came.astype(f32)).astype(bf16)

    def halves(grad):
        return grad[0], swap_y(grad[1])

    def out_halves(grad_out):
        size = width // 2
        keep = lax.dynamic_slice_in_dim(grad_out, y * size, size, 1)
        give = lax.dynamic_slice_in_dim(grad_out, (1 - y) * size, size, 1)
        return keep.reshape(2, LANES, size), swap_y(give.reshape(2, LANES, size))

    def out_pair(keep, came):
        out = jax.ShapeDtypeStruct((2, LANES, 2 * LANES), bf16)
        near, give = small_call(fold_out_kernel, chip_array, [keep, came], [out, out], "fold_out")
        return near, swap_x(give)

    def pack(keep, came, near, cross, gain_grads):
        out = jax.ShapeDtypeStruct((4 * (rows + 16), 4 * LANES), bf16)
        operands = [keep, came, near, cross, gain_grads]
        return small_call(pack_kernel, chip_array, operands, [out], "pack_gradients")[0]

    def spread_start(value, y_first):
        return value, (swap_y if y_first else swap_x)(value)

    def spread_end(pair, y_first):
        value, first = pair
        if y_first:
            return [value, swap_x(value), first, swap_x(first)]
        return [value, first, swap_y(value), swap_y(first)]

    def spread(value, y_first):
        return spread_end(spread_start(value, y_first), y_first)

    def reduce_plain(grads, grad_qkv):
        keep, came = out_halves(grads["out"])
        both = fold(keep, came[::-1])
        placed = jnp.zeros((4, 2, LANES, width // 2), bf16)
        placed = lax.dynamic_update_slice(placed, both[:1, None], (chip, core, 0, 0))
        placed = lax.dynamic_update_slice(placed, both[1:, None], (chip ^ 2, core, 0, 0))
        gain_rows = grads["gains"].reshape(2, fsdp_count, rows).transpose(1, 0, 2)
        gain_rows = gain_rows.reshape(fsdp_count, 1, 2 * rows).astype(bf16)
        gain_rows = jnp.pad(gain_rows, ((0, 0), (0, 15), (0, width // 2 - 2 * rows)))
        packed = jnp.concatenate([placed.reshape(fsdp_count, rows, width // 2), gain_rows], axis=1)
        return [
            spread(scatter_rows(fold(*halves(grad_qkv))), False),
            spread(scatter_rows(packed.reshape(fsdp_count * (rows + 16), width // 2)), True),
            spread(scatter_rows(fold(*halves(grads["up"]))), False),
            spread(scatter_rows(fold(*halves(grads["down"]))), True),
        ]

    inputs = own_rows(tokens)
    out_grads = own_rows(cotangent)
    grads0, grads1 = {}, {}
    if even:
        down_got, up_got = {}, {}

        def hook_forward0(name, value):
            if name == "attend1":
                value, up, out_grads[1] = sync(value, up_gathered[0], out_grads[1])
                weights[0]["up"] = with_far(up)
            elif name == "norm0":
                value, far = sync(value, weights[0]["up"][1])
                weights[0]["up"] = weights[0]["up"][0], far
            elif name == "norm1":
                value, down = sync(value, down_gathered[0])
                weights[0]["down"] = with_far(down)
            elif name == "feed1":
                value, packed = sync(value, packed_gathered)
                near = packed.reshape(4, rows + 16, 4 * LANES)[:, :rows, : 3 * LANES]
                far = swap_y(near.reshape(4 * rows, 3 * LANES))
                qkv, columns, gains[1] = place([packed], [far], depth_array, True)
                weights[1].update(qkv=qkv, out=out_from_columns(columns))
            return value

        def hook_forward1(name, value):
            if name == "attend0":
                value, up = sync(value, up_gathered[1])
                weights[1]["up"] = with_far(up)
            elif name == "attend1":
                value, weights[1]["out"] = sync(value, weights[1]["out"])
            elif name == "norm0":
                value, far = sync(value, weights[1]["up"][1])
                weights[1]["up"] = weights[1]["up"][0], far
            elif name == "norm1":
                value, down = sync(value, down_gathered[1])
                weights[1]["down"] = with_far(down)
            return value

        def hook_backward1(name, value, **grads):
            if name == "norm0":
                value, *down = sync(value, *grads["down"])
                grads1["down"] = halves(down)
            elif name == "attend0":
                value, came, *up = sync(value, grads1["down"][1], *grads["up"])
                grads1["down"] = scatter_rows(fold(grads1["down"][0], came))
                grads1["up"] = halves(up)
            elif name == "attend1":
                value, grads1["whole_out"], grads1["gains"] = sync(
                    value, grads["out"], grads["gains"]
                )
            elif name == "stacked":
                value, came, *outputs = sync(value, grads1["up"][1], *hidden_away)
                grads1["up"] = scatter_rows(fold(grads1["up"][0], came))
                grads1["out"] = out_halves(grads1["whole_out"])
                hidden_away[:] = outputs
            elif name == "last0":
                value, came = sync(value, grads1["out"][1])
                grads1["out"] = out_pair(grads1["out"][0], came)
            return value

        def hook_backward0(name, value, **grads):
            if name == "feed0":
                value, down, out_came, *qkv = sync(
                    value, grads1["down"], grads1["out"][1], *grads1["qkv"]
                )
                grads1["out"] = grads1["out"][0], out_came
                grads1["qkv"] = halves(qkv)
                grads1["down"] = spread_start(down, True)
            elif name == "norm0":
                value, came, up1, hop, *down = sync(
                    value, grads1["qkv"][1], grads1["up"], grads1["down"][1], *grads["down"]
                )
                grads1["packed"] = scatter_rows(
                    pack(grads1["qkv"][0], came, *grads1["out"], grads1["gains"])
                )
                grads1["down"] = grads1["down"][0], hop
                grads1["up"] = up1
                grads0["down"] = halves(down)
            elif name == "attend0":
                value, came, *up = sync(value, grads0["down"][1], *grads["up"])
                grads0["down"] = scatter_rows(fold(grads0["down"][0], came))
                grads0["up"] = halves(up)
                grads1["up"] = spread_start(grads1["up"], False)
            elif name == "attend1":
                value, grads0["whole_out"], grads0["gains"], hop, packed1 = sync(
                    value, grads["out"], grads["gains"], grads1["up"][1], grads1["packed"]
                )
                grads1["up"] = grads1["up"][0], hop
                grads1["down"] = spread_end(grads1["down"], True)
                grads1["packed"] = spread_start(packed1, False)
            elif name == "stacked":
                value, came, hop, down, away, *ends = sync(
                    value,
                    grads0["up"][1],
                    grads1["packed"][1],
                    grads0["down"],
                    in_away[0],
                    *grads1["down"],
                )
                in_away[0] = away
                grads1["down"] = ends
                grads0["up"] = scatter_rows(fold(grads0["up"][0], came))
                grads0["out"] = out_halves(grads0["whole_out"])
                grads1["packed"] = grads1["packed"][0], hop
                grads0["down"] = spread_start(down, True)
                grads1["up"] = spread_end(grads1["up"], False)
            elif name == "last0":
                value, came = sync(value, grads0["out"][1])
                grads0["out"] = out_pair(grads0["out"][0], came)
            return value

    else:

        def hook_forward0(name, value):
            return value

        hook_forward1 = hook_forward0

        def hook_backward1(name, value, **grads):
            grads1.update(grads)
            return value

        def hook_backward0(name, value, **grads):
            grads0.update(grads)
            return value

    hidden0, saved0 = forward(inputs, 0, hook_forward0)
    hidden1, saved1 = forward(hidden0, 1, hook_forward1)
    hidden_away = [swap_y(hidden0[1]), swap_y(hidden1[1])]
    in_grads1, grad_qkv1 = backward(out_grads, saved1, 1, hook_backward1)
    grads1["qkv"] = grad_qkv1
    in_away = [swap_y(in_grads1[1])]
    in_grads0, grad_qkv0 = backward(in_grads1, saved0, 0, hook_backward0)
    if even:
        qkv_keep, qkv_came = halves(grad_qkv0)
        in_grads0[0], up0, hop = sync(in_grads0[0], grads0["up"], grads0["down"][1])
        grads0["down"] = grads0["down"][0], hop
        packed0 = scatter_rows(pack(qkv_keep, qkv_came, *grads0["out"], grads0["gains"]))
        near1 = [spread_end(grads1["packed"], False), grads1["up"], grads1["down"]]
        near0 = [spread(packed0, False), spread(up0, False), spread_end(grads0["down"], True)]
    else:
        near1, near0 = reduce_plain(grads1, grad_qkv1), reduce_plain(grads0, grad_qkv0)

    def to_owner(layer0, layer1, away):
        pairs = [jnp.stack([runs[0], far]) for runs, far in zip((layer0, layer1), away)]
        keep = jnp.where(first_core, pairs[0], pairs[1])
        take = swap_core(jnp.where(first_core, pairs[1], pairs[0]))
        both = flipped(~first_core, jnp.stack([keep, take], axis=1), 1)
        return flipped(~first_y, both, 0).reshape(2, block, width)

    hidden_out = to_owner(hidden0, hidden1, hidden_away)
    in_grads_out = to_owner(in_grads0, in_grads1, [swap_y(in_grads0[1]), in_away[0]])

    def natural(position):
        layers = jnp.stack(near0[position]), jnp.stack(near1[position])
        near = jnp.where(first_core, layers[0], layers[1])
        far = jnp.where(first_core, swap_core(layers[0]), swap_core(layers[1]))
        both = jnp.stack([near, far], axis=1)
        shape = both.shape
        both = both.reshape((2, 2, 2) + shape[2:])
        both = flipped(~first_y, flipped(~first_x, flipped(~first_core, both, 2), 1), 0)
        return both.reshape((8,) + shape[2:])

    rows_old = (row_qkv, row_out, row_up, row_down)
    if even:
        where = jnp.stack([at_eighth, core]).astype(jnp.int32)

        def build(position, kind, olds, shapes):
            return assemble(
                near0[position],
                near1[position],
                [swap_core(value) for value in near0[position]],
                [swap_core(value) for value in near1[position]],
                olds,
                where,
                kind,
                shapes,
            )

        def column(row):
            return row.reshape(-1, 1)

        down = build(2, "rows", [column(row_down)], ((8 * unit, width),))
        up = build(1, "columns", [column(row_up)], ((rows, hidden_width),))
        built = [None, None, up[:2], down[:2]]
        sums = {2: jnp.concatenate([up[2], down[2]], axis=1)}
        places = {2: (0, LANES), 3: (LANES + 2 * hidden_width, 2 * LANES + 2 * hidden_width)}
        places.update({0: (0, LANES), 1: (1, LANES + 6 * width)})

        def build_first(*tokens):
            first = build(
                0,
                "packed",
                [after(column(row_qkv), *tokens), column(row_out)],
                ((rows, 3 * width), (rows, width)),
            )
            built[:2] = (first[0], first[2]), (first[1], first[3])
            sums[0] = first[5]
            return first[4].reshape(2, rows)

    else:
        qkv = natural(0).reshape(8, rows, 3, LANES).transpose(1, 2, 0, 3).reshape(rows, 3 * width)
        out = natural(1).reshape(2, 4, rows + 16, width // 2).astype(f32).sum(axis=1)
        gain_shard = out[:, rows].sum(axis=0)[: 2 * rows].reshape(2, rows)
        out = out[:, :rows].transpose(1, 0, 2).reshape(rows, width)
        up = natural(2).reshape(8, rows, fsdp_count, unit).transpose(1, 2, 0, 3)
        up = up.reshape(rows, hidden_width)
        down = natural(3).reshape(8 * unit, width)
        built, parts = [], []
        for gradient, row_old in zip((qkv, out, up, down), rows_old):
            gradient = gradient.astype(f32)
            square = gradient * gradient
            row_new = decay_rate * row_old.reshape(-1, 1) + (1.0 - decay_rate) * jnp.mean(
                square, axis=1, keepdims=True
            )
            built.append((gradient, row_new))
            total_new = jnp.pad(jnp.sum(row_new).reshape(1, 1), ((0, 0), (0, LANES - 1)))
            parts.append(
                [
                    total_new,
                    jnp.sum(square, axis=0, keepdims=True),
                    jnp.sum(square / row_new, axis=0, keepdims=True),
                ]
            )
        blank = jnp.zeros_like(parts[0][0])
        sums = {
            2: jnp.concatenate(parts[2] + parts[3], axis=1),
            0: jnp.concatenate([blank] + parts[0] + parts[1], axis=1),
        }
        places = {2: (0, LANES), 3: (LANES + 2 * hidden_width, 2 * LANES + 2 * hidden_width)}
        places.update(
            {0: (LANES, 2 * LANES), 1: (2 * LANES + 6 * width, 3 * LANES + 6 * width)}
        )

        def build_first(*tokens):
            return gain_shard

    def sum_line(value):
        if fsdp_count != 4:
            return lax.psum(value, "fsdp")
        near, two, three = rotations(value)[1:]
        return (value + two) + (near + three)

    masters = (w_qkv[0], w_out[0], w_up[0], w_down[0])
    cols_old = (col_qkv, col_out, col_up, col_down)
    gain_masters = (gain_attn, gain_mlp)
    moments_old = (var_attn, var_mlp)

    def total(value):
        return jnp.sum(value).reshape(1, 1)

    new_rows, new_cols, ratios, new_masters = [None] * 4, [None] * 4, [None] * 4, [None] * 4

    def update(position, summed, weight_total):
        gradient, row_new = built[position]
        at_total, start = places[position]
        cols = gradient.shape[1]
        row_count = gradient.shape[0] * fsdp_count
        entry_count = row_count * cols
        col_all = summed[:, start : start + cols]
        ratio_all = summed[:, start + cols : start + 2 * cols]
        row_mean = summed[:, at_total : at_total + 1] / row_count
        new_rows[position] = row_new.reshape(1, -1)
        new_cols[position] = (
            decay_rate * cols_old[position] + (1.0 - decay_rate) * col_all / row_count
        )
        ratios[position] = jnp.sqrt(
            row_mean * total(ratio_all / new_cols[position]) / entry_count
        )
        weight_scale = jnp.sqrt(weight_total / entry_count + weight_eps)
        factor = step_rate * weight_scale / jnp.maximum(1.0, ratios[position] / clip_level)
        raw = gradient * lax.rsqrt(row_new * new_cols[position] / row_mean)
        new_masters[position] = masters[position] - factor * raw

    def lanes(values, start):
        row = jnp.concatenate(values, axis=1)
        return jnp.pad(row, ((0, 0), (start, LANES - start - row.shape[1])))

    def with_lanes(row, values):
        return jnp.concatenate([row[:, :LANES] + lanes(values, 2), row[:, LANES:]], axis=1)

    weight_totals = [total(master * master) for master in masters + gain_masters]
    summed = sum_line(with_lanes(sums[2], weight_totals))
    weight_all = [summed[:, 2 + i : 3 + i] for i in range(6)]
    for position in (2, 3):
        update(position, summed, weight_all[position])
    gain_shard = build_first(new_masters[2], new_masters[3])
    moments, gain_updates = [], []
    for gain_pos in range(2):
        grad = gain_shard[gain_pos : gain_pos + 1]
        moment = decay_rate * moments_old[gain_pos] + (1.0 - decay_rate) * grad * grad
        moments.append(moment)
        gain_updates.append(grad * lax.rsqrt(moment))
    summed = sum_line(with_lanes(sums[0], [total(step * step) for step in gain_updates]))
    for position in (0, 1):
        update(position, summed, weight_all[position])
    for gain_pos in range(2):
        clip_ratio = jnp.sqrt(summed[:, 2 + gain_pos : 3 + gain_pos] / width)
        weight_scale = jnp.sqrt(weight_all[4 + gain_pos] / width + weight_eps)
        factor = step_rate * weight_scale / jnp.maximum(1.0, clip_ratio / clip_level)
        new_masters.append(gain_masters[gain_pos] - factor * gain_updates[gain_pos])
        ratios.append(clip_ratio)
    return (
        hidden_out[None],
        in_grads_out[None],
        *[entry[0][None] for entry in built],
        gain_shard[:1],
        gain_shard[1:],
        *[master[None] for master in new_masters[:4]],
        new_masters[4],
        new_masters[5],
        new_rows[0],
        new_cols[0],
        new_rows[1],
        new_cols[1],
        new_rows[2],
        new_cols[2],
        new_rows[3],
        new_cols[3],
        moments[0],
        moments[1],
        jnp.concatenate(ratios, axis=1),
    )


def solution(mesh):
    in_specs = (
        P("fsdp", "ctx", None),
        P("fsdp", "ctx", None),
        P("fsdp", None),
        P("section", "fsdp", None),
        P("section", "fsdp", None),
        P("section", "fsdp", None),
        P("section", "fsdp", None),
        P("section", "fsdp"),
        P("section", "fsdp"),
        P("section", "fsdp"),
        P("section", None),
        P("section", "fsdp"),
        P("section", None),
        P("section", "fsdp"),
        P("section", None),
        P("section", "fsdp"),
        P("section", None),
        P("section", "fsdp"),
        P("section", "fsdp"),
    )
    out_specs = (
        P("section", "fsdp", "ctx", None),
        P("section", "fsdp", "ctx", None),
        P("section", "fsdp", None),
        P("section", "fsdp", None),
        P("section", "fsdp", None),
        P("section", "fsdp", None),
        P("section", "fsdp"),
        P("section", "fsdp"),
        P("section", "fsdp", None),
        P("section", "fsdp", None),
        P("section", "fsdp", None),
        P("section", "fsdp", None),
        P("section", "fsdp"),
        P("section", "fsdp"),
        P("section", "fsdp"),
        P("section", None),
        P("section", "fsdp"),
        P("section", None),
        P("section", "fsdp"),
        P("section", None),
        P("section", "fsdp"),
        P("section", None),
        P("section", "fsdp"),
        P("section", "fsdp"),
        P("section", None),
    )
    return jax.shard_map(
        per_device, mesh=mesh, in_specs=in_specs, out_specs=out_specs, check_vma=False
    )
```

time: 980 us -> 817 us (0.83)
  blocking collectives: 156 us -> 0 us
  local copies, waits for them, and re-layouts: 102 us -> 62.7 us
  other arithmetic: 157 us -> 122 us
  matrix products: 90.8 us -> 124 us
  Pallas kernels: 66.3 us -> 94 us
  starting transfers between devices: 102 us -> 117 us
  waiting for transfers between devices: 268 us -> 255 us
    all_gather x5 -> x0, blocking collectives: 83.5 us -> none  [the longest x4 72.4 us: gather_rows(): return lax.all_gather(value, 'fsdp', axis=0, tiled=True)]
    psum x3 -> x0, blocking collectives: 72.1 us -> none  [the longest x1 44.7 us: per_device(): lax.psum(jnp.stack([gain_grads0, gain_grads1]), ('section', 'ctx', 'fsdp'))]
    ppermute x30 -> x36, waiting for transfers between devices: 138 us -> 96.3 us  [swap_y(): return lax.ppermute(value, 'ctx', [(i, i ^ 2) for i in range(4)])]
    pallas_call x0 -> x12, Pallas kernels: none -> 27.7 us  [the longest x9 22.5 us: small_call(): pl.pallas_call(kernel, grid_spec=pltpu.PrefetchScalarGridSpec(num_scalar_...]
    dot_general x16 -> x28, matrix products: 34.5 us -> 52.6 us  [rows_product(): lax.dot_general(left, right, (((0,), (0,)), ((), ())), preferred_element_...]
    convert_element_type x9 -> x0, local copies, waits for them, and re-layouts: 16.7 us -> none  [the longest x4 5.78 us: eighth(): return [part.astype(bf16) for part in parts]]
    ppermute x0 -> x9, starting transfers between devices: none -> 16.6 us  [rotations(): lax.ppermute(value, 'fsdp', [(i, (i + k) % fsdp_count) for i in range(fsd...]
    ppermute x0 -> x9, waiting for transfers between devices: none -> 14.8 us  [rotations(): lax.ppermute(value, 'fsdp', [(i, (i + k) % fsdp_count) for i in range(fsd...]
  transfers between devices with their start and end apart: 129 -> 162, of which waited for: 54 -> 61; matrix products, arithmetic and copies ran while one was open for 27% -> 28% of each run, Pallas kernels for 7% -> 8%
where the time goes in v2:
time: 817 us; the launch traced here: 806 us
  waiting for transfers between devices  255 us (31%)
  matrix products  124 us (15%)
  other arithmetic  122 us (15%)
  starting transfers between devices  117 us (14%)
  Pallas kernels  94 us (12%)
  local copies, waits for them, and re-layouts  62.7 us (8%)
  between operations  30.5 us (4%)
    ppermute x44, waiting for transfers between devices, swap_x(): return lax.ppermute(value, 'ctx', [(i, i ^ 1) for i in range(4)])  123 us
    ppermute x36, waiting for transfers between devices, swap_y(): return lax.ppermute(value, 'ctx', [(i, i ^ 2) for i in range(4)])  96.3 us
    dot_general x28, matrix products, rows_product(): lax.dot_general(left, right, (((0,), (0,)), ((), ())), preferred_element_...  52.6 us
    ppermute x44, starting transfers between devices, swap_x(): return lax.ppermute(value, 'ctx', [(i, i ^ 1) for i in range(4)])  46.5 us
    ppermute x36, starting transfers between devices, swap_y(): return lax.ppermute(value, 'ctx', [(i, i ^ 2) for i in range(4)])  43.8 us
    pallas_call x4, Pallas kernels, attention_backward(): pl.pallas_call(functools.partial(attention_back_kernel, scale=scale), gri...  39 us
    dot_general x24, matrix products, times_transposed(): lax.dot_general(left, right, (((1,), (1,)), ((), ())), preferred_element_...  36.6 us
    unnamed x722, local copies, waits for them, and re-layouts  35.4 us
  transfers between devices with their start and end apart: 162, of which 61 were waited for; matrix products, arithmetic and copies ran while one was open for 28% of the time, Pallas kernels for 8%

profile of v2, /device:TPU:0, one launch (start us, length us, event | category | flops | bytes accessed | tf_op | source)
XLA Modules:
  0.0 805.7 jit_solution(6359092612642366811)
XLA Ops:
  7.3 3.8 cut_weights.1
  11.8 3.0 collective-permute-start.10
  26.8 3.3 collective-permute-done.3.refs_1_
  30.1 11.6 %collective-permute-done.4.refs_2_ = bf16[272,512]{1,0:T(8,128)(2,1)S(1)} collective-permute-done((bf16[272,512]{1,0:T(8,128)(2,1)S(1)}, bf16[272,512]{1,0:T(8,128)(2,1)S(1)}, u32[]{:S(2)}, u32[]{:S(2)}) %collective-permute-start.4) | collective-permute-done | bytes 278560 | tf_op jit(solution)/shard_map/ppermute | solution.py:509
  49.4 4.2 collective-permute-done.8.refs_6_
  53.6 3.2 collective-permute-done.9.refs_7_
  71.2 6.8 attention_forward.4
  84.8 5.3 collective-permute-done.19
  92.3 6.7 attention_forward.5
  104.9 4.5 collective-permute-done.17
  109.4 12.6 %all-gather.8.cloned.1.call-done = bf16[512,1024]{1,0:T(8,128)(2,1)} async-done(((bf16[128,1024]{1,0:T(8,128)(2,1)}), bf16[512,1024]{1,0:T(8,128)(2,1)}) %all-gather.8.cloned.1.call-update) | async-done | bytes 1048592 | tf_op jit(solution)/shard_map/all_gather | solution.py:505
  123.4 5.3 collective-permute-done.21
  132.3 6.6 collective-permute-done.22
  142.2 6.7 collective-permute-done.29
  155.7 10.2 %collective-permute-done.26 = bf16[512,1024]{1,0:T(8,128)(2,1)} collective-permute-done((bf16[512,1024]{1,0:T(8,128)(2,1)S(1)}, bf16[512,1024]{1,0:T(8,128)(2,1)}, u32[]{:S(2)}, u32[]{:S(2)}) %collective-permute-start.26) | collective-permute-done | bytes 1048608 | tf_op jit(solution)/shard_map/ppermute | solution.py:34
  175.1 3.3 multiply_convert_fusion.4
  188.0 3.7 collective-permute-done.28
  191.8 4.9 collective-permute-done.35
  201.6 4.4 collective-permute-done.34.refs_4_.refs_5_.refs_6_.refs_7_
  210.5 3.0 collective-permute-done.36
  229.6 6.7 attention_forward.6
  244.1 7.1 attention_forward.7
  256.9 4.4 collective-permute-done.42
  264.6 3.0 all-gather.14.cloned.1.call-done
  271.8 6.4 collective-permute-done.45
  281.4 5.7 collective-permute-done.51
  291.2 13.9 %collective-permute-done.48 = bf16[512,1024]{1,0:T(8,128)(2,1)S(1)} collective-permute-done((bf16[512,1024]{1,0:T(8,128)(2,1)S(1)}, bf16[512,1024]{1,0:T(8,128)(2,1)S(1)}, u32[]{:S(2)}, u32[]{:S(2)}) %collective-permute-start.48) | collective-permute-done | bytes 1048608 | tf_op jit(solution)/shard_map/ppermute | solution.py:34
  310.9 3.3 multiply_convert_fusion
  324.8 3.3 fusion.2
  333.2 4.1 collective-permute-done.50
  337.3 5.1 collective-permute-done.56
  348.9 7.2 collective-permute-done.54
  361.3 4.4 concatenate.284
  398.9 3.8 collective-permute-done.64
  409.0 6.0 collective-permute-done.62
  419.2 3.3 collective-permute-done.65
  423.0 9.8 %attention_backward.4 = (bf16[512,256]{1,0:T(8,128)(2,1)S(1)}, f32[1024,256]{1,0:T(8,128)S(1)}, f32[1024,256]{1,0:T(8,128)S(1)}) custom-call(bf16[512,768]{1,0:T(8,128)(2,1)S(1)} %copy-done.22, bf16[1024,768]{1,0:T(8,128)(2,1)S(1)} %pad_maximum_fusion.1.k_ref.v_ref, bf16[1024,768]{1,0:T(8,128)(2,1)S(1)} %pad_maximum_fusion.1.k_ref.v_ref, ...), custom_call_target="tpu_custom_call" | custom-call | flops 2684354560 | bytes 6291456 | tf_op jit(solution)/shard_map/attention_backward/pallas_call | solution.py:170
  436.0 9.7 %attention_backward.5 = (bf16[512,256]{1,0:T(8,128)(2,1)S(1)}, f32[1024,256]{1,0:T(8,128)S(1)}, f32[1024,256]{1,0:T(8,128)S(1)}) custom-call(bf16[512,768]{1,0:T(8,128)(2,1)S(1)} %copy-done.20, bf16[1024,768]{1,0:T(8,128)(2,1)S(1)} %pad_maximum_fusion.1.k_ref.v_ref, bf16[1024,768]{1,0:T(8,128)(2,1)S(1)} %pad_maximum_fusion.1.k_ref.v_ref, ...), custom_call_target="tpu_custom_call" | custom-call | flops 2684354560 | bytes 6291456 | tf_op jit(solution)/shard_map/attention_backward/pallas_call | solution.py:170
  462.7 3.0 fusion.90
  465.8 3.1 fusion.84
  470.2 8.7 %collective-permute-done.69 = bf16[128,1024]{1,0:T(8,128)(2,1)S(1)} collective-permute-done((bf16[128,1024]{1,0:T(8,128)(2,1)S(1)}, bf16[128,1024]{1,0:T(8,128)(2,1)S(1)}, u32[]{:S(2)}, u32[]{:S(2)}) %collective-permute-start.69) | collective-permute-done | bytes 262176 | tf_op jit(solution)/shard_map/ppermute | solution.py:34
  478.9 5.6 collective-permute-done.70
  490.7 3.5 add_convert_fusion.22
  496.4 6.9 collective-permute-done.73
  506.5 7.0 collective-permute-done.76
  526.3 3.0 fusion.8
  563.7 3.4 multiply_reduce_fusion.1
  571.2 3.2 collective-permute-done.89
  583.0 5.4 collective-permute-done.87
  588.5 3.8 collective-permute-done.91
  600.7 9.8 %attention_backward.6 = (bf16[512,256]{1,0:T(8,128)(2,1)S(1)}, f32[1024,256]{1,0:T(8,128)S(1)}, f32[1024,256]{1,0:T(8,128)S(1)}) custom-call(bf16[512,768]{1,0:T(8,128)(2,1)S(1)} %copy-done.17, bf16[1024,768]{1,0:T(8,128)(2,1)S(1)} %pad_maximum_fusion.k_ref.v_ref, bf16[1024,768]{1,0:T(8,128)(2,1)S(1)} %pad_maximum_fusion.k_ref.v_ref, ...), custom_call_target="tpu_custom_call" | custom-call | flops 2684354560 | bytes 6291456 | tf_op jit(solution)/shard_map/attention_backward/pallas_call | solution.py:170
  623.9 9.7 %attention_backward.7 = (bf16[512,256]{1,0:T(8,128)(2,1)S(1)}, f32[1024,256]{1,0:T(8,128)S(1)}, f32[1024,256]{1,0:T(8,128)S(1)}) custom-call(bf16[512,768]{1,0:T(8,128)(2,1)S(1)} %copy-done.15, bf16[1024,768]{1,0:T(8,128)(2,1)S(1)} %pad_maximum_fusion.k_ref.v_ref, bf16[1024,768]{1,0:T(8,128)(2,1)S(1)} %pad_maximum_fusion.k_ref.v_ref, ...), custom_call_target="tpu_custom_call" | custom-call | flops 2684354560 | bytes 6291456 | tf_op jit(solution)/shard_map/attention_backward/pallas_call | solution.py:170
  670.8 3.0 collective-permute-done.116.refs_10_
  673.9 5.7 collective-permute-done.105
  694.5 6.1 collective-permute-done.107.came
  702.3 4.5 collective-permute-done.122.refs_1_
  711.7 3.4 collective-permute-done.124.refs_3_
  719.8 7.5 assemble_rows.1
  729.4 5.9 assemble_columns.1
  749.4 4.8 collective-permute-done.109.refs_1_
  754.6 7.0 bitcast_subtract_fusion.1
  765.5 2.9 bitcast_subtract_fusion
  768.7 6.4 assemble_packed.1
  794.5 4.4 fusion.3
  (1312 shorter events, 417.7 us)
Async XLA Ops:
  7.2 85.1 %all-gather.6.cloned.1.call-start = ((), (), s32[]{:S(2)}) async-start(), calls=%async_computation.6 | async-start | bytes 1310720 | tf_op jit(solution)/shard_map/all_gather | solution.py:505
  16.3 27.5 %collective-permute-start.18 = (bf16[256,512]{1,0:T(8,128)(2,1)}, bf16[256,512]{1,0:T(8,128)(2,1)}, u32[]{:S(2)}, u32[]{:S(2)}) collective-permute-start(bf16[256,512]{1,0:T(8,128)(2,1)} %get-tuple-element.176), channel_id=1, source_target_pairs={{0,16},{16,0},{1,17},{17,1},{2,18},{18,2},{3,19},{19,3},{4,20},{20... | collective-permute-start | bytes 786440 | tf_op jit(solution)/shard_map/ppermute | solution.py:26
  20.3 21.4 %collective-permute-start.4 = (bf16[272,512]{1,0:T(8,128)(2,1)S(1)}, bf16[272,512]{1,0:T(8,128)(2,1)S(1)}, u32[]{:S(2)}, u32[]{:S(2)}) collective-permute-start(bf16[272,512]{1,0:T(8,128)(2,1)S(1)} %get-tuple-element.384.refs_0_), channel_id=1, source_target_pairs={{0,2},{1,3},{2,0},{3,1},{4,6},{5,7},{6,4},{7,5},{8,10},{9,11},{10,... | collective-permute-start | bytes 835592 | tf_op jit(solution)/shard_map/ppermute | solution.py:509
  22.9 19.3 %collective-permute-start.5 = (bf16[272,512]{1,0:T(8,128)(2,1)S(1)}, bf16[272,512]{1,0:T(8,128)(2,1)S(1)}, u32[]{:S(2)}, u32[]{:S(2)}) collective-permute-start(bf16[272,512]{1,0:T(8,128)(2,1)S(1)} %get-tuple-element.384.refs_0_), channel_id=1, source_target_pairs={{0,3},{1,0},{2,1},{3,2},{4,7},{5,4},{6,5},{7,6},{8,11},{9,8},{10,9... | collective-permute-start | bytes 835592 | tf_op jit(solution)/shard_map/ppermute | solution.py:509
  25.2 21.0 %collective-permute-start.11 = (bf16[128,1024]{1,0:T(8,128)(2,1)S(1)}, bf16[128,1024]{1,0:T(8,128)(2,1)S(1)}, u32[]{:S(2)}, u32[]{:S(2)}) collective-permute-start(bf16[128,1024]{1,0:T(8,128)(2,1)S(1)} %collective-permute-done.10), channel_id=1, source_target_pairs={{0,4},{4,0},{8,12},{12,8},{1,5},{5,1},{9,13},{13,9},{2,6},{6,2},{1... | collective-permute-start | bytes 786440 | tf_op jit(solution)/shard_map/ppermute | solution.py:30
  30.1 34.2 %collective-permute-start.1 = (bf16[256,1024]{1,0:T(8,128)(2,1)S(1)}, bf16[256,1024]{1,0:T(8,128)(2,1)}, u32[]{:S(2)}, u32[]{:S(2)}) collective-permute-start(bf16[256,1024]{1,0:T(8,128)(2,1)S(1)} %pad_maximum_fusion.17), channel_id=1, source_target_pairs={{0,16},{16,0},{1,17},{17,1},{2,18},{18,2},{3,19},{19,3},{4,20},{20... | collective-permute-start | bytes 1572872 | tf_op jit(solution)/shard_map/ppermute | solution.py:26
  47.0 21.8 %collective-permute-start.12 = (bf16[256,1024]{1,0:T(8,128)(2,1)}, bf16[256,1024]{1,0:T(8,128)(2,1)}, u32[]{:S(2)}, u32[]{:S(2)}) collective-permute-start(bf16[256,1024]{1,0:T(8,128)(2,1)} %pad_maximum_fusion.18), channel_id=1, source_target_pairs={{0,16},{16,0},{1,17},{17,1},{2,18},{18,2},{3,19},{19,3},{4,20},{20... | collective-permute-start | bytes 1572872 | tf_op jit(solution)/shard_map/ppermute | solution.py:26
  60.3 61.6 %all-gather.8.cloned.1.call-start = ((), (), s32[]{:S(2)}) async-start(), calls=%async_computation.7 | async-start | bytes 1310720 | tf_op jit(solution)/shard_map/all_gather | solution.py:505
  82.9 89.9 %all-gather.10.cloned.1.call-start = ((), (), s32[]{:S(2)}) async-start(), calls=%async_computation.8 | async-start | bytes 1392640 | tf_op jit(solution)/shard_map/all_gather | solution.py:505
  101.9 20.1 %collective-permute-start.24 = (bf16[128,1024]{1,0:T(8,128)(2,1)S(1)}, bf16[128,1024]{1,0:T(8,128)(2,1)S(1)}, u32[]{:S(2)}, u32[]{:S(2)}) collective-permute-start(bf16[128,1024]{1,0:T(8,128)(2,1)S(1)} %add_convert_fusion.46), channel_id=1, source_target_pairs={{0,4},{4,0},{8,12},{12,8},{1,5},{5,1},{9,13},{13,9},{2,6},{6,2},{1... | collective-permute-start | bytes 786440 | tf_op jit(solution)/shard_map/ppermute | solution.py:30
  103.4 25.2 %collective-permute-start.21 = (bf16[1024,512]{1,0:T(8,128)(2,1)}, bf16[1024,512]{1,0:T(8,128)(2,1)}, u32[]{:S(2)}, u32[]{:S(2)}) collective-permute-start(bf16[1024,512]{1,0:T(8,128)(2,1)} %all-gather.6.cloned.1.call-done), channel_id=1, source_target_pairs={{0,8},{4,12},{8,0},{12,4},{1,9},{5,13},{9,1},{13,5},{2,10},{6,14},... | collective-permute-start | bytes 3145736 | tf_op jit(solution)/shard_map/ppermute | solution.py:34
  140.4 25.4 %collective-permute-start.26 = (bf16[512,1024]{1,0:T(8,128)(2,1)S(1)}, bf16[512,1024]{1,0:T(8,128)(2,1)}, u32[]{:S(2)}, u32[]{:S(2)}) collective-permute-start(bf16[512,1024]{1,0:T(8,128)(2,1)S(1)} %copy-done.96), channel_id=1, source_target_pairs={{0,8},{4,12},{8,0},{12,4},{1,9},{5,13},{9,1},{13,5},{2,10},{6,14},... | collective-permute-start | bytes 3145736 | tf_op jit(solution)/shard_map/ppermute | solution.py:34
  141.9 83.9 %all-gather.12.cloned.1.call-start = ((), (), s32[]{:S(2)}) async-start(), calls=%async_computation.9 | async-start | bytes 1310720 | tf_op jit(solution)/shard_map/all_gather | solution.py:505
  150.0 18.7 %collective-permute-start.30 = (bf16[256,1024]{1,0:T(8,128)(2,1)S(1)}, bf16[256,1024]{1,0:T(8,128)(2,1)S(1)}, u32[]{:S(2)}, u32[]{:S(2)}) collective-permute-start(bf16[256,1024]{1,0:T(8,128)(2,1)S(1)} %pad_maximum_fusion.20), channel_id=1, source_target_pairs={{0,16},{16,0},{1,17},{17,1},{2,18},{18,2},{3,19},{19,3},{4,20},{20... | collective-permute-start | bytes 1572872 | tf_op jit(solution)/shard_map/ppermute | solution.py:26
  186.4 81.3 %all-gather.14.cloned.1.call-start = ((), (), s32[]{:S(2)}) async-start(), calls=%async_computation.10 | async-start | bytes 1310720 | tf_op jit(solution)/shard_map/all_gather | solution.py:505
  186.5 19.5 %collective-permute-start.34 = (bf16[1024,384]{1,0:T(8,128)(2,1)S(1)}, bf16[1024,384]{1,0:T(8,128)(2,1)S(1)}, u32[]{:S(2)}, u32[]{:S(2)}) collective-permute-start(bf16[1024,384]{1,0:T(8,128)(2,1)S(1)} %bitcast.271), channel_id=1, source_target_pairs={{0,8},{4,12},{8,0},{12,4},{1,9},{5,13},{9,1},{13,5},{2,10},{6,14},... | collective-permute-start | bytes 2359304 | tf_op jit(solution)/shard_map/ppermute | solution.py:34
  208.9 14.3 %collective-permute-start.33 = (bf16[256,1024]{1,0:T(8,128)(2,1)S(1)}, bf16[256,1024]{1,0:T(8,128)(2,1)S(1)}, u32[]{:S(2)}, u32[]{:S(2)}) collective-permute-start(bf16[256,1024]{1,0:T(8,128)(2,1)S(1)} %pad_maximum_fusion.21), channel_id=1, source_target_pairs={{0,16},{16,0},{1,17},{17,1},{2,18},{18,2},{3,19},{19,3},{4,20},{20... | collective-permute-start | bytes 1572872 | tf_op jit(solution)/shard_map/ppermute | solution.py:26
  238.6 287.7 %reduce-scatter.7.cloned.1.call-start = ((), (), s32[]{:S(2)}) async-start(), calls=%async_computation.11 | async-start | bytes 1310720 | tf_op jit(solution)/shard_map/reduce_scatter | solution.py:744
  238.7 26.0 %collective-permute-start.44 = (bf16[1024,512]{1,0:T(8,128)(2,1)}, bf16[1024,512]{1,0:T(8,128)(2,1)}, u32[]{:S(2)}, u32[]{:S(2)}) collective-permute-start(bf16[1024,512]{1,0:T(8,128)(2,1)} %all-gather.12.cloned.1.call-done), channel_id=1, source_target_pairs={{0,8},{4,12},{8,0},{12,4},{1,9},{5,13},{9,1},{13,5},{2,10},{6,14},... | collective-permute-start | bytes 3145736 | tf_op jit(solution)/shard_map/ppermute | solution.py:34
  279.9 25.2 %collective-permute-start.48 = (bf16[512,1024]{1,0:T(8,128)(2,1)S(1)}, bf16[512,1024]{1,0:T(8,128)(2,1)S(1)}, u32[]{:S(2)}, u32[]{:S(2)}) collective-permute-start(bf16[512,1024]{1,0:T(8,128)(2,1)S(1)} %copy-done.100), channel_id=1, source_target_pairs={{0,8},{4,12},{8,0},{12,4},{1,9},{5,13},{9,1},{13,5},{2,10},{6,14},... | collective-permute-start | bytes 3145736 | tf_op jit(solution)/shard_map/ppermute | solution.py:34
  287.2 19.6 %collective-permute-start.52 = (bf16[256,1024]{1,0:T(8,128)(2,1)S(1)}, bf16[256,1024]{1,0:T(8,128)(2,1)S(1)}, u32[]{:S(2)}, u32[]{:S(2)}) collective-permute-start(bf16[256,1024]{1,0:T(8,128)(2,1)S(1)} %pad_maximum_fusion.24), channel_id=1, source_target_pairs={{0,16},{16,0},{1,17},{17,1},{2,18},{18,2},{3,19},{19,3},{4,20},{20... | collective-permute-start | bytes 1572872 | tf_op jit(solution)/shard_map/ppermute | solution.py:26
  397.4 25.1 %collective-permute-start.65 = (bf16[512,1024]{1,0:T(8,128)(2,1)S(1)}, bf16[512,1024]{1,0:T(8,128)(2,1)S(1)}, u32[]{:S(2)}, u32[]{:S(2)}) collective-permute-start(bf16[512,1024]{1,0:T(8,128)(2,1)S(1)} %add_convert_fusion.12), channel_id=1, source_target_pairs={{0,8},{4,12},{8,0},{12,4},{1,9},{5,13},{9,1},{13,5},{2,10},{6,14},... | collective-permute-start | bytes 3145736 | tf_op jit(solution)/shard_map/ppermute | solution.py:34
  419.0 13.8 %collective-permute-start.67 = (bf16[256,1024]{1,0:T(8,128)(2,1)S(1)}, bf16[256,1024]{1,0:T(8,128)(2,1)S(1)}, u32[]{:S(2)}, u32[]{:S(2)}) collective-permute-start(bf16[256,1024]{1,0:T(8,128)(2,1)S(1)} %pad_maximum_fusion.28), channel_id=1, source_target_pairs={{0,16},{16,0},{1,17},{17,1},{2,18},{18,2},{3,19},{19,3},{4,20},{20... | collective-permute-start | bytes 1572872 | tf_op jit(solution)/shard_map/ppermute | solution.py:26
  447.0 37.5 %collective-permute-start.68 = (bf16[1024,512]{1,0:T(8,128)(2,1)}, bf16[1024,512]{1,0:T(8,128)(2,1)}, u32[]{:S(2)}, u32[]{:S(2)}) collective-permute-start(bf16[1024,512]{1,0:T(8,128)(2,1)} %add_convert_fusion.10), channel_id=1, source_target_pairs={{0,8},{4,12},{8,0},{12,4},{1,9},{5,13},{9,1},{13,5},{2,10},{6,14},... | collective-permute-start | bytes 3145736 | tf_op jit(solution)/shard_map/ppermute | solution.py:34
  453.2 110.6 %reduce-scatter.9.cloned.1.call-start = ((), (), s32[]{:S(2)}) async-start(), calls=%async_computation.12 | async-start | bytes 1310720 | tf_op jit(solution)/shard_map/reduce_scatter | solution.py:744
  459.4 19.5 %collective-permute-start.69 = (bf16[128,1024]{1,0:T(8,128)(2,1)S(1)}, bf16[128,1024]{1,0:T(8,128)(2,1)S(1)}, u32[]{:S(2)}, u32[]{:S(2)}) collective-permute-start(bf16[128,1024]{1,0:T(8,128)(2,1)S(1)} %copy-done.123), channel_id=1, source_target_pairs={{0,8},{4,12},{8,0},{12,4},{1,9},{5,13},{9,1},{13,5},{2,10},{6,14},... | collective-permute-start | bytes 786440 | tf_op jit(solution)/shard_map/ppermute | solution.py:34
  459.9 24.6 %collective-permute-start.70 = (bf16[128,1024]{1,0:T(8,128)(2,1)S(1)}, bf16[128,1024]{1,0:T(8,128)(2,1)S(1)}, u32[]{:S(2)}, u32[]{:S(2)}) collective-permute-start(bf16[128,1024]{1,0:T(8,128)(2,1)S(1)} %copy-done.225), channel_id=1, source_target_pairs={{0,8},{4,12},{8,0},{12,4},{1,9},{5,13},{9,1},{13,5},{2,10},{6,14},... | collective-permute-start | bytes 786440 | tf_op jit(solution)/shard_map/ppermute | solution.py:34
  462.1 41.2 %collective-permute-start.75 = (bf16[2,128,512]{2,1,0:T(8,128)(2,1)}, bf16[2,128,512]{2,1,0:T(8,128)(2,1)S(1)}, u32[]{:S(2)}, u32[]{:S(2)}) collective-permute-start(bf16[2,128,512]{2,1,0:T(8,128)(2,1)} %bitcast.33), channel_id=1, source_target_pairs={{0,8},{4,12},{8,0},{12,4},{1,9},{5,13},{9,1},{13,5},{2,10},{6,14},... | collective-permute-start | bytes 786440 | tf_op jit(solution)/shard_map/ppermute | solution.py:34
  469.7 34.1 %collective-permute-start.78 = (bf16[128,1024]{1,0:T(8,128)(2,1)}, bf16[128,1024]{1,0:T(8,128)(2,1)}, u32[]{:S(2)}, u32[]{:S(2)}) collective-permute-start(bf16[128,1024]{1,0:T(8,128)(2,1)} %add_convert_fusion.36), channel_id=1, source_target_pairs={{0,4},{4,0},{8,12},{12,8},{1,5},{5,1},{9,13},{13,9},{2,6},{6,2},{1... | collective-permute-start | bytes 786440 | tf_op jit(solution)/shard_map/ppermute | solution.py:30
  487.4 28.1 %collective-permute-start.71 = (bf16[2,128,1024]{2,1,0:T(8,128)(2,1)}, bf16[2,128,1024]{2,1,0:T(8,128)(2,1)}, u32[]{:S(2)}, u32[]{:S(2)}) collective-permute-start(bf16[2,128,1024]{2,1,0:T(8,128)(2,1)} %maximum_select_fusion.4), channel_id=1, source_target_pairs={{0,16},{16,0},{1,17},{17,1},{2,18},{18,2},{3,19},{19,3},{4,20},{20... | collective-permute-start | bytes 1572872 | tf_op jit(solution)/shard_map/ppermute | solution.py:26
  490.4 131.1 %reduce-scatter.11.cloned.1.call-start = ((), (), s32[]{:S(2)}) async-start(), calls=%async_computation.13 | async-start | bytes 1392640 | tf_op jit(solution)/shard_map/reduce_scatter | solution.py:744
  517.8 122.7 %collective-permute-start.96 = (bf16[128,1024]{1,0:T(8,128)(2,1)}, bf16[128,1024]{1,0:T(8,128)(2,1)}, u32[]{:S(2)}, u32[]{:S(2)}) collective-permute-start(bf16[128,1024]{1,0:T(8,128)(2,1)} %get-tuple-element.354), channel_id=1, source_target_pairs={{0,8},{4,12},{8,0},{12,4},{1,9},{5,13},{9,1},{13,5},{2,10},{6,14},... | collective-permute-start | bytes 786440 | tf_op jit(solution)/shard_map/ppermute | solution.py:34
  536.1 27.6 %collective-permute-start.85 = (bf16[1024,384]{1,0:T(8,128)(2,1)}, bf16[1024,384]{1,0:T(8,128)(2,1)S(1)}, u32[]{:S(2)}, u32[]{:S(2)}) collective-permute-start(bf16[1024,384]{1,0:T(8,128)(2,1)} %add_convert_fusion.22), channel_id=1, source_target_pairs={{0,8},{4,12},{8,0},{12,4},{1,9},{5,13},{9,1},{13,5},{2,10},{6,14},... | collective-permute-start | bytes 2359304 | tf_op jit(solution)/shard_map/ppermute | solution.py:34
  537.6 26.1 %collective-permute-start.86 = (bf16[128,1024]{1,0:T(8,128)(2,1)}, bf16[128,1024]{1,0:T(8,128)(2,1)}, u32[]{:S(2)}, u32[]{:S(2)}) collective-permute-start(bf16[128,1024]{1,0:T(8,128)(2,1)} %reduce-scatter.7.cloned.1.call-done.refs_8_), channel_id=1, source_target_pairs={{0,8},{4,12},{8,0},{12,4},{1,9},{5,13},{9,1},{13,5},{2,10},{6,14},... | collective-permute-start | bytes 786440 | tf_op jit(solution)/shard_map/ppermute | solution.py:34
  546.7 15.7 %collective-permute-start.81 = (bf16[128,1024]{1,0:T(8,128)(2,1)S(1)}, bf16[128,1024]{1,0:T(8,128)(2,1)S(1)}, u32[]{:S(2)}, u32[]{:S(2)}) collective-permute-start(bf16[128,1024]{1,0:T(8,128)(2,1)S(1)} %add_convert_fusion.33), channel_id=1, source_target_pairs={{0,4},{4,0},{8,12},{12,8},{1,5},{5,1},{9,13},{13,9},{2,6},{6,2},{1... | collective-permute-start | bytes 786440 | tf_op jit(solution)/shard_map/ppermute | solution.py:30
  560.2 82.0 %collective-permute-start.97 = (bf16[128,1024]{1,0:T(8,128)(2,1)}, bf16[128,1024]{1,0:T(8,128)(2,1)}, u32[]{:S(2)}, u32[]{:S(2)}) collective-permute-start(bf16[128,1024]{1,0:T(8,128)(2,1)} %reduce-scatter.7.cloned.1.call-done.refs_8_), channel_id=1, source_target_pairs={{0,4},{4,0},{8,12},{12,8},{1,5},{5,1},{9,13},{13,9},{2,6},{6,2},{1... | collective-permute-start | bytes 786440 | tf_op jit(solution)/shard_map/ppermute | solution.py:30
  567.7 29.3 %collective-permute-start.90 = (bf16[512,1024]{1,0:T(8,128)(2,1)}, bf16[512,1024]{1,0:T(8,128)(2,1)}, u32[]{:S(2)}, u32[]{:S(2)}) collective-permute-start(bf16[512,1024]{1,0:T(8,128)(2,1)} %add_convert_fusion.4), channel_id=1, source_target_pairs={{0,8},{4,12},{8,0},{12,4},{1,9},{5,13},{9,1},{13,5},{2,10},{6,14},... | collective-permute-start | bytes 3145736 | tf_op jit(solution)/shard_map/ppermute | solution.py:34
  570.5 78.0 %reduce-scatter.13.cloned.1.call-start = ((), (), s32[]{:S(2)}) async-start(), calls=%async_computation.14 | async-start | bytes 1310720 | tf_op jit(solution)/shard_map/reduce_scatter | solution.py:744
  595.3 25.7 %collective-permute-start.93 = (bf16[256,512]{1,0:T(8,128)(2,1)}, bf16[256,512]{1,0:T(8,128)(2,1)}, u32[]{:S(2)}, u32[]{:S(2)}) collective-permute-start(bf16[256,512]{1,0:T(8,128)(2,1)} %reduce-scatter.9.cloned.1.call-done.refs_8_), channel_id=1, source_target_pairs={{0,4},{4,0},{8,12},{12,8},{1,5},{5,1},{9,13},{13,9},{2,6},{6,2},{1... | collective-permute-start | bytes 786440 | tf_op jit(solution)/shard_map/ppermute | solution.py:30
  597.0 47.5 %collective-permute-start.129 = (bf16[256,512]{1,0:T(8,128)(2,1)}, bf16[256,512]{1,0:T(8,128)(2,1)}, u32[]{:S(2)}, u32[]{:S(2)}) collective-permute-start(bf16[256,512]{1,0:T(8,128)(2,1)} %reduce-scatter.9.cloned.1.call-done.refs_8_), channel_id=1, source_target_pairs={{0,8},{4,12},{8,0},{12,4},{1,9},{5,13},{9,1},{13,5},{2,10},{6,14},... | collective-permute-start | bytes 786440 | tf_op jit(solution)/shard_map/ppermute | solution.py:34
  598.5 45.4 %collective-permute-start.98 = (bf16[128,1024]{1,0:T(8,128)(2,1)}, bf16[128,1024]{1,0:T(8,128)(2,1)}, u32[]{:S(2)}, u32[]{:S(2)}) collective-permute-start(bf16[128,1024]{1,0:T(8,128)(2,1)} %collective-permute-done.86.refs_10_), channel_id=1, source_target_pairs={{0,4},{4,0},{8,12},{12,8},{1,5},{5,1},{9,13},{13,9},{2,6},{6,2},{1... | collective-permute-start | bytes 786440 | tf_op jit(solution)/shard_map/ppermute | solution.py:30
  616.5 71.1 %reduce-scatter.15.cloned.1.call-start = ((), (), s32[]{:S(2)}) async-start(), calls=%async_computation.15 | async-start | bytes 1310720 | tf_op jit(solution)/shard_map/reduce_scatter | solution.py:744
  621.0 25.0 %collective-permute-start.94 = (bf16[1024,512]{1,0:T(8,128)(2,1)}, bf16[1024,512]{1,0:T(8,128)(2,1)}, u32[]{:S(2)}, u32[]{:S(2)}) collective-permute-start(bf16[1024,512]{1,0:T(8,128)(2,1)} %add_convert_fusion.2), channel_id=1, source_target_pairs={{0,8},{4,12},{8,0},{12,4},{1,9},{5,13},{9,1},{13,5},{2,10},{6,14},... | collective-permute-start | bytes 3145736 | tf_op jit(solution)/shard_map/ppermute | solution.py:34
  644.0 17.9 %collective-permute-start.131 = (bf16[256,512]{1,0:T(8,128)(2,1)}, bf16[256,512]{1,0:T(8,128)(2,1)S(1)}, u32[]{:S(2)}, u32[]{:S(2)}) collective-permute-start(bf16[256,512]{1,0:T(8,128)(2,1)} %reduce-scatter.9.cloned.1.call-done.refs_8_), channel_id=1, source_target_pairs={{0,16},{16,0},{1,17},{17,1},{2,18},{18,2},{3,19},{19,3},{4,20},{20... | collective-permute-start | bytes 786440 | tf_op jit(solution)/shard_map/ppermute | solution.py:26
  644.5 18.0 %collective-permute-start.133 = (bf16[256,512]{1,0:T(8,128)(2,1)}, bf16[256,512]{1,0:T(8,128)(2,1)S(1)}, u32[]{:S(2)}, u32[]{:S(2)}) collective-permute-start(bf16[256,512]{1,0:T(8,128)(2,1)} %collective-permute-done.129.refs_10_), channel_id=1, source_target_pairs={{0,16},{16,0},{1,17},{17,1},{2,18},{18,2},{3,19},{19,3},{4,20},{20... | collective-permute-start | bytes 786440 | tf_op jit(solution)/shard_map/ppermute | solution.py:26
  646.0 18.0 %collective-permute-start.102 = (bf16[2,128,512]{2,1,0:T(8,128)(2,1)}, bf16[2,128,512]{2,1,0:T(8,128)(2,1)S(1)}, u32[]{:S(2)}, u32[]{:S(2)}) collective-permute-start(bf16[2,128,512]{2,1,0:T(8,128)(2,1)} %bitcast.39), channel_id=1, source_target_pairs={{0,8},{4,12},{8,0},{12,4},{1,9},{5,13},{9,1},{13,5},{2,10},{6,14},... | collective-permute-start | bytes 786440 | tf_op jit(solution)/shard_map/ppermute | solution.py:34
  651.0 93.9 %reduce-scatter.17.cloned.1.call-start = ((), (), s32[]{:S(2)}) async-start(), calls=%async_computation.16 | async-start | bytes 1392640 | tf_op jit(solution)/shard_map/reduce_scatter | solution.py:744
  662.5 17.1 %collective-permute-start.105 = (bf16[128,1024]{1,0:T(8,128)(2,1)S(1)}, bf16[128,1024]{1,0:T(8,128)(2,1)}, u32[]{:S(2)}, u32[]{:S(2)}) collective-permute-start(bf16[128,1024]{1,0:T(8,128)(2,1)S(1)} %add_convert_fusion.28), channel_id=1, source_target_pairs={{0,8},{4,12},{8,0},{12,4},{1,9},{5,13},{9,1},{13,5},{2,10},{6,14},... | collective-permute-start | bytes 786440 | tf_op jit(solution)/shard_map/ppermute | solution.py:34
  664.0 15.6 %collective-permute-start.100 = (bf16[128,1024]{1,0:T(8,128)(2,1)S(1)}, bf16[128,1024]{1,0:T(8,128)(2,1)S(1)}, u32[]{:S(2)}, u32[]{:S(2)}) collective-permute-start(bf16[128,1024]{1,0:T(8,128)(2,1)S(1)} %add_convert_fusion.31), channel_id=1, source_target_pairs={{0,4},{4,0},{8,12},{12,8},{1,5},{5,1},{9,13},{13,9},{2,6},{6,2},{1... | collective-permute-start | bytes 786440 | tf_op jit(solution)/shard_map/ppermute | solution.py:30
  668.1 16.2 %collective-permute-start.103 = (bf16[128,1024]{1,0:T(8,128)(2,1)S(1)}, bf16[128,1024]{1,0:T(8,128)(2,1)}, u32[]{:S(2)}, u32[]{:S(2)}) collective-permute-start(bf16[128,1024]{1,0:T(8,128)(2,1)S(1)} %copy-done.36), channel_id=1, source_target_pairs={{0,8},{4,12},{8,0},{12,4},{1,9},{5,13},{9,1},{13,5},{2,10},{6,14},... | collective-permute-start | bytes 786440 | tf_op jit(solution)/shard_map/ppermute | solution.py:34
  670.8 13.5 %collective-permute-start.135 = (bf16[128,1024]{1,0:T(8,128)(2,1)S(1)}, bf16[128,1024]{1,0:T(8,128)(2,1)}, u32[]{:S(2)}, u32[]{:S(2)}) collective-permute-start(bf16[128,1024]{1,0:T(8,128)(2,1)S(1)} %copy-done.36), channel_id=1, source_target_pairs={{0,4},{4,0},{8,12},{12,8},{1,5},{5,1},{9,13},{13,9},{2,6},{6,2},{1... | collective-permute-start | bytes 786440 | tf_op jit(solution)/shard_map/ppermute | solution.py:30
  679.6 21.0 %collective-permute-start.107 = (bf16[1024,384]{1,0:T(8,128)(2,1)}, bf16[1024,384]{1,0:T(8,128)(2,1)S(1)}, u32[]{:S(2)}, u32[]{:S(2)}) collective-permute-start(bf16[1024,384]{1,0:T(8,128)(2,1)} %add_convert_fusion.20), channel_id=1, source_target_pairs={{0,8},{4,12},{8,0},{12,4},{1,9},{5,13},{9,1},{13,5},{2,10},{6,14},... | collective-permute-start | bytes 2359304 | tf_op jit(solution)/shard_map/ppermute | solution.py:34
  691.8 14.9 %collective-permute-start.122 = (bf16[256,512]{1,0:T(8,128)(2,1)}, bf16[256,512]{1,0:T(8,128)(2,1)}, u32[]{:S(2)}, u32[]{:S(2)}) collective-permute-start(bf16[256,512]{1,0:T(8,128)(2,1)} %reduce-scatter.15.cloned.1.call-done.refs_0_), channel_id=1, source_target_pairs={{0,4},{4,0},{8,12},{12,8},{1,5},{5,1},{9,13},{13,9},{2,6},{6,2},{1... | collective-permute-start | bytes 786440 | tf_op jit(solution)/shard_map/ppermute | solution.py:30
  692.4 22.6 %collective-permute-start.106 = (bf16[2,128,1024]{2,1,0:T(8,128)(2,1)}, bf16[2,128,1024]{2,1,0:T(8,128)(2,1)}, u32[]{:S(2)}, u32[]{:S(2)}) collective-permute-start(bf16[2,128,1024]{2,1,0:T(8,128)(2,1)} %maximum_select_fusion.6), channel_id=1, source_target_pairs={{0,16},{16,0},{1,17},{17,1},{2,18},{18,2},{3,19},{19,3},{4,20},{20... | collective-permute-start | bytes 1572872 | tf_op jit(solution)/shard_map/ppermute | solution.py:26
  711.0 17.8 %collective-permute-start.134 = (bf16[256,512]{1,0:T(8,128)(2,1)}, bf16[256,512]{1,0:T(8,128)(2,1)S(1)}, u32[]{:S(2)}, u32[]{:S(2)}) collective-permute-start(bf16[256,512]{1,0:T(8,128)(2,1)} %collective-permute-done.130.refs_11_), channel_id=1, source_target_pairs={{0,16},{16,0},{1,17},{17,1},{2,18},{18,2},{3,19},{19,3},{4,20},{20... | collective-permute-start | bytes 786440 | tf_op jit(solution)/shard_map/ppermute | solution.py:26
  711.1 17.8 %collective-permute-start.125 = (bf16[256,512]{1,0:T(8,128)(2,1)S(1)}, bf16[256,512]{1,0:T(8,128)(2,1)S(1)}, u32[]{:S(2)}, u32[]{:S(2)}) collective-permute-start(bf16[256,512]{1,0:T(8,128)(2,1)S(1)} %copy-done.37), channel_id=1, source_target_pairs={{0,16},{16,0},{1,17},{17,1},{2,18},{18,2},{3,19},{19,3},{4,20},{20... | collective-permute-start | bytes 786440 | tf_op jit(solution)/shard_map/ppermute | solution.py:26
  711.6 17.8 %collective-permute-start.126 = (bf16[256,512]{1,0:T(8,128)(2,1)}, bf16[256,512]{1,0:T(8,128)(2,1)S(1)}, u32[]{:S(2)}, u32[]{:S(2)}) collective-permute-start(bf16[256,512]{1,0:T(8,128)(2,1)} %collective-permute-done.122.refs_1_), channel_id=1, source_target_pairs={{0,16},{16,0},{1,17},{17,1},{2,18},{18,2},{3,19},{19,3},{4,20},{20... | collective-permute-start | bytes 786440 | tf_op jit(solution)/shard_map/ppermute | solution.py:26
  715.0 14.4 %collective-permute-start.127 = (bf16[256,512]{1,0:T(8,128)(2,1)}, bf16[256,512]{1,0:T(8,128)(2,1)S(1)}, u32[]{:S(2)}, u32[]{:S(2)}) collective-permute-start(bf16[256,512]{1,0:T(8,128)(2,1)} %collective-permute-done.123.refs_2_), channel_id=1, source_target_pairs={{0,16},{16,0},{1,17},{17,1},{2,18},{18,2},{3,19},{19,3},{4,20},{20... | collective-permute-start | bytes 786440 | tf_op jit(solution)/shard_map/ppermute | solution.py:26
  715.0 14.4 %collective-permute-start.128 = (bf16[256,512]{1,0:T(8,128)(2,1)}, bf16[256,512]{1,0:T(8,128)(2,1)S(1)}, u32[]{:S(2)}, u32[]{:S(2)}) collective-permute-start(bf16[256,512]{1,0:T(8,128)(2,1)} %collective-permute-done.124.refs_3_), channel_id=1, source_target_pairs={{0,16},{16,0},{1,17},{17,1},{2,18},{18,2},{3,19},{19,3},{4,20},{20... | collective-permute-start | bytes 786440 | tf_op jit(solution)/shard_map/ppermute | solution.py:26
  728.8 20.1 %collective-permute-start.118 = (bf16[272,512]{1,0:T(8,128)(2,1)S(1)}, bf16[272,512]{1,0:T(8,128)(2,1)S(1)}, u32[]{:S(2)}, u32[]{:S(2)}) collective-permute-start(bf16[272,512]{1,0:T(8,128)(2,1)S(1)} %copy-done.29), channel_id=1, source_target_pairs={{0,16},{16,0},{1,17},{17,1},{2,18},{18,2},{3,19},{19,3},{4,20},{20... | collective-permute-start | bytes 835592 | tf_op jit(solution)/shard_map/ppermute | solution.py:26
  728.9 35.5 %collective-permute-start.120 = (bf16[272,512]{1,0:T(8,128)(2,1)S(1)}, bf16[272,512]{1,0:T(8,128)(2,1)S(1)}, u32[]{:S(2)}, u32[]{:S(2)}) collective-permute-start(bf16[272,512]{1,0:T(8,128)(2,1)S(1)} %collective-permute-done.116.refs_10_), channel_id=1, source_target_pairs={{0,16},{16,0},{1,17},{17,1},{2,18},{18,2},{3,19},{19,3},{4,20},{20... | collective-permute-start | bytes 835592 | tf_op jit(solution)/shard_map/ppermute | solution.py:26
  743.0 21.2 %collective-permute-start.117 = (bf16[272,512]{1,0:T(8,128)(2,1)S(1)}, bf16[272,512]{1,0:T(8,128)(2,1)S(1)}, u32[]{:S(2)}, u32[]{:S(2)}) collective-permute-start(bf16[272,512]{1,0:T(8,128)(2,1)S(1)} %collective-permute-done.95.refs_9_), channel_id=1, source_target_pairs={{0,8},{4,12},{8,0},{12,4},{1,9},{5,13},{9,1},{13,5},{2,10},{6,14},... | collective-permute-start | bytes 835592 | tf_op jit(solution)/shard_map/ppermute | solution.py:34
  744.8 20.1 %collective-permute-start.119 = (bf16[272,512]{1,0:T(8,128)(2,1)S(1)}, bf16[272,512]{1,0:T(8,128)(2,1)S(1)}, u32[]{:S(2)}, u32[]{:S(2)}) collective-permute-start(bf16[272,512]{1,0:T(8,128)(2,1)S(1)} %collective-permute-done.95.refs_9_), channel_id=1, source_target_pairs={{0,16},{16,0},{1,17},{17,1},{2,18},{18,2},{3,19},{19,3},{4,20},{20... | collective-permute-start | bytes 835592 | tf_op jit(solution)/shard_map/ppermute | solution.py:26
  748.9 16.1 %collective-permute-start.110 = (bf16[272,512]{1,0:T(8,128)(2,1)}, bf16[272,512]{1,0:T(8,128)(2,1)S(1)}, u32[]{:S(2)}, u32[]{:S(2)}) collective-permute-start(bf16[272,512]{1,0:T(8,128)(2,1)} %reduce-scatter.17.cloned.1.call-done.refs_0_), channel_id=1, source_target_pairs={{0,8},{4,12},{8,0},{12,4},{1,9},{5,13},{9,1},{13,5},{2,10},{6,14},... | collective-permute-start | bytes 835592 | tf_op jit(solution)/shard_map/ppermute | solution.py:34
  (452 other events, 4032.5 us)
Sparse Core Ops, SparseCore 0:
  60.4 31.8 all-gather.5
  94.5 27.4 all-gather.7
  142.1 29.7 all-gather.9
  186.5 28.6 all-gather.11
  238.7 28.8 all-gather.13
  453.3 26.6 reduce-scatter.6
  490.5 26.6 reduce-scatter.8
  570.6 27.6 reduce-scatter.10
  616.6 26.5 reduce-scatter.12
  651.1 27.2 reduce-scatter.14
  711.1 27.5 reduce-scatter.16

commit v3 on v2

--- a/solution.py
+++ b/solution.py
@@ -1,4 +1,5 @@
 import functools
+import types
 
 import jax
 import jax.numpy as jnp
@@ -20,18 +21,20 @@
 bf16 = jnp.bfloat16
 f32 = jnp.float32
 LANES = 128
+SECTION, CTX, FSDP = "section", "ctx", "fsdp"
+ROWS, COLUMNS, PACKED = range(3)
 
 
 def swap_core(value):
-    return lax.ppermute(value, "section", [(0, 1), (1, 0)])
+    return lax.ppermute(value, SECTION, [(0, 1), (1, 0)])
 
 
 def swap_x(value):
-    return lax.ppermute(value, "ctx", [(i, i ^ 1) for i in range(4)])
+    return lax.ppermute(value, CTX, [(i, i ^ 1) for i in range(4)])
 
 
 def swap_y(value):
-    return lax.ppermute(value, "ctx", [(i, i ^ 2) for i in range(4)])
+    return lax.ppermute(value, CTX, [(i, i ^ 2) for i in range(4)])
 
 
 def dot(left, right):
@@ -50,18 +53,21 @@
     return lax.optimization_barrier((value, *tokens))[0]
 
 
-def gather4(value):
-    pair = jnp.concatenate([value, swap_x(value)], axis=0)
-    return jnp.concatenate([pair, swap_core(pair)], axis=0)
+def with_core(value):
+    return jnp.concatenate([value, swap_core(value)], axis=0)
+
+
+def gather_tiles(value):
+    return [with_core(value), with_core(swap_x(value))]
 
 
 def fold_core(partial):
-    half = partial.shape[0] // 2
-    rows = half // 2
+    rows = partial.shape[0] // 2
     partial = partial.astype(bf16)
-    mine, theirs = partial[:half], swap_core(partial[half:])
-    keep = mine[:rows].astype(f32) + theirs[:rows].astype(f32)
-    return keep, (mine[rows:].astype(f32) + theirs[rows:].astype(f32)).astype(bf16)
+    return partial[:rows].astype(f32) + swap_core(partial[rows:]).astype(f32)
+
+
+(PROJECT, ATTEND0, ATTEND1, STACKED, LAST, NORM, FEED0, FEED1) = range(8)
 
 
 def norm_parts(values):
@@ -127,7 +133,6 @@
         cost_estimate=pl.CostEstimate(
             flops=elems * 4 * 128, bytes_accessed=4 << 20, transcendentals=elems
         ),
-        name="attention_forward",
     )(projected, keys_values, keys_values, query_ids, key_ids)
 
 
@@ -193,7 +198,6 @@
         cost_estimate=pl.CostEstimate(
             flops=elems * 10 * 128, bytes_accessed=6 << 20, transcendentals=elems
         ),
-        name="attention_backward",
     )(projected, keys_values, keys_values, grads, lse, query_ids, key_ids)
 
 
@@ -262,7 +266,6 @@
         ),
         out_shape=outs,
         compiler_params=pltpu.CompilerParams(vmem_limit_bytes=56 << 20),
-        name="cut_weights",
     )(at_eighth, *operands)
 
 
@@ -312,11 +315,10 @@
         ),
         out_shape=outs,
         compiler_params=pltpu.CompilerParams(vmem_limit_bytes=24 << 20),
-        name="place_rows",
     )(depth, *(list(packed) * (count if fixed else 1)), *(list(far) * (count if fixed else 1)))
 
 
-def small_call(kernel, at, operands, outs, name):
+def small_call(kernel, at, operands, outs):
     return pl.pallas_call(
         kernel,
         grid_spec=pltpu.PrefetchScalarGridSpec(
@@ -327,7 +329,6 @@
         ),
         out_shape=outs,
         compiler_params=pltpu.CompilerParams(vmem_limit_bytes=40 << 20),
-        name=name,
     )(at, *operands)
 
 
@@ -382,10 +383,10 @@
             eighth = (2 * chip + core) ^ at[0]
             value = jnp.where(first_core, groups[core][chip][...], groups[2 + core][chip][...])
             value = value.astype(f32)
-            if kind == "rows":
+            if kind == ROWS:
                 rows = value.shape[0]
                 grads[0][pl.ds(pl.multiple_of(eighth * rows, rows), rows), :] = value
-            elif kind == "columns":
+            elif kind == COLUMNS:
                 for i in range(value.shape[1] // LANES):
                     start = pl.multiple_of((8 * i + eighth) * LANES, LANES)
                     grads[0][:, pl.ds(start, LANES)] = value[:, LANES * i : LANES * (i + 1)]
@@ -400,7 +401,7 @@
                     block = value[half * LANES : (half + 1) * LANES, 3 * LANES :]
                     grads[1][part, pl.ds(start, LANES)] = block
                 gain = gain + value[rows : rows + 1, :]
-    if kind == "packed":
+    if kind == PACKED:
         outs[-2][...] = gain
     sums_ref[...] = jnp.zeros_like(sums_ref)
     lane = lax.broadcasted_iota(jnp.int32, (1, LANES), 1)
@@ -430,7 +431,7 @@
 def assemble(near0, near1, far0, far1, rows_old, where, kind, shapes):
     outs = [jax.ShapeDtypeStruct(shape, f32) for shape in shapes]
     outs += [jax.ShapeDtypeStruct((shape[0], 1), f32) for shape in shapes]
-    if kind == "packed":
+    if kind == PACKED:
         outs.append(jax.ShapeDtypeStruct((1, near0[0].shape[1]), f32))
     outs.append(
         jax.ShapeDtypeStruct((1, LANES + 2 * sum(shape[1] for shape in shapes)), f32)
@@ -440,7 +441,6 @@
         where,
         [*near0, *far0, *near1, *far1, *rows_old],
         outs,
-        "assemble_" + kind,
     )
 
 
@@ -465,12 +465,12 @@
     var_attn,
     var_mlp,
 ):
-    core = lax.axis_index("section")
-    chip = lax.axis_index("ctx")
-    depth = lax.axis_index("fsdp")
+    core = lax.axis_index(SECTION)
+    chip = lax.axis_index(CTX)
+    depth = lax.axis_index(FSDP)
     y, x = chip // 2, chip % 2
-    fsdp_count = lax.axis_size("fsdp")
-    assert lax.axis_size("section") == 2 and lax.axis_size("ctx") == 4
+    fsdp_count = lax.axis_size(FSDP)
+    assert lax.axis_size(SECTION) == 2 and lax.axis_size(CTX) == 4
     _, block, width = tokens.shape
     half = block // 2
     rows = w_qkv.shape[1]
@@ -502,12 +502,12 @@
         return jnp.where(first_core, mine, taken), jnp.where(first_core, taken, mine)
 
     def gather_rows(value):
-        return lax.all_gather(value, "fsdp", axis=0, tiled=True)
+        return lax.all_gather(value, FSDP, axis=0, tiled=True)
 
     def rotations(value):
         return [value] + [
             lax.ppermute(
-                value, "fsdp", [(i, (i + k) % fsdp_count) for i in range(fsdp_count)]
+                value, FSDP, [(i, (i + k) % fsdp_count) for i in range(fsdp_count)]
             )
             for k in range(1, fsdp_count)
         ]
@@ -521,9 +521,9 @@
         keep, came = columns[:2], swap_x(columns[2:])
         out = jax.ShapeDtypeStruct((2 * LANES, width), bf16)
         operands = [keep, came, swap_y(keep), swap_y(came)]
-        return small_call(join_out_kernel, chip_array, operands, [out], "join_out")[0]
-
-    weights, gains = [{}, {}], [None, None]
+        return small_call(join_out_kernel, chip_array, operands, [out])[0]
+
+    weights, gains = [types.SimpleNamespace(), types.SimpleNamespace()], [None, None]
     depth_array = jnp.stack([depth, chip]).astype(jnp.int32)
     if even:
         cuts = cut_weights(
@@ -536,8 +536,8 @@
         turns = rotations(packed_parts[0])
         fars = [swap_y(value[:rows, : 3 * LANES]) for value in turns[1:]]
         qkv, columns, gains[0] = place(turns, [far_parts[0]] + fars, depth_array, False)
-        weights[0]["qkv"] = qkv
-        weights[0]["out"] = out_from_columns(columns)
+        weights[0].qkv = qkv
+        weights[0].out = out_from_columns(columns)
         up_gathered = [gather_rows(after(up_parts[0], *turns[1:])), gather_rows(up_parts[1])]
         down_gathered = [gather_rows(after(down_parts[0], *turns[1:])), gather_rows(down_parts[1])]
         packed_gathered = gather_rows(packed_parts[1])
@@ -547,13 +547,13 @@
         whole_out = gather_rows(w_out[0].astype(bf16))
         out_parts = by_layer(whole_out, whole_out)
         gains_own = lax.all_gather(
-            jnp.concatenate([gain_attn, gain_mlp], axis=0).astype(bf16), "fsdp", axis=1, tiled=True
+            jnp.concatenate([gain_attn, gain_mlp], axis=0).astype(bf16), FSDP, axis=1, tiled=True
         )
         gains = [part.astype(f32) for part in by_layer(gains_own, gains_own)]
         for layer in range(2):
             blocks = out_parts[layer].reshape(4, 2, LANES, width)
             blocks = lax.dynamic_index_in_dim(blocks, core, 1, keepdims=False)
-            weights[layer] = dict(
+            weights[layer] = types.SimpleNamespace(
                 qkv=jnp.concatenate(with_far(gather_rows(qkv_parts[layer])), axis=1),
                 out=jnp.concatenate(
                     [
@@ -569,62 +569,49 @@
     def own_rows(value):
         near = lax.dynamic_slice(value, (y, core * half, 0), (1, half, width))[0]
         away = lax.dynamic_slice(value, (1 - y, core * half, 0), (1, half, width))[0]
-        return [near, swap_y(away)]
+        return jnp.concatenate([near, swap_y(away)], axis=0)
 
     ids = lax.dynamic_index_in_dim(segment_ids, y, 0, keepdims=False).reshape(2, 2, 2, half)
     ids = flipped(~first_y, flipped(~first_x, flipped(~first_core, ids, 2), 1), 0)
-    ids = ids.transpose(0, 2, 1, 3)
+    ids = ids.transpose(1, 2, 0, 3)
     key_ids = ids.reshape(8 * half, 1)
     query_ids = [ids[k].reshape(1, 4 * half) for k in range(2)]
 
     def forward(inputs, layer, hook):
         held = weights[layer]
         attn_gain, mlp_gain = gains[layer][0], gains[layer][1]
-        inputs_all = [gather4(value) for value in inputs]
-        first_in = hook("project", inputs_all[0])
-        projected = [dot(value, held["qkv"]).astype(bf16) for value in (first_in, inputs_all[1])]
+        inputs_all = gather_tiles(inputs)
+        projected = [dot(value, held.qkv).astype(bf16) for value in inputs_all]
         keys_values = jnp.concatenate(projected, axis=0)
 
         def attend(k, queries):
             context, lse = attention_forward(queries, keys_values, query_ids[k], key_ids, scale)
-            return context, lse, *fold_core(dot(context, held["out"]))
-
-        context0, lse0, keep0, across0 = attend(0, hook("attend0", projected[0]))
-        context1, lse1, keep1, across1 = attend(1, hook("attend1", after(projected[1], across0)))
-        came0 = hook("norm0", after(swap_x(across0), across1))
-        came1 = hook("norm1", swap_x(across1))
-        unit_attn, scale_attn, normed, normed_all = [], [], [], []
-        for k, (keep, came) in enumerate(((keep0, came0), (keep1, came1))):
-            pre_attn = inputs[k].astype(f32) + keep + came.astype(f32)
-            unit, factor = norm_parts(pre_attn)
-            unit_attn.append(unit)
-            scale_attn.append(factor)
-            normed.append(unit * attn_gain)
-        low = [value.astype(bf16) for value in normed]
-        normed_all = [gather4(value) for value in low]
+            return context, lse, fold_core(dot(context, held.out))
+
+        context1, lse1, across = attend(1, hook(ATTEND0, projected[1]))
+        across = across.astype(bf16)
+        context0, lse0, keep = attend(0, hook(ATTEND1, after(projected[0], across)))
+        came = hook(NORM, after(swap_x(across), keep))
+        unit_attn, scale_attn = norm_parts(inputs.astype(f32) + keep + came.astype(f32))
+        normed = unit_attn * attn_gain
+        normed_all = gather_tiles(normed.astype(bf16))
 
         def feed(value):
             activated, slope, partial = [], [], 0.0
-            for half_up, half_down in zip(held["up"], held["down"]):
+            for half_up, half_down in zip(held.up, held.down):
                 upward = dot(value, half_up)
                 phi_whole = 0.5 * (1.0 + lax.erf(upward * (0.5**0.5)))
                 activated.append((upward * phi_whole).astype(bf16))
                 density = jnp.exp(-0.5 * upward * upward) * 0.3989422804014327
                 slope.append((phi_whole + upward * density).astype(bf16))
                 partial += dot(activated[-1], half_down)
-            return activated, slope, *fold_core(partial)
-
-        activated0, slope0, keep0, across0 = feed(hook("feed0", after(normed_all[0], low[1])))
-        activated1, slope1, keep1, across1 = feed(hook("feed1", after(normed_all[1], across0)))
-        came0 = hook("last0", after(swap_x(across0), across1))
-        came1 = swap_x(across1)
-        unit_mlp, scale_mlp, outputs = [], [], []
-        for k, (keep, came) in enumerate(((keep0, came0), (keep1, came1))):
-            unit, factor = norm_parts(normed[k] + keep + came.astype(f32))
-            unit_mlp.append(unit)
-            scale_mlp.append(factor)
-            outputs.append((unit * mlp_gain).astype(bf16))
-        return outputs, dict(
+            return activated, slope, fold_core(partial)
+
+        activated0, slope0, keep = feed(hook(FEED0, normed_all[0]))
+        activated1, slope1, across = feed(hook(FEED1, after(normed_all[1], keep)))
+        came = hook(LAST, swap_x(across.astype(bf16)))
+        unit_mlp, scale_mlp = norm_parts(normed + keep + came.astype(f32))
+        return (unit_mlp * mlp_gain).astype(bf16), types.SimpleNamespace(
             inputs_all=inputs_all,
             projected=projected,
             keys_values=keys_values,
@@ -641,6 +628,7 @@
 
     def backward(out_grads, kept, layer, hook):
         held = weights[layer]
+        attn_gain, mlp_gain = gains[layer][0], gains[layer][1]
 
         def over_tokens(left, right):
             return (rows_product(left[0], right[0]) + rows_product(left[1], right[1])).astype(bf16)
@@ -652,68 +640,43 @@
                 for at in (0, size)
             ]
 
-        attn_gain, mlp_gain = gains[layer][0], gains[layer][1]
-        mlp_in, mlp_gain_grad = [], 0.0
-        for k in range(2):
-            grad, gain_part = norm_back(
-                out_grads[k].astype(f32), kept["unit_mlp"][k], kept["scale_mlp"][k], mlp_gain
-            )
-            mlp_in.append(grad)
-            mlp_gain_grad += gain_part
-        low = [value.astype(bf16) for value in mlp_in]
-        down_all = [gather4(value) for value in low]
+        mlp_in, mlp_gain_grad = norm_back(
+            out_grads.astype(f32), kept.unit_mlp, kept.scale_mlp, mlp_gain
+        )
+        down_all = gather_tiles(mlp_in.astype(bf16))
 
         def feed_back(k, value):
             grads, partial = [], 0.0
-            for half_up, half_down, slope in zip(held["up"], held["down"], kept["slope"][k]):
+            for half_up, half_down, slope in zip(held.up, held.down, kept.slope[k]):
                 grad = times_transposed(value, half_down) * slope.astype(f32)
                 grads.append(grad.astype(bf16))
                 partial += times_transposed(grads[-1], half_up)
-            return grads, *fold_core(partial)
-
-        upward0, keep0, across0 = feed_back(0, hook("feed0", after(down_all[0], low[1])))
-        upward1, keep1, across1 = feed_back(1, hook("feed1", after(down_all[1], across0)))
-        came0 = hook(
-            "norm0",
-            after(swap_x(across0), across1),
-            down=[over_tokens(left, down_all) for left in zip(*kept["activated"])],
+            return grads, fold_core(partial)
+
+        upward0, keep = feed_back(0, hook(FEED0, down_all[0]))
+        upward1, across = feed_back(1, hook(FEED1, after(down_all[1], keep)))
+        grad_down = [over_tokens(left, down_all) for left in zip(*kept.activated)]
+        came = hook(NORM, swap_x(across.astype(bf16)), grad_down)
+        attn_in, attn_gain_grad = norm_back(
+            mlp_in + keep + came.astype(f32), kept.unit_attn, kept.scale_attn, attn_gain
         )
-        came1 = swap_x(across1)
-        upward_grad = (upward0, upward1)
-        attn_in, attn_gain_grad = [], 0.0
-        for k, (keep, came) in enumerate(((keep0, came0), (keep1, came1))):
-            grad, gain_part = norm_back(
-                mlp_in[k] + keep + came.astype(f32),
-                kept["unit_attn"][k],
-                kept["scale_attn"][k],
-                attn_gain,
-            )
-            attn_in.append(grad)
-            attn_gain_grad += gain_part
-        low = [value.astype(bf16) for value in attn_in]
-        branch_all = [gather4(value) for value in low]
+        branch_all = gather_tiles(attn_in.astype(bf16))
 
         def attend_back(k, value):
-            grads = times_transposed(value, held["out"]).astype(bf16)
+            grads = times_transposed(value, held.out).astype(bf16)
             return attention_backward(
-                kept["projected"][k],
-                kept["keys_values"],
+                kept.projected[k],
+                kept.keys_values,
                 grads,
-                kept["lse"][k],
+                kept.lse[k],
                 query_ids[k],
                 key_ids,
                 scale,
             )
 
-        grad_up = [over_tokens(kept["normed_all"], right) for right in zip(*upward_grad)]
-        query0, key0, value0 = attend_back(
-            0, hook("attend0", after(branch_all[0], low[1]), up=grad_up)
-        )
-        grad_out = over_tokens(kept["context"], branch_all)
-        gain_grads = jnp.stack([attn_gain_grad, mlp_gain_grad])
-        query1, key1, value1 = attend_back(
-            1, hook("attend1", after(branch_all[1], query0), out=grad_out, gains=gain_grads)
-        )
+        grad_up = [over_tokens(kept.normed_all, right) for right in zip(upward0, upward1)]
+        query0, key0, value0 = attend_back(0, hook(ATTEND0, branch_all[0], grad_up))
+        query1, key1, value1 = attend_back(1, hook(ATTEND1, after(branch_all[1], query0)))
         key_grad, value_grad = (key0 + key1).astype(bf16), (value0 + value1).astype(bf16)
         stacked = []
         for k, query_grad in enumerate((query0, query1)):
@@ -728,20 +691,17 @@
                     axis=1,
                 )
             )
-        stacked[0] = hook("stacked", stacked[0])
-        keep0, across0 = fold_core(times_transposed(stacked[0], held["qkv"]))
-        stacked[1] = hook("stacked1", stacked[1])
-        keep1, across1 = fold_core(times_transposed(stacked[1], held["qkv"]))
-        came = (hook("last0", after(swap_x(across0), across1)), swap_x(across1))
-        grad_qkv = by_half(kept["inputs_all"], stacked)
-        in_grads = [
-            (attn_in[k] + keep + came[k].astype(f32)).astype(bf16)
-            for k, keep in enumerate((keep0, keep1))
-        ]
-        return in_grads, grad_qkv
+        stacked[1] = hook(STACKED, stacked[1])
+        across = fold_core(times_transposed(stacked[1], held.qkv)).astype(bf16)
+        keep = fold_core(times_transposed(after(stacked[0], across), held.qkv))
+        gain_grads = jnp.stack([attn_gain_grad, mlp_gain_grad])
+        grad_out = over_tokens(kept.context, branch_all)
+        came = hook(LAST, after(swap_x(across), keep), grad_out, gain_grads)
+        grad_qkv = by_half(kept.inputs_all, stacked)
+        return (attn_in + keep + came.astype(f32)).astype(bf16), grad_qkv
 
     def scatter_rows(value):
-        return lax.psum_scatter(value, "fsdp", scatter_dimension=0, tiled=True)
+        return lax.psum_scatter(value, FSDP, scatter_dimension=0, tiled=True)
 
     def sync(value, *others):
         return lax.optimization_barrier((value, *others))
@@ -760,13 +720,13 @@
 
     def out_pair(keep, came):
         out = jax.ShapeDtypeStruct((2, LANES, 2 * LANES), bf16)
-        near, give = small_call(fold_out_kernel, chip_array, [keep, came], [out, out], "fold_out")
+        near, give = small_call(fold_out_kernel, chip_array, [keep, came], [out, out])
         return near, swap_x(give)
 
     def pack(keep, came, near, cross, gain_grads):
         out = jax.ShapeDtypeStruct((4 * (rows + 16), 4 * LANES), bf16)
         operands = [keep, came, near, cross, gain_grads]
-        return small_call(pack_kernel, chip_array, operands, [out], "pack_gradients")[0]
+        return small_call(pack_kernel, chip_array, operands, [out])[0]
 
     def spread_start(value, y_first):
         return value, (swap_y if y_first else swap_x)(value)
@@ -780,175 +740,167 @@
     def spread(value, y_first):
         return spread_end(spread_start(value, y_first), y_first)
 
-    def reduce_plain(grads, grad_qkv):
-        keep, came = out_halves(grads["out"])
+    def reduce_plain(found):
+        keep, came = out_halves(found.out)
         both = fold(keep, came[::-1])
         placed = jnp.zeros((4, 2, LANES, width // 2), bf16)
         placed = lax.dynamic_update_slice(placed, both[:1, None], (chip, core, 0, 0))
         placed = lax.dynamic_update_slice(placed, both[1:, None], (chip ^ 2, core, 0, 0))
-        gain_rows = grads["gains"].reshape(2, fsdp_count, rows).transpose(1, 0, 2)
+        gain_rows = found.gains.reshape(2, fsdp_count, rows).transpose(1, 0, 2)
         gain_rows = gain_rows.reshape(fsdp_count, 1, 2 * rows).astype(bf16)
         gain_rows = jnp.pad(gain_rows, ((0, 0), (0, 15), (0, width // 2 - 2 * rows)))
         packed = jnp.concatenate([placed.reshape(fsdp_count, rows, width // 2), gain_rows], axis=1)
         return [
-            spread(scatter_rows(fold(*halves(grad_qkv))), False),
+            spread(scatter_rows(fold(*halves(found.qkv))), False),
             spread(scatter_rows(packed.reshape(fsdp_count * (rows + 16), width // 2)), True),
-            spread(scatter_rows(fold(*halves(grads["up"]))), False),
-            spread(scatter_rows(fold(*halves(grads["down"]))), True),
+            spread(scatter_rows(fold(*halves(found.up))), False),
+            spread(scatter_rows(fold(*halves(found.down))), True),
         ]
 
     inputs = own_rows(tokens)
-    out_grads = own_rows(cotangent)
-    grads0, grads1 = {}, {}
+    of0, of1 = types.SimpleNamespace(), types.SimpleNamespace()
+    state = types.SimpleNamespace(out_grads=own_rows(cotangent))
     if even:
-        down_got, up_got = {}, {}
-
-        def hook_forward0(name, value):
-            if name == "attend1":
-                value, up, out_grads[1] = sync(value, up_gathered[0], out_grads[1])
-                weights[0]["up"] = with_far(up)
-            elif name == "norm0":
-                value, far = sync(value, weights[0]["up"][1])
-                weights[0]["up"] = weights[0]["up"][0], far
-            elif name == "norm1":
+
+        def hook_forward0(point, value):
+            if point == ATTEND1:
+                value, state.out_grads = sync(value, state.out_grads)
+            elif point == NORM:
+                value, up = sync(value, up_gathered[0])
+                weights[0].up = with_far(up)
+            elif point == FEED0:
                 value, down = sync(value, down_gathered[0])
-                weights[0]["down"] = with_far(down)
-            elif name == "feed1":
+                weights[0].down = with_far(down)
+            elif point == FEED1:
                 value, packed = sync(value, packed_gathered)
                 near = packed.reshape(4, rows + 16, 4 * LANES)[:, :rows, : 3 * LANES]
                 far = swap_y(near.reshape(4 * rows, 3 * LANES))
                 qkv, columns, gains[1] = place([packed], [far], depth_array, True)
-                weights[1].update(qkv=qkv, out=out_from_columns(columns))
+                weights[1].qkv, weights[1].out = qkv, out_from_columns(columns)
             return value
 
-        def hook_forward1(name, value):
-            if name == "attend0":
-                value, up = sync(value, up_gathered[1])
-                weights[1]["up"] = with_far(up)
-            elif name == "attend1":
-                value, weights[1]["out"] = sync(value, weights[1]["out"])
-            elif name == "norm0":
-                value, far = sync(value, weights[1]["up"][1])
-                weights[1]["up"] = weights[1]["up"][0], far
-            elif name == "norm1":
-                value, down = sync(value, down_gathered[1])
-                weights[1]["down"] = with_far(down)
+        def hook_forward1(point, value):
+            if point == ATTEND0:
+                value, weights[1].out, up = sync(value, weights[1].out, up_gathered[1])
+                weights[1].up = with_far(up)
+            elif point == NORM:
+                value, far, down = sync(value, weights[1].up[1], down_gathered[1])
+                weights[1].up = weights[1].up[0], far
+                weights[1].down = with_far(down)
             return value
 
-        def hook_backward1(name, value, **grads):
-            if name == "norm0":
-                value, *down = sync(value, *grads["down"])
-                grads1["down"] = halves(down)
-            elif name == "attend0":
-                value, came, *up = sync(value, grads1["down"][1], *grads["up"])
-                grads1["down"] = scatter_rows(fold(grads1["down"][0], came))
-                grads1["up"] = halves(up)
-            elif name == "attend1":
-                value, grads1["whole_out"], grads1["gains"] = sync(
-                    value, grads["out"], grads["gains"]
+        def hook_backward1(point, value, *grads):
+            if point == NORM:
+                value, *down = sync(value, *grads[0])
+                of1.down = halves(down)
+            elif point == ATTEND0:
+                value, *up = sync(value, *grads[0])
+                of1.up_grads = up
+            elif point == ATTEND1:
+                value, came, *outputs = sync(value, of1.down[1], *state.away)
+                of1.down = scatter_rows(fold(of1.down[0], came))
+                of1.up = halves(of1.up_grads)
+                state.away = outputs
+            elif point == LAST:
+                value, came, out, of1.gains = sync(value, of1.up[1], *grads)
+                of1.up = scatter_rows(fold(of1.up[0], came))
+                of1.out = out_halves(out)
+            return value
+
+        def hook_backward0(point, value, *grads):
+            if point == FEED0:
+                value, down, *qkv = sync(value, of1.down, *of1.qkv)
+                of1.qkv = halves(qkv)
+                of1.down = spread_start(down, True)
+            elif point == FEED1:
+                value, came = sync(value, of1.out[1])
+                of1.out = out_pair(of1.out[0], came)
+            elif point == NORM:
+                value, came, cross, up, hop, *down = sync(
+                    value, of1.qkv[1], of1.out[1], of1.up, of1.down[1], *grads[0]
                 )
-            elif name == "stacked":
-                value, came, *outputs = sync(value, grads1["up"][1], *hidden_away)
-                grads1["up"] = scatter_rows(fold(grads1["up"][0], came))
-                grads1["out"] = out_halves(grads1["whole_out"])
-                hidden_away[:] = outputs
-            elif name == "last0":
-                value, came = sync(value, grads1["out"][1])
-                grads1["out"] = out_pair(grads1["out"][0], came)
+                of1.packed = scatter_rows(
+                    pack(of1.qkv[0], came, of1.out[0], cross, of1.gains)
+                )
+                of1.down = of1.down[0], hop
+                of1.up = up
+                of0.down = halves(down)
+            elif point == ATTEND0:
+                value, *up = sync(value, *grads[0])
+                of0.up_grads = up
+            elif point == ATTEND1:
+                value, came = sync(value, of0.down[1])
+                of0.down = scatter_rows(fold(of0.down[0], came))
+                of0.up = halves(of0.up_grads)
+                of1.up = spread_start(of1.up, False)
+                of1.down = spread_end(of1.down, True)
+            elif point == STACKED:
+                value, hop, packed, *ends = sync(value, of1.up[1], of1.packed, *of1.down)
+                of1.up = of1.up[0], hop
+                of1.down = ends
+                of1.packed = spread_start(packed, False)
+            elif point == LAST:
+                value, came, hop, down, away, out, of0.gains = sync(
+                    value, of0.up[1], of1.packed[1], of0.down, state.in_away, *grads
+                )
+                of0.up = scatter_rows(fold(of0.up[0], came))
+                of0.out = out_halves(out)
+                of1.packed = of1.packed[0], hop
+                of0.down = spread_start(down, True)
+                of1.up = spread_end(of1.up, False)
+                state.in_away = away
             return value
 
-        def hook_backward0(name, value, **grads):
-            if name == "feed0":
-                value, down, out_came, *qkv = sync(
-                    value, grads1["down"], grads1["out"][1], *grads1["qkv"]
-                )
-                grads1["out"] = grads1["out"][0], out_came
-                grads1["qkv"] = halves(qkv)
-                grads1["down"] = spread_start(down, True)
-            elif name == "norm0":
-                value, came, up1, hop, *down = sync(
-                    value, grads1["qkv"][1], grads1["up"], grads1["down"][1], *grads["down"]
-                )
-                grads1["packed"] = scatter_rows(
-                    pack(grads1["qkv"][0], came, *grads1["out"], grads1["gains"])
-                )
-                grads1["down"] = grads1["down"][0], hop
-                grads1["up"] = up1
-                grads0["down"] = halves(down)
-            elif name == "attend0":
-                value, came, *up = sync(value, grads0["down"][1], *grads["up"])
-                grads0["down"] = scatter_rows(fold(grads0["down"][0], came))
-                grads0["up"] = halves(up)
-                grads1["up"] = spread_start(grads1["up"], False)
-            elif name == "attend1":
-                value, grads0["whole_out"], grads0["gains"], hop, packed1 = sync(
-                    value, grads["out"], grads["gains"], grads1["up"][1], grads1["packed"]
-                )
-                grads1["up"] = grads1["up"][0], hop
-                grads1["down"] = spread_end(grads1["down"], True)
-                grads1["packed"] = spread_start(packed1, False)
-            elif name == "stacked":
-                value, came, hop, down, away, *ends = sync(
-                    value,
-                    grads0["up"][1],
-                    grads1["packed"][1],
-                    grads0["down"],
-                    in_away[0],
-                    *grads1["down"],
-                )
-                in_away[0] = away
-                grads1["down"] = ends
-                grads0["up"] = scatter_rows(fold(grads0["up"][0], came))
-                grads0["out"] = out_halves(grads0["whole_out"])
-                grads1["packed"] = grads1["packed"][0], hop
-                grads0["down"] = spread_start(down, True)
-                grads1["up"] = spread_end(grads1["up"], False)
-            elif name == "last0":
-                value, came = sync(value, grads0["out"][1])
-                grads0["out"] = out_pair(grads0["out"][0], came)
+    else:
+
+        def hook_forward0(point, value):
             return value
 
-    else:
-
-        def hook_forward0(name, value):
-            return value
-
         hook_forward1 = hook_forward0
 
-        def hook_backward1(name, value, **grads):
-            grads1.update(grads)
-            return value
-
-        def hook_backward0(name, value, **grads):
-            grads0.update(grads)
-            return value
+        def hook_plain(found):
+            def hook(point, value, *grads):
+                if point == NORM:
+                    found.down = grads[0]
+                elif point == ATTEND0:
+                    found.up = grads[0]
+                elif point == LAST:
+                    found.out, found.gains = grads
+                return value
+
+            return hook
+
+        hook_backward0, hook_backward1 = hook_plain(of0), hook_plain(of1)
 
     hidden0, saved0 = forward(inputs, 0, hook_forward0)
     hidden1, saved1 = forward(hidden0, 1, hook_forward1)
-    hidden_away = [swap_y(hidden0[1]), swap_y(hidden1[1])]
-    in_grads1, grad_qkv1 = backward(out_grads, saved1, 1, hook_backward1)
-    grads1["qkv"] = grad_qkv1
-    in_away = [swap_y(in_grads1[1])]
-    in_grads0, grad_qkv0 = backward(in_grads1, saved0, 0, hook_backward0)
+    state.away = [swap_y(hidden0[half:]), swap_y(hidden1[half:])]
+    in_grads1, of1.qkv = backward(state.out_grads, saved1, 1, hook_backward1)
+    state.in_away = swap_y(in_grads1[half:])
+    in_grads0, of0.qkv = backward(in_grads1, saved0, 0, hook_backward0)
     if even:
-        qkv_keep, qkv_came = halves(grad_qkv0)
-        in_grads0[0], up0, hop = sync(in_grads0[0], grads0["up"], grads0["down"][1])
-        grads0["down"] = grads0["down"][0], hop
-        packed0 = scatter_rows(pack(qkv_keep, qkv_came, *grads0["out"], grads0["gains"]))
-        near1 = [spread_end(grads1["packed"], False), grads1["up"], grads1["down"]]
-        near0 = [spread(packed0, False), spread(up0, False), spread_end(grads0["down"], True)]
+        near, came = of0.out
+        qkv_near, qkv_came = halves(of0.qkv)
+        packed0 = pack(qkv_near, qkv_came, *out_pair(near, came), of0.gains)
+        packed0 = scatter_rows(packed0)
+        near1 = [spread_end(of1.packed, False), of1.up, of1.down]
+        near0 = [
+            spread(packed0, False),
+            spread(of0.up, False),
+            spread_end(of0.down, True),
+        ]
     else:
-        near1, near0 = reduce_plain(grads1, grad_qkv1), reduce_plain(grads0, grad_qkv0)
+        near1, near0 = reduce_plain(of1), reduce_plain(of0)
 
     def to_owner(layer0, layer1, away):
-        pairs = [jnp.stack([runs[0], far]) for runs, far in zip((layer0, layer1), away)]
+        pairs = [jnp.stack([runs[:half], far]) for runs, far in zip((layer0, layer1), away)]
         keep = jnp.where(first_core, pairs[0], pairs[1])
         take = swap_core(jnp.where(first_core, pairs[1], pairs[0]))
         both = flipped(~first_core, jnp.stack([keep, take], axis=1), 1)
         return flipped(~first_y, both, 0).reshape(2, block, width)
 
-    hidden_out = to_owner(hidden0, hidden1, hidden_away)
-    in_grads_out = to_owner(in_grads0, in_grads1, [swap_y(in_grads0[1]), in_away[0]])
+    hidden_out = to_owner(hidden0, hidden1, state.away)
+    in_grads_out = to_owner(in_grads0, in_grads1, [swap_y(in_grads0[half:]), state.in_away])
 
     def natural(position):
         layers = jnp.stack(near0[position]), jnp.stack(near1[position])
@@ -979,8 +931,8 @@
         def column(row):
             return row.reshape(-1, 1)
 
-        down = build(2, "rows", [column(row_down)], ((8 * unit, width),))
-        up = build(1, "columns", [column(row_up)], ((rows, hidden_width),))
+        down = build(2, ROWS, [column(row_down)], ((8 * unit, width),))
+        up = build(1, COLUMNS, [column(row_up)], ((rows, hidden_width),))
         built = [None, None, up[:2], down[:2]]
         sums = {2: jnp.concatenate([up[2], down[2]], axis=1)}
         places = {2: (0, LANES), 3: (LANES + 2 * hidden_width, 2 * LANES + 2 * hidden_width)}
@@ -989,7 +941,7 @@
         def build_first(*tokens):
             first = build(
                 0,
-                "packed",
+                PACKED,
                 [after(column(row_qkv), *tokens), column(row_out)],
                 ((rows, 3 * width), (rows, width)),
             )
@@ -1036,7 +988,7 @@
 
     def sum_line(value):
         if fsdp_count != 4:
-            return lax.psum(value, "fsdp")
+            return lax.psum(value, FSDP)
         near, two, three = rotations(value)[1:]
         return (value + two) + (near + three)
 
@@ -1072,8 +1024,8 @@
         new_masters[position] = masters[position] - factor * raw
 
     def lanes(values, start):
-        row = jnp.concatenate(values, axis=1)
-        return jnp.pad(row, ((0, 0), (start, LANES - start - row.shape[1])))
+        lane = lax.broadcasted_iota(jnp.int32, (1, LANES), 1)
+        return sum(jnp.where(lane == start + i, value, 0.0) for i, value in enumerate(values))
 
     def with_lanes(row, values):
         return jnp.concatenate([row[:, :LANES] + lanes(values, 2), row[:, LANES:]], axis=1)
@@ -1124,52 +1076,52 @@
 
 def solution(mesh):
     in_specs = (
-        P("fsdp", "ctx", None),
-        P("fsdp", "ctx", None),
-        P("fsdp", None),
-        P("section", "fsdp", None),
-        P("section", "fsdp", None),
-        P("section", "fsdp", None),
-        P("section", "fsdp", None),
-        P("section", "fsdp"),
-        P("section", "fsdp"),
-        P("section", "fsdp"),
-        P("section", None),
-        P("section", "fsdp"),
-        P("section", None),
-        P("section", "fsdp"),
-        P("section", None),
-        P("section", "fsdp"),
-        P("section", None),
-        P("section", "fsdp"),
-        P("section", "fsdp"),
+        P(FSDP, CTX, None),
+        P(FSDP, CTX, None),
+        P(FSDP, None),
+        P(SECTION, FSDP, None),
+        P(SECTION, FSDP, None),
+        P(SECTION, FSDP, None),
+        P(SECTION, FSDP, None),
+        P(SECTION, FSDP),
+        P(SECTION, FSDP),
+        P(SECTION, FSDP),
+        P(SECTION, None),
+        P(SECTION, FSDP),
+        P(SECTION, None),
+        P(SECTION, FSDP),
+        P(SECTION, None),
+        P(SECTION, FSDP),
+        P(SECTION, None),
+        P(SECTION, FSDP),
+        P(SECTION, FSDP),
     )
     out_specs = (
-        P("section", "fsdp", "ctx", None),
-        P("section", "fsdp", "ctx", None),
-        P("section", "fsdp", None),
-        P("section", "fsdp", None),
-        P("section", "fsdp", None),
-        P("section", "fsdp", None),
-        P("section", "fsdp"),
-        P("section", "fsdp"),
-        P("section", "fsdp", None),
-        P("section", "fsdp", None),
-        P("section", "fsdp", None),
-        P("section", "fsdp", None),
-        P("section", "fsdp"),
-        P("section", "fsdp"),
-        P("section", "fsdp"),
-        P("section", None),
-        P("section", "fsdp"),
-        P("section", None),
-        P("section", "fsdp"),
-        P("section", None),
-        P("section", "fsdp"),
-        P("section", None),
-        P("section", "fsdp"),
-        P("section", "fsdp"),
-        P("section", None),
+        P(SECTION, FSDP, CTX, None),
+        P(SECTION, FSDP, CTX, None),
+        P(SECTION, FSDP, None),
+        P(SECTION, FSDP, None),
+        P(SECTION, FSDP, None),
+        P(SECTION, FSDP, None),
+        P(SECTION, FSDP),
+        P(SECTION, FSDP),
+        P(SECTION, FSDP, None),
+        P(SECTION, FSDP, None),
+        P(SECTION, FSDP, None),
+        P(SECTION, FSDP, None),
+        P(SECTION, FSDP),
+        P(SECTION, FSDP),
+        P(SECTION, FSDP),
+        P(SECTION, None),
+        P(SECTION, FSDP),
+        P(SECTION, None),
+        P(SECTION, FSDP),
+        P(SECTION, None),
+        P(SECTION, FSDP),
+        P(SECTION, None),
+        P(SECTION, FSDP),
+        P(SECTION, FSDP),
+        P(SECTION, None),
     )
     return jax.shard_map(
         per_device, mesh=mesh, in_specs=in_specs, out_specs=out_specs, check_vma=False

time: 817 us -> 756 us (0.925)
  other arithmetic: 122 us -> 92 us
  starting transfers between devices: 117 us -> 105 us
  waiting for transfers between devices: 255 us -> 243 us
    ppermute x151 -> x135, waiting for transfers between devices: 237 us -> 222 us  [the longest x28 119 us: swap_x(): return lax.ppermute(value, CTX, [(i, i ^ 1) for i in range(4)])]
    ppermute x151 -> x135, starting transfers between devices: 116 us -> 104 us  [the longest x36 45.5 us: swap_y(): return lax.ppermute(value, CTX, [(i, i ^ 2) for i in range(4)])]
    convert_element_type x26 -> x16, other arithmetic: 23.4 us -> 11.7 us  [the longest x2 3.02 us: backward(): branch_all = gather_tiles(attn_in.astype(bf16))]
    concatenate x28 -> x6, other arithmetic: 15.8 us -> 5.59 us  [the longest x4 4.7 us: with_core(): return jnp.concatenate([value, swap_core(value)], axis=0)]
    unnamed x722 -> x581, local copies, waits for them, and re-layouts: 35.4 us -> 33.7 us
  transfers between devices with their start and end apart: 162 -> 146, of which waited for: 61 -> 47; matrix products, arithmetic and copies ran while one was open for 28% -> 31% of each run, Pallas kernels for 8% -> 10%
where the time goes in v3:
time: 756 us; the launch traced here: 747 us
  waiting for transfers between devices  243 us (32%)
  matrix products  121 us (16%)
  starting transfers between devices  105 us (14%)
  Pallas kernels  94.4 us (12%)
  other arithmetic  92 us (12%)
  local copies, waits for them, and re-layouts  61.1 us (8%)
  between operations  29.8 us (4%)
    ppermute x28, waiting for transfers between devices, swap_x(): return lax.ppermute(value, CTX, [(i, i ^ 1) for i in range(4)])  119 us
    ppermute x36, waiting for transfers between devices, swap_y(): return lax.ppermute(value, CTX, [(i, i ^ 2) for i in range(4)])  87.7 us
    ppermute x36, starting transfers between devices, swap_y(): return lax.ppermute(value, CTX, [(i, i ^ 2) for i in range(4)])  45.5 us
    dot_general x28, matrix products, rows_product(): lax.dot_general(left, right, (((0,), (0,)), ((), ())), preferred_element_...  44.9 us
    dot_general x24, matrix products, times_transposed(): lax.dot_general(left, right, (((1,), (1,)), ((), ())), preferred_element_...  39.1 us
    pallas_call x4, Pallas kernels, attention_backward(): pl.pallas_call(functools.partial(attention_back_kernel, scale=scale), gri...  39 us
    dot_general x24, matrix products, dot(): return jnp.dot(left, right, preferred_element_type=f32)  37.5 us
    unnamed x581, local copies, waits for them, and re-layouts  33.7 us
  transfers between devices with their start and end apart: 146, of which 47 were waited for; matrix products, arithmetic and copies ran while one was open for 31% of the time, Pallas kernels for 10%

profile of v3, /device:TPU:0, one launch (start us, length us, event | category | flops | bytes accessed | tf_op | source)
XLA Modules:
  0.0 746.7 jit_solution(6253033815272541412)
XLA Ops:
  7.3 3.8 shard_map.378
  14.7 2.9 collective-permute-start.3
  17.6 2.6 collective-permute-start.4
  27.2 11.4 %collective-permute-done.4.refs_2_ = bf16[272,512]{1,0:T(8,128)(2,1)S(1)} collective-permute-done((bf16[272,512]{1,0:T(8,128)(2,1)S(1)}, bf16[272,512]{1,0:T(8,128)(2,1)S(1)}, u32[]{:S(2)}, u32[]{:S(2)}) %collective-permute-start.4) | collective-permute-done | bytes 278560 | tf_op jit(solution)/shard_map/ppermute | solution.py:509
  43.1 2.5 collective-permute-done.7.refs_5_
  50.3 3.8 collective-permute-done.9.refs_7_
  62.5 2.6 convolution_convert_fusion.11.q_ref
  69.5 6.8 shard_map.380
  79.2 6.5 collective-permute-done.16
  88.2 6.7 shard_map.382
  96.1 4.7 collective-permute-done.18
  107.1 10.6 %collective-permute-done.25 = bf16[256,1024]{1,0:T(8,128)(2,1)} collective-permute-done((bf16[256,1024]{1,0:T(8,128)(2,1)S(1)}, bf16[256,1024]{1,0:T(8,128)(2,1)}, u32[]{:S(2)}, u32[]{:S(2)}) %collective-permute-start.25) | collective-permute-done | bytes 524320 | tf_op jit(solution)/shard_map/ppermute | solution.py:33
  117.7 3.2 multiply_convert_fusion.9
  123.6 3.3 fusion.181
  126.9 5.3 all-gather.10.cloned.1.call-done.refs_0_.refs_1_.refs_2_.refs_3_
  138.8 13.0 %collective-permute-done.23 = bf16[512,1024]{1,0:T(8,128)(2,1)} collective-permute-done((bf16[512,1024]{1,0:T(8,128)(2,1)}, bf16[512,1024]{1,0:T(8,128)(2,1)}, u32[]{:S(2)}, u32[]{:S(2)}) %collective-permute-start.23) | collective-permute-done | bytes 1048608 | tf_op jit(solution)/shard_map/ppermute | solution.py:37
  163.8 9.9 %collective-permute-done.28 = bf16[256,1024]{1,0:T(8,128)(2,1)S(1)} collective-permute-done((bf16[256,1024]{1,0:T(8,128)(2,1)S(1)}, bf16[256,1024]{1,0:T(8,128)(2,1)S(1)}, u32[]{:S(2)}, u32[]{:S(2)}) %collective-permute-start.28) | collective-permute-done | bytes 524320 | tf_op jit(solution)/shard_map/ppermute | solution.py:33
  177.9 3.9 collective-permute-done.30.refs_4_.refs_5_.refs_6_.refs_7_
  185.3 7.2 collective-permute-done.33.came
  193.9 3.5 collective-permute-done.35.far_came
  204.2 5.1 all-gather.12.cloned.1.call-done
  211.5 6.7 shard_map.385
  227.9 7.2 shard_map.386
  238.3 10.0 %all-gather.14.cloned.1.call-done = bf16[512,1024]{1,0:T(8,128)(2,1)} async-done(((bf16[128,1024]{1,0:T(8,128)(2,1)}), bf16[512,1024]{1,0:T(8,128)(2,1)}) %all-gather.14.cloned.1.call-update) | async-done | bytes 1048592 | tf_op jit(solution)/shard_map/all_gather | solution.py:505
  256.5 8.3 %collective-permute-done.43 = bf16[256,1024]{1,0:T(8,128)(2,1)S(1)} collective-permute-done((bf16[256,1024]{1,0:T(8,128)(2,1)S(1)}, bf16[256,1024]{1,0:T(8,128)(2,1)S(1)}, u32[]{:S(2)}, u32[]{:S(2)}) %collective-permute-start.43) | collective-permute-done | bytes 524320 | tf_op jit(solution)/shard_map/ppermute | solution.py:33
  265.6 3.2 multiply_convert_fusion.3
  271.9 8.6 %collective-permute-done.41 = bf16[512,1024]{1,0:T(8,128)(2,1)S(1)} collective-permute-done((bf16[512,1024]{1,0:T(8,128)(2,1)S(1)}, bf16[512,1024]{1,0:T(8,128)(2,1)S(1)}, u32[]{:S(2)}, u32[]{:S(2)}) %collective-permute-start.41) | collective-permute-done | bytes 1048608 | tf_op jit(solution)/shard_map/ppermute | solution.py:37
  288.6 9.8 %collective-permute-done.46 = bf16[256,1024]{1,0:T(8,128)(2,1)S(1)} collective-permute-done((bf16[256,1024]{1,0:T(8,128)(2,1)S(1)}, bf16[256,1024]{1,0:T(8,128)(2,1)S(1)}, u32[]{:S(2)}, u32[]{:S(2)}) %collective-permute-start.46) | collective-permute-done | bytes 524320 | tf_op jit(solution)/shard_map/ppermute | solution.py:33
  319.4 3.6 collective-permute-done.49
  337.0 11.8 %collective-permute-done.52 = bf16[256,1024]{1,0:T(8,128)(2,1)S(1)} collective-permute-done((bf16[256,1024]{1,0:T(8,128)(2,1)S(1)}, bf16[256,1024]{1,0:T(8,128)(2,1)S(1)}, u32[]{:S(2)}, u32[]{:S(2)}) %collective-permute-start.52) | collective-permute-done | bytes 524320 | tf_op jit(solution)/shard_map/ppermute | solution.py:33
  359.5 7.8 %collective-permute-done.53 = bf16[256,1024]{1,0:T(8,128)(2,1)S(1)} collective-permute-done((bf16[256,1024]{1,0:T(8,128)(2,1)S(1)}, bf16[256,1024]{1,0:T(8,128)(2,1)S(1)}, u32[]{:S(2)}, u32[]{:S(2)}) %collective-permute-start.53) | collective-permute-done | bytes 524320 | tf_op jit(solution)/shard_map/ppermute | solution.py:33
  367.9 9.8 %shard_map.387 = (bf16[512,256]{1,0:T(8,128)(2,1)S(1)}, f32[1024,256]{1,0:T(8,128)S(1)}, f32[1024,256]{1,0:T(8,128)S(1)}) custom-call(bf16[512,768]{1,0:T(8,128)(2,1)S(1)} %copy-done.23, bf16[1024,768]{1,0:T(8,128)(2,1)S(1)} %pad_maximum_fusion.1.k_ref.v_ref, bf16[1024,768]{1,0:T(8,128)(2,1)S(1)} %pad_maximum_fusion.1.k_ref.v_ref, ...), custom_call_target="tpu_custom_call" | custom-call | flops 2684354560 | bytes 6291456 | tf_op jit(solution)/shard_map/pallas_call | solution.py:175
  378.8 2.7 collective-permute-done.56
  382.0 9.8 %shard_map.388 = (bf16[512,256]{1,0:T(8,128)(2,1)S(1)}, f32[1024,256]{1,0:T(8,128)S(1)}, f32[1024,256]{1,0:T(8,128)S(1)}) custom-call(bf16[512,768]{1,0:T(8,128)(2,1)S(1)} %copy-done.20, bf16[1024,768]{1,0:T(8,128)(2,1)S(1)} %pad_maximum_fusion.1.k_ref.v_ref, bf16[1024,768]{1,0:T(8,128)(2,1)S(1)} %pad_maximum_fusion.1.k_ref.v_ref, ...), custom_call_target="tpu_custom_call" | custom-call | flops 2684354560 | bytes 6291456 | tf_op jit(solution)/shard_map/pallas_call | solution.py:175
  412.4 7.4 collective-permute-done.62
  426.0 2.5 add_convert_fusion.6
  431.1 3.4 fusion.144
  438.8 3.3 fusion.145
  442.1 3.0 fusion.14
  476.9 10.6 %collective-permute-done.72.cross = bf16[2,128,256]{2,1,0:T(8,128)(2,1)S(1)} collective-permute-done((bf16[2,128,256]{2,1,0:T(8,128)(2,1)S(1)}, bf16[2,128,256]{2,1,0:T(8,128)(2,1)S(1)}, u32[]{:S(2)}, u32[]{:S(2)}) %collective-permute-start.72) | collective-permute-done | bytes 131104 | tf_op jit(solution)/shard_map/ppermute | solution.py:33
  490.3 3.9 multiply_reduce_fusion
  506.5 7.2 collective-permute-done.74
  515.3 9.7 %shard_map.390 = (bf16[512,256]{1,0:T(8,128)(2,1)S(1)}, f32[1024,256]{1,0:T(8,128)S(1)}, f32[1024,256]{1,0:T(8,128)S(1)}) custom-call(bf16[512,768]{1,0:T(8,128)(2,1)S(1)} %copy-done.17, bf16[1024,768]{1,0:T(8,128)(2,1)S(1)} %pad_maximum_fusion.k_ref.v_ref, bf16[1024,768]{1,0:T(8,128)(2,1)S(1)} %pad_maximum_fusion.k_ref.v_ref, ...), custom_call_target="tpu_custom_call" | custom-call | flops 2684354560 | bytes 6291456 | tf_op jit(solution)/shard_map/pallas_call | solution.py:175
  528.6 9.8 %shard_map.391 = (bf16[512,256]{1,0:T(8,128)(2,1)S(1)}, f32[1024,256]{1,0:T(8,128)S(1)}, f32[1024,256]{1,0:T(8,128)S(1)}) custom-call(bf16[512,768]{1,0:T(8,128)(2,1)S(1)} %copy-done.15, bf16[1024,768]{1,0:T(8,128)(2,1)S(1)} %pad_maximum_fusion.k_ref.v_ref, bf16[1024,768]{1,0:T(8,128)(2,1)S(1)} %pad_maximum_fusion.k_ref.v_ref, ...), custom_call_target="tpu_custom_call" | custom-call | flops 2684354560 | bytes 6291456 | tf_op jit(solution)/shard_map/pallas_call | solution.py:175
  540.5 2.6 add_convert_fusion.1
  558.8 8.9 %collective-permute-done.82 = bf16[256,1024]{1,0:T(8,128)(2,1)S(1)} collective-permute-done((bf16[256,1024]{1,0:T(8,128)(2,1)S(1)}, bf16[256,1024]{1,0:T(8,128)(2,1)S(1)}, u32[]{:S(2)}, u32[]{:S(2)}) %collective-permute-start.82) | collective-permute-done | bytes 524320 | tf_op jit(solution)/shard_map/ppermute | solution.py:33
  568.5 2.8 collective-permute-done.84
  573.2 2.5 add_convert_fusion
  576.2 2.7 convolution_convert_fusion
  588.4 3.7 collective-permute-done.90.came
  596.9 17.7 %collective-permute-done.113.refs_11_ = bf16[256,512]{1,0:T(8,128)(2,1)S(1)} collective-permute-done((bf16[256,512]{1,0:T(8,128)(2,1)S(1)}, bf16[256,512]{1,0:T(8,128)(2,1)S(1)}, u32[]{:S(2)}, u32[]{:S(2)}) %collective-permute-start.113) | collective-permute-done | bytes 262176 | tf_op jit(solution)/shard_map/ppermute | solution.py:37
  617.5 2.7 collective-permute-done.87
  626.7 4.4 collective-permute-done.119.refs_2_
  650.0 5.0 collective-permute-done.107.refs_3_
  657.4 7.3 shard_map.396
  667.1 5.5 shard_map.395
  672.6 3.7 fusion.126
  678.8 3.5 collective-permute-start.131
  690.8 2.6 collective-permute-done.92.refs_1_
  695.1 7.0 bitcast_subtract_fusion.1
  706.0 2.9 bitcast_subtract_fusion
  709.1 6.3 shard_map.397
  719.6 2.6 collective-permute-start.134
  735.6 4.3 fusion.3
  (1088 shorter events, 339.0 us)
Async XLA Ops:
  7.2 93.6 %all-gather.6.cloned.1.call-start = ((), (), s32[]{:S(2)}) async-start(), calls=%async_computation.6 | async-start | bytes 1310720 | tf_op jit(solution)/shard_map/all_gather | solution.py:505
  11.6 30.9 %collective-permute-start.6 = (bf16[256,384]{1,0:T(8,128)(2,1)}, bf16[256,384]{1,0:T(8,128)(2,1)}, u32[]{:S(2)}, u32[]{:S(2)}) collective-permute-start(bf16[256,384]{1,0:T(8,128)(2,1)} %get-tuple-element.155), channel_id=1, source_target_pairs={{0,16},{16,0},{1,17},{17,1},{2,18},{18,2},{3,19},{19,3},{4,20},{20... | collective-permute-start | bytes 589832 | tf_op jit(solution)/shard_map/ppermute | solution.py:29
  17.6 21.1 %collective-permute-start.4 = (bf16[272,512]{1,0:T(8,128)(2,1)S(1)}, bf16[272,512]{1,0:T(8,128)(2,1)S(1)}, u32[]{:S(2)}, u32[]{:S(2)}) collective-permute-start(bf16[272,512]{1,0:T(8,128)(2,1)S(1)} %get-tuple-element.331.refs_0_), channel_id=1, source_target_pairs={{0,2},{1,3},{2,0},{3,1},{4,6},{5,7},{6,4},{7,5},{8,10},{9,11},{10,... | collective-permute-start | bytes 835592 | tf_op jit(solution)/shard_map/ppermute | solution.py:509
  20.2 18.5 %collective-permute-start.5 = (bf16[272,512]{1,0:T(8,128)(2,1)S(1)}, bf16[272,512]{1,0:T(8,128)(2,1)S(1)}, u32[]{:S(2)}, u32[]{:S(2)}) collective-permute-start(bf16[272,512]{1,0:T(8,128)(2,1)S(1)} %get-tuple-element.331.refs_0_), channel_id=1, source_target_pairs={{0,3},{1,0},{2,1},{3,2},{4,7},{5,4},{6,5},{7,6},{8,11},{9,8},{10,9... | collective-permute-start | bytes 835592 | tf_op jit(solution)/shard_map/ppermute | solution.py:509
  22.6 17.8 %collective-permute-start = (bf16[128,1024]{1,0:T(8,128)(2,1)S(1)}, bf16[128,1024]{1,0:T(8,128)(2,1)S(1)}, u32[]{:S(2)}, u32[]{:S(2)}) collective-permute-start(bf16[128,1024]{1,0:T(8,128)(2,1)S(1)} %get-tuple-element.329), channel_id=1, source_target_pairs={{0,8},{4,12},{8,0},{12,4},{1,9},{5,13},{9,1},{13,5},{2,10},{6,14},... | collective-permute-start | bytes 786440 | tf_op jit(solution)/shard_map/ppermute | solution.py:37
  27.2 30.3 %collective-permute-start.21 = (bf16[128,1024]{1,0:T(8,128)(2,1)}, bf16[128,1024]{1,0:T(8,128)(2,1)}, u32[]{:S(2)}, u32[]{:S(2)}) collective-permute-start(bf16[128,1024]{1,0:T(8,128)(2,1)} %get-tuple-element.169), channel_id=1, source_target_pairs={{0,16},{16,0},{1,17},{17,1},{2,18},{18,2},{3,19},{19,3},{4,20},{20... | collective-permute-start | bytes 786440 | tf_op jit(solution)/shard_map/ppermute | solution.py:29
  38.7 68.4 %all-gather.8.cloned.1.call-start = ((), (), s32[]{:S(2)}) async-start(), calls=%async_computation.7 | async-start | bytes 1310720 | tf_op jit(solution)/shard_map/all_gather | solution.py:505
  40.5 17.1 %collective-permute-start.10 = (bf16[256,1024]{1,0:T(8,128)(2,1)S(1)}, bf16[256,1024]{1,0:T(8,128)(2,1)}, u32[]{:S(2)}, u32[]{:S(2)}) collective-permute-start(bf16[256,1024]{1,0:T(8,128)(2,1)S(1)} %pad_maximum_fusion.10), channel_id=1, source_target_pairs={{0,4},{4,0},{8,12},{12,8},{1,5},{5,1},{9,13},{13,9},{2,6},{6,2},{1... | collective-permute-start | bytes 1572872 | tf_op jit(solution)/shard_map/ppermute | solution.py:33
  42.4 20.1 %collective-permute-start.1 = (bf16[256,1024]{1,0:T(8,128)(2,1)S(1)}, bf16[256,1024]{1,0:T(8,128)(2,1)}, u32[]{:S(2)}, u32[]{:S(2)}) collective-permute-start(bf16[256,1024]{1,0:T(8,128)(2,1)S(1)} %pad_maximum_fusion.10), channel_id=1, source_target_pairs={{0,16},{16,0},{1,17},{17,1},{2,18},{18,2},{3,19},{19,3},{4,20},{20... | collective-permute-start | bytes 1572872 | tf_op jit(solution)/shard_map/ppermute | solution.py:29
  59.3 72.9 %all-gather.10.cloned.1.call-start = ((), (), s32[]{:S(2)}) async-start(), calls=%async_computation.8 | async-start | bytes 1392640 | tf_op jit(solution)/shard_map/all_gather | solution.py:505
  95.8 113.6 %all-gather.12.cloned.1.call-start = ((), (), s32[]{:S(2)}) async-start(), calls=%async_computation.9 | async-start | bytes 1310720 | tf_op jit(solution)/shard_map/all_gather | solution.py:505
  103.8 30.3 %collective-permute-start.22 = (bf16[1024,512]{1,0:T(8,128)(2,1)}, bf16[1024,512]{1,0:T(8,128)(2,1)}, u32[]{:S(2)}, u32[]{:S(2)}) collective-permute-start(bf16[1024,512]{1,0:T(8,128)(2,1)} %all-gather.6.cloned.1.call-done), channel_id=1, source_target_pairs={{0,8},{4,12},{8,0},{12,4},{1,9},{5,13},{9,1},{13,5},{2,10},{6,14},... | collective-permute-start | bytes 3145736 | tf_op jit(solution)/shard_map/ppermute | solution.py:37
  121.0 30.8 %collective-permute-start.23 = (bf16[512,1024]{1,0:T(8,128)(2,1)}, bf16[512,1024]{1,0:T(8,128)(2,1)}, u32[]{:S(2)}, u32[]{:S(2)}) collective-permute-start(bf16[512,1024]{1,0:T(8,128)(2,1)} %all-gather.8.cloned.1.call-done), channel_id=1, source_target_pairs={{0,8},{4,12},{8,0},{12,4},{1,9},{5,13},{9,1},{13,5},{2,10},{6,14},... | collective-permute-start | bytes 3145736 | tf_op jit(solution)/shard_map/ppermute | solution.py:37
  162.3 19.5 %collective-permute-start.30 = (bf16[1024,384]{1,0:T(8,128)(2,1)}, bf16[1024,384]{1,0:T(8,128)(2,1)S(1)}, u32[]{:S(2)}, u32[]{:S(2)}) collective-permute-start(bf16[1024,384]{1,0:T(8,128)(2,1)} %bitcast.15), channel_id=1, source_target_pairs={{0,8},{4,12},{8,0},{12,4},{1,9},{5,13},{9,1},{13,5},{2,10},{6,14},... | collective-permute-start | bytes 2359304 | tf_op jit(solution)/shard_map/ppermute | solution.py:37
  176.3 17.7 %collective-permute-start.31 = (bf16[256,1024]{1,0:T(8,128)(2,1)}, bf16[256,1024]{1,0:T(8,128)(2,1)}, u32[]{:S(2)}, u32[]{:S(2)}) collective-permute-start(bf16[256,1024]{1,0:T(8,128)(2,1)} %multiply_convert_fusion.5), channel_id=1, source_target_pairs={{0,4},{4,0},{8,12},{12,8},{1,5},{5,1},{9,13},{13,9},{2,6},{6,2},{1... | collective-permute-start | bytes 1572872 | tf_op jit(solution)/shard_map/ppermute | solution.py:33
  177.8 70.5 %all-gather.14.cloned.1.call-start = ((), (), s32[]{:S(2)}) async-start(), calls=%async_computation.10 | async-start | bytes 1310720 | tf_op jit(solution)/shard_map/all_gather | solution.py:505
  182.6 16.2 %collective-permute-start.29 = (bf16[256,1024]{1,0:T(8,128)(2,1)}, bf16[256,1024]{1,0:T(8,128)(2,1)S(1)}, u32[]{:S(2)}, u32[]{:S(2)}) collective-permute-start(bf16[256,1024]{1,0:T(8,128)(2,1)} %multiply_convert_fusion.5), channel_id=1, source_target_pairs={{0,16},{16,0},{1,17},{17,1},{2,18},{18,2},{3,19},{19,3},{4,20},{20... | collective-permute-start | bytes 1572872 | tf_op jit(solution)/shard_map/ppermute | solution.py:29
  220.6 221.5 %reduce-scatter.7.cloned.1.call-start = ((), (), s32[]{:S(2)}) async-start(), calls=%async_computation.11 | async-start | bytes 1310720 | tf_op jit(solution)/shard_map/reduce_scatter | solution.py:704
  220.6 27.7 %collective-permute-start.39 = (bf16[1024,512]{1,0:T(8,128)(2,1)}, bf16[1024,512]{1,0:T(8,128)(2,1)}, u32[]{:S(2)}, u32[]{:S(2)}) collective-permute-start(bf16[1024,512]{1,0:T(8,128)(2,1)} %all-gather.12.cloned.1.call-done), channel_id=1, source_target_pairs={{0,8},{4,12},{8,0},{12,4},{1,9},{5,13},{9,1},{13,5},{2,10},{6,14},... | collective-permute-start | bytes 3145736 | tf_op jit(solution)/shard_map/ppermute | solution.py:37
  255.0 25.6 %collective-permute-start.41 = (bf16[512,1024]{1,0:T(8,128)(2,1)S(1)}, bf16[512,1024]{1,0:T(8,128)(2,1)S(1)}, u32[]{:S(2)}, u32[]{:S(2)}) collective-permute-start(bf16[512,1024]{1,0:T(8,128)(2,1)S(1)} %copy-done.125), channel_id=1, source_target_pairs={{0,8},{4,12},{8,0},{12,4},{1,9},{5,13},{9,1},{13,5},{2,10},{6,14},... | collective-permute-start | bytes 3145736 | tf_op jit(solution)/shard_map/ppermute | solution.py:37
  307.2 71.5 %collective-permute-start.57 = (bf16[128,1024]{1,0:T(8,128)(2,1)S(1)}, bf16[128,1024]{1,0:T(8,128)(2,1)S(1)}, u32[]{:S(2)}, u32[]{:S(2)}) collective-permute-start(bf16[128,1024]{1,0:T(8,128)(2,1)S(1)} %get-tuple-element.368), channel_id=1, source_target_pairs={{0,8},{4,12},{8,0},{12,4},{1,9},{5,13},{9,1},{13,5},{2,10},{6,14},... | collective-permute-start | bytes 786440 | tf_op jit(solution)/shard_map/ppermute | solution.py:37
  311.2 67.6 %collective-permute-start.58 = (bf16[128,1024]{1,0:T(8,128)(2,1)S(1)}, bf16[128,1024]{1,0:T(8,128)(2,1)S(1)}, u32[]{:S(2)}, u32[]{:S(2)}) collective-permute-start(bf16[128,1024]{1,0:T(8,128)(2,1)S(1)} %get-tuple-element.371), channel_id=1, source_target_pairs={{0,8},{4,12},{8,0},{12,4},{1,9},{5,13},{9,1},{13,5},{2,10},{6,14},... | collective-permute-start | bytes 786440 | tf_op jit(solution)/shard_map/ppermute | solution.py:37
  319.3 29.5 %collective-permute-start.48 = (bf16[256,1024]{1,0:T(8,128)(2,1)S(1)}, bf16[256,1024]{1,0:T(8,128)(2,1)S(1)}, u32[]{:S(2)}, u32[]{:S(2)}) collective-permute-start(bf16[256,1024]{1,0:T(8,128)(2,1)S(1)} %slice.500), channel_id=1, source_target_pairs={{0,16},{16,0},{1,17},{17,1},{2,18},{18,2},{3,19},{19,3},{4,20},{20... | collective-permute-start | bytes 1572872 | tf_op jit(solution)/shard_map/ppermute | solution.py:29
  355.4 26.0 %collective-permute-start.56 = (bf16[512,1024]{1,0:T(8,128)(2,1)S(1)}, bf16[512,1024]{1,0:T(8,128)(2,1)S(1)}, u32[]{:S(2)}, u32[]{:S(2)}) collective-permute-start(bf16[512,1024]{1,0:T(8,128)(2,1)S(1)} %add_convert_fusion.12), channel_id=1, source_target_pairs={{0,8},{4,12},{8,0},{12,4},{1,9},{5,13},{9,1},{13,5},{2,10},{6,14},... | collective-permute-start | bytes 3145736 | tf_op jit(solution)/shard_map/ppermute | solution.py:37
  356.1 63.8 %collective-permute-start.63 = (bf16[1024,512]{1,0:T(8,128)(2,1)}, bf16[1024,512]{1,0:T(8,128)(2,1)}, u32[]{:S(2)}, u32[]{:S(2)}) collective-permute-start(bf16[1024,512]{1,0:T(8,128)(2,1)} %add_convert_fusion.10), channel_id=1, source_target_pairs={{0,8},{4,12},{8,0},{12,4},{1,9},{5,13},{9,1},{13,5},{2,10},{6,14},... | collective-permute-start | bytes 3145736 | tf_op jit(solution)/shard_map/ppermute | solution.py:37
  396.0 94.2 %reduce-scatter.9.cloned.1.call-start = ((), (), s32[]{:S(2)}) async-start(), calls=%async_computation.12 | async-start | bytes 1310720 | tf_op jit(solution)/shard_map/reduce_scatter | solution.py:704
  424.5 31.4 %collective-permute-start.68 = (bf16[2,128,512]{2,1,0:T(8,128)(2,1)}, bf16[2,128,512]{2,1,0:T(8,128)(2,1)}, u32[]{:S(2)}, u32[]{:S(2)}) collective-permute-start(bf16[2,128,512]{2,1,0:T(8,128)(2,1)} %bitcast.33), channel_id=1, source_target_pairs={{0,8},{4,12},{8,0},{12,4},{1,9},{5,13},{9,1},{13,5},{2,10},{6,14},... | collective-permute-start | bytes 786440 | tf_op jit(solution)/shard_map/ppermute | solution.py:37
  428.5 118.0 %reduce-scatter.11.cloned.1.call-start = ((), (), s32[]{:S(2)}) async-start(), calls=%async_computation.13 | async-start | bytes 1392640 | tf_op jit(solution)/shard_map/reduce_scatter | solution.py:704
  438.8 16.0 %collective-permute-start.67 = (bf16[256,1024]{1,0:T(8,128)(2,1)}, bf16[256,1024]{1,0:T(8,128)(2,1)}, u32[]{:S(2)}, u32[]{:S(2)}) collective-permute-start(bf16[256,1024]{1,0:T(8,128)(2,1)} %collective-permute-done.66), channel_id=1, source_target_pairs={{0,16},{16,0},{1,17},{17,1},{2,18},{18,2},{3,19},{19,3},{4,20},{20... | collective-permute-start | bytes 1572872 | tf_op jit(solution)/shard_map/ppermute | solution.py:29
  452.3 37.9 %collective-permute-start.65 = (bf16[256,1024]{1,0:T(8,128)(2,1)}, bf16[256,1024]{1,0:T(8,128)(2,1)}, u32[]{:S(2)}, u32[]{:S(2)}) collective-permute-start(bf16[256,1024]{1,0:T(8,128)(2,1)} %slice.520), channel_id=1, source_target_pairs={{0,16},{16,0},{1,17},{17,1},{2,18},{18,2},{3,19},{19,3},{4,20},{20... | collective-permute-start | bytes 1572872 | tf_op jit(solution)/shard_map/ppermute | solution.py:29
  452.8 37.5 %collective-permute-start.71 = (bf16[1024,384]{1,0:T(8,128)(2,1)S(1)}, bf16[1024,384]{1,0:T(8,128)(2,1)S(1)}, u32[]{:S(2)}, u32[]{:S(2)}) collective-permute-start(bf16[1024,384]{1,0:T(8,128)(2,1)S(1)} %copy-done.276), channel_id=1, source_target_pairs={{0,8},{4,12},{8,0},{12,4},{1,9},{5,13},{9,1},{13,5},{2,10},{6,14},... | collective-permute-start | bytes 2359304 | tf_op jit(solution)/shard_map/ppermute | solution.py:37
  453.4 34.7 %collective-permute-start.73 = (bf16[128,1024]{1,0:T(8,128)(2,1)}, bf16[128,1024]{1,0:T(8,128)(2,1)S(1)}, u32[]{:S(2)}, u32[]{:S(2)}) collective-permute-start(bf16[128,1024]{1,0:T(8,128)(2,1)} %reduce-scatter.7.cloned.1.call-done.refs_8_), channel_id=1, source_target_pairs={{0,8},{4,12},{8,0},{12,4},{1,9},{5,13},{9,1},{13,5},{2,10},{6,14},... | collective-permute-start | bytes 786440 | tf_op jit(solution)/shard_map/ppermute | solution.py:37
  470.1 20.1 %collective-permute-start.70 = (bf16[256,1024]{1,0:T(8,128)(2,1)}, bf16[256,1024]{1,0:T(8,128)(2,1)}, u32[]{:S(2)}, u32[]{:S(2)}) collective-permute-start(bf16[256,1024]{1,0:T(8,128)(2,1)} %add_convert_fusion.28), channel_id=1, source_target_pairs={{0,4},{4,0},{8,12},{12,8},{1,5},{5,1},{9,13},{13,9},{2,6},{6,2},{1... | collective-permute-start | bytes 1572872 | tf_op jit(solution)/shard_map/ppermute | solution.py:33
  487.5 80.2 %collective-permute-start.86 = (bf16[128,1024]{1,0:T(8,128)(2,1)}, bf16[128,1024]{1,0:T(8,128)(2,1)}, u32[]{:S(2)}, u32[]{:S(2)}) collective-permute-start(bf16[128,1024]{1,0:T(8,128)(2,1)} %get-tuple-element.346), channel_id=1, source_target_pairs={{0,8},{4,12},{8,0},{12,4},{1,9},{5,13},{9,1},{13,5},{2,10},{6,14},... | collective-permute-start | bytes 786440 | tf_op jit(solution)/shard_map/ppermute | solution.py:37
  488.8 57.1 %collective-permute-start.79 = (bf16[128,1024]{1,0:T(8,128)(2,1)}, bf16[128,1024]{1,0:T(8,128)(2,1)}, u32[]{:S(2)}, u32[]{:S(2)}) collective-permute-start(bf16[128,1024]{1,0:T(8,128)(2,1)} %reduce-scatter.7.cloned.1.call-done.refs_8_), channel_id=1, source_target_pairs={{0,4},{4,0},{8,12},{12,8},{1,5},{5,1},{9,13},{13,9},{2,6},{6,2},{1... | collective-permute-start | bytes 786440 | tf_op jit(solution)/shard_map/ppermute | solution.py:33
  498.5 15.2 %collective-permute-start.74 = (bf16[256,1024]{1,0:T(8,128)(2,1)}, bf16[256,1024]{1,0:T(8,128)(2,1)}, u32[]{:S(2)}, u32[]{:S(2)}) collective-permute-start(bf16[256,1024]{1,0:T(8,128)(2,1)} %get-tuple-element.305), channel_id=1, source_target_pairs={{0,4},{4,0},{8,12},{12,8},{1,5},{5,1},{9,13},{13,9},{2,6},{6,2},{1... | collective-permute-start | bytes 1572872 | tf_op jit(solution)/shard_map/ppermute | solution.py:33
  500.9 26.6 %collective-permute-start.77 = (bf16[512,1024]{1,0:T(8,128)(2,1)}, bf16[512,1024]{1,0:T(8,128)(2,1)}, u32[]{:S(2)}, u32[]{:S(2)}) collective-permute-start(bf16[512,1024]{1,0:T(8,128)(2,1)} %add_convert_fusion.4), channel_id=1, source_target_pairs={{0,8},{4,12},{8,0},{12,4},{1,9},{5,13},{9,1},{13,5},{2,10},{6,14},... | collective-permute-start | bytes 3145736 | tf_op jit(solution)/shard_map/ppermute | solution.py:37
  503.5 69.6 %reduce-scatter.13.cloned.1.call-start = ((), (), s32[]{:S(2)}) async-start(), calls=%async_computation.14 | async-start | bytes 1310720 | tf_op jit(solution)/shard_map/reduce_scatter | solution.py:704
  503.7 42.8 %collective-permute-start.78 = (bf16[256,512]{1,0:T(8,128)(2,1)}, bf16[256,512]{1,0:T(8,128)(2,1)S(1)}, u32[]{:S(2)}, u32[]{:S(2)}) collective-permute-start(bf16[256,512]{1,0:T(8,128)(2,1)} %reduce-scatter.9.cloned.1.call-done.refs_8_), channel_id=1, source_target_pairs={{0,4},{4,0},{8,12},{12,8},{1,5},{5,1},{9,13},{13,9},{2,6},{6,2},{1... | collective-permute-start | bytes 786440 | tf_op jit(solution)/shard_map/ppermute | solution.py:33
  525.9 42.3 %collective-permute-start.112 = (bf16[256,512]{1,0:T(8,128)(2,1)S(1)}, bf16[256,512]{1,0:T(8,128)(2,1)}, u32[]{:S(2)}, u32[]{:S(2)}) collective-permute-start(bf16[256,512]{1,0:T(8,128)(2,1)S(1)} %copy-done.42), channel_id=1, source_target_pairs={{0,8},{4,12},{8,0},{12,4},{1,9},{5,13},{9,1},{13,5},{2,10},{6,14},... | collective-permute-start | bytes 786440 | tf_op jit(solution)/shard_map/ppermute | solution.py:37
  527.5 19.0 %collective-permute-start.80 = (bf16[128,1024]{1,0:T(8,128)(2,1)S(1)}, bf16[128,1024]{1,0:T(8,128)(2,1)S(1)}, u32[]{:S(2)}, u32[]{:S(2)}) collective-permute-start(bf16[128,1024]{1,0:T(8,128)(2,1)S(1)} %copy-done.45), channel_id=1, source_target_pairs={{0,4},{4,0},{8,12},{12,8},{1,5},{5,1},{9,13},{13,9},{2,6},{6,2},{1... | collective-permute-start | bytes 786440 | tf_op jit(solution)/shard_map/ppermute | solution.py:33
  543.1 89.5 %reduce-scatter.17.cloned.1.call-start = ((), (), s32[]{:S(2)}) async-start(), calls=%async_computation.16 | async-start | bytes 1310720 | tf_op jit(solution)/shard_map/reduce_scatter | solution.py:704
  545.9 25.4 %collective-permute-start.84 = (bf16[1024,512]{1,0:T(8,128)(2,1)}, bf16[1024,512]{1,0:T(8,128)(2,1)}, u32[]{:S(2)}, u32[]{:S(2)}) collective-permute-start(bf16[1024,512]{1,0:T(8,128)(2,1)} %add_convert_fusion.2), channel_id=1, source_target_pairs={{0,8},{4,12},{8,0},{12,4},{1,9},{5,13},{9,1},{13,5},{2,10},{6,14},... | collective-permute-start | bytes 3145736 | tf_op jit(solution)/shard_map/ppermute | solution.py:37
  555.0 18.1 %collective-permute-start.85 = (bf16[272,512]{1,0:T(8,128)(2,1)S(1)}, bf16[272,512]{1,0:T(8,128)(2,1)S(1)}, u32[]{:S(2)}, u32[]{:S(2)}) collective-permute-start(bf16[272,512]{1,0:T(8,128)(2,1)S(1)} %copy-done.38), channel_id=1, source_target_pairs={{0,4},{4,0},{8,12},{12,8},{1,5},{5,1},{9,13},{13,9},{2,6},{6,2},{1... | collective-permute-start | bytes 835592 | tf_op jit(solution)/shard_map/ppermute | solution.py:33
  567.7 14.9 %collective-permute-start.114 = (bf16[256,512]{1,0:T(8,128)(2,1)S(1)}, bf16[256,512]{1,0:T(8,128)(2,1)S(1)}, u32[]{:S(2)}, u32[]{:S(2)}) collective-permute-start(bf16[256,512]{1,0:T(8,128)(2,1)S(1)} %copy-done.42), channel_id=1, source_target_pairs={{0,16},{16,0},{1,17},{17,1},{2,18},{18,2},{3,19},{19,3},{4,20},{20... | collective-permute-start | bytes 786440 | tf_op jit(solution)/shard_map/ppermute | solution.py:29
  568.2 16.6 %collective-permute-start.116 = (bf16[256,512]{1,0:T(8,128)(2,1)}, bf16[256,512]{1,0:T(8,128)(2,1)S(1)}, u32[]{:S(2)}, u32[]{:S(2)}) collective-permute-start(bf16[256,512]{1,0:T(8,128)(2,1)} %collective-permute-done.112.refs_10_), channel_id=1, source_target_pairs={{0,16},{16,0},{1,17},{17,1},{2,18},{18,2},{3,19},{19,3},{4,20},{20... | collective-permute-start | bytes 786440 | tf_op jit(solution)/shard_map/ppermute | solution.py:29
  575.7 108.5 %reduce-scatter.15.cloned.1.call-start = ((), (), s32[]{:S(2)}) async-start(), calls=%async_computation.15 | async-start | bytes 1392640 | tf_op jit(solution)/shard_map/reduce_scatter | solution.py:704
  584.8 41.4 %collective-permute-start.89 = (bf16[1024,384]{1,0:T(8,128)(2,1)S(1)}, bf16[1024,384]{1,0:T(8,128)(2,1)S(1)}, u32[]{:S(2)}, u32[]{:S(2)}) collective-permute-start(bf16[1024,384]{1,0:T(8,128)(2,1)S(1)} %add_convert_fusion.20), channel_id=1, source_target_pairs={{0,8},{4,12},{8,0},{12,4},{1,9},{5,13},{9,1},{13,5},{2,10},{6,14},... | collective-permute-start | bytes 2359304 | tf_op jit(solution)/shard_map/ppermute | solution.py:37
  586.3 28.3 %collective-permute-start.113 = (bf16[256,512]{1,0:T(8,128)(2,1)S(1)}, bf16[256,512]{1,0:T(8,128)(2,1)S(1)}, u32[]{:S(2)}, u32[]{:S(2)}) collective-permute-start(bf16[256,512]{1,0:T(8,128)(2,1)S(1)} %collective-permute-done.78.refs_9_), channel_id=1, source_target_pairs={{0,8},{4,12},{8,0},{12,4},{1,9},{5,13},{9,1},{13,5},{2,10},{6,14},... | collective-permute-start | bytes 786440 | tf_op jit(solution)/shard_map/ppermute | solution.py:37
  587.8 28.2 %collective-permute-start.115 = (bf16[256,512]{1,0:T(8,128)(2,1)S(1)}, bf16[256,512]{1,0:T(8,128)(2,1)S(1)}, u32[]{:S(2)}, u32[]{:S(2)}) collective-permute-start(bf16[256,512]{1,0:T(8,128)(2,1)S(1)} %collective-permute-done.78.refs_9_), channel_id=1, source_target_pairs={{0,16},{16,0},{1,17},{17,1},{2,18},{18,2},{3,19},{19,3},{4,20},{20... | collective-permute-start | bytes 786440 | tf_op jit(solution)/shard_map/ppermute | solution.py:29
  592.1 28.1 %collective-permute-start.87 = (bf16[128,1024]{1,0:T(8,128)(2,1)S(1)}, bf16[128,1024]{1,0:T(8,128)(2,1)S(1)}, u32[]{:S(2)}, u32[]{:S(2)}) collective-permute-start(bf16[128,1024]{1,0:T(8,128)(2,1)S(1)} %get-tuple-element.344), channel_id=1, source_target_pairs={{0,8},{4,12},{8,0},{12,4},{1,9},{5,13},{9,1},{13,5},{2,10},{6,14},... | collective-permute-start | bytes 786440 | tf_op jit(solution)/shard_map/ppermute | solution.py:37
  596.3 29.9 %collective-permute-start.99 = (bf16[272,512]{1,0:T(8,128)(2,1)S(1)}, bf16[272,512]{1,0:T(8,128)(2,1)S(1)}, u32[]{:S(2)}, u32[]{:S(2)}) collective-permute-start(bf16[272,512]{1,0:T(8,128)(2,1)S(1)} %copy-done.38), channel_id=1, source_target_pairs={{0,8},{4,12},{8,0},{12,4},{1,9},{5,13},{9,1},{13,5},{2,10},{6,14},... | collective-permute-start | bytes 835592 | tf_op jit(solution)/shard_map/ppermute | solution.py:37
  614.6 16.5 %collective-permute-start.119 = (bf16[128,1024]{1,0:T(8,128)(2,1)}, bf16[128,1024]{1,0:T(8,128)(2,1)}, u32[]{:S(2)}, u32[]{:S(2)}) collective-permute-start(bf16[128,1024]{1,0:T(8,128)(2,1)} %reduce-scatter.13.cloned.1.call-done.refs_0_), channel_id=1, source_target_pairs={{0,8},{4,12},{8,0},{12,4},{1,9},{5,13},{9,1},{13,5},{2,10},{6,14},... | collective-permute-start | bytes 786440 | tf_op jit(solution)/shard_map/ppermute | solution.py:37
  616.0 16.5 %collective-permute-start.118 = (bf16[128,1024]{1,0:T(8,128)(2,1)}, bf16[128,1024]{1,0:T(8,128)(2,1)}, u32[]{:S(2)}, u32[]{:S(2)}) collective-permute-start(bf16[128,1024]{1,0:T(8,128)(2,1)} %reduce-scatter.13.cloned.1.call-done.refs_0_), channel_id=1, source_target_pairs={{0,4},{4,0},{8,12},{12,8},{1,5},{5,1},{9,13},{13,9},{2,6},{6,2},{1... | collective-permute-start | bytes 786440 | tf_op jit(solution)/shard_map/ppermute | solution.py:33
  626.2 21.8 %collective-permute-start.88 = (bf16[2,128,1024]{2,1,0:T(8,128)(2,1)}, bf16[2,128,1024]{2,1,0:T(8,128)(2,1)}, u32[]{:S(2)}, u32[]{:S(2)}) collective-permute-start(bf16[2,128,1024]{2,1,0:T(8,128)(2,1)} %maximum_select_fusion.6), channel_id=1, source_target_pairs={{0,16},{16,0},{1,17},{17,1},{2,18},{18,2},{3,19},{19,3},{4,20},{20... | collective-permute-start | bytes 1572872 | tf_op jit(solution)/shard_map/ppermute | solution.py:29
  647.4 19.0 %collective-permute-start.117 = (bf16[256,512]{1,0:T(8,128)(2,1)S(1)}, bf16[256,512]{1,0:T(8,128)(2,1)S(1)}, u32[]{:S(2)}, u32[]{:S(2)}) collective-permute-start(bf16[256,512]{1,0:T(8,128)(2,1)S(1)} %copy-done.61), channel_id=1, source_target_pairs={{0,16},{16,0},{1,17},{17,1},{2,18},{18,2},{3,19},{19,3},{4,20},{20... | collective-permute-start | bytes 786440 | tf_op jit(solution)/shard_map/ppermute | solution.py:29
  647.5 19.5 %collective-permute-start.108 = (bf16[256,512]{1,0:T(8,128)(2,1)S(1)}, bf16[256,512]{1,0:T(8,128)(2,1)S(1)}, u32[]{:S(2)}, u32[]{:S(2)}) collective-permute-start(bf16[256,512]{1,0:T(8,128)(2,1)S(1)} %copy-done.54), channel_id=1, source_target_pairs={{0,16},{16,0},{1,17},{17,1},{2,18},{18,2},{3,19},{19,3},{4,20},{20... | collective-permute-start | bytes 786440 | tf_op jit(solution)/shard_map/ppermute | solution.py:29
  648.0 19.1 %collective-permute-start.109 = (bf16[256,512]{1,0:T(8,128)(2,1)}, bf16[256,512]{1,0:T(8,128)(2,1)S(1)}, u32[]{:S(2)}, u32[]{:S(2)}) collective-permute-start(bf16[256,512]{1,0:T(8,128)(2,1)} %collective-permute-done.105.refs_1_), channel_id=1, source_target_pairs={{0,16},{16,0},{1,17},{17,1},{2,18},{18,2},{3,19},{19,3},{4,20},{20... | collective-permute-start | bytes 786440 | tf_op jit(solution)/shard_map/ppermute | solution.py:29
  650.0 17.1 %collective-permute-start.110 = (bf16[256,512]{1,0:T(8,128)(2,1)S(1)}, bf16[256,512]{1,0:T(8,128)(2,1)S(1)}, u32[]{:S(2)}, u32[]{:S(2)}) collective-permute-start(bf16[256,512]{1,0:T(8,128)(2,1)S(1)} %collective-permute-done.106.refs_2_), channel_id=1, source_target_pairs={{0,16},{16,0},{1,17},{17,1},{2,18},{18,2},{3,19},{19,3},{4,20},{20... | collective-permute-start | bytes 786440 | tf_op jit(solution)/shard_map/ppermute | solution.py:29
  666.4 22.8 %collective-permute-start.101 = (bf16[272,512]{1,0:T(8,128)(2,1)S(1)}, bf16[272,512]{1,0:T(8,128)(2,1)S(1)}, u32[]{:S(2)}, u32[]{:S(2)}) collective-permute-start(bf16[272,512]{1,0:T(8,128)(2,1)S(1)} %copy-done.38), channel_id=1, source_target_pairs={{0,16},{16,0},{1,17},{17,1},{2,18},{18,2},{3,19},{19,3},{4,20},{20... | collective-permute-start | bytes 835592 | tf_op jit(solution)/shard_map/ppermute | solution.py:29
  667.0 37.9 %collective-permute-start.103 = (bf16[272,512]{1,0:T(8,128)(2,1)S(1)}, bf16[272,512]{1,0:T(8,128)(2,1)S(1)}, u32[]{:S(2)}, u32[]{:S(2)}) collective-permute-start(bf16[272,512]{1,0:T(8,128)(2,1)S(1)} %collective-permute-done.99.refs_10_), channel_id=1, source_target_pairs={{0,16},{16,0},{1,17},{17,1},{2,18},{18,2},{3,19},{19,3},{4,20},{20... | collective-permute-start | bytes 835592 | tf_op jit(solution)/shard_map/ppermute | solution.py:29
  683.7 21.1 %collective-permute-start.100 = (bf16[272,512]{1,0:T(8,128)(2,1)S(1)}, bf16[272,512]{1,0:T(8,128)(2,1)S(1)}, u32[]{:S(2)}, u32[]{:S(2)}) collective-permute-start(bf16[272,512]{1,0:T(8,128)(2,1)S(1)} %collective-permute-done.85.refs_9_), channel_id=1, source_target_pairs={{0,8},{4,12},{8,0},{12,4},{1,9},{5,13},{9,1},{13,5},{2,10},{6,14},... | collective-permute-start | bytes 835592 | tf_op jit(solution)/shard_map/ppermute | solution.py:37
  684.2 21.2 %collective-permute-start.102 = (bf16[272,512]{1,0:T(8,128)(2,1)S(1)}, bf16[272,512]{1,0:T(8,128)(2,1)S(1)}, u32[]{:S(2)}, u32[]{:S(2)}) collective-permute-start(bf16[272,512]{1,0:T(8,128)(2,1)S(1)} %collective-permute-done.85.refs_9_), channel_id=1, source_target_pairs={{0,16},{16,0},{1,17},{17,1},{2,18},{18,2},{3,19},{19,3},{4,20},{20... | collective-permute-start | bytes 835592 | tf_op jit(solution)/shard_map/ppermute | solution.py:29
  689.2 16.3 %collective-permute-start.93 = (bf16[272,512]{1,0:T(8,128)(2,1)}, bf16[272,512]{1,0:T(8,128)(2,1)S(1)}, u32[]{:S(2)}, u32[]{:S(2)}) collective-permute-start(bf16[272,512]{1,0:T(8,128)(2,1)} %reduce-scatter.15.cloned.1.call-done.refs_0_), channel_id=1, source_target_pairs={{0,8},{4,12},{8,0},{12,4},{1,9},{5,13},{9,1},{13,5},{2,10},{6,14},... | collective-permute-start | bytes 835592 | tf_op jit(solution)/shard_map/ppermute | solution.py:37
  (364 other events, 3592.3 us)
Sparse Core Ops, SparseCore 0:
  38.8 33.0 all-gather.5
  74.0 27.4 all-gather.7
  103.7 28.4 all-gather.9
  178.0 31.3 all-gather.11
  220.7 27.5 all-gather.13
  396.1 25.7 reduce-scatter.6
  428.7 25.7 reduce-scatter.8
  503.7 26.7 reduce-scatter.10
  543.2 25.7 reduce-scatter.12
  575.8 26.6 reduce-scatter.16
  640.4 27.6 reduce-scatter.14

commit v4 on v3

--- a/solution.py
+++ b/solution.py
@@ -67,7 +67,7 @@
     return partial[:rows].astype(f32) + swap_core(partial[rows:]).astype(f32)
 
 
-(PROJECT, ATTEND0, ATTEND1, STACKED, LAST, NORM, FEED0, FEED1) = range(8)
+(SEND, ATTEND0, ATTEND1, STACKED, LAST, NORM, FEED0, FEED1, OUT) = range(9)
 
 
 def norm_parts(values):
@@ -137,18 +137,23 @@
 
 
 def attention_back_kernel(
-    q_ref, k_ref, v_ref, g_ref, lse_ref, qid_ref, kid_ref, dq_ref, dk_ref, dv_ref, *, scale
+    q_ref, k_ref, v_ref, g_ref, lse_ref, qid_ref, kid_ref, *refs, scale, last
 ):
     queries = q_ref[...] * jnp.asarray(scale, bf16)
     keys, values, grads = k_ref[...], v_ref[...], g_ref[...]
     keys_t = keys.T
     same = kid_ref[...] == qid_ref[...]
     first = lax.broadcasted_iota(jnp.int32, queries.shape, 1) < queries.shape[1] // 2
-
-    @pl.when(pl.program_id(1) == 0)
+    step = pl.program_id(1)
+    if last:
+        early_q, early_k, early_v, out_ref, dk_ref, dv_ref = refs
+    else:
+        dq_ref, dk_ref, dv_ref = refs
+
+    @pl.when(step == 0)
     def _():
-        dk_ref[...] = jnp.zeros_like(dk_ref)
-        dv_ref[...] = jnp.zeros_like(dv_ref)
+        dk_ref[...] = early_k[...] if last else jnp.zeros_like(dk_ref)
+        dv_ref[...] = early_v[...] if last else jnp.zeros_like(dv_ref)
 
     parts = []
     for head in range(2):
@@ -165,40 +170,104 @@
         parts.append(dot(keys_t, score_grad))
     width = keys_t.shape[0] // 2
     stacked = jnp.concatenate([parts[0][:width], parts[1][width:]], axis=0)
-    dq_ref[...] = (stacked.T * scale).astype(bf16)
-
-
-def attention_backward(projected, keys_values, grads, lse, query_ids, key_ids, scale):
+    query_grad = (stacked.T * scale).astype(bf16)
+    if not last:
+        dq_ref[...] = query_grad
+        return
+    early, tile = early_q.shape[0], query_grad.shape[0]
+    start = pl.multiple_of(early + step * tile, tile)
+    out_ref[pl.ds(start, tile), :LANES] = query_grad
+
+    @pl.when(step == pl.num_programs(1) - 1)
+    def _():
+        out_ref[:early, :LANES] = early_q[...]
+        out_ref[:, LANES : 2 * LANES] = dk_ref[...].astype(bf16)
+        out_ref[:, 2 * LANES :] = dv_ref[...].astype(bf16)
+
+
+def attention_backward(projected, keys_values, grads, lse, query_ids, key_ids, scale, early=None):
     rows, seq_len = projected.shape[0], keys_values.shape[0]
     tile = min(256, rows)
     elems = 4 * rows * seq_len
-    return pl.pallas_call(
-        functools.partial(attention_back_kernel, scale=scale),
-        grid=(2, rows // tile),
-        in_specs=[
-            pl.BlockSpec((tile, LANES), lambda p, i: (i, 3 * p)),
-            pl.BlockSpec((seq_len, LANES), lambda p, i: (0, 3 * p + 1)),
-            pl.BlockSpec((seq_len, LANES), lambda p, i: (0, 3 * p + 2)),
-            pl.BlockSpec((tile, LANES), lambda p, i: (i, p)),
-            pl.BlockSpec((1, 2, tile), lambda p, i: (p, 0, i)),
-            pl.BlockSpec((1, tile), lambda p, i: (0, i)),
-            pl.BlockSpec((seq_len, 1), lambda p, i: (0, 0)),
-        ],
-        out_specs=[
-            pl.BlockSpec((tile, LANES), lambda p, i: (i, p)),
-            pl.BlockSpec((seq_len, LANES), lambda p, i: (0, p)),
-            pl.BlockSpec((seq_len, LANES), lambda p, i: (0, p)),
-        ],
-        out_shape=[
+
+    def column(size):
+        return pl.BlockSpec((size, LANES), lambda p, i: (0, p))
+
+    in_specs = [
+        pl.BlockSpec((tile, LANES), lambda p, i: (i, 3 * p)),
+        pl.BlockSpec((seq_len, LANES), lambda p, i: (0, 3 * p + 1)),
+        pl.BlockSpec((seq_len, LANES), lambda p, i: (0, 3 * p + 2)),
+        pl.BlockSpec((tile, LANES), lambda p, i: (i, p)),
+        pl.BlockSpec((1, 2, tile), lambda p, i: (p, 0, i)),
+        pl.BlockSpec((1, tile), lambda p, i: (0, i)),
+        pl.BlockSpec((seq_len, 1), lambda p, i: (0, 0)),
+    ]
+    if early is None:
+        out_specs = [pl.BlockSpec((tile, LANES), lambda p, i: (i, p))] + [column(seq_len)] * 2
+        out_shape = [
             jax.ShapeDtypeStruct((rows, 2 * LANES), bf16),
             jax.ShapeDtypeStruct((seq_len, 2 * LANES), f32),
             jax.ShapeDtypeStruct((seq_len, 2 * LANES), f32),
-        ],
+        ]
+        scratch = []
+    else:
+        in_specs += [column(early[0].shape[0]), column(seq_len), column(seq_len)]
+        out_specs = pl.BlockSpec((seq_len, 3 * LANES), lambda p, i: (0, p))
+        out_shape = jax.ShapeDtypeStruct((seq_len, 6 * LANES), bf16)
+        scratch = [pltpu.VMEM((seq_len, LANES), f32)] * 2
+    return pl.pallas_call(
+        functools.partial(attention_back_kernel, scale=scale, last=early is not None),
+        grid=(2, rows // tile),
+        in_specs=in_specs,
+        out_specs=out_specs,
+        out_shape=out_shape,
+        scratch_shapes=scratch,
         compiler_params=pltpu.CompilerParams(vmem_limit_bytes=32 << 20),
         cost_estimate=pl.CostEstimate(
             flops=elems * 10 * 128, bytes_accessed=6 << 20, transcendentals=elems
         ),
-    )(projected, keys_values, keys_values, grads, lse, query_ids, key_ids)
+    )(projected, keys_values, keys_values, grads, lse, query_ids, key_ids, *(early or ()))
+
+
+def weight_grad_kernel(*refs, lefts, rights):
+    outs = refs[-lefts * rights :]
+    for i in range(lefts):
+        turned = [refs[2 * i + k][...].T for k in range(2)]
+        for j in range(rights):
+            at = 2 * lefts + 2 * j
+            total = dot(turned[0], refs[at][...]) + dot(turned[1], refs[at + 1][...])
+            outs[i * rights + j][...] = total.astype(bf16)
+
+
+def weight_grad(lefts, rights):
+    size = lefts[0][0].shape[1]
+    depth = lefts[0][0].shape[0]
+    tile = min(256, size)
+    operands, specs, outs = [], [], []
+    for pair in lefts:
+        for value in pair:
+            operands.append(value)
+            specs.append(pl.BlockSpec((depth, tile), lambda i: (0, i)))
+    for pair, cols, at in rights:
+        for value, row in pair:
+            operands.append(value)
+            specs.append(pl.BlockSpec((depth, cols), lambda i, row=row, at=at: (row, at)))
+    for _ in lefts:
+        outs += [jax.ShapeDtypeStruct((size, cols), bf16) for _, cols, _ in rights]
+    columns = sum(cols for _, cols, _ in rights)
+    return pl.pallas_call(
+        functools.partial(weight_grad_kernel, lefts=len(lefts), rights=len(rights)),
+        grid=(size // tile,),
+        in_specs=specs,
+        out_specs=[pl.BlockSpec((tile, out.shape[1]), lambda i: (i, 0)) for out in outs],
+        out_shape=outs,
+        compiler_params=pltpu.CompilerParams(vmem_limit_bytes=32 << 20),
+        cost_estimate=pl.CostEstimate(
+            flops=4 * depth * size * len(lefts) * columns,
+            bytes_accessed=4 * depth * (size * len(lefts) + columns),
+            transcendentals=0,
+        ),
+    )(*operands)
 
 
 def whole(shape):
@@ -269,16 +338,22 @@
     )(at_eighth, *operands)
 
 
-def place_kernel(at, *refs, fixed):
-    qkv_ref, out_ref, gain_ref = refs[-3:]
-    count = (len(refs) - 3) // 2
-    rows, cols = refs[count].shape
-    for k in range(count):
-        slot = k if fixed else lax.rem(at[0] + count - k, count)
-        packed, far = refs[k], refs[count + k]
+def place_qkv_kernel(at, *refs, fixed):
+    out_ref = refs[-1]
+    rows, cols = refs[4].shape
+    for k in range(4):
+        slot = k if fixed else lax.rem(at[0] + 4 - k, 4)
         part = pl.ds(pl.multiple_of(slot * rows, rows), rows)
-        qkv_ref[part, :cols] = packed[:rows, :cols]
-        qkv_ref[part, cols:] = far[...]
+        out_ref[part, :cols] = refs[k][:rows, :cols]
+        out_ref[part, cols:] = refs[4 + k][...]
+
+
+def place_out_kernel(at, *refs, fixed):
+    out_ref, gain_ref = refs[-2:]
+    rows, cols = refs[0].shape[0] - 16, refs[0].shape[1] - LANES
+    for k in range(4):
+        slot = k if fixed else lax.rem(at[0] + 4 - k, 4)
+        packed = refs[k]
         away = slot ^ at[1]
         away = 2 * (away & 1) + (away >> 1)
         out_ref[away, :, :LANES] = packed[:LANES, cols:]
@@ -289,24 +364,16 @@
         gain_ref[1:2, part] = gains[0:1, rows:]
 
 
-def place(packed, far, depth, fixed):
-    count = 4
-    rows, cols = far[0].shape
-    if fixed:
-        rows = rows // count
-    shapes = ((rows + 16, cols + LANES), (rows, cols))
+def place(kernel, operands, shapes, outs, at, fixed):
     specs = [
         pl.BlockSpec(shape, (lambda g, at, k=k: (k, 0)) if fixed else (lambda g, at: (0, 0)))
         for shape in shapes
-        for k in range(count)
+        for k in range(4)
     ]
-    outs = [
-        jax.ShapeDtypeStruct((rows * count, 2 * cols), bf16),
-        jax.ShapeDtypeStruct((count, LANES, 2 * LANES), bf16),
-        jax.ShapeDtypeStruct((2, rows * count), f32),
-    ]
+    if fixed:
+        operands = [value for value in operands for _ in range(4)]
     return pl.pallas_call(
-        functools.partial(place_kernel, fixed=fixed),
+        functools.partial(kernel, fixed=fixed),
         grid_spec=pltpu.PrefetchScalarGridSpec(
             num_scalar_prefetch=1,
             grid=(1,),
@@ -315,10 +382,10 @@
         ),
         out_shape=outs,
         compiler_params=pltpu.CompilerParams(vmem_limit_bytes=24 << 20),
-    )(depth, *(list(packed) * (count if fixed else 1)), *(list(far) * (count if fixed else 1)))
-
-
-def small_call(kernel, at, operands, outs):
+    )(at, *operands)
+
+
+def small_call(kernel, at, operands, outs, room=40):
     return pl.pallas_call(
         kernel,
         grid_spec=pltpu.PrefetchScalarGridSpec(
@@ -328,7 +395,7 @@
             out_specs=[whole(out.shape) for out in outs],
         ),
         out_shape=outs,
-        compiler_params=pltpu.CompilerParams(vmem_limit_bytes=40 << 20),
+        compiler_params=pltpu.CompilerParams(vmem_limit_bytes=room << 20),
     )(at, *operands)
 
 
@@ -374,7 +441,8 @@
 def assemble_kernel(at, *refs, kind, shapes):
     groups = [refs[4 * i : 4 * i + 4] for i in range(4)]
     rows_old = refs[16 : 16 + len(shapes)]
-    outs = refs[16 + len(shapes) :]
+    extra = refs[16 + len(shapes)]
+    outs = refs[17 + len(shapes) :]
     grads, rows_new, sums_ref = outs[: len(shapes)], outs[len(shapes) : 2 * len(shapes)], outs[-1]
     first_core = at[1] == 0
     gain = 0.0
@@ -401,10 +469,18 @@
                     block = value[half * LANES : (half + 1) * LANES, 3 * LANES :]
                     grads[1][part, pl.ds(start, LANES)] = block
                 gain = gain + value[rows : rows + 1, :]
+    lane = lax.broadcasted_iota(jnp.int32, (1, LANES), 1)
+    sums_ref[...] = jnp.zeros_like(sums_ref)
     if kind == PACKED:
         outs[-2][...] = gain
-    sums_ref[...] = jnp.zeros_like(sums_ref)
-    lane = lax.broadcasted_iota(jnp.int32, (1, LANES), 1)
+        moment = decay_rate * extra[...] + (1.0 - decay_rate) * gain * gain
+        square = (gain * lax.rsqrt(moment)) ** 2
+        middle = square.shape[1] // 2
+        attn_total = jnp.sum(square[:, :middle], axis=1, keepdims=True)
+        mlp_total = jnp.sum(square[:, middle:], axis=1, keepdims=True)
+        sums_ref[:, :LANES] = jnp.where(lane == 2, attn_total, jnp.where(lane == 3, mlp_total, 0.0))
+    else:
+        sums_ref[:, :LANES] = extra[...]
     begin = LANES
     for index, (total_rows, cols) in enumerate(shapes):
         grad_ref, row_ref, new_ref = grads[index], rows_old[index], rows_new[index]
@@ -428,7 +504,7 @@
         sums_ref[:, :LANES] += jnp.where(lane == index, total, 0.0)
 
 
-def assemble(near0, near1, far0, far1, rows_old, where, kind, shapes):
+def assemble(near0, near1, far0, far1, rows_old, extra, where, kind, shapes):
     outs = [jax.ShapeDtypeStruct(shape, f32) for shape in shapes]
     outs += [jax.ShapeDtypeStruct((shape[0], 1), f32) for shape in shapes]
     if kind == PACKED:
@@ -439,8 +515,9 @@
     return small_call(
         functools.partial(assemble_kernel, kind=kind, shapes=shapes),
         where,
-        [*near0, *far0, *near1, *far1, *rows_old],
+        [*near0, *far0, *near1, *far1, *rows_old, extra],
         outs,
+        56,
     )
 
 
@@ -517,11 +594,13 @@
 
     chip_array = chip.reshape(1).astype(jnp.int32)
 
-    def out_from_columns(columns):
+    def out_parts(columns):
         keep, came = columns[:2], swap_x(columns[2:])
+        return [keep, came, swap_y(keep), swap_y(came)]
+
+    def join_out(parts):
         out = jax.ShapeDtypeStruct((2 * LANES, width), bf16)
-        operands = [keep, came, swap_y(keep), swap_y(came)]
-        return small_call(join_out_kernel, chip_array, operands, [out])[0]
+        return small_call(join_out_kernel, chip_array, parts, [out])[0]
 
     weights, gains = [types.SimpleNamespace(), types.SimpleNamespace()], [None, None]
     depth_array = jnp.stack([depth, chip]).astype(jnp.int32)
@@ -535,9 +614,23 @@
         down_parts = by_layer(*cuts[6:])
         turns = rotations(packed_parts[0])
         fars = [swap_y(value[:rows, : 3 * LANES]) for value in turns[1:]]
-        qkv, columns, gains[0] = place(turns, [far_parts[0]] + fars, depth_array, False)
-        weights[0].qkv = qkv
-        weights[0].out = out_from_columns(columns)
+
+        def place_qkv(packed, far, fixed):
+            shapes = ((rows + 16, 4 * LANES), (rows, 3 * LANES))
+            out = jax.ShapeDtypeStruct((4 * rows, 6 * LANES), bf16)
+            return place(place_qkv_kernel, [*packed, *far], shapes, [out], depth_array, fixed)[0]
+
+        def place_out(packed, fixed):
+            outs = [
+                jax.ShapeDtypeStruct((4, LANES, 2 * LANES), bf16),
+                jax.ShapeDtypeStruct((2, 4 * rows), f32),
+            ]
+            shapes = ((rows + 16, 4 * LANES),)
+            columns, gain = place(place_out_kernel, packed, shapes, outs, depth_array, fixed)
+            return out_parts(columns), gain
+
+        weights[0].qkv = place_qkv(turns, [far_parts[0]] + fars, False)
+        weights[0].out, gains[0] = place_out(turns, False)
         up_gathered = [gather_rows(after(up_parts[0], *turns[1:])), gather_rows(up_parts[1])]
         down_gathered = [gather_rows(after(down_parts[0], *turns[1:])), gather_rows(down_parts[1])]
         packed_gathered = gather_rows(packed_parts[1])
@@ -586,6 +679,7 @@
 
         def attend(k, queries):
             context, lse = attention_forward(queries, keys_values, query_ids[k], key_ids, scale)
+            context = hook(OUT, context) if k == 1 else context
             return context, lse, fold_core(dot(context, held.out))
 
         context1, lse1, across = attend(1, hook(ATTEND0, projected[1]))
@@ -609,7 +703,7 @@
 
         activated0, slope0, keep = feed(hook(FEED0, normed_all[0]))
         activated1, slope1, across = feed(hook(FEED1, after(normed_all[1], keep)))
-        came = hook(LAST, swap_x(across.astype(bf16)))
+        came = hook(LAST, swap_x(hook(SEND, across.astype(bf16))))
         unit_mlp, scale_mlp = norm_parts(normed + keep + came.astype(f32))
         return (unit_mlp * mlp_gain).astype(bf16), types.SimpleNamespace(
             inputs_all=inputs_all,
@@ -630,15 +724,8 @@
         held = weights[layer]
         attn_gain, mlp_gain = gains[layer][0], gains[layer][1]
 
-        def over_tokens(left, right):
-            return (rows_product(left[0], right[0]) + rows_product(left[1], right[1])).astype(bf16)
-
-        def by_half(left, right):
-            size = right[0].shape[1] // 2
-            return [
-                over_tokens(left, [value[:, at : at + size] for value in right])
-                for at in (0, size)
-            ]
+        def both(pair):
+            return [(value, 0) for value in pair]
 
         mlp_in, mlp_gain_grad = norm_back(
             out_grads.astype(f32), kept.unit_mlp, kept.scale_mlp, mlp_gain
@@ -655,14 +742,14 @@
 
         upward0, keep = feed_back(0, hook(FEED0, down_all[0]))
         upward1, across = feed_back(1, hook(FEED1, after(down_all[1], keep)))
-        grad_down = [over_tokens(left, down_all) for left in zip(*kept.activated)]
+        grad_down = weight_grad(list(zip(*kept.activated)), [(both(down_all), width, 0)])
         came = hook(NORM, swap_x(across.astype(bf16)), grad_down)
         attn_in, attn_gain_grad = norm_back(
             mlp_in + keep + came.astype(f32), kept.unit_attn, kept.scale_attn, attn_gain
         )
         branch_all = gather_tiles(attn_in.astype(bf16))
 
-        def attend_back(k, value):
+        def attend_back(k, value, early=None):
             grads = times_transposed(value, held.out).astype(bf16)
             return attention_backward(
                 kept.projected[k],
@@ -672,32 +759,25 @@
                 query_ids[k],
                 key_ids,
                 scale,
+                early,
             )
 
-        grad_up = [over_tokens(kept.normed_all, right) for right in zip(upward0, upward1)]
-        query0, key0, value0 = attend_back(0, hook(ATTEND0, branch_all[0], grad_up))
-        query1, key1, value1 = attend_back(1, hook(ATTEND1, after(branch_all[1], query0)))
-        key_grad, value_grad = (key0 + key1).astype(bf16), (value0 + value1).astype(bf16)
-        stacked = []
-        for k, query_grad in enumerate((query0, query1)):
-            part = slice(4 * half * k, 4 * half * (k + 1))
-            stacked.append(
-                jnp.concatenate(
-                    [
-                        piece[:, LANES * p : LANES * (p + 1)]
-                        for p in range(2)
-                        for piece in (query_grad, key_grad[part], value_grad[part])
-                    ],
-                    axis=1,
-                )
-            )
-        stacked[1] = hook(STACKED, stacked[1])
-        across = fold_core(times_transposed(stacked[1], held.qkv)).astype(bf16)
-        keep = fold_core(times_transposed(after(stacked[0], across), held.qkv))
+        grad_up = weight_grad(
+            [kept.normed_all],
+            [(both(right), right[0].shape[1], 0) for right in zip(upward0, upward1)],
+        )
+        early = attend_back(0, hook(ATTEND0, branch_all[0], grad_up))
+        stacked = attend_back(1, hook(ATTEND1, after(branch_all[1], early[0])), early)
         gain_grads = jnp.stack([attn_gain_grad, mlp_gain_grad])
-        grad_out = over_tokens(kept.context, branch_all)
-        came = hook(LAST, after(swap_x(across), keep), grad_out, gain_grads)
-        grad_qkv = by_half(kept.inputs_all, stacked)
+        (grad_out,) = weight_grad([kept.context], [(both(branch_all), width, 0)])
+        stacked = hook(STACKED, stacked, grad_out, gain_grads)
+        tile = 4 * half
+        across = fold_core(times_transposed(stacked[tile:], held.qkv)).astype(bf16)
+        across = hook(SEND, across)
+        keep = fold_core(times_transposed(after(stacked, across)[:tile], held.qkv))
+        came = hook(LAST, after(swap_x(across), keep))
+        tiles = [(stacked, 0), (stacked, 1)]
+        grad_qkv = weight_grad([kept.inputs_all], [(tiles, 3 * LANES, at) for at in range(2)])
         return (attn_in + keep + came.astype(f32)).astype(bf16), grad_qkv
 
     def scatter_rows(value):
@@ -759,34 +839,65 @@
 
     inputs = own_rows(tokens)
     of0, of1 = types.SimpleNamespace(), types.SimpleNamespace()
-    state = types.SimpleNamespace(out_grads=own_rows(cotangent))
+
+    def total(value):
+        return jnp.sum(value).reshape(1, 1)
+
+    def lanes(values, start):
+        lane = lax.broadcasted_iota(jnp.int32, (1, LANES), 1)
+        return sum(jnp.where(lane == start + i, value, 0.0) for i, value in enumerate(values))
+
+    def with_lanes(row, values):
+        if even:
+            return row
+        return jnp.concatenate([row[:, :LANES] + values, row[:, LANES:]], axis=1)
+
+    masters = (w_qkv[0], w_out[0], w_up[0], w_down[0])
+    gain_masters = (gain_attn, gain_mlp)
+    state = types.SimpleNamespace(
+        out_grads=own_rows(cotangent),
+        weight_totals=lanes([total(master * master) for master in masters + gain_masters], 2),
+    )
     if even:
 
         def hook_forward0(point, value):
-            if point == ATTEND1:
-                value, state.out_grads = sync(value, state.out_grads)
+            if point == OUT:
+                value, up, *parts = sync(value, up_gathered[0], *weights[0].out)
+                weights[0].out = join_out(parts)
+                weights[0].up = with_far(up)
             elif point == NORM:
-                value, up = sync(value, up_gathered[0])
-                weights[0].up = with_far(up)
+                value, far, down = sync(value, weights[0].up[1], down_gathered[0])
+                weights[0].up = weights[0].up[0], far
+                weights[0].down = with_far(down)
             elif point == FEED0:
-                value, down = sync(value, down_gathered[0])
-                weights[0].down = with_far(down)
-            elif point == FEED1:
+                value, far = sync(value, weights[0].down[1])
+                weights[0].down = weights[0].down[0], far
+            elif point == SEND:
                 value, packed = sync(value, packed_gathered)
                 near = packed.reshape(4, rows + 16, 4 * LANES)[:, :rows, : 3 * LANES]
                 far = swap_y(near.reshape(4 * rows, 3 * LANES))
-                qkv, columns, gains[1] = place([packed], [far], depth_array, True)
-                weights[1].qkv, weights[1].out = qkv, out_from_columns(columns)
+                weights[1].qkv = place_qkv([packed], [far], True)
+                weights[1].out, gains[1] = place_out([packed], True)
+            elif point == LAST:
+                value, up = sync(value, up_gathered[1])
+                weights[1].up = with_far(up)
             return value
 
         def hook_forward1(point, value):
-            if point == ATTEND0:
-                value, weights[1].out, up = sync(value, weights[1].out, up_gathered[1])
-                weights[1].up = with_far(up)
+            if point == OUT:
+                value, down, *parts = sync(value, down_gathered[1], *weights[1].out)
+                weights[1].out = join_out(parts)
+                weights[1].down = with_far(down)
             elif point == NORM:
-                value, far, down = sync(value, weights[1].up[1], down_gathered[1])
+                value, far = sync(value, weights[1].up[1])
                 weights[1].up = weights[1].up[0], far
-                weights[1].down = with_far(down)
+            elif point == FEED0:
+                value, far = sync(value, weights[1].down[1])
+                weights[1].down = weights[1].down[0], far
+            elif point == LAST:
+                value, state.out_grads, state.weight_totals = sync(
+                    value, state.out_grads, state.weight_totals
+                )
             return value
 
         def hook_backward1(point, value, *grads):
@@ -797,58 +908,57 @@
                 value, *up = sync(value, *grads[0])
                 of1.up_grads = up
             elif point == ATTEND1:
-                value, came, *outputs = sync(value, of1.down[1], *state.away)
+                value, *outputs = sync(value, *state.away)
+                state.away = outputs
+            elif point == STACKED:
+                value, came, out, of1.gains = sync(value, of1.down[1], *grads)
                 of1.down = scatter_rows(fold(of1.down[0], came))
                 of1.up = halves(of1.up_grads)
-                state.away = outputs
-            elif point == LAST:
-                value, came, out, of1.gains = sync(value, of1.up[1], *grads)
-                of1.up = scatter_rows(fold(of1.up[0], came))
-                of1.out = out_halves(out)
+                of1.out = out
             return value
 
         def hook_backward0(point, value, *grads):
             if point == FEED0:
-                value, down, *qkv = sync(value, of1.down, *of1.qkv)
+                value, came, *qkv = sync(value, of1.up[1], *of1.qkv)
+                of1.up = scatter_rows(fold(of1.up[0], came))
                 of1.qkv = halves(qkv)
+                of1.out = out_halves(of1.out)
+            elif point == NORM:
+                value, came, out_came, down, *grad_down = sync(
+                    value, of1.qkv[1], of1.out[1], of1.down, *grads[0]
+                )
+                of1.qkv = of1.qkv[0], came
+                of1.out = out_pair(of1.out[0], out_came)
                 of1.down = spread_start(down, True)
-            elif point == FEED1:
-                value, came = sync(value, of1.out[1])
-                of1.out = out_pair(of1.out[0], came)
-            elif point == NORM:
-                value, came, cross, up, hop, *down = sync(
-                    value, of1.qkv[1], of1.out[1], of1.up, of1.down[1], *grads[0]
+                of0.down = halves(grad_down)
+            elif point == ATTEND0:
+                value, cross, up, *up_grads = sync(value, of1.out[1], of1.up, *grads[0])
+                of1.packed = scatter_rows(pack(*of1.qkv, of1.out[0], cross, of1.gains))
+                of1.up = up
+                of0.up_grads = up_grads
+            elif point == ATTEND1:
+                value, came, hop, state.in_away = sync(
+                    value, of0.down[1], of1.down[1], state.in_away
                 )
-                of1.packed = scatter_rows(
-                    pack(of1.qkv[0], came, of1.out[0], cross, of1.gains)
-                )
-                of1.down = of1.down[0], hop
-                of1.up = up
-                of0.down = halves(down)
-            elif point == ATTEND0:
-                value, *up = sync(value, *grads[0])
-                of0.up_grads = up
-            elif point == ATTEND1:
-                value, came = sync(value, of0.down[1])
                 of0.down = scatter_rows(fold(of0.down[0], came))
                 of0.up = halves(of0.up_grads)
                 of1.up = spread_start(of1.up, False)
-                of1.down = spread_end(of1.down, True)
+                of1.down = spread_end((of1.down[0], hop), True)
             elif point == STACKED:
-                value, hop, packed, *ends = sync(value, of1.up[1], of1.packed, *of1.down)
+                value, came, hop, packed, out, of0.gains, *ends = sync(
+                    value, of0.up[1], of1.up[1], of1.packed, *grads, *of1.down
+                )
+                of0.up = scatter_rows(fold(of0.up[0], came))
                 of1.up = of1.up[0], hop
                 of1.down = ends
                 of1.packed = spread_start(packed, False)
+                of0.out = out_halves(out)
+            elif point == SEND:
+                value, out_came, hop = sync(value, of0.out[1], of1.packed[1])
+                of0.out = out_pair(of0.out[0], out_came)
+                of1.packed = of1.packed[0], hop
             elif point == LAST:
-                value, came, hop, down, away, out, of0.gains = sync(
-                    value, of0.up[1], of1.packed[1], of0.down, state.in_away, *grads
-                )
-                of0.up = scatter_rows(fold(of0.up[0], came))
-                of0.out = out_halves(out)
-                of1.packed = of1.packed[0], hop
-                of0.down = spread_start(down, True)
-                of1.up = spread_end(of1.up, False)
-                state.in_away = away
+                value, of0.down = sync(value, of0.down)
             return value
 
     else:
@@ -864,7 +974,7 @@
                     found.down = grads[0]
                 elif point == ATTEND0:
                     found.up = grads[0]
-                elif point == LAST:
+                elif point == STACKED:
                     found.out, found.gains = grads
                 return value
 
@@ -879,16 +989,16 @@
     state.in_away = swap_y(in_grads1[half:])
     in_grads0, of0.qkv = backward(in_grads1, saved0, 0, hook_backward0)
     if even:
-        near, came = of0.out
         qkv_near, qkv_came = halves(of0.qkv)
-        packed0 = pack(qkv_near, qkv_came, *out_pair(near, came), of0.gains)
+        packed0 = pack(qkv_near, qkv_came, *of0.out, of0.gains)
+        packed0, of0.up, of0.down, *rest = sync(
+            packed0, of0.up, of0.down, *of1.packed, *of1.up, hidden0, hidden1, in_grads0, in_grads1
+        )
+        of1.packed, of1.up = rest[:2], rest[2:4]
+        hidden0, hidden1, in_grads0, in_grads1 = rest[4:]
         packed0 = scatter_rows(packed0)
-        near1 = [spread_end(of1.packed, False), of1.up, of1.down]
-        near0 = [
-            spread(packed0, False),
-            spread(of0.up, False),
-            spread_end(of0.down, True),
-        ]
+        near0 = [None, spread(of0.up, False), spread(of0.down, True)]
+        near1 = [spread_end(of1.packed, False), spread_end(of1.up, False), of1.down]
     else:
         near1, near0 = reduce_plain(of1), reduce_plain(of0)
 
@@ -916,13 +1026,14 @@
     if even:
         where = jnp.stack([at_eighth, core]).astype(jnp.int32)
 
-        def build(position, kind, olds, shapes):
+        def build(position, kind, olds, extra, shapes):
             return assemble(
                 near0[position],
                 near1[position],
                 [swap_core(value) for value in near0[position]],
                 [swap_core(value) for value in near1[position]],
                 olds,
+                extra,
                 where,
                 kind,
                 shapes,
@@ -931,18 +1042,22 @@
         def column(row):
             return row.reshape(-1, 1)
 
-        down = build(2, ROWS, [column(row_down)], ((8 * unit, width),))
-        up = build(1, COLUMNS, [column(row_up)], ((rows, hidden_width),))
+        down = build(2, ROWS, [column(row_down)], jnp.zeros((1, LANES), f32), ((8 * unit, width),))
+        up = build(
+            1, COLUMNS, [column(row_up)], state.weight_totals, ((rows, hidden_width),)
+        )
+        near0[0] = spread(after(packed0, up[1], down[1]), False)
         built = [None, None, up[:2], down[:2]]
         sums = {2: jnp.concatenate([up[2], down[2]], axis=1)}
         places = {2: (0, LANES), 3: (LANES + 2 * hidden_width, 2 * LANES + 2 * hidden_width)}
         places.update({0: (0, LANES), 1: (1, LANES + 6 * width)})
 
-        def build_first(*tokens):
+        def build_first():
             first = build(
                 0,
                 PACKED,
-                [after(column(row_qkv), *tokens), column(row_out)],
+                [after(column(row_qkv), sums[2]), column(row_out)],
+                jnp.concatenate([var_attn, var_mlp], axis=1),
                 ((rows, 3 * width), (rows, width)),
             )
             built[:2] = (first[0], first[2]), (first[1], first[3])
@@ -983,7 +1098,7 @@
             {0: (LANES, 2 * LANES), 1: (2 * LANES + 6 * width, 3 * LANES + 6 * width)}
         )
 
-        def build_first(*tokens):
+        def build_first():
             return gain_shard
 
     def sum_line(value):
@@ -992,14 +1107,8 @@
         near, two, three = rotations(value)[1:]
         return (value + two) + (near + three)
 
-    masters = (w_qkv[0], w_out[0], w_up[0], w_down[0])
     cols_old = (col_qkv, col_out, col_up, col_down)
-    gain_masters = (gain_attn, gain_mlp)
     moments_old = (var_attn, var_mlp)
-
-    def total(value):
-        return jnp.sum(value).reshape(1, 1)
-
     new_rows, new_cols, ratios, new_masters = [None] * 4, [None] * 4, [None] * 4, [None] * 4
 
     def update(position, summed, weight_total):
@@ -1023,26 +1132,19 @@
         raw = gradient * lax.rsqrt(row_new * new_cols[position] / row_mean)
         new_masters[position] = masters[position] - factor * raw
 
-    def lanes(values, start):
-        lane = lax.broadcasted_iota(jnp.int32, (1, LANES), 1)
-        return sum(jnp.where(lane == start + i, value, 0.0) for i, value in enumerate(values))
-
-    def with_lanes(row, values):
-        return jnp.concatenate([row[:, :LANES] + lanes(values, 2), row[:, LANES:]], axis=1)
-
-    weight_totals = [total(master * master) for master in masters + gain_masters]
-    summed = sum_line(with_lanes(sums[2], weight_totals))
-    weight_all = [summed[:, 2 + i : 3 + i] for i in range(6)]
-    for position in (2, 3):
-        update(position, summed, weight_all[position])
-    gain_shard = build_first(new_masters[2], new_masters[3])
+    early = sum_line(with_lanes(sums[2], state.weight_totals))
+    gain_shard = build_first()
     moments, gain_updates = [], []
     for gain_pos in range(2):
         grad = gain_shard[gain_pos : gain_pos + 1]
         moment = decay_rate * moments_old[gain_pos] + (1.0 - decay_rate) * grad * grad
         moments.append(moment)
         gain_updates.append(grad * lax.rsqrt(moment))
-    summed = sum_line(with_lanes(sums[0], [total(step * step) for step in gain_updates]))
+    last = with_lanes(sums[0], lanes([total(step * step) for step in gain_updates], 2))
+    summed, early = sum_line(last), after(early, last)
+    weight_all = [early[:, 2 + i : 3 + i] for i in range(6)]
+    for position in (2, 3):
+        update(position, early, weight_all[position])
     for position in (0, 1):
         update(position, summed, weight_all[position])
     for gain_pos in range(2):

time: 756 us -> 729 us (0.964)
  matrix products: 121 us -> 70.9 us
  Pallas kernels: 94.4 us -> 124 us
  other arithmetic: 92 us -> 84.2 us
    dot_general x28 -> x0, matrix products: 44.9 us -> none  [rows_product(): lax.dot_general(left, right, (((0,), (0,)), ((), ())), preferred_element_...]
    pallas_call x6 -> x16, Pallas kernels: 40.5 us -> 66.8 us  [the longest x4 39.7 us: attention_backward(): pl.pallas_call(functools.partial(attention_back_kernel, scale=scale, last...]
    all_gather x5, waiting for transfers between devices: 20.3 us -> 5.55 us  [gather_rows(): return lax.all_gather(value, FSDP, axis=0, tiled=True)]
    sub x2 -> x0, other arithmetic: 9.86 us -> none  [update(): new_masters[position] = masters[position] - factor * raw]
    unnamed x581 -> x407, local copies, waits for them, and re-layouts: 33.7 us -> 42.5 us
    broadcast_in_dim x2 -> x4, other arithmetic: 5.61 us -> 14.3 us  [per_device(): master[None]]
  transfers between devices with their start and end apart: 146 -> 146, of which waited for: 47 -> 50; matrix products, arithmetic and copies ran while one was open for 31% -> 23% of each run, Pallas kernels for 10% -> 16%
where the time goes in v4:
time: 729 us; the launch traced here: 719 us
  waiting for transfers between devices  245 us (34%)
  Pallas kernels  124 us (17%)
  starting transfers between devices  99.6 us (14%)
  other arithmetic  84.2 us (12%)
  matrix products  70.9 us (10%)
  local copies, waits for them, and re-layouts  66.3 us (9%)
  between operations  28.6 us (4%)
    ppermute x28, waiting for transfers between devices, swap_x(): return lax.ppermute(value, CTX, [(i, i ^ 1) for i in range(4)])  126 us
    ppermute x36, waiting for transfers between devices, swap_y(): return lax.ppermute(value, CTX, [(i, i ^ 2) for i in range(4)])  90.7 us
    unnamed x407, local copies, waits for them, and re-layouts  42.5 us
    pallas_call x4, Pallas kernels, attention_backward(): pl.pallas_call(functools.partial(attention_back_kernel, scale=scale, last...  39.7 us
    ppermute x36, starting transfers between devices, swap_y(): return lax.ppermute(value, CTX, [(i, i ^ 2) for i in range(4)])  39.4 us
    dot_general x24, matrix products, dot(): return jnp.dot(left, right, preferred_element_type=f32)  36.2 us
    dot_general x24, matrix products, times_transposed(): lax.dot_general(left, right, (((1,), (1,)), ((), ())), preferred_element_...  34.6 us
    ppermute x28, starting transfers between devices, swap_x(): return lax.ppermute(value, CTX, [(i, i ^ 1) for i in range(4)])  32.2 us
  transfers between devices with their start and end apart: 146, of which 50 were waited for; matrix products, arithmetic and copies ran while one was open for 23% of the time, Pallas kernels for 16%

profile of v4, /device:TPU:0, one launch (start us, length us, event | category | flops | bytes accessed | tf_op | source)
XLA Modules:
  0.0 719.2 jit_solution(5413098159266690987)
XLA Ops:
  8.4 3.0 collective-permute-start
  11.4 3.7 shard_map.378
  25.2 10.4 %collective-permute-done.6.refs_2_ = bf16[272,512]{1,0:T(8,128)(2,1)S(1)} collective-permute-done((bf16[272,512]{1,0:T(8,128)(2,1)S(1)}, bf16[272,512]{1,0:T(8,128)(2,1)S(1)}, u32[]{:S(2)}, u32[]{:S(2)}) %collective-permute-start.6) | collective-permute-done | bytes 278560 | tf_op jit(solution)/shard_map/ppermute | solution.py:586
  35.6 5.7 collective-permute-done.5.refs_1_
  49.6 9.4 %collective-permute-done.13.came = bf16[2,128,256]{2,1,0:T(8,128)(2,1)S(1)} collective-permute-done((bf16[2,128,256]{2,1,0:T(8,128)(2,1)S(1)}, bf16[2,128,256]{2,1,0:T(8,128)(2,1)S(1)}, u32[]{:S(2)}, u32[]{:S(2)}) %collective-permute-start.13) | collective-permute-done | bytes 131104 | tf_op jit(solution)/shard_map/ppermute | solution.py:33
  72.4 6.7 shard_map.380
  86.4 6.7 shard_map.383
  94.8 4.4 collective-permute-done.18
  99.2 4.0 all-gather.8.cloned.1.call-done
  103.2 5.4 collective-permute-done.19
  113.7 11.9 %collective-permute-done.24 = bf16[256,1024]{1,0:T(8,128)(2,1)} collective-permute-done((bf16[256,1024]{1,0:T(8,128)(2,1)}, bf16[256,1024]{1,0:T(8,128)(2,1)}, u32[]{:S(2)}, u32[]{:S(2)}) %collective-permute-start.24) | collective-permute-done | bytes 524320 | tf_op jit(solution)/shard_map/ppermute | solution.py:33
  129.7 3.3 multiply_convert_fusion.7
  133.0 6.1 collective-permute-done.22
  139.1 2.9 multiply_convert_fusion.6
  146.9 3.1 multiply_convert_fusion.9
  150.0 2.9 multiply_convert_fusion.8
  152.9 3.3 fusion.112
  158.5 2.9 add_convert_fusion.11
  164.9 7.7 %collective-permute-done.27 = bf16[256,1024]{1,0:T(8,128)(2,1)} collective-permute-done((bf16[256,1024]{1,0:T(8,128)(2,1)}, bf16[256,1024]{1,0:T(8,128)(2,1)}, u32[]{:S(2)}, u32[]{:S(2)}) %collective-permute-start.27) | collective-permute-done | bytes 524320 | tf_op jit(solution)/shard_map/ppermute | solution.py:33
  179.7 12.3 %collective-permute-done.30 = bf16[256,1024]{1,0:T(8,128)(2,1)} collective-permute-done((bf16[256,1024]{1,0:T(8,128)(2,1)}, bf16[256,1024]{1,0:T(8,128)(2,1)}, u32[]{:S(2)}, u32[]{:S(2)}) %collective-permute-start.30) | collective-permute-done | bytes 524320 | tf_op jit(solution)/shard_map/ppermute | solution.py:33
  201.8 6.7 shard_map.385
  216.6 6.9 shard_map.388
  229.1 9.9 %collective-permute-done.38 = bf16[1024,512]{1,0:T(8,128)(2,1)S(1)} collective-permute-done((bf16[1024,512]{1,0:T(8,128)(2,1)S(1)}, bf16[1024,512]{1,0:T(8,128)(2,1)S(1)}, u32[]{:S(2)}, u32[]{:S(2)}) %collective-permute-start.38) | collective-permute-done | bytes 1048608 | tf_op jit(solution)/shard_map/ppermute | solution.py:37
  247.5 19.1 %collective-permute-done.40 = bf16[512,1024]{1,0:T(8,128)(2,1)S(1)} collective-permute-done((bf16[512,1024]{1,0:T(8,128)(2,1)S(1)}, bf16[512,1024]{1,0:T(8,128)(2,1)S(1)}, u32[]{:S(2)}, u32[]{:S(2)}) %collective-permute-start.40) | collective-permute-done | bytes 1048608 | tf_op jit(solution)/shard_map/ppermute | solution.py:37
  277.6 4.4 fusion.87.refs_17_
  282.1 6.1 collective-permute-done.45
  291.5 11.8 %collective-permute-done.49 = bf16[256,1024]{1,0:T(8,128)(2,1)S(1)} collective-permute-done((bf16[256,1024]{1,0:T(8,128)(2,1)S(1)}, bf16[256,1024]{1,0:T(8,128)(2,1)S(1)}, u32[]{:S(2)}, u32[]{:S(2)}) %collective-permute-start.49) | collective-permute-done | bytes 524320 | tf_op jit(solution)/shard_map/ppermute | solution.py:33
  316.5 9.0 %collective-permute-done.52 = bf16[256,1024]{1,0:T(8,128)(2,1)S(1)} collective-permute-done((bf16[256,1024]{1,0:T(8,128)(2,1)S(1)}, bf16[256,1024]{1,0:T(8,128)(2,1)S(1)}, u32[]{:S(2)}, u32[]{:S(2)}) %collective-permute-start.52) | collective-permute-done | bytes 524320 | tf_op jit(solution)/shard_map/ppermute | solution.py:33
  332.5 4.0 shard_map.390
  339.1 3.1 collective-permute-done.53
  342.7 9.9 %shard_map.391 = (bf16[512,256]{1,0:T(8,128)(2,1)S(1)}, f32[1024,256]{1,0:T(8,128)S(1)}, f32[1024,256]{1,0:T(8,128)S(1)}) custom-call(bf16[512,768]{1,0:T(8,128)(2,1)S(1)} %copy-done.18, bf16[1024,768]{1,0:T(8,128)(2,1)S(1)} %copy-done.4, bf16[1024,768]{1,0:T(8,128)(2,1)S(1)} %copy-done.4, bf16[512,256]{1,0:T(8,128)(2,1)S(1)} %convolution_convert_fusion.15.g_ref, ...), custom_call_target="tpu_custom_call" | custom-call | flops 2684354560 | bytes 6291456 | tf_op jit(solution)/shard_map/pallas_call | solution.py:218
  354.4 10.0 %shard_map.392.refs_2_.refs_3_.refs_4_.refs_5_ = bf16[1024,768]{1,0:T(8,128)(2,1)S(1)} custom-call(bf16[512,768]{1,0:T(8,128)(2,1)S(1)} %convolution_convert_fusion.8.q_ref, bf16[1024,768]{1,0:T(8,128)(2,1)S(1)} %copy-done.4, bf16[1024,768]{1,0:T(8,128)(2,1)S(1)} %copy-done.4, bf16[512,256]{1,0:T(8,128)(2,1)S(1)} %convolution_convert_fusion.14.g_ref, ...), custom_call_target="tpu_custom_call" | custom-call | flops 2684354560 | bytes 6291456 | tf_op jit(solution)/shard_map/pallas_call | solution.py:218
  375.9 9.4 %collective-permute-done.61 = bf16[256,1024]{1,0:T(8,128)(2,1)} collective-permute-done((bf16[256,1024]{1,0:T(8,128)(2,1)}, bf16[256,1024]{1,0:T(8,128)(2,1)}, u32[]{:S(2)}, u32[]{:S(2)}) %collective-permute-start.61) | collective-permute-done | bytes 524320 | tf_op jit(solution)/shard_map/ppermute | solution.py:33
  394.7 4.4 shard_map.394
  400.7 3.9 collective-permute-done.65
  442.7 9.2 %collective-permute-done.70.came = bf16[2,128,512]{2,1,0:T(8,128)(2,1)S(1)} collective-permute-done((bf16[2,128,512]{2,1,0:T(8,128)(2,1)S(1)}, bf16[2,128,512]{2,1,0:T(8,128)(2,1)S(1)}, u32[]{:S(2)}, u32[]{:S(2)}) %collective-permute-start.70) | collective-permute-done | bytes 262176 | tf_op jit(solution)/shard_map/ppermute | solution.py:37
  452.6 3.4 multiply_reduce_fusion
  458.2 3.3 shard_map.397
  465.2 3.6 collective-permute-done.74.cross
  478.0 7.9 %collective-permute-done.71 = bf16[256,1024]{1,0:T(8,128)(2,1)S(1)} collective-permute-done((bf16[256,1024]{1,0:T(8,128)(2,1)}, bf16[256,1024]{1,0:T(8,128)(2,1)S(1)}, u32[]{:S(2)}, u32[]{:S(2)}) %collective-permute-start.71) | collective-permute-done | bytes 524320 | tf_op jit(solution)/shard_map/ppermute | solution.py:33
  487.6 9.7 %shard_map.398 = (bf16[512,256]{1,0:T(8,128)(2,1)S(1)}, f32[1024,256]{1,0:T(8,128)S(1)}, f32[1024,256]{1,0:T(8,128)S(1)}) custom-call(bf16[512,768]{1,0:T(8,128)(2,1)S(1)} %copy-done.16, bf16[1024,768]{1,0:T(8,128)(2,1)S(1)} %pad_maximum_fusion.k_ref.v_ref, bf16[1024,768]{1,0:T(8,128)(2,1)S(1)} %pad_maximum_fusion.k_ref.v_ref, ...), custom_call_target="tpu_custom_call" | custom-call | flops 2684354560 | bytes 6291456 | tf_op jit(solution)/shard_map/pallas_call | solution.py:218
  499.7 5.7 collective-permute-done.77
  505.4 3.2 collective-permute-done.76.refs_10_
  519.8 10.1 %shard_map.399.refs_2_.refs_3_.refs_4_.refs_5_ = bf16[1024,768]{1,0:T(8,128)(2,1)S(1)} custom-call(bf16[512,768]{1,0:T(8,128)(2,1)S(1)} %copy-done.14, bf16[1024,768]{1,0:T(8,128)(2,1)S(1)} %pad_maximum_fusion.k_ref.v_ref, bf16[1024,768]{1,0:T(8,128)(2,1)S(1)} %pad_maximum_fusion.k_ref.v_ref, bf16[512,256]{1,0:T(8,128)(2,1)S(1)} %convolution_convert_fusion.12.g_ref, ...), custom_call_target="tpu_custom_call" | custom-call | flops 2684354560 | bytes 6291456 | tf_op jit(solution)/shard_map/pallas_call | solution.py:218
  531.0 3.0 collective-permute-done.78
  534.0 2.8 add_convert_fusion.1
  544.0 3.5 shard_map.402
  555.5 12.6 %collective-permute-done.86.cross = bf16[2,128,256]{2,1,0:T(8,128)(2,1)S(1)} collective-permute-done((bf16[2,128,256]{2,1,0:T(8,128)(2,1)S(1)}, bf16[2,128,256]{2,1,0:T(8,128)(2,1)S(1)}, u32[]{:S(2)}, u32[]{:S(2)}) %collective-permute-start.86) | collective-permute-done | bytes 131104 | tf_op jit(solution)/shard_map/ppermute | solution.py:33
  583.8 4.4 collective-permute-done.106.refs_2_
  589.3 4.5 collective-permute-done.99.refs_10_
  593.8 5.6 collective-permute-done.100.refs_11_
  602.2 2.8 collective-permute-done.93.refs_2_
  606.0 4.2 collective-permute-done.94.refs_3_
  614.6 6.7 shard_map.405
  626.8 3.2 collective-permute-done.123.refs_10_
  632.1 8.4 %shard_map.406 = (f32[1024,1024]{1,0:T(8,128)}, f32[1024,1]{1,0:T(8,128)}, f32[1,2176]{1,0:T(1,128)}) custom-call(s32[2]{0:T(128)} %pad_add_fusion.1.at, bf16[128,1024]{1,0:T(8,128)(2,1)} %reduce-scatter.15.cloned.1.call-done.refs_0_, bf16[128,1024]{1,0:T(8,128)(2,1)} %copy-done.151, bf16[128,1024]{1,0:T(8,128)(2,1)} %copy-done.142, ...), custom_call_target="tpu_custom_call" | custom-call | tf_op jit(solution)/shard_map/pallas_call | solution.py:389
  645.4 5.4 collective-permute-done.116.refs_1_
  652.0 6.9 collective-permute-start.129
  659.0 4.0 collective-permute-start.131
  669.9 7.6 %shard_map.407 = (f32[256,3072]{1,0:T(8,128)}, f32[256,1024]{1,0:T(8,128)}, f32[256,1]{1,0:T(8,128)}, f32[256,1]{1,0:T(8,128)}, f32[1,512]{1,0:T(1,128)}, /*index=5*/f32[1,8320]{1,0:T(1,128)}) custom-call(s32[2]{0:T(128)} %pad_add_fusion.1.at, bf16[272,512]{1,0:T(8,128)(2,1)} %reduce-scatter.17.cloned.1.call-done.refs_0_, ...), custom_call_target="tpu_custom_call" | custom-call | tf_op jit(solution)/shard_map/pallas_call | solution.py:389
  677.6 3.3 collective-permute-start.133
  687.5 5.7 fusion.3
  693.4 2.9 fusion.1
  708.0 4.4 fusion.5
  (888 shorter events, 297.9 us)
Async XLA Ops:
  7.2 73.3 %all-gather.6.cloned.1.call-start = ((), (), s32[]{:S(2)}) async-start(), calls=%async_computation.6 | async-start | bytes 1310720 | tf_op jit(solution)/shard_map/all_gather | solution.py:582
  8.4 33.7 %collective-permute-start = (bf16[128,1024]{1,0:T(8,128)(2,1)S(1)}, bf16[128,1024]{1,0:T(8,128)(2,1)S(1)}, u32[]{:S(2)}, u32[]{:S(2)}) collective-permute-start(bf16[128,1024]{1,0:T(8,128)(2,1)S(1)} %get-tuple-element.392), channel_id=1, source_target_pairs={{0,8},{4,12},{8,0},{12,4},{1,9},{5,13},{9,1},{13,5},{2,10},{6,14},... | collective-permute-start | bytes 786440 | tf_op jit(solution)/shard_map/ppermute | solution.py:37
  18.6 17.0 %collective-permute-start.6 = (bf16[272,512]{1,0:T(8,128)(2,1)S(1)}, bf16[272,512]{1,0:T(8,128)(2,1)S(1)}, u32[]{:S(2)}, u32[]{:S(2)}) collective-permute-start(bf16[272,512]{1,0:T(8,128)(2,1)S(1)} %get-tuple-element.394.refs_0_), channel_id=1, source_target_pairs={{0,2},{1,3},{2,0},{3,1},{4,6},{5,7},{6,4},{7,5},{8,10},{9,11},{10,... | collective-permute-start | bytes 835592 | tf_op jit(solution)/shard_map/ppermute | solution.py:586
  22.6 18.8 %collective-permute-start.5 = (bf16[272,512]{1,0:T(8,128)(2,1)S(1)}, bf16[272,512]{1,0:T(8,128)(2,1)S(1)}, u32[]{:S(2)}, u32[]{:S(2)}) collective-permute-start(bf16[272,512]{1,0:T(8,128)(2,1)S(1)} %get-tuple-element.394.refs_0_), channel_id=1, source_target_pairs={{0,1},{1,2},{2,3},{3,0},{4,5},{5,6},{6,7},{7,4},{8,9},{9,10},{10,1... | collective-permute-start | bytes 835592 | tf_op jit(solution)/shard_map/ppermute | solution.py:586
  23.3 22.8 %collective-permute-start.8 = (bf16[256,384]{1,0:T(8,128)(2,1)}, bf16[256,384]{1,0:T(8,128)(2,1)S(1)}, u32[]{:S(2)}, u32[]{:S(2)}) collective-permute-start(bf16[256,384]{1,0:T(8,128)(2,1)} %get-tuple-element.187), channel_id=1, source_target_pairs={{0,16},{16,0},{1,17},{17,1},{2,18},{18,2},{3,19},{19,3},{4,20},{20... | collective-permute-start | bytes 589832 | tf_op jit(solution)/shard_map/ppermute | solution.py:29
  41.4 61.8 %all-gather.8.cloned.1.call-start = ((), (), s32[]{:S(2)}) async-start(), calls=%async_computation.7 | async-start | bytes 1310720 | tf_op jit(solution)/shard_map/all_gather | solution.py:582
  42.9 16.6 %collective-permute-start.2 = (bf16[256,1024]{1,0:T(8,128)(2,1)}, bf16[256,1024]{1,0:T(8,128)(2,1)}, u32[]{:S(2)}, u32[]{:S(2)}) collective-permute-start(bf16[256,1024]{1,0:T(8,128)(2,1)} %pad_maximum_fusion.10), channel_id=1, source_target_pairs={{0,4},{4,0},{8,12},{12,8},{1,5},{5,1},{9,13},{13,9},{2,6},{6,2},{1... | collective-permute-start | bytes 1572872 | tf_op jit(solution)/shard_map/ppermute | solution.py:33
  44.7 22.2 %collective-permute-start.1 = (bf16[256,1024]{1,0:T(8,128)(2,1)}, bf16[256,1024]{1,0:T(8,128)(2,1)}, u32[]{:S(2)}, u32[]{:S(2)}) collective-permute-start(bf16[256,1024]{1,0:T(8,128)(2,1)} %pad_maximum_fusion.10), channel_id=1, source_target_pairs={{0,16},{16,0},{1,17},{17,1},{2,18},{18,2},{3,19},{19,3},{4,20},{20... | collective-permute-start | bytes 1572872 | tf_op jit(solution)/shard_map/ppermute | solution.py:29
  48.0 15.0 %collective-permute-start.11 = (bf16[256,384]{1,0:T(8,128)(2,1)}, bf16[256,384]{1,0:T(8,128)(2,1)S(1)}, u32[]{:S(2)}, u32[]{:S(2)}) collective-permute-start(bf16[256,384]{1,0:T(8,128)(2,1)} %slice.330), channel_id=1, source_target_pairs={{0,8},{4,12},{8,0},{12,4},{1,9},{5,13},{9,1},{13,5},{2,10},{6,14},... | collective-permute-start | bytes 589832 | tf_op jit(solution)/shard_map/ppermute | solution.py:37
  61.3 96.6 %all-gather.10.cloned.1.call-start = ((), (), s32[]{:S(2)}) async-start(), calls=%async_computation.8 | async-start | bytes 1392640 | tf_op jit(solution)/shard_map/all_gather | solution.py:582
  61.4 18.4 %collective-permute-start.14 = (bf16[2,128,256]{2,1,0:T(8,128)(2,1)S(1)}, bf16[2,128,256]{2,1,0:T(8,128)(2,1)S(1)}, u32[]{:S(2)}, u32[]{:S(2)}) collective-permute-start(bf16[2,128,256]{2,1,0:T(8,128)(2,1)S(1)} %get-tuple-element.194.keep), channel_id=1, source_target_pairs={{0,8},{4,12},{8,0},{12,4},{1,9},{5,13},{9,1},{13,5},{2,10},{6,14},... | collective-permute-start | bytes 393224 | tf_op jit(solution)/shard_map/ppermute | solution.py:37
  63.0 16.8 %collective-permute-start.15 = (bf16[2,128,256]{2,1,0:T(8,128)(2,1)S(1)}, bf16[2,128,256]{2,1,0:T(8,128)(2,1)S(1)}, u32[]{:S(2)}, u32[]{:S(2)}) collective-permute-start(bf16[2,128,256]{2,1,0:T(8,128)(2,1)S(1)} %collective-permute-done.13.came), channel_id=1, source_target_pairs={{0,8},{4,12},{8,0},{12,4},{1,9},{5,13},{9,1},{13,5},{2,10},{6,14},... | collective-permute-start | bytes 393224 | tf_op jit(solution)/shard_map/ppermute | solution.py:37
  82.7 25.9 %collective-permute-start.19 = (bf16[1024,512]{1,0:T(8,128)(2,1)}, bf16[1024,512]{1,0:T(8,128)(2,1)}, u32[]{:S(2)}, u32[]{:S(2)}) collective-permute-start(bf16[1024,512]{1,0:T(8,128)(2,1)} %all-gather.6.cloned.1.call-done), channel_id=1, source_target_pairs={{0,8},{4,12},{8,0},{12,4},{1,9},{5,13},{9,1},{13,5},{2,10},{6,14},... | collective-permute-start | bytes 3145736 | tf_op jit(solution)/shard_map/ppermute | solution.py:37
  94.8 70.2 %all-gather.12.cloned.1.call-start = ((), (), s32[]{:S(2)}) async-start(), calls=%async_computation.9 | async-start | bytes 1310720 | tf_op jit(solution)/shard_map/all_gather | solution.py:582
  113.2 25.9 %collective-permute-start.22 = (bf16[512,1024]{1,0:T(8,128)(2,1)}, bf16[512,1024]{1,0:T(8,128)(2,1)}, u32[]{:S(2)}, u32[]{:S(2)}) collective-permute-start(bf16[512,1024]{1,0:T(8,128)(2,1)} %all-gather.8.cloned.1.call-done), channel_id=1, source_target_pairs={{0,8},{4,12},{8,0},{12,4},{1,9},{5,13},{9,1},{13,5},{2,10},{6,14},... | collective-permute-start | bytes 3145736 | tf_op jit(solution)/shard_map/ppermute | solution.py:37
  125.6 85.7 %all-gather.14.cloned.1.call-start = ((), (), s32[]{:S(2)}) async-start(), calls=%async_computation.10 | async-start | bytes 1310720 | tf_op jit(solution)/shard_map/all_gather | solution.py:582
  164.4 29.6 %collective-permute-start.29 = (bf16[1024,384]{1,0:T(8,128)(2,1)}, bf16[1024,384]{1,0:T(8,128)(2,1)}, u32[]{:S(2)}, u32[]{:S(2)}) collective-permute-start(bf16[1024,384]{1,0:T(8,128)(2,1)} %bitcast.13), channel_id=1, source_target_pairs={{0,8},{4,12},{8,0},{12,4},{1,9},{5,13},{9,1},{13,5},{2,10},{6,14},... | collective-permute-start | bytes 2359304 | tf_op jit(solution)/shard_map/ppermute | solution.py:37
  176.8 15.1 %collective-permute-start.30 = (bf16[256,1024]{1,0:T(8,128)(2,1)}, bf16[256,1024]{1,0:T(8,128)(2,1)}, u32[]{:S(2)}, u32[]{:S(2)}) collective-permute-start(bf16[256,1024]{1,0:T(8,128)(2,1)} %multiply_convert_fusion.5), channel_id=1, source_target_pairs={{0,4},{4,0},{8,12},{12,8},{1,5},{5,1},{9,13},{13,9},{2,6},{6,2},{1... | collective-permute-start | bytes 1572872 | tf_op jit(solution)/shard_map/ppermute | solution.py:33
  177.4 275.2 %reduce-scatter.7.cloned.1.call-start = ((), (), s32[]{:S(2)}) async-start(), calls=%async_computation.11 | async-start | bytes 1310720 | tf_op jit(solution)/shard_map/reduce_scatter | solution.py:784
  177.5 19.9 %collective-permute-start.28 = (bf16[256,1024]{1,0:T(8,128)(2,1)}, bf16[256,1024]{1,0:T(8,128)(2,1)S(1)}, u32[]{:S(2)}, u32[]{:S(2)}) collective-permute-start(bf16[256,1024]{1,0:T(8,128)(2,1)} %multiply_convert_fusion.5), channel_id=1, source_target_pairs={{0,16},{16,0},{1,17},{17,1},{2,18},{18,2},{3,19},{19,3},{4,20},{20... | collective-permute-start | bytes 1572872 | tf_op jit(solution)/shard_map/ppermute | solution.py:29
  178.2 15.2 %collective-permute-start.32 = (bf16[2,128,256]{2,1,0:T(8,128)(2,1)S(1)}, bf16[2,128,256]{2,1,0:T(8,128)(2,1)S(1)}, u32[]{:S(2)}, u32[]{:S(2)}) collective-permute-start(bf16[2,128,256]{2,1,0:T(8,128)(2,1)S(1)} %get-tuple-element.412), channel_id=1, source_target_pairs={{0,4},{4,0},{8,12},{12,8},{1,5},{5,1},{9,13},{13,9},{2,6},{6,2},{1... | collective-permute-start | bytes 393224 | tf_op jit(solution)/shard_map/ppermute | solution.py:33
  192.0 19.3 %collective-permute-start.33 = (bf16[2,128,256]{2,1,0:T(8,128)(2,1)S(1)}, bf16[2,128,256]{2,1,0:T(8,128)(2,1)}, u32[]{:S(2)}, u32[]{:S(2)}) collective-permute-start(bf16[2,128,256]{2,1,0:T(8,128)(2,1)S(1)} %get-tuple-element.218.keep), channel_id=1, source_target_pairs={{0,8},{4,12},{8,0},{12,4},{1,9},{5,13},{9,1},{13,5},{2,10},{6,14},... | collective-permute-start | bytes 393224 | tf_op jit(solution)/shard_map/ppermute | solution.py:37
  193.4 17.9 %collective-permute-start.34 = (bf16[2,128,256]{2,1,0:T(8,128)(2,1)S(1)}, bf16[2,128,256]{2,1,0:T(8,128)(2,1)}, u32[]{:S(2)}, u32[]{:S(2)}) collective-permute-start(bf16[2,128,256]{2,1,0:T(8,128)(2,1)S(1)} %collective-permute-done.32.came), channel_id=1, source_target_pairs={{0,8},{4,12},{8,0},{12,4},{1,9},{5,13},{9,1},{13,5},{2,10},{6,14},... | collective-permute-start | bytes 393224 | tf_op jit(solution)/shard_map/ppermute | solution.py:37
  213.0 26.0 %collective-permute-start.38 = (bf16[1024,512]{1,0:T(8,128)(2,1)S(1)}, bf16[1024,512]{1,0:T(8,128)(2,1)S(1)}, u32[]{:S(2)}, u32[]{:S(2)}) collective-permute-start(bf16[1024,512]{1,0:T(8,128)(2,1)S(1)} %copy-done.101), channel_id=1, source_target_pairs={{0,8},{4,12},{8,0},{12,4},{1,9},{5,13},{9,1},{13,5},{2,10},{6,14},... | collective-permute-start | bytes 3145736 | tf_op jit(solution)/shard_map/ppermute | solution.py:37
  224.1 15.0 %collective-permute-start.36 = (bf16[256,1024]{1,0:T(8,128)(2,1)S(1)}, bf16[256,1024]{1,0:T(8,128)(2,1)S(1)}, u32[]{:S(2)}, u32[]{:S(2)}) collective-permute-start(bf16[256,1024]{1,0:T(8,128)(2,1)S(1)} %slice.345), channel_id=1, source_target_pairs={{0,16},{16,0},{1,17},{17,1},{2,18},{18,2},{3,19},{19,3},{4,20},{20... | collective-permute-start | bytes 1572872 | tf_op jit(solution)/shard_map/ppermute | solution.py:29
  224.2 57.8 %collective-permute-start.46 = (bf16[128,1024]{1,0:T(8,128)(2,1)S(1)}, bf16[128,1024]{1,0:T(8,128)(2,1)S(1)}, u32[]{:S(2)}, u32[]{:S(2)}) collective-permute-start(bf16[128,1024]{1,0:T(8,128)(2,1)S(1)} %get-tuple-element.390), channel_id=1, source_target_pairs={{0,8},{4,12},{8,0},{12,4},{1,9},{5,13},{9,1},{13,5},{2,10},{6,14},... | collective-permute-start | bytes 786440 | tf_op jit(solution)/shard_map/ppermute | solution.py:37
  225.8 40.9 %collective-permute-start.40 = (bf16[512,1024]{1,0:T(8,128)(2,1)S(1)}, bf16[512,1024]{1,0:T(8,128)(2,1)S(1)}, u32[]{:S(2)}, u32[]{:S(2)}) collective-permute-start(bf16[512,1024]{1,0:T(8,128)(2,1)S(1)} %copy-done.102), channel_id=1, source_target_pairs={{0,8},{4,12},{8,0},{12,4},{1,9},{5,13},{9,1},{13,5},{2,10},{6,14},... | collective-permute-start | bytes 3145736 | tf_op jit(solution)/shard_map/ppermute | solution.py:37
  242.9 23.8 %collective-permute-start.42 = (bf16[256,1024]{1,0:T(8,128)(2,1)S(1)}, bf16[256,1024]{1,0:T(8,128)(2,1)S(1)}, u32[]{:S(2)}, u32[]{:S(2)}) collective-permute-start(bf16[256,1024]{1,0:T(8,128)(2,1)S(1)} %multiply_convert_fusion.10), channel_id=1, source_target_pairs={{0,4},{4,0},{8,12},{12,8},{1,5},{5,1},{9,13},{13,9},{2,6},{6,2},{1... | collective-permute-start | bytes 1572872 | tf_op jit(solution)/shard_map/ppermute | solution.py:33
  330.3 22.4 %collective-permute-start.56 = (bf16[128,1024]{1,0:T(8,128)(2,1)S(1)}, bf16[128,1024]{1,0:T(8,128)(2,1)S(1)}, u32[]{:S(2)}, u32[]{:S(2)}) collective-permute-start(bf16[128,1024]{1,0:T(8,128)(2,1)S(1)} %slice.354), channel_id=1, source_target_pairs={{0,8},{4,12},{8,0},{12,4},{1,9},{5,13},{9,1},{13,5},{2,10},{6,14},... | collective-permute-start | bytes 786440 | tf_op jit(solution)/shard_map/ppermute | solution.py:37
  331.9 20.9 %collective-permute-start.57 = (bf16[128,1024]{1,0:T(8,128)(2,1)S(1)}, bf16[128,1024]{1,0:T(8,128)(2,1)S(1)}, u32[]{:S(2)}, u32[]{:S(2)}) collective-permute-start(bf16[128,1024]{1,0:T(8,128)(2,1)S(1)} %slice.355), channel_id=1, source_target_pairs={{0,8},{4,12},{8,0},{12,4},{1,9},{5,13},{9,1},{13,5},{2,10},{6,14},... | collective-permute-start | bytes 786440 | tf_op jit(solution)/shard_map/ppermute | solution.py:37
  337.5 29.4 %collective-permute-start.58 = (bf16[512,1024]{1,0:T(8,128)(2,1)S(1)}, bf16[512,1024]{1,0:T(8,128)(2,1)S(1)}, u32[]{:S(2)}, u32[]{:S(2)}) collective-permute-start(bf16[512,1024]{1,0:T(8,128)(2,1)S(1)} %get-tuple-element.249), channel_id=1, source_target_pairs={{0,8},{4,12},{8,0},{12,4},{1,9},{5,13},{9,1},{13,5},{2,10},{6,14},... | collective-permute-start | bytes 3145736 | tf_op jit(solution)/shard_map/ppermute | solution.py:37
  374.4 26.3 %collective-permute-start.63 = (bf16[1024,512]{1,0:T(8,128)(2,1)}, bf16[1024,512]{1,0:T(8,128)(2,1)}, u32[]{:S(2)}, u32[]{:S(2)}) collective-permute-start(bf16[1024,512]{1,0:T(8,128)(2,1)} %get-tuple-element.253), channel_id=1, source_target_pairs={{0,8},{4,12},{8,0},{12,4},{1,9},{5,13},{9,1},{13,5},{2,10},{6,14},... | collective-permute-start | bytes 3145736 | tf_op jit(solution)/shard_map/ppermute | solution.py:37
  392.0 76.8 %reduce-scatter.9.cloned.1.call-start = ((), (), s32[]{:S(2)}) async-start(), calls=%async_computation.12 | async-start | bytes 1310720 | tf_op jit(solution)/shard_map/reduce_scatter | solution.py:784
  426.1 26.5 %collective-permute-start.64 = (bf16[256,1024]{1,0:T(8,128)(2,1)}, bf16[256,1024]{1,0:T(8,128)(2,1)}, u32[]{:S(2)}, u32[]{:S(2)}) collective-permute-start(bf16[256,1024]{1,0:T(8,128)(2,1)} %slice.361), channel_id=1, source_target_pairs={{0,16},{16,0},{1,17},{17,1},{2,18},{18,2},{3,19},{19,3},{4,20},{20... | collective-permute-start | bytes 1572872 | tf_op jit(solution)/shard_map/ppermute | solution.py:29
  426.1 26.5 %collective-permute-start.69 = (bf16[1024,384]{1,0:T(8,128)(2,1)}, bf16[1024,384]{1,0:T(8,128)(2,1)}, u32[]{:S(2)}, u32[]{:S(2)}) collective-permute-start(bf16[1024,384]{1,0:T(8,128)(2,1)} %get-tuple-element.258), channel_id=1, source_target_pairs={{0,8},{4,12},{8,0},{12,4},{1,9},{5,13},{9,1},{13,5},{2,10},{6,14},... | collective-permute-start | bytes 2359304 | tf_op jit(solution)/shard_map/ppermute | solution.py:37
  428.6 24.0 %collective-permute-start.68 = (bf16[256,1024]{1,0:T(8,128)(2,1)}, bf16[256,1024]{1,0:T(8,128)(2,1)}, u32[]{:S(2)}, u32[]{:S(2)}) collective-permute-start(bf16[256,1024]{1,0:T(8,128)(2,1)} %add_convert_fusion.14), channel_id=1, source_target_pairs={{0,4},{4,0},{8,12},{12,8},{1,5},{5,1},{9,13},{13,9},{2,6},{6,2},{1... | collective-permute-start | bytes 1572872 | tf_op jit(solution)/shard_map/ppermute | solution.py:33
  431.7 102.3 %reduce-scatter.11.cloned.1.call-start = ((), (), s32[]{:S(2)}) async-start(), calls=%async_computation.13 | async-start | bytes 1392640 | tf_op jit(solution)/shard_map/reduce_scatter | solution.py:784
  431.8 20.1 %collective-permute-start.70 = (bf16[2,128,512]{2,1,0:T(8,128)(2,1)S(1)}, bf16[2,128,512]{2,1,0:T(8,128)(2,1)S(1)}, u32[]{:S(2)}, u32[]{:S(2)}) collective-permute-start(bf16[2,128,512]{2,1,0:T(8,128)(2,1)S(1)} %bitcast.249), channel_id=1, source_target_pairs={{0,8},{4,12},{8,0},{12,4},{1,9},{5,13},{9,1},{13,5},{2,10},{6,14},... | collective-permute-start | bytes 786440 | tf_op jit(solution)/shard_map/ppermute | solution.py:37
  472.4 97.0 %reduce-scatter.15.cloned.1.call-start = ((), (), s32[]{:S(2)}) async-start(), calls=%async_computation.15 | async-start | bytes 1310720 | tf_op jit(solution)/shard_map/reduce_scatter | solution.py:784
  473.5 35.2 %collective-permute-start.75 = (bf16[512,1024]{1,0:T(8,128)(2,1)}, bf16[512,1024]{1,0:T(8,128)(2,1)S(1)}, u32[]{:S(2)}, u32[]{:S(2)}) collective-permute-start(bf16[512,1024]{1,0:T(8,128)(2,1)} %copy-done.70), channel_id=1, source_target_pairs={{0,8},{4,12},{8,0},{12,4},{1,9},{5,13},{9,1},{13,5},{2,10},{6,14},... | collective-permute-start | bytes 3145736 | tf_op jit(solution)/shard_map/ppermute | solution.py:37
  475.9 29.5 %collective-permute-start.77 = (bf16[128,1024]{1,0:T(8,128)(2,1)S(1)}, bf16[128,1024]{1,0:T(8,128)(2,1)S(1)}, u32[]{:S(2)}, u32[]{:S(2)}) collective-permute-start(bf16[128,1024]{1,0:T(8,128)(2,1)S(1)} %slice.364), channel_id=1, source_target_pairs={{0,8},{4,12},{8,0},{12,4},{1,9},{5,13},{9,1},{13,5},{2,10},{6,14},... | collective-permute-start | bytes 786440 | tf_op jit(solution)/shard_map/ppermute | solution.py:37
  476.5 32.1 %collective-permute-start.76 = (bf16[128,1024]{1,0:T(8,128)(2,1)}, bf16[128,1024]{1,0:T(8,128)(2,1)S(1)}, u32[]{:S(2)}, u32[]{:S(2)}) collective-permute-start(bf16[128,1024]{1,0:T(8,128)(2,1)} %reduce-scatter.7.cloned.1.call-done.refs_8_), channel_id=1, source_target_pairs={{0,8},{4,12},{8,0},{12,4},{1,9},{5,13},{9,1},{13,5},{2,10},{6,14},... | collective-permute-start | bytes 786440 | tf_op jit(solution)/shard_map/ppermute | solution.py:37
  510.7 60.2 %reduce-scatter.13.cloned.1.call-start = ((), (), s32[]{:S(2)}) async-start(), calls=%async_computation.14 | async-start | bytes 1310720 | tf_op jit(solution)/shard_map/reduce_scatter | solution.py:784
  510.8 23.2 %collective-permute-start.78 = (bf16[1024,512]{1,0:T(8,128)(2,1)}, bf16[1024,512]{1,0:T(8,128)(2,1)}, u32[]{:S(2)}, u32[]{:S(2)}) collective-permute-start(bf16[1024,512]{1,0:T(8,128)(2,1)} %copy-done.69), channel_id=1, source_target_pairs={{0,8},{4,12},{8,0},{12,4},{1,9},{5,13},{9,1},{13,5},{2,10},{6,14},... | collective-permute-start | bytes 3145736 | tf_op jit(solution)/shard_map/ppermute | solution.py:37
  512.4 18.6 %collective-permute-start.80 = (bf16[128,1024]{1,0:T(8,128)(2,1)}, bf16[128,1024]{1,0:T(8,128)(2,1)}, u32[]{:S(2)}, u32[]{:S(2)}) collective-permute-start(bf16[128,1024]{1,0:T(8,128)(2,1)} %reduce-scatter.7.cloned.1.call-done.refs_8_), channel_id=1, source_target_pairs={{0,4},{4,0},{8,12},{12,8},{1,5},{5,1},{9,13},{13,9},{2,6},{6,2},{1... | collective-permute-start | bytes 786440 | tf_op jit(solution)/shard_map/ppermute | solution.py:33
  513.9 17.1 %collective-permute-start.79 = (bf16[256,512]{1,0:T(8,128)(2,1)}, bf16[256,512]{1,0:T(8,128)(2,1)}, u32[]{:S(2)}, u32[]{:S(2)}) collective-permute-start(bf16[256,512]{1,0:T(8,128)(2,1)} %reduce-scatter.9.cloned.1.call-done.refs_8_), channel_id=1, source_target_pairs={{0,4},{4,0},{8,12},{12,8},{1,5},{5,1},{9,13},{13,9},{2,6},{6,2},{1... | collective-permute-start | bytes 786440 | tf_op jit(solution)/shard_map/ppermute | solution.py:33
  514.5 16.5 %collective-permute-start.81 = (bf16[128,1024]{1,0:T(8,128)(2,1)}, bf16[128,1024]{1,0:T(8,128)(2,1)}, u32[]{:S(2)}, u32[]{:S(2)}) collective-permute-start(bf16[128,1024]{1,0:T(8,128)(2,1)} %copy-done.138), channel_id=1, source_target_pairs={{0,4},{4,0},{8,12},{12,8},{1,5},{5,1},{9,13},{13,9},{2,6},{6,2},{1... | collective-permute-start | bytes 786440 | tf_op jit(solution)/shard_map/ppermute | solution.py:33
  536.8 104.9 %reduce-scatter.17.cloned.1.call-start = ((), (), s32[]{:S(2)}) async-start(), calls=%async_computation.16 | async-start | bytes 1392640 | tf_op jit(solution)/shard_map/reduce_scatter | solution.py:784
  547.5 20.6 %collective-permute-start.82 = (bf16[1024,384]{1,0:T(8,128)(2,1)S(1)}, bf16[1024,384]{1,0:T(8,128)(2,1)S(1)}, u32[]{:S(2)}, u32[]{:S(2)}) collective-permute-start(bf16[1024,384]{1,0:T(8,128)(2,1)S(1)} %get-tuple-element.291), channel_id=1, source_target_pairs={{0,8},{4,12},{8,0},{12,4},{1,9},{5,13},{9,1},{13,5},{2,10},{6,14},... | collective-permute-start | bytes 2359304 | tf_op jit(solution)/shard_map/ppermute | solution.py:37
  551.9 17.4 %collective-permute-start.87 = (bf16[256,1024]{1,0:T(8,128)(2,1)}, bf16[256,1024]{1,0:T(8,128)(2,1)}, u32[]{:S(2)}, u32[]{:S(2)}) collective-permute-start(bf16[256,1024]{1,0:T(8,128)(2,1)} %add_convert_fusion.13), channel_id=1, source_target_pairs={{0,4},{4,0},{8,12},{12,8},{1,5},{5,1},{9,13},{13,9},{2,6},{6,2},{1... | collective-permute-start | bytes 1572872 | tf_op jit(solution)/shard_map/ppermute | solution.py:33
  555.3 24.7 %collective-permute-start.112 = (bf16[128,1024]{1,0:T(8,128)(2,1)}, bf16[128,1024]{1,0:T(8,128)(2,1)}, u32[]{:S(2)}, u32[]{:S(2)}) collective-permute-start(bf16[128,1024]{1,0:T(8,128)(2,1)} %reduce-scatter.7.cloned.1.call-done.refs_8_), channel_id=1, source_target_pairs={{0,16},{16,0},{1,17},{17,1},{2,18},{18,2},{3,19},{19,3},{4,20},{20... | collective-permute-start | bytes 786440 | tf_op jit(solution)/shard_map/ppermute | solution.py:29
  575.1 24.3 %collective-permute-start.89 = (bf16[2,128,1024]{2,1,0:T(8,128)(2,1)}, bf16[2,128,1024]{2,1,0:T(8,128)(2,1)}, u32[]{:S(2)}, u32[]{:S(2)}) collective-permute-start(bf16[2,128,1024]{2,1,0:T(8,128)(2,1)} %maximum_select_fusion.4), channel_id=1, source_target_pairs={{0,16},{16,0},{1,17},{17,1},{2,18},{18,2},{3,19},{19,3},{4,20},{20... | collective-permute-start | bytes 1572872 | tf_op jit(solution)/shard_map/ppermute | solution.py:29
  582.5 16.9 %collective-permute-start.100 = (bf16[256,512]{1,0:T(8,128)(2,1)}, bf16[256,512]{1,0:T(8,128)(2,1)S(1)}, u32[]{:S(2)}, u32[]{:S(2)}) collective-permute-start(bf16[256,512]{1,0:T(8,128)(2,1)} %collective-permute-done.79.refs_9_), channel_id=1, source_target_pairs={{0,8},{4,12},{8,0},{12,4},{1,9},{5,13},{9,1},{13,5},{2,10},{6,14},... | collective-permute-start | bytes 786440 | tf_op jit(solution)/shard_map/ppermute | solution.py:37
  588.2 16.9 %collective-permute-start.93 = (bf16[256,512]{1,0:T(8,128)(2,1)S(1)}, bf16[256,512]{1,0:T(8,128)(2,1)S(1)}, u32[]{:S(2)}, u32[]{:S(2)}) collective-permute-start(bf16[256,512]{1,0:T(8,128)(2,1)S(1)} %copy-done.141), channel_id=1, source_target_pairs={{0,8},{4,12},{8,0},{12,4},{1,9},{5,13},{9,1},{13,5},{2,10},{6,14},... | collective-permute-start | bytes 786440 | tf_op jit(solution)/shard_map/ppermute | solution.py:37
  589.3 15.7 %collective-permute-start.101 = (bf16[256,512]{1,0:T(8,128)(2,1)}, bf16[256,512]{1,0:T(8,128)(2,1)S(1)}, u32[]{:S(2)}, u32[]{:S(2)}) collective-permute-start(bf16[256,512]{1,0:T(8,128)(2,1)} %reduce-scatter.9.cloned.1.call-done.refs_8_), channel_id=1, source_target_pairs={{0,16},{16,0},{1,17},{17,1},{2,18},{18,2},{3,19},{19,3},{4,20},{20... | collective-permute-start | bytes 786440 | tf_op jit(solution)/shard_map/ppermute | solution.py:29
  622.3 19.5 %collective-permute-start.91 = (bf16[2,128,1024]{2,1,0:T(8,128)(2,1)S(1)}, bf16[2,128,1024]{2,1,0:T(8,128)(2,1)S(1)}, u32[]{:S(2)}, u32[]{:S(2)}) collective-permute-start(bf16[2,128,1024]{2,1,0:T(8,128)(2,1)S(1)} %maximum_select_fusion.6), channel_id=1, source_target_pairs={{0,16},{16,0},{1,17},{17,1},{2,18},{18,2},{3,19},{19,3},{4,20},{20... | collective-permute-start | bytes 1572872 | tf_op jit(solution)/shard_map/ppermute | solution.py:29
  630.0 22.0 %collective-permute-start.125 = (bf16[272,512]{1,0:T(8,128)(2,1)S(1)}, bf16[272,512]{1,0:T(8,128)(2,1)S(1)}, u32[]{:S(2)}, u32[]{:S(2)}) collective-permute-start(bf16[272,512]{1,0:T(8,128)(2,1)S(1)} %copy-done.124), channel_id=1, source_target_pairs={{0,16},{16,0},{1,17},{17,1},{2,18},{18,2},{3,19},{19,3},{4,20},{20... | collective-permute-start | bytes 835592 | tf_op jit(solution)/shard_map/ppermute | solution.py:29
  631.0 28.0 %collective-permute-start.126 = (bf16[272,512]{1,0:T(8,128)(2,1)S(1)}, bf16[272,512]{1,0:T(8,128)(2,1)S(1)}, u32[]{:S(2)}, u32[]{:S(2)}) collective-permute-start(bf16[272,512]{1,0:T(8,128)(2,1)S(1)} %copy-done.126), channel_id=1, source_target_pairs={{0,16},{16,0},{1,17},{17,1},{2,18},{18,2},{3,19},{19,3},{4,20},{20... | collective-permute-start | bytes 835592 | tf_op jit(solution)/shard_map/ppermute | solution.py:29
  631.2 27.8 %collective-permute-start.127 = (bf16[272,512]{1,0:T(8,128)(2,1)S(1)}, bf16[272,512]{1,0:T(8,128)(2,1)S(1)}, u32[]{:S(2)}, u32[]{:S(2)}) collective-permute-start(bf16[272,512]{1,0:T(8,128)(2,1)S(1)} %collective-permute-done.123.refs_10_), channel_id=1, source_target_pairs={{0,16},{16,0},{1,17},{17,1},{2,18},{18,2},{3,19},{19,3},{4,20},{20... | collective-permute-start | bytes 835592 | tf_op jit(solution)/shard_map/ppermute | solution.py:29
  644.3 22.2 %collective-permute-start.117 = (bf16[272,512]{1,0:T(8,128)(2,1)S(1)}, bf16[272,512]{1,0:T(8,128)(2,1)}, u32[]{:S(2)}, u32[]{:S(2)}) collective-permute-start(bf16[272,512]{1,0:T(8,128)(2,1)S(1)} %copy-done.127), channel_id=1, source_target_pairs={{0,8},{4,12},{8,0},{12,4},{1,9},{5,13},{9,1},{13,5},{2,10},{6,14},... | collective-permute-start | bytes 835592 | tf_op jit(solution)/shard_map/ppermute | solution.py:37
  650.9 15.6 %collective-permute-start.118 = (bf16[272,512]{1,0:T(8,128)(2,1)}, bf16[272,512]{1,0:T(8,128)(2,1)}, u32[]{:S(2)}, u32[]{:S(2)}) collective-permute-start(bf16[272,512]{1,0:T(8,128)(2,1)} %collective-permute-done.116.refs_1_), channel_id=1, source_target_pairs={{0,8},{4,12},{8,0},{12,4},{1,9},{5,13},{9,1},{13,5},{2,10},{6,14},... | collective-permute-start | bytes 835592 | tf_op jit(solution)/shard_map/ppermute | solution.py:37
  677.5 21.8 %collective-permute-start.132 = (f32[1,8320]{1,0:T(1,128)}, f32[1,8320]{1,0:T(1,128)S(1)}, u32[]{:S(2)}, u32[]{:S(2)}) collective-permute-start(f32[1,8320]{1,0:T(1,128)} %get-tuple-element.339), channel_id=1, source_target_pairs={{0,2},{1,3},{2,0},{3,1},{4,6},{5,7},{6,4},{7,5},{8,10},{9,11},{10,... | collective-permute-start | bytes 99848 | tf_op jit(solution)/shard_map/ppermute | solution.py:586
  677.6 21.8 %collective-permute-start.133 = (f32[1,8320]{1,0:T(1,128)}, f32[1,8320]{1,0:T(1,128)S(1)}, u32[]{:S(2)}, u32[]{:S(2)}) collective-permute-start(f32[1,8320]{1,0:T(1,128)} %get-tuple-element.339), channel_id=1, source_target_pairs={{0,1},{1,2},{2,3},{3,0},{4,5},{5,6},{6,7},{7,4},{8,9},{9,10},{10,1... | collective-permute-start | bytes 99848 | tf_op jit(solution)/shard_map/ppermute | solution.py:586
  680.8 18.5 %collective-permute-start.134 = (f32[1,8320]{1,0:T(1,128)}, f32[1,8320]{1,0:T(1,128)S(1)}, u32[]{:S(2)}, u32[]{:S(2)}) collective-permute-start(f32[1,8320]{1,0:T(1,128)} %get-tuple-element.339), channel_id=1, source_target_pairs={{0,3},{1,0},{2,1},{3,2},{4,7},{5,4},{6,5},{7,6},{8,11},{9,8},{10,9... | collective-permute-start | bytes 99848 | tf_op jit(solution)/shard_map/ppermute | solution.py:586
  (281 other events, 2165.8 us)
Sparse Core Ops, SparseCore 0:
  41.5 32.0 all-gather.5
  75.7 27.4 all-gather.7
  105.3 28.5 all-gather.9
  135.4 27.4 all-gather.11
  177.5 33.7 all-gather.13
  392.1 31.3 reduce-scatter.6
  431.8 30.4 reduce-scatter.8
  472.5 32.2 reduce-scatter.10
  510.9 31.2 reduce-scatter.14
  544.9 25.7 reduce-scatter.12
  580.1 31.4 reduce-scatter.16

commit v5 on v4

--- a/solution.py
+++ b/solution.py
@@ -837,7 +837,7 @@
             spread(scatter_rows(fold(*halves(found.down))), True),
         ]
 
-    inputs = own_rows(tokens)
+    inputs, out_grads = sync(own_rows(tokens), own_rows(cotangent))
     of0, of1 = types.SimpleNamespace(), types.SimpleNamespace()
 
     def total(value):
@@ -855,7 +855,7 @@
     masters = (w_qkv[0], w_out[0], w_up[0], w_down[0])
     gain_masters = (gain_attn, gain_mlp)
     state = types.SimpleNamespace(
-        out_grads=own_rows(cotangent),
+        out_grads=out_grads,
         weight_totals=lanes([total(master * master) for master in masters + gain_masters], 2),
     )
     if even:
@@ -895,9 +895,7 @@
                 value, far = sync(value, weights[1].down[1])
                 weights[1].down = weights[1].down[0], far
             elif point == LAST:
-                value, state.out_grads, state.weight_totals = sync(
-                    value, state.out_grads, state.weight_totals
-                )
+                value, state.weight_totals = sync(value, state.weight_totals)
             return value
 
         def hook_backward1(point, value, *grads):
@@ -991,13 +989,26 @@
     if even:
         qkv_near, qkv_came = halves(of0.qkv)
         packed0 = pack(qkv_near, qkv_came, *of0.out, of0.gains)
-        packed0, of0.up, of0.down, *rest = sync(
-            packed0, of0.up, of0.down, *of1.packed, *of1.up, hidden0, hidden1, in_grads0, in_grads1
+        packed0, of0.up, of0.down = sync(packed0, of0.up, of0.down)
+        packed0 = scatter_rows(packed0)
+        of0.down, of0.up = spread_start(of0.down, True), spread_start(of0.up, False)
+        down_hop, up_hop, *rest = sync(
+            of0.down[1],
+            of0.up[1],
+            *of1.packed,
+            *of1.up,
+            hidden0,
+            hidden1,
+            in_grads0,
+            in_grads1,
         )
         of1.packed, of1.up = rest[:2], rest[2:4]
         hidden0, hidden1, in_grads0, in_grads1 = rest[4:]
-        packed0 = scatter_rows(packed0)
-        near0 = [None, spread(of0.up, False), spread(of0.down, True)]
+        near0 = [
+            None,
+            spread_end((of0.up[0], up_hop), False),
+            spread_end((of0.down[0], down_hop), True),
+        ]
         near1 = [spread_end(of1.packed, False), spread_end(of1.up, False), of1.down]
     else:
         near1, near0 = reduce_plain(of1), reduce_plain(of0)

time: 729 us -> 726 us (level)
    ppermute x36, waiting for transfers between devices: 90.7 us -> 103 us  [swap_y(): return lax.ppermute(value, CTX, [(i, i ^ 2) for i in range(4)])]
    ppermute x28, waiting for transfers between devices: 126 us -> 119 us  [swap_x(): return lax.ppermute(value, CTX, [(i, i ^ 1) for i in range(4)])]
    unnamed x407 -> x390, local copies, waits for them, and re-layouts: 42.5 us -> 45.2 us
  transfers between devices with their start and end apart: 146 -> 146, of which waited for: 50 -> 47; matrix products, arithmetic and copies ran while one was open for 23% -> 22% of each run, Pallas kernels for 16% -> 16%
where the time goes in v5:
time: 726 us; the launch traced here: 716 us
  waiting for transfers between devices  243 us (33%)
  Pallas kernels  126 us (17%)
  starting transfers between devices  98 us (13%)
  other arithmetic  82.2 us (11%)
  matrix products  70.8 us (10%)
  local copies, waits for them, and re-layouts  67.7 us (9%)
  between operations  28.5 us (4%)
    ppermute x28, waiting for transfers between devices, swap_x(): return lax.ppermute(value, CTX, [(i, i ^ 1) for i in range(4)])  119 us
    ppermute x36, waiting for transfers between devices, swap_y(): return lax.ppermute(value, CTX, [(i, i ^ 2) for i in range(4)])  103 us
    unnamed x390, local copies, waits for them, and re-layouts  45.2 us
    pallas_call x4, Pallas kernels, attention_backward(): pl.pallas_call(functools.partial(attention_back_kernel, scale=scale, last...  40 us
    ppermute x36, starting transfers between devices, swap_y(): return lax.ppermute(value, CTX, [(i, i ^ 2) for i in range(4)])  38.9 us
    dot_general x24, matrix products, dot(): return jnp.dot(left, right, preferred_element_type=f32)  36.3 us
    dot_general x24, matrix products, times_transposed(): lax.dot_general(left, right, (((1,), (1,)), ((), ())), preferred_element_...  34.5 us
    ppermute x28, starting transfers between devices, swap_x(): return lax.ppermute(value, CTX, [(i, i ^ 1) for i in range(4)])  31.3 us
  transfers between devices with their start and end apart: 146, of which 47 were waited for; matrix products, arithmetic and copies ran while one was open for 22% of the time, Pallas kernels for 16%

profile of v5, /device:TPU:0, one launch (start us, length us, event | category | flops | bytes accessed | tf_op | source)
XLA Modules:
  0.0 715.9 jit_solution(6497745544605854400)
XLA Ops:
  8.4 3.0 collective-permute-start.1
  11.4 3.7 shard_map.378
  26.6 3.4 collective-permute-done.6.refs_1_
  30.1 11.2 %collective-permute-done.7.refs_2_ = bf16[272,512]{1,0:T(8,128)(2,1)S(1)} collective-permute-done((bf16[272,512]{1,0:T(8,128)(2,1)S(1)}, bf16[272,512]{1,0:T(8,128)(2,1)S(1)}, u32[]{:S(2)}, u32[]{:S(2)}) %collective-permute-start.7) | collective-permute-done | bytes 278560 | tf_op jit(solution)/shard_map/ppermute | solution.py:586
  53.4 8.4 %collective-permute-done.14.came = bf16[2,128,256]{2,1,0:T(8,128)(2,1)} collective-permute-done((bf16[2,128,256]{2,1,0:T(8,128)(2,1)S(1)}, bf16[2,128,256]{2,1,0:T(8,128)(2,1)}, u32[]{:S(2)}, u32[]{:S(2)}) %collective-permute-start.14) | collective-permute-done | bytes 131104 | tf_op jit(solution)/shard_map/ppermute | solution.py:33
  66.3 3.6 collective-permute-done.12.refs_7_
  76.4 6.8 shard_map.380
  94.1 6.7 shard_map.383
  102.6 4.3 collective-permute-done.19
  106.9 8.7 %collective-permute-done.20 = bf16[1024,512]{1,0:T(8,128)(2,1)} collective-permute-done((bf16[1024,512]{1,0:T(8,128)(2,1)}, bf16[1024,512]{1,0:T(8,128)(2,1)}, u32[]{:S(2)}, u32[]{:S(2)}) %collective-permute-start.20) | collective-permute-done | bytes 1048608 | tf_op jit(solution)/shard_map/ppermute | solution.py:37
  120.5 12.1 %collective-permute-done.25 = bf16[256,1024]{1,0:T(8,128)(2,1)} collective-permute-done((bf16[256,1024]{1,0:T(8,128)(2,1)}, bf16[256,1024]{1,0:T(8,128)(2,1)}, u32[]{:S(2)}, u32[]{:S(2)}) %collective-permute-start.25) | collective-permute-done | bytes 524320 | tf_op jit(solution)/shard_map/ppermute | solution.py:33
  136.7 3.3 multiply_convert_fusion.7
  140.0 6.1 collective-permute-done.23
  146.1 2.9 multiply_convert_fusion.6
  154.0 3.1 multiply_convert_fusion.9
  157.1 2.9 multiply_convert_fusion.8
  160.0 3.3 fusion.112
  165.6 2.9 add_convert_fusion.11
  171.8 7.9 %collective-permute-done.28 = bf16[256,1024]{1,0:T(8,128)(2,1)} collective-permute-done((bf16[256,1024]{1,0:T(8,128)(2,1)}, bf16[256,1024]{1,0:T(8,128)(2,1)}, u32[]{:S(2)}, u32[]{:S(2)}) %collective-permute-start.28) | collective-permute-done | bytes 524320 | tf_op jit(solution)/shard_map/ppermute | solution.py:33
  186.7 12.3 %collective-permute-done.31 = bf16[256,1024]{1,0:T(8,128)(2,1)} collective-permute-done((bf16[256,1024]{1,0:T(8,128)(2,1)}, bf16[256,1024]{1,0:T(8,128)(2,1)}, u32[]{:S(2)}, u32[]{:S(2)}) %collective-permute-start.31) | collective-permute-done | bytes 524320 | tf_op jit(solution)/shard_map/ppermute | solution.py:33
  208.8 6.7 shard_map.385
  222.0 7.1 shard_map.388
  234.6 9.9 %collective-permute-done.39 = bf16[1024,512]{1,0:T(8,128)(2,1)S(1)} collective-permute-done((bf16[1024,512]{1,0:T(8,128)(2,1)S(1)}, bf16[1024,512]{1,0:T(8,128)(2,1)S(1)}, u32[]{:S(2)}, u32[]{:S(2)}) %collective-permute-start.39) | collective-permute-done | bytes 1048608 | tf_op jit(solution)/shard_map/ppermute | solution.py:37
  252.2 14.3 %collective-permute-done.41 = bf16[512,1024]{1,0:T(8,128)(2,1)S(1)} collective-permute-done((bf16[512,1024]{1,0:T(8,128)(2,1)S(1)}, bf16[512,1024]{1,0:T(8,128)(2,1)S(1)}, u32[]{:S(2)}, u32[]{:S(2)}) %collective-permute-start.41) | collective-permute-done | bytes 1048608 | tf_op jit(solution)/shard_map/ppermute | solution.py:37
  277.9 4.4 fusion.87.refs_17_
  282.3 5.7 collective-permute-done.46
  291.3 11.8 %collective-permute-done.49 = bf16[256,1024]{1,0:T(8,128)(2,1)S(1)} collective-permute-done((bf16[256,1024]{1,0:T(8,128)(2,1)S(1)}, bf16[256,1024]{1,0:T(8,128)(2,1)S(1)}, u32[]{:S(2)}, u32[]{:S(2)}) %collective-permute-start.49) | collective-permute-done | bytes 524320 | tf_op jit(solution)/shard_map/ppermute | solution.py:33
  313.3 2.7 shard_map.389
  316.1 9.0 %collective-permute-done.52 = bf16[256,1024]{1,0:T(8,128)(2,1)S(1)} collective-permute-done((bf16[256,1024]{1,0:T(8,128)(2,1)S(1)}, bf16[256,1024]{1,0:T(8,128)(2,1)S(1)}, u32[]{:S(2)}, u32[]{:S(2)}) %collective-permute-start.52) | collective-permute-done | bytes 524320 | tf_op jit(solution)/shard_map/ppermute | solution.py:33
  332.1 4.0 shard_map.390
  338.6 3.2 collective-permute-done.53
  342.3 9.8 %shard_map.391 = (bf16[512,256]{1,0:T(8,128)(2,1)S(1)}, f32[1024,256]{1,0:T(8,128)S(1)}, f32[1024,256]{1,0:T(8,128)S(1)}) custom-call(bf16[512,768]{1,0:T(8,128)(2,1)S(1)} %copy-done.18, bf16[1024,768]{1,0:T(8,128)(2,1)S(1)} %copy-done.4, bf16[1024,768]{1,0:T(8,128)(2,1)S(1)} %copy-done.4, bf16[512,256]{1,0:T(8,128)(2,1)S(1)} %convolution_convert_fusion.15.g_ref, ...), custom_call_target="tpu_custom_call" | custom-call | flops 2684354560 | bytes 6291456 | tf_op jit(solution)/shard_map/pallas_call | solution.py:218
  353.8 10.4 %shard_map.392.refs_2_.refs_3_.refs_4_.refs_5_ = bf16[1024,768]{1,0:T(8,128)(2,1)S(1)} custom-call(bf16[512,768]{1,0:T(8,128)(2,1)S(1)} %convolution_convert_fusion.8.q_ref, bf16[1024,768]{1,0:T(8,128)(2,1)S(1)} %copy-done.4, bf16[1024,768]{1,0:T(8,128)(2,1)S(1)} %copy-done.4, bf16[512,256]{1,0:T(8,128)(2,1)S(1)} %convolution_convert_fusion.14.g_ref, ...), custom_call_target="tpu_custom_call" | custom-call | flops 2684354560 | bytes 6291456 | tf_op jit(solution)/shard_map/pallas_call | solution.py:218
  375.4 9.4 %collective-permute-done.61 = bf16[256,1024]{1,0:T(8,128)(2,1)} collective-permute-done((bf16[256,1024]{1,0:T(8,128)(2,1)}, bf16[256,1024]{1,0:T(8,128)(2,1)}, u32[]{:S(2)}, u32[]{:S(2)}) %collective-permute-start.61) | collective-permute-done | bytes 524320 | tf_op jit(solution)/shard_map/ppermute | solution.py:33
  394.3 4.2 shard_map.394
  400.1 4.1 collective-permute-done.65
  437.6 2.7 shard_map.395
  442.3 9.1 %collective-permute-done.70.came = bf16[2,128,512]{2,1,0:T(8,128)(2,1)S(1)} collective-permute-done((bf16[2,128,512]{2,1,0:T(8,128)(2,1)S(1)}, bf16[2,128,512]{2,1,0:T(8,128)(2,1)S(1)}, u32[]{:S(2)}, u32[]{:S(2)}) %collective-permute-start.70) | collective-permute-done | bytes 262176 | tf_op jit(solution)/shard_map/ppermute | solution.py:37
  452.2 3.4 multiply_reduce_fusion
  457.8 3.3 shard_map.397
  464.8 3.6 collective-permute-done.74.cross
  477.3 7.9 %collective-permute-done.71 = bf16[256,1024]{1,0:T(8,128)(2,1)S(1)} collective-permute-done((bf16[256,1024]{1,0:T(8,128)(2,1)}, bf16[256,1024]{1,0:T(8,128)(2,1)S(1)}, u32[]{:S(2)}, u32[]{:S(2)}) %collective-permute-start.71) | collective-permute-done | bytes 524320 | tf_op jit(solution)/shard_map/ppermute | solution.py:33
  486.9 9.7 %shard_map.398 = (bf16[512,256]{1,0:T(8,128)(2,1)S(1)}, f32[1024,256]{1,0:T(8,128)S(1)}, f32[1024,256]{1,0:T(8,128)S(1)}) custom-call(bf16[512,768]{1,0:T(8,128)(2,1)S(1)} %copy-done.16, bf16[1024,768]{1,0:T(8,128)(2,1)S(1)} %pad_maximum_fusion.k_ref.v_ref, bf16[1024,768]{1,0:T(8,128)(2,1)S(1)} %pad_maximum_fusion.k_ref.v_ref, ...), custom_call_target="tpu_custom_call" | custom-call | flops 2684354560 | bytes 6291456 | tf_op jit(solution)/shard_map/pallas_call | solution.py:218
  499.1 5.7 collective-permute-done.77
  504.7 3.2 collective-permute-done.76.refs_10_
  519.8 10.1 %shard_map.399.refs_2_.refs_3_.refs_4_.refs_5_ = bf16[1024,768]{1,0:T(8,128)(2,1)S(1)} custom-call(bf16[512,768]{1,0:T(8,128)(2,1)S(1)} %copy-done.14, bf16[1024,768]{1,0:T(8,128)(2,1)S(1)} %pad_maximum_fusion.k_ref.v_ref, bf16[1024,768]{1,0:T(8,128)(2,1)S(1)} %pad_maximum_fusion.k_ref.v_ref, bf16[512,256]{1,0:T(8,128)(2,1)S(1)} %convolution_convert_fusion.12.g_ref, ...), custom_call_target="tpu_custom_call" | custom-call | flops 2684354560 | bytes 6291456 | tf_op jit(solution)/shard_map/pallas_call | solution.py:218
  540.3 3.5 shard_map.402
  547.1 6.1 collective-permute-done.84.came
  557.3 11.4 %collective-permute-done.86.cross = bf16[2,128,256]{2,1,0:T(8,128)(2,1)S(1)} collective-permute-done((bf16[2,128,256]{2,1,0:T(8,128)(2,1)S(1)}, bf16[2,128,256]{2,1,0:T(8,128)(2,1)S(1)}, u32[]{:S(2)}, u32[]{:S(2)}) %collective-permute-start.86) | collective-permute-done | bytes 131104 | tf_op jit(solution)/shard_map/ppermute | solution.py:33
  575.1 4.9 collective-permute-done.89.refs_2_
  587.4 3.6 collective-permute-done.100.refs_10_
  592.1 4.4 collective-permute-done.101.refs_11_
  598.4 3.7 collective-permute-done.95.refs_3_
  603.8 2.7 collective-permute-done.92
  609.4 6.6 shard_map.405
  617.1 3.8 collective-permute-done.107.refs_3_
  624.6 8.4 %shard_map.406 = (f32[1024,1024]{1,0:T(8,128)}, f32[1024,1]{1,0:T(8,128)}, f32[1,2176]{1,0:T(1,128)}) custom-call(s32[2]{0:T(128)} %pad_add_fusion.1.at, bf16[128,1024]{1,0:T(8,128)(2,1)} %reduce-scatter.15.cloned.1.call-done.refs_0_, bf16[128,1024]{1,0:T(8,128)(2,1)} %copy-done.150, bf16[128,1024]{1,0:T(8,128)(2,1)} %copy-done.138, ...), custom_call_target="tpu_custom_call" | custom-call | tf_op jit(solution)/shard_map/pallas_call | solution.py:389
  633.7 4.5 collective-permute-start.129
  651.8 5.8 collective-permute-done.117.refs_2_
  657.6 5.5 collective-permute-done.118.refs_3_
  666.1 7.7 %shard_map.407 = (f32[256,3072]{1,0:T(8,128)}, f32[256,1024]{1,0:T(8,128)}, f32[256,1]{1,0:T(8,128)}, f32[256,1]{1,0:T(8,128)}, f32[1,512]{1,0:T(1,128)}, /*index=5*/f32[1,8320]{1,0:T(1,128)}) custom-call(s32[2]{0:T(128)} %pad_add_fusion.1.at, bf16[272,512]{1,0:T(8,128)(2,1)} %reduce-scatter.17.cloned.1.call-done.refs_0_, ...), custom_call_target="tpu_custom_call" | custom-call | tf_op jit(solution)/shard_map/pallas_call | solution.py:389
  684.2 5.7 fusion.3
  690.0 2.9 fusion.1
  704.7 4.4 fusion.5
  (871 shorter events, 299.6 us)
Async XLA Ops:
  7.2 78.0 %all-gather.6.cloned.1.call-start = ((), (), s32[]{:S(2)}) async-start(), calls=%async_computation.6 | async-start | bytes 1310720 | tf_op jit(solution)/shard_map/all_gather | solution.py:582
  8.4 33.4 %collective-permute-start.1 = (bf16[128,1024]{1,0:T(8,128)(2,1)S(1)}, bf16[128,1024]{1,0:T(8,128)(2,1)S(1)}, u32[]{:S(2)}, u32[]{:S(2)}) collective-permute-start(bf16[128,1024]{1,0:T(8,128)(2,1)S(1)} %get-tuple-element.396), channel_id=1, source_target_pairs={{0,8},{4,12},{8,0},{12,4},{1,9},{5,13},{9,1},{13,5},{2,10},{6,14},... | collective-permute-start | bytes 786440 | tf_op jit(solution)/shard_map/ppermute | solution.py:37
  20.2 21.1 %collective-permute-start.7 = (bf16[272,512]{1,0:T(8,128)(2,1)S(1)}, bf16[272,512]{1,0:T(8,128)(2,1)S(1)}, u32[]{:S(2)}, u32[]{:S(2)}) collective-permute-start(bf16[272,512]{1,0:T(8,128)(2,1)S(1)} %get-tuple-element.400.refs_0_), channel_id=1, source_target_pairs={{0,2},{1,3},{2,0},{3,1},{4,6},{5,7},{6,4},{7,5},{8,10},{9,11},{10,... | collective-permute-start | bytes 835592 | tf_op jit(solution)/shard_map/ppermute | solution.py:586
  22.8 18.5 %collective-permute-start.8 = (bf16[272,512]{1,0:T(8,128)(2,1)S(1)}, bf16[272,512]{1,0:T(8,128)(2,1)S(1)}, u32[]{:S(2)}, u32[]{:S(2)}) collective-permute-start(bf16[272,512]{1,0:T(8,128)(2,1)S(1)} %get-tuple-element.400.refs_0_), channel_id=1, source_target_pairs={{0,3},{1,0},{2,1},{3,2},{4,7},{5,4},{6,5},{7,6},{8,11},{9,8},{10,9... | collective-permute-start | bytes 835592 | tf_op jit(solution)/shard_map/ppermute | solution.py:586
  25.2 17.3 %collective-permute-start = (bf16[128,1024]{1,0:T(8,128)(2,1)S(1)}, bf16[128,1024]{1,0:T(8,128)(2,1)}, u32[]{:S(2)}, u32[]{:S(2)}) collective-permute-start(bf16[128,1024]{1,0:T(8,128)(2,1)S(1)} %get-tuple-element.398), channel_id=1, source_target_pairs={{0,8},{4,12},{8,0},{12,4},{1,9},{5,13},{9,1},{13,5},{2,10},{6,14},... | collective-permute-start | bytes 786440 | tf_op jit(solution)/shard_map/ppermute | solution.py:37
  30.1 18.1 %collective-permute-start.9 = (bf16[256,384]{1,0:T(8,128)(2,1)}, bf16[256,384]{1,0:T(8,128)(2,1)S(1)}, u32[]{:S(2)}, u32[]{:S(2)}) collective-permute-start(bf16[256,384]{1,0:T(8,128)(2,1)} %get-tuple-element.191), channel_id=1, source_target_pairs={{0,16},{16,0},{1,17},{17,1},{2,18},{18,2},{3,19},{19,3},{4,20},{20... | collective-permute-start | bytes 589832 | tf_op jit(solution)/shard_map/ppermute | solution.py:29
  41.3 65.6 %all-gather.8.cloned.1.call-start = ((), (), s32[]{:S(2)}) async-start(), calls=%async_computation.7 | async-start | bytes 1310720 | tf_op jit(solution)/shard_map/all_gather | solution.py:582
  44.4 27.8 %collective-permute-start.2 = (bf16[256,1024]{1,0:T(8,128)(2,1)}, bf16[256,1024]{1,0:T(8,128)(2,1)}, u32[]{:S(2)}, u32[]{:S(2)}) collective-permute-start(bf16[256,1024]{1,0:T(8,128)(2,1)} %pad_maximum_fusion.9), channel_id=1, source_target_pairs={{0,16},{16,0},{1,17},{17,1},{2,18},{18,2},{3,19},{19,3},{4,20},{20... | collective-permute-start | bytes 1572872 | tf_op jit(solution)/shard_map/ppermute | solution.py:29
  44.9 25.7 %collective-permute-start.3 = (bf16[256,1024]{1,0:T(8,128)(2,1)}, bf16[256,1024]{1,0:T(8,128)(2,1)}, u32[]{:S(2)}, u32[]{:S(2)}) collective-permute-start(bf16[256,1024]{1,0:T(8,128)(2,1)} %pad_maximum_fusion.9), channel_id=1, source_target_pairs={{0,4},{4,0},{8,12},{12,8},{1,5},{5,1},{9,13},{13,9},{2,6},{6,2},{1... | collective-permute-start | bytes 1572872 | tf_op jit(solution)/shard_map/ppermute | solution.py:33
  64.1 100.9 %all-gather.10.cloned.1.call-start = ((), (), s32[]{:S(2)}) async-start(), calls=%async_computation.8 | async-start | bytes 1392640 | tf_op jit(solution)/shard_map/all_gather | solution.py:582
  64.2 19.6 %collective-permute-start.15 = (bf16[2,128,256]{2,1,0:T(8,128)(2,1)}, bf16[2,128,256]{2,1,0:T(8,128)(2,1)S(1)}, u32[]{:S(2)}, u32[]{:S(2)}) collective-permute-start(bf16[2,128,256]{2,1,0:T(8,128)(2,1)} %get-tuple-element.198.keep), channel_id=1, source_target_pairs={{0,8},{4,12},{8,0},{12,4},{1,9},{5,13},{9,1},{13,5},{2,10},{6,14},... | collective-permute-start | bytes 393224 | tf_op jit(solution)/shard_map/ppermute | solution.py:37
  65.8 18.7 %collective-permute-start.16 = (bf16[2,128,256]{2,1,0:T(8,128)(2,1)}, bf16[2,128,256]{2,1,0:T(8,128)(2,1)S(1)}, u32[]{:S(2)}, u32[]{:S(2)}) collective-permute-start(bf16[2,128,256]{2,1,0:T(8,128)(2,1)} %collective-permute-done.14.came), channel_id=1, source_target_pairs={{0,8},{4,12},{8,0},{12,4},{1,9},{5,13},{9,1},{13,5},{2,10},{6,14},... | collective-permute-start | bytes 393224 | tf_op jit(solution)/shard_map/ppermute | solution.py:37
  89.8 25.8 %collective-permute-start.20 = (bf16[1024,512]{1,0:T(8,128)(2,1)}, bf16[1024,512]{1,0:T(8,128)(2,1)}, u32[]{:S(2)}, u32[]{:S(2)}) collective-permute-start(bf16[1024,512]{1,0:T(8,128)(2,1)} %all-gather.6.cloned.1.call-done), channel_id=1, source_target_pairs={{0,8},{4,12},{8,0},{12,4},{1,9},{5,13},{9,1},{13,5},{2,10},{6,14},... | collective-permute-start | bytes 3145736 | tf_op jit(solution)/shard_map/ppermute | solution.py:37
  102.5 69.3 %all-gather.12.cloned.1.call-start = ((), (), s32[]{:S(2)}) async-start(), calls=%async_computation.9 | async-start | bytes 1310720 | tf_op jit(solution)/shard_map/all_gather | solution.py:582
  120.2 25.9 %collective-permute-start.23 = (bf16[512,1024]{1,0:T(8,128)(2,1)}, bf16[512,1024]{1,0:T(8,128)(2,1)}, u32[]{:S(2)}, u32[]{:S(2)}) collective-permute-start(bf16[512,1024]{1,0:T(8,128)(2,1)} %all-gather.8.cloned.1.call-done), channel_id=1, source_target_pairs={{0,8},{4,12},{8,0},{12,4},{1,9},{5,13},{9,1},{13,5},{2,10},{6,14},... | collective-permute-start | bytes 3145736 | tf_op jit(solution)/shard_map/ppermute | solution.py:37
  132.6 84.1 %all-gather.14.cloned.1.call-start = ((), (), s32[]{:S(2)}) async-start(), calls=%async_computation.10 | async-start | bytes 1310720 | tf_op jit(solution)/shard_map/all_gather | solution.py:582
  165.0 14.6 %collective-permute-start.28 = (bf16[256,1024]{1,0:T(8,128)(2,1)}, bf16[256,1024]{1,0:T(8,128)(2,1)}, u32[]{:S(2)}, u32[]{:S(2)}) collective-permute-start(bf16[256,1024]{1,0:T(8,128)(2,1)} %add_convert_fusion.20), channel_id=1, source_target_pairs={{0,4},{4,0},{8,12},{12,8},{1,5},{5,1},{9,13},{13,9},{2,6},{6,2},{1... | collective-permute-start | bytes 1572872 | tf_op jit(solution)/shard_map/ppermute | solution.py:33
  171.5 29.6 %collective-permute-start.30 = (bf16[1024,384]{1,0:T(8,128)(2,1)}, bf16[1024,384]{1,0:T(8,128)(2,1)}, u32[]{:S(2)}, u32[]{:S(2)}) collective-permute-start(bf16[1024,384]{1,0:T(8,128)(2,1)} %bitcast.15), channel_id=1, source_target_pairs={{0,8},{4,12},{8,0},{12,4},{1,9},{5,13},{9,1},{13,5},{2,10},{6,14},... | collective-permute-start | bytes 2359304 | tf_op jit(solution)/shard_map/ppermute | solution.py:37
  183.9 15.1 %collective-permute-start.31 = (bf16[256,1024]{1,0:T(8,128)(2,1)}, bf16[256,1024]{1,0:T(8,128)(2,1)}, u32[]{:S(2)}, u32[]{:S(2)}) collective-permute-start(bf16[256,1024]{1,0:T(8,128)(2,1)} %multiply_convert_fusion.5), channel_id=1, source_target_pairs={{0,4},{4,0},{8,12},{12,8},{1,5},{5,1},{9,13},{13,9},{2,6},{6,2},{1... | collective-permute-start | bytes 1572872 | tf_op jit(solution)/shard_map/ppermute | solution.py:33
  184.5 267.6 %reduce-scatter.7.cloned.1.call-start = ((), (), s32[]{:S(2)}) async-start(), calls=%async_computation.11 | async-start | bytes 1310720 | tf_op jit(solution)/shard_map/reduce_scatter | solution.py:784
  184.5 19.9 %collective-permute-start.29 = (bf16[256,1024]{1,0:T(8,128)(2,1)}, bf16[256,1024]{1,0:T(8,128)(2,1)S(1)}, u32[]{:S(2)}, u32[]{:S(2)}) collective-permute-start(bf16[256,1024]{1,0:T(8,128)(2,1)} %multiply_convert_fusion.5), channel_id=1, source_target_pairs={{0,16},{16,0},{1,17},{17,1},{2,18},{18,2},{3,19},{19,3},{4,20},{20... | collective-permute-start | bytes 1572872 | tf_op jit(solution)/shard_map/ppermute | solution.py:29
  185.2 15.2 %collective-permute-start.33 = (bf16[2,128,256]{2,1,0:T(8,128)(2,1)S(1)}, bf16[2,128,256]{2,1,0:T(8,128)(2,1)S(1)}, u32[]{:S(2)}, u32[]{:S(2)}) collective-permute-start(bf16[2,128,256]{2,1,0:T(8,128)(2,1)S(1)} %get-tuple-element.418), channel_id=1, source_target_pairs={{0,4},{4,0},{8,12},{12,8},{1,5},{5,1},{9,13},{13,9},{2,6},{6,2},{1... | collective-permute-start | bytes 393224 | tf_op jit(solution)/shard_map/ppermute | solution.py:33
  199.0 17.7 %collective-permute-start.34 = (bf16[2,128,256]{2,1,0:T(8,128)(2,1)S(1)}, bf16[2,128,256]{2,1,0:T(8,128)(2,1)}, u32[]{:S(2)}, u32[]{:S(2)}) collective-permute-start(bf16[2,128,256]{2,1,0:T(8,128)(2,1)S(1)} %get-tuple-element.222.keep), channel_id=1, source_target_pairs={{0,8},{4,12},{8,0},{12,4},{1,9},{5,13},{9,1},{13,5},{2,10},{6,14},... | collective-permute-start | bytes 393224 | tf_op jit(solution)/shard_map/ppermute | solution.py:37
  200.4 16.3 %collective-permute-start.35 = (bf16[2,128,256]{2,1,0:T(8,128)(2,1)S(1)}, bf16[2,128,256]{2,1,0:T(8,128)(2,1)}, u32[]{:S(2)}, u32[]{:S(2)}) collective-permute-start(bf16[2,128,256]{2,1,0:T(8,128)(2,1)S(1)} %collective-permute-done.33.came), channel_id=1, source_target_pairs={{0,8},{4,12},{8,0},{12,4},{1,9},{5,13},{9,1},{13,5},{2,10},{6,14},... | collective-permute-start | bytes 393224 | tf_op jit(solution)/shard_map/ppermute | solution.py:37
  218.4 26.0 %collective-permute-start.39 = (bf16[1024,512]{1,0:T(8,128)(2,1)S(1)}, bf16[1024,512]{1,0:T(8,128)(2,1)S(1)}, u32[]{:S(2)}, u32[]{:S(2)}) collective-permute-start(bf16[1024,512]{1,0:T(8,128)(2,1)S(1)} %copy-done.104), channel_id=1, source_target_pairs={{0,8},{4,12},{8,0},{12,4},{1,9},{5,13},{9,1},{13,5},{2,10},{6,14},... | collective-permute-start | bytes 3145736 | tf_op jit(solution)/shard_map/ppermute | solution.py:37
  229.7 14.8 %collective-permute-start.37 = (bf16[256,1024]{1,0:T(8,128)(2,1)S(1)}, bf16[256,1024]{1,0:T(8,128)(2,1)S(1)}, u32[]{:S(2)}, u32[]{:S(2)}) collective-permute-start(bf16[256,1024]{1,0:T(8,128)(2,1)S(1)} %slice.345), channel_id=1, source_target_pairs={{0,16},{16,0},{1,17},{17,1},{2,18},{18,2},{3,19},{19,3},{4,20},{20... | collective-permute-start | bytes 1572872 | tf_op jit(solution)/shard_map/ppermute | solution.py:29
  230.4 36.1 %collective-permute-start.41 = (bf16[512,1024]{1,0:T(8,128)(2,1)S(1)}, bf16[512,1024]{1,0:T(8,128)(2,1)S(1)}, u32[]{:S(2)}, u32[]{:S(2)}) collective-permute-start(bf16[512,1024]{1,0:T(8,128)(2,1)S(1)} %copy-done.105), channel_id=1, source_target_pairs={{0,8},{4,12},{8,0},{12,4},{1,9},{5,13},{9,1},{13,5},{2,10},{6,14},... | collective-permute-start | bytes 3145736 | tf_op jit(solution)/shard_map/ppermute | solution.py:37
  247.8 18.7 %collective-permute-start.43 = (bf16[256,1024]{1,0:T(8,128)(2,1)S(1)}, bf16[256,1024]{1,0:T(8,128)(2,1)S(1)}, u32[]{:S(2)}, u32[]{:S(2)}) collective-permute-start(bf16[256,1024]{1,0:T(8,128)(2,1)S(1)} %multiply_convert_fusion.10), channel_id=1, source_target_pairs={{0,4},{4,0},{8,12},{12,8},{1,5},{5,1},{9,13},{13,9},{2,6},{6,2},{1... | collective-permute-start | bytes 1572872 | tf_op jit(solution)/shard_map/ppermute | solution.py:33
  273.3 14.7 %collective-permute-start.42 = (bf16[256,1024]{1,0:T(8,128)(2,1)S(1)}, bf16[256,1024]{1,0:T(8,128)(2,1)S(1)}, u32[]{:S(2)}, u32[]{:S(2)}) collective-permute-start(bf16[256,1024]{1,0:T(8,128)(2,1)S(1)} %slice.347), channel_id=1, source_target_pairs={{0,16},{16,0},{1,17},{17,1},{2,18},{18,2},{3,19},{19,3},{4,20},{20... | collective-permute-start | bytes 1572872 | tf_op jit(solution)/shard_map/ppermute | solution.py:29
  329.9 22.3 %collective-permute-start.56 = (bf16[128,1024]{1,0:T(8,128)(2,1)S(1)}, bf16[128,1024]{1,0:T(8,128)(2,1)S(1)}, u32[]{:S(2)}, u32[]{:S(2)}) collective-permute-start(bf16[128,1024]{1,0:T(8,128)(2,1)S(1)} %slice.354), channel_id=1, source_target_pairs={{0,8},{4,12},{8,0},{12,4},{1,9},{5,13},{9,1},{13,5},{2,10},{6,14},... | collective-permute-start | bytes 786440 | tf_op jit(solution)/shard_map/ppermute | solution.py:37
  331.5 20.7 %collective-permute-start.57 = (bf16[128,1024]{1,0:T(8,128)(2,1)S(1)}, bf16[128,1024]{1,0:T(8,128)(2,1)S(1)}, u32[]{:S(2)}, u32[]{:S(2)}) collective-permute-start(bf16[128,1024]{1,0:T(8,128)(2,1)S(1)} %slice.355), channel_id=1, source_target_pairs={{0,8},{4,12},{8,0},{12,4},{1,9},{5,13},{9,1},{13,5},{2,10},{6,14},... | collective-permute-start | bytes 786440 | tf_op jit(solution)/shard_map/ppermute | solution.py:37
  337.1 29.4 %collective-permute-start.58 = (bf16[512,1024]{1,0:T(8,128)(2,1)S(1)}, bf16[512,1024]{1,0:T(8,128)(2,1)S(1)}, u32[]{:S(2)}, u32[]{:S(2)}) collective-permute-start(bf16[512,1024]{1,0:T(8,128)(2,1)S(1)} %get-tuple-element.253), channel_id=1, source_target_pairs={{0,8},{4,12},{8,0},{12,4},{1,9},{5,13},{9,1},{13,5},{2,10},{6,14},... | collective-permute-start | bytes 3145736 | tf_op jit(solution)/shard_map/ppermute | solution.py:37
  374.0 26.1 %collective-permute-start.63 = (bf16[1024,512]{1,0:T(8,128)(2,1)}, bf16[1024,512]{1,0:T(8,128)(2,1)}, u32[]{:S(2)}, u32[]{:S(2)}) collective-permute-start(bf16[1024,512]{1,0:T(8,128)(2,1)} %get-tuple-element.257), channel_id=1, source_target_pairs={{0,8},{4,12},{8,0},{12,4},{1,9},{5,13},{9,1},{13,5},{2,10},{6,14},... | collective-permute-start | bytes 3145736 | tf_op jit(solution)/shard_map/ppermute | solution.py:37
  389.5 14.7 %collective-permute-start.65 = (bf16[256,1024]{1,0:T(8,128)(2,1)}, bf16[256,1024]{1,0:T(8,128)(2,1)}, u32[]{:S(2)}, u32[]{:S(2)}) collective-permute-start(bf16[256,1024]{1,0:T(8,128)(2,1)} %fusion.88), channel_id=1, source_target_pairs={{0,4},{4,0},{8,12},{12,8},{1,5},{5,1},{9,13},{13,9},{2,6},{6,2},{1... | collective-permute-start | bytes 1572872 | tf_op jit(solution)/shard_map/ppermute | solution.py:33
  391.6 76.7 %reduce-scatter.9.cloned.1.call-start = ((), (), s32[]{:S(2)}) async-start(), calls=%async_computation.12 | async-start | bytes 1310720 | tf_op jit(solution)/shard_map/reduce_scatter | solution.py:784
  425.6 26.5 %collective-permute-start.64 = (bf16[256,1024]{1,0:T(8,128)(2,1)}, bf16[256,1024]{1,0:T(8,128)(2,1)}, u32[]{:S(2)}, u32[]{:S(2)}) collective-permute-start(bf16[256,1024]{1,0:T(8,128)(2,1)} %slice.361), channel_id=1, source_target_pairs={{0,16},{16,0},{1,17},{17,1},{2,18},{18,2},{3,19},{19,3},{4,20},{20... | collective-permute-start | bytes 1572872 | tf_op jit(solution)/shard_map/ppermute | solution.py:29
  425.7 26.5 %collective-permute-start.69 = (bf16[1024,384]{1,0:T(8,128)(2,1)}, bf16[1024,384]{1,0:T(8,128)(2,1)}, u32[]{:S(2)}, u32[]{:S(2)}) collective-permute-start(bf16[1024,384]{1,0:T(8,128)(2,1)} %get-tuple-element.262), channel_id=1, source_target_pairs={{0,8},{4,12},{8,0},{12,4},{1,9},{5,13},{9,1},{13,5},{2,10},{6,14},... | collective-permute-start | bytes 2359304 | tf_op jit(solution)/shard_map/ppermute | solution.py:37
  428.1 24.0 %collective-permute-start.68 = (bf16[256,1024]{1,0:T(8,128)(2,1)}, bf16[256,1024]{1,0:T(8,128)(2,1)}, u32[]{:S(2)}, u32[]{:S(2)}) collective-permute-start(bf16[256,1024]{1,0:T(8,128)(2,1)} %add_convert_fusion.14), channel_id=1, source_target_pairs={{0,4},{4,0},{8,12},{12,8},{1,5},{5,1},{9,13},{13,9},{2,6},{6,2},{1... | collective-permute-start | bytes 1572872 | tf_op jit(solution)/shard_map/ppermute | solution.py:33
  431.2 102.1 %reduce-scatter.11.cloned.1.call-start = ((), (), s32[]{:S(2)}) async-start(), calls=%async_computation.13 | async-start | bytes 1392640 | tf_op jit(solution)/shard_map/reduce_scatter | solution.py:784
  431.3 20.1 %collective-permute-start.70 = (bf16[2,128,512]{2,1,0:T(8,128)(2,1)S(1)}, bf16[2,128,512]{2,1,0:T(8,128)(2,1)S(1)}, u32[]{:S(2)}, u32[]{:S(2)}) collective-permute-start(bf16[2,128,512]{2,1,0:T(8,128)(2,1)S(1)} %bitcast.251), channel_id=1, source_target_pairs={{0,8},{4,12},{8,0},{12,4},{1,9},{5,13},{9,1},{13,5},{2,10},{6,14},... | collective-permute-start | bytes 786440 | tf_op jit(solution)/shard_map/ppermute | solution.py:37
  471.9 98.6 %reduce-scatter.15.cloned.1.call-start = ((), (), s32[]{:S(2)}) async-start(), calls=%async_computation.15 | async-start | bytes 1310720 | tf_op jit(solution)/shard_map/reduce_scatter | solution.py:784
  472.8 35.2 %collective-permute-start.75 = (bf16[512,1024]{1,0:T(8,128)(2,1)}, bf16[512,1024]{1,0:T(8,128)(2,1)S(1)}, u32[]{:S(2)}, u32[]{:S(2)}) collective-permute-start(bf16[512,1024]{1,0:T(8,128)(2,1)} %copy-done.77), channel_id=1, source_target_pairs={{0,8},{4,12},{8,0},{12,4},{1,9},{5,13},{9,1},{13,5},{2,10},{6,14},... | collective-permute-start | bytes 3145736 | tf_op jit(solution)/shard_map/ppermute | solution.py:37
  475.2 29.5 %collective-permute-start.77 = (bf16[128,1024]{1,0:T(8,128)(2,1)S(1)}, bf16[128,1024]{1,0:T(8,128)(2,1)S(1)}, u32[]{:S(2)}, u32[]{:S(2)}) collective-permute-start(bf16[128,1024]{1,0:T(8,128)(2,1)S(1)} %slice.364), channel_id=1, source_target_pairs={{0,8},{4,12},{8,0},{12,4},{1,9},{5,13},{9,1},{13,5},{2,10},{6,14},... | collective-permute-start | bytes 786440 | tf_op jit(solution)/shard_map/ppermute | solution.py:37
  475.9 32.1 %collective-permute-start.76 = (bf16[128,1024]{1,0:T(8,128)(2,1)}, bf16[128,1024]{1,0:T(8,128)(2,1)S(1)}, u32[]{:S(2)}, u32[]{:S(2)}) collective-permute-start(bf16[128,1024]{1,0:T(8,128)(2,1)} %reduce-scatter.7.cloned.1.call-done.refs_8_), channel_id=1, source_target_pairs={{0,8},{4,12},{8,0},{12,4},{1,9},{5,13},{9,1},{13,5},{2,10},{6,14},... | collective-permute-start | bytes 786440 | tf_op jit(solution)/shard_map/ppermute | solution.py:37
  510.1 60.5 %reduce-scatter.13.cloned.1.call-start = ((), (), s32[]{:S(2)}) async-start(), calls=%async_computation.14 | async-start | bytes 1310720 | tf_op jit(solution)/shard_map/reduce_scatter | solution.py:784
  510.1 23.2 %collective-permute-start.78 = (bf16[1024,512]{1,0:T(8,128)(2,1)}, bf16[1024,512]{1,0:T(8,128)(2,1)}, u32[]{:S(2)}, u32[]{:S(2)}) collective-permute-start(bf16[1024,512]{1,0:T(8,128)(2,1)} %copy-done.76), channel_id=1, source_target_pairs={{0,8},{4,12},{8,0},{12,4},{1,9},{5,13},{9,1},{13,5},{2,10},{6,14},... | collective-permute-start | bytes 3145736 | tf_op jit(solution)/shard_map/ppermute | solution.py:37
  511.6 19.4 %collective-permute-start.80 = (bf16[128,1024]{1,0:T(8,128)(2,1)}, bf16[128,1024]{1,0:T(8,128)(2,1)}, u32[]{:S(2)}, u32[]{:S(2)}) collective-permute-start(bf16[128,1024]{1,0:T(8,128)(2,1)} %reduce-scatter.7.cloned.1.call-done.refs_8_), channel_id=1, source_target_pairs={{0,4},{4,0},{8,12},{12,8},{1,5},{5,1},{9,13},{13,9},{2,6},{6,2},{1... | collective-permute-start | bytes 786440 | tf_op jit(solution)/shard_map/ppermute | solution.py:33
  513.2 17.8 %collective-permute-start.79 = (bf16[256,512]{1,0:T(8,128)(2,1)}, bf16[256,512]{1,0:T(8,128)(2,1)}, u32[]{:S(2)}, u32[]{:S(2)}) collective-permute-start(bf16[256,512]{1,0:T(8,128)(2,1)} %reduce-scatter.9.cloned.1.call-done.refs_8_), channel_id=1, source_target_pairs={{0,4},{4,0},{8,12},{12,8},{1,5},{5,1},{9,13},{13,9},{2,6},{6,2},{1... | collective-permute-start | bytes 786440 | tf_op jit(solution)/shard_map/ppermute | solution.py:33
  513.8 17.2 %collective-permute-start.81 = (bf16[128,1024]{1,0:T(8,128)(2,1)}, bf16[128,1024]{1,0:T(8,128)(2,1)}, u32[]{:S(2)}, u32[]{:S(2)}) collective-permute-start(bf16[128,1024]{1,0:T(8,128)(2,1)} %copy-done.135), channel_id=1, source_target_pairs={{0,4},{4,0},{8,12},{12,8},{1,5},{5,1},{9,13},{13,9},{2,6},{6,2},{1... | collective-permute-start | bytes 786440 | tf_op jit(solution)/shard_map/ppermute | solution.py:33
  535.8 102.6 %reduce-scatter.17.cloned.1.call-start = ((), (), s32[]{:S(2)}) async-start(), calls=%async_computation.16 | async-start | bytes 1392640 | tf_op jit(solution)/shard_map/reduce_scatter | solution.py:784
  545.5 23.7 %collective-permute-start.82 = (bf16[1024,384]{1,0:T(8,128)(2,1)S(1)}, bf16[1024,384]{1,0:T(8,128)(2,1)S(1)}, u32[]{:S(2)}, u32[]{:S(2)}) collective-permute-start(bf16[1024,384]{1,0:T(8,128)(2,1)S(1)} %get-tuple-element.295), channel_id=1, source_target_pairs={{0,8},{4,12},{8,0},{12,4},{1,9},{5,13},{9,1},{13,5},{2,10},{6,14},... | collective-permute-start | bytes 2359304 | tf_op jit(solution)/shard_map/ppermute | solution.py:37
  553.2 17.3 %collective-permute-start.87 = (bf16[256,1024]{1,0:T(8,128)(2,1)}, bf16[256,1024]{1,0:T(8,128)(2,1)}, u32[]{:S(2)}, u32[]{:S(2)}) collective-permute-start(bf16[256,1024]{1,0:T(8,128)(2,1)} %add_convert_fusion.13), channel_id=1, source_target_pairs={{0,4},{4,0},{8,12},{12,8},{1,5},{5,1},{9,13},{13,9},{2,6},{6,2},{1... | collective-permute-start | bytes 1572872 | tf_op jit(solution)/shard_map/ppermute | solution.py:33
  554.8 18.2 %collective-permute-start.88 = (bf16[256,1024]{1,0:T(8,128)(2,1)S(1)}, bf16[256,1024]{1,0:T(8,128)(2,1)}, u32[]{:S(2)}, u32[]{:S(2)}) collective-permute-start(bf16[256,1024]{1,0:T(8,128)(2,1)S(1)} %slice.368), channel_id=1, source_target_pairs={{0,16},{16,0},{1,17},{17,1},{2,18},{18,2},{3,19},{19,3},{4,20},{20... | collective-permute-start | bytes 1572872 | tf_op jit(solution)/shard_map/ppermute | solution.py:29
  557.1 28.0 %collective-permute-start.112 = (bf16[128,1024]{1,0:T(8,128)(2,1)}, bf16[128,1024]{1,0:T(8,128)(2,1)}, u32[]{:S(2)}, u32[]{:S(2)}) collective-permute-start(bf16[128,1024]{1,0:T(8,128)(2,1)} %reduce-scatter.7.cloned.1.call-done.refs_8_), channel_id=1, source_target_pairs={{0,16},{16,0},{1,17},{17,1},{2,18},{18,2},{3,19},{19,3},{4,20},{20... | collective-permute-start | bytes 786440 | tf_op jit(solution)/shard_map/ppermute | solution.py:29
  584.9 17.2 %collective-permute-start.102 = (bf16[256,512]{1,0:T(8,128)(2,1)}, bf16[256,512]{1,0:T(8,128)(2,1)S(1)}, u32[]{:S(2)}, u32[]{:S(2)}) collective-permute-start(bf16[256,512]{1,0:T(8,128)(2,1)} %reduce-scatter.9.cloned.1.call-done.refs_8_), channel_id=1, source_target_pairs={{0,16},{16,0},{1,17},{17,1},{2,18},{18,2},{3,19},{19,3},{4,20},{20... | collective-permute-start | bytes 786440 | tf_op jit(solution)/shard_map/ppermute | solution.py:29
  585.7 16.9 %collective-permute-start.103 = (bf16[256,512]{1,0:T(8,128)(2,1)}, bf16[256,512]{1,0:T(8,128)(2,1)S(1)}, u32[]{:S(2)}, u32[]{:S(2)}) collective-permute-start(bf16[256,512]{1,0:T(8,128)(2,1)} %collective-permute-done.79.refs_9_), channel_id=1, source_target_pairs={{0,16},{16,0},{1,17},{17,1},{2,18},{18,2},{3,19},{19,3},{4,20},{20... | collective-permute-start | bytes 786440 | tf_op jit(solution)/shard_map/ppermute | solution.py:29
  585.9 16.2 %collective-permute-start.95 = (bf16[256,512]{1,0:T(8,128)(2,1)}, bf16[256,512]{1,0:T(8,128)(2,1)S(1)}, u32[]{:S(2)}, u32[]{:S(2)}) collective-permute-start(bf16[256,512]{1,0:T(8,128)(2,1)} %copy-done.140), channel_id=1, source_target_pairs={{0,8},{4,12},{8,0},{12,4},{1,9},{5,13},{9,1},{13,5},{2,10},{6,14},... | collective-permute-start | bytes 786440 | tf_op jit(solution)/shard_map/ppermute | solution.py:37
  616.6 21.6 %collective-permute-start.91 = (bf16[2,128,1024]{2,1,0:T(8,128)(2,1)S(1)}, bf16[2,128,1024]{2,1,0:T(8,128)(2,1)S(1)}, u32[]{:S(2)}, u32[]{:S(2)}) collective-permute-start(bf16[2,128,1024]{2,1,0:T(8,128)(2,1)S(1)} %maximum_select_fusion.4), channel_id=1, source_target_pairs={{0,16},{16,0},{1,17},{17,1},{2,18},{18,2},{3,19},{19,3},{4,20},{20... | collective-permute-start | bytes 1572872 | tf_op jit(solution)/shard_map/ppermute | solution.py:29
  621.7 18.3 %collective-permute-start.123 = (bf16[272,512]{1,0:T(8,128)(2,1)S(1)}, bf16[272,512]{1,0:T(8,128)(2,1)}, u32[]{:S(2)}, u32[]{:S(2)}) collective-permute-start(bf16[272,512]{1,0:T(8,128)(2,1)S(1)} %copy-done.123), channel_id=1, source_target_pairs={{0,8},{4,12},{8,0},{12,4},{1,9},{5,13},{9,1},{13,5},{2,10},{6,14},... | collective-permute-start | bytes 835592 | tf_op jit(solution)/shard_map/ppermute | solution.py:37
  623.3 19.4 %collective-permute-start.124 = (bf16[272,512]{1,0:T(8,128)(2,1)}, bf16[272,512]{1,0:T(8,128)(2,1)}, u32[]{:S(2)}, u32[]{:S(2)}) collective-permute-start(bf16[272,512]{1,0:T(8,128)(2,1)} %collective-permute-done.85.refs_9_), channel_id=1, source_target_pairs={{0,8},{4,12},{8,0},{12,4},{1,9},{5,13},{9,1},{13,5},{2,10},{6,14},... | collective-permute-start | bytes 835592 | tf_op jit(solution)/shard_map/ppermute | solution.py:37
  623.8 24.1 %collective-permute-start.93 = (bf16[2,128,1024]{2,1,0:T(8,128)(2,1)S(1)}, bf16[2,128,1024]{2,1,0:T(8,128)(2,1)S(1)}, u32[]{:S(2)}, u32[]{:S(2)}) collective-permute-start(bf16[2,128,1024]{2,1,0:T(8,128)(2,1)S(1)} %maximum_select_fusion.6), channel_id=1, source_target_pairs={{0,16},{16,0},{1,17},{17,1},{2,18},{18,2},{3,19},{19,3},{4,20},{20... | collective-permute-start | bytes 1572872 | tf_op jit(solution)/shard_map/ppermute | solution.py:29
  673.8 22.2 %collective-permute-start.132 = (f32[1,8320]{1,0:T(1,128)}, f32[1,8320]{1,0:T(1,128)S(1)}, u32[]{:S(2)}, u32[]{:S(2)}) collective-permute-start(f32[1,8320]{1,0:T(1,128)} %get-tuple-element.345), channel_id=1, source_target_pairs={{0,2},{1,3},{2,0},{3,1},{4,6},{5,7},{6,4},{7,5},{8,10},{9,11},{10,... | collective-permute-start | bytes 99848 | tf_op jit(solution)/shard_map/ppermute | solution.py:586
  674.3 21.7 %collective-permute-start.133 = (f32[1,8320]{1,0:T(1,128)}, f32[1,8320]{1,0:T(1,128)S(1)}, u32[]{:S(2)}, u32[]{:S(2)}) collective-permute-start(f32[1,8320]{1,0:T(1,128)} %get-tuple-element.345), channel_id=1, source_target_pairs={{0,1},{1,2},{2,3},{3,0},{4,5},{5,6},{6,7},{7,4},{8,9},{9,10},{10,1... | collective-permute-start | bytes 99848 | tf_op jit(solution)/shard_map/ppermute | solution.py:586
  676.6 19.4 %collective-permute-start.134 = (f32[1,8320]{1,0:T(1,128)}, f32[1,8320]{1,0:T(1,128)S(1)}, u32[]{:S(2)}, u32[]{:S(2)}) collective-permute-start(f32[1,8320]{1,0:T(1,128)} %get-tuple-element.345), channel_id=1, source_target_pairs={{0,3},{1,0},{2,1},{3,2},{4,7},{5,4},{6,5},{7,6},{8,11},{9,8},{10,9... | collective-permute-start | bytes 99848 | tf_op jit(solution)/shard_map/ppermute | solution.py:586
  (272 other events, 2093.6 us)
Sparse Core Ops, SparseCore 0:
  41.4 32.2 all-gather.5
  75.8 27.4 all-gather.7
  105.5 29.5 all-gather.9
  136.5 28.4 all-gather.11
  184.6 32.0 all-gather.13
  391.7 31.2 reduce-scatter.6
  431.4 30.4 reduce-scatter.8
  472.0 32.2 reduce-scatter.10
  510.2 31.2 reduce-scatter.14
  544.2 25.7 reduce-scatter.12
  585.0 31.3 reduce-scatter.16

commit v6 on v5

--- a/solution.py
+++ b/solution.py
@@ -866,12 +866,11 @@
                 weights[0].out = join_out(parts)
                 weights[0].up = with_far(up)
             elif point == NORM:
-                value, far, down = sync(value, weights[0].up[1], down_gathered[0])
-                weights[0].up = weights[0].up[0], far
+                value, down = sync(value, down_gathered[0])
                 weights[0].down = with_far(down)
             elif point == FEED0:
-                value, far = sync(value, weights[0].down[1])
-                weights[0].down = weights[0].down[0], far
+                value, far = sync(value, weights[0].up[1])
+                weights[0].up = weights[0].up[0], far
             elif point == SEND:
                 value, packed = sync(value, packed_gathered)
                 near = packed.reshape(4, rows + 16, 4 * LANES)[:, :rows, : 3 * LANES]

time: 726 us -> 711 us (0.979)
  matrix products: 70.8 us -> 56.4 us
    dot_general x24, matrix products: 34.5 us -> 26.2 us  [times_transposed(): lax.dot_general(left, right, (((1,), (1,)), ((), ())), preferred_element_...]
    unnamed x390 -> x402, local copies, waits for them, and re-layouts: 45.2 us -> 46 us
  transfers between devices with their start and end apart: 146 -> 146, of which waited for: 47 -> 47; matrix products, arithmetic and copies ran while one was open for 22% -> 21% of each run, Pallas kernels for 16% -> 16%
where the time goes in v6:
time: 711 us; the launch traced here: 701 us
  waiting for transfers between devices  243 us (34%)
  Pallas kernels  126 us (18%)
  starting transfers between devices  97.9 us (14%)
  other arithmetic  82.3 us (12%)
  local copies, waits for them, and re-layouts  67.1 us (9%)
  matrix products  56.4 us (8%)
  between operations  28.5 us (4%)
    ppermute x28, waiting for transfers between devices, swap_x(): return lax.ppermute(value, CTX, [(i, i ^ 1) for i in range(4)])  118 us
    ppermute x36, waiting for transfers between devices, swap_y(): return lax.ppermute(value, CTX, [(i, i ^ 2) for i in range(4)])  103 us
    unnamed x402, local copies, waits for them, and re-layouts  46 us
    pallas_call x4, Pallas kernels, attention_backward(): pl.pallas_call(functools.partial(attention_back_kernel, scale=scale, last...  40 us
    ppermute x36, starting transfers between devices, swap_y(): return lax.ppermute(value, CTX, [(i, i ^ 2) for i in range(4)])  38.9 us
    ppermute x28, starting transfers between devices, swap_x(): return lax.ppermute(value, CTX, [(i, i ^ 1) for i in range(4)])  31.3 us
    dot_general x24, matrix products, dot(): return jnp.dot(left, right, preferred_element_type=f32)  30.2 us
    pallas_call x9, Pallas kernels, small_call(): pl.pallas_call(kernel, grid_spec=pltpu.PrefetchScalarGridSpec(num_scalar_...  27.6 us
  transfers between devices with their start and end apart: 146, of which 47 were waited for; matrix products, arithmetic and copies ran while one was open for 21% of the time, Pallas kernels for 16%

profile of v6, /device:TPU:0, one launch (start us, length us, event | category | flops | bytes accessed | tf_op | source)
XLA Modules:
  0.0 700.7 jit_solution(2010114717892866042)
XLA Ops:
  8.4 3.0 collective-permute-start.1
  11.4 3.7 shard_map.378
  20.2 2.6 collective-permute-start.7
  26.6 3.4 collective-permute-done.6.refs_1_
  30.1 11.2 %collective-permute-done.7.refs_2_ = bf16[272,512]{1,0:T(8,128)(2,1)S(1)} collective-permute-done((bf16[272,512]{1,0:T(8,128)(2,1)S(1)}, bf16[272,512]{1,0:T(8,128)(2,1)S(1)}, u32[]{:S(2)}, u32[]{:S(2)}) %collective-permute-start.7) | collective-permute-done | bytes 278560 | tf_op jit(solution)/shard_map/ppermute | solution.py:586
  53.4 8.4 %collective-permute-done.14.came = bf16[2,128,256]{2,1,0:T(8,128)(2,1)} collective-permute-done((bf16[2,128,256]{2,1,0:T(8,128)(2,1)S(1)}, bf16[2,128,256]{2,1,0:T(8,128)(2,1)}, u32[]{:S(2)}, u32[]{:S(2)}) %collective-permute-start.14) | collective-permute-done | bytes 131104 | tf_op jit(solution)/shard_map/ppermute | solution.py:33
  66.3 3.6 collective-permute-done.12.refs_7_
  76.4 6.7 shard_map.380
  94.1 6.7 shard_map.383
  102.6 4.2 collective-permute-done.19
  111.8 11.7 %collective-permute-done.25 = bf16[256,1024]{1,0:T(8,128)(2,1)} collective-permute-done((bf16[256,1024]{1,0:T(8,128)(2,1)}, bf16[256,1024]{1,0:T(8,128)(2,1)}, u32[]{:S(2)}, u32[]{:S(2)}) %collective-permute-start.25) | collective-permute-done | bytes 524320 | tf_op jit(solution)/shard_map/ppermute | solution.py:33
  124.8 4.1 collective-permute-done.22
  130.0 3.1 multiply_convert_fusion.8
  133.1 3.3 multiply_convert_fusion.6
  139.7 11.2 %collective-permute-done.23 = bf16[512,1024]{1,0:T(8,128)(2,1)S(1)} collective-permute-done((bf16[512,1024]{1,0:T(8,128)(2,1)}, bf16[512,1024]{1,0:T(8,128)(2,1)S(1)}, u32[]{:S(2)}, u32[]{:S(2)}) %collective-permute-start.23) | collective-permute-done | bytes 1048608 | tf_op jit(solution)/shard_map/ppermute | solution.py:37
  158.1 2.9 add_convert_fusion.11
  164.2 7.9 %collective-permute-done.28 = bf16[256,1024]{1,0:T(8,128)(2,1)} collective-permute-done((bf16[256,1024]{1,0:T(8,128)(2,1)}, bf16[256,1024]{1,0:T(8,128)(2,1)}, u32[]{:S(2)}, u32[]{:S(2)}) %collective-permute-start.28) | collective-permute-done | bytes 524320 | tf_op jit(solution)/shard_map/ppermute | solution.py:33
  179.2 12.3 %collective-permute-done.31 = bf16[256,1024]{1,0:T(8,128)(2,1)} collective-permute-done((bf16[256,1024]{1,0:T(8,128)(2,1)}, bf16[256,1024]{1,0:T(8,128)(2,1)}, u32[]{:S(2)}, u32[]{:S(2)}) %collective-permute-start.31) | collective-permute-done | bytes 524320 | tf_op jit(solution)/shard_map/ppermute | solution.py:33
  201.3 6.7 shard_map.385
  214.5 7.1 %shard_map.388 = (bf16[512,256]{1,0:T(8,128)(2,1)S(1)}, f32[2,2,512]{2,1,0:T(2,128)S(1)}) custom-call(bf16[512,768]{1,0:T(8,128)(2,1)S(1)} %copy-done.18, bf16[1024,768]{1,0:T(8,128)(2,1)S(1)} %copy-done.4, bf16[1024,768]{1,0:T(8,128)(2,1)S(1)} %copy-done.4, s32[1,512]{1,0:T(1,128)S(1)} %bitcast.227, s32[1024,1]{1,0:T(8,128)S(1)} %copy.46.kid_ref), custom_call_target="tpu_custom_call" | custom-call | flops 1073741824 | bytes 4194304 | tf_op jit(solution)/shard_map/pallas_call | solution.py:114
  224.3 2.7 collective-permute-done.38
  227.0 9.9 %collective-permute-done.39 = bf16[1024,512]{1,0:T(8,128)(2,1)S(1)} collective-permute-done((bf16[1024,512]{1,0:T(8,128)(2,1)S(1)}, bf16[1024,512]{1,0:T(8,128)(2,1)S(1)}, u32[]{:S(2)}, u32[]{:S(2)}) %collective-permute-start.39) | collective-permute-done | bytes 1048608 | tf_op jit(solution)/shard_map/ppermute | solution.py:37
  244.6 14.3 %collective-permute-done.41 = bf16[512,1024]{1,0:T(8,128)(2,1)S(1)} collective-permute-done((bf16[512,1024]{1,0:T(8,128)(2,1)S(1)}, bf16[512,1024]{1,0:T(8,128)(2,1)S(1)}, u32[]{:S(2)}, u32[]{:S(2)}) %collective-permute-start.41) | collective-permute-done | bytes 1048608 | tf_op jit(solution)/shard_map/ppermute | solution.py:37
  270.4 4.4 fusion.87.refs_17_
  274.8 5.7 collective-permute-done.46
  283.8 11.8 %collective-permute-done.49 = bf16[256,1024]{1,0:T(8,128)(2,1)S(1)} collective-permute-done((bf16[256,1024]{1,0:T(8,128)(2,1)S(1)}, bf16[256,1024]{1,0:T(8,128)(2,1)S(1)}, u32[]{:S(2)}, u32[]{:S(2)}) %collective-permute-start.49) | collective-permute-done | bytes 524320 | tf_op jit(solution)/shard_map/ppermute | solution.py:33
  305.8 2.7 shard_map.389
  308.6 9.0 %collective-permute-done.52 = bf16[256,1024]{1,0:T(8,128)(2,1)S(1)} collective-permute-done((bf16[256,1024]{1,0:T(8,128)(2,1)S(1)}, bf16[256,1024]{1,0:T(8,128)(2,1)S(1)}, u32[]{:S(2)}, u32[]{:S(2)}) %collective-permute-start.52) | collective-permute-done | bytes 524320 | tf_op jit(solution)/shard_map/ppermute | solution.py:33
  324.6 4.0 shard_map.390
  331.1 3.2 collective-permute-done.53
  334.8 9.8 %shard_map.391 = (bf16[512,256]{1,0:T(8,128)(2,1)S(1)}, f32[1024,256]{1,0:T(8,128)S(1)}, f32[1024,256]{1,0:T(8,128)S(1)}) custom-call(bf16[512,768]{1,0:T(8,128)(2,1)S(1)} %copy-done.18, bf16[1024,768]{1,0:T(8,128)(2,1)S(1)} %copy-done.4, bf16[1024,768]{1,0:T(8,128)(2,1)S(1)} %copy-done.4, bf16[512,256]{1,0:T(8,128)(2,1)S(1)} %convolution_convert_fusion.15.g_ref, ...), custom_call_target="tpu_custom_call" | custom-call | flops 2684354560 | bytes 6291456 | tf_op jit(solution)/shard_map/pallas_call | solution.py:218
  346.3 10.4 %shard_map.392.refs_2_.refs_3_.refs_4_.refs_5_ = bf16[1024,768]{1,0:T(8,128)(2,1)S(1)} custom-call(bf16[512,768]{1,0:T(8,128)(2,1)S(1)} %convolution_convert_fusion.8.q_ref, bf16[1024,768]{1,0:T(8,128)(2,1)S(1)} %copy-done.4, bf16[1024,768]{1,0:T(8,128)(2,1)S(1)} %copy-done.4, bf16[512,256]{1,0:T(8,128)(2,1)S(1)} %convolution_convert_fusion.14.g_ref, ...), custom_call_target="tpu_custom_call" | custom-call | flops 2684354560 | bytes 6291456 | tf_op jit(solution)/shard_map/pallas_call | solution.py:218
  367.9 9.4 %collective-permute-done.61 = bf16[256,1024]{1,0:T(8,128)(2,1)} collective-permute-done((bf16[256,1024]{1,0:T(8,128)(2,1)}, bf16[256,1024]{1,0:T(8,128)(2,1)}, u32[]{:S(2)}, u32[]{:S(2)}) %collective-permute-start.61) | collective-permute-done | bytes 524320 | tf_op jit(solution)/shard_map/ppermute | solution.py:33
  386.8 4.2 shard_map.394
  392.7 4.1 collective-permute-done.65
  422.3 2.7 shard_map.395
  427.1 9.1 %collective-permute-done.70.came = bf16[2,128,512]{2,1,0:T(8,128)(2,1)S(1)} collective-permute-done((bf16[2,128,512]{2,1,0:T(8,128)(2,1)S(1)}, bf16[2,128,512]{2,1,0:T(8,128)(2,1)S(1)}, u32[]{:S(2)}, u32[]{:S(2)}) %collective-permute-start.70) | collective-permute-done | bytes 262176 | tf_op jit(solution)/shard_map/ppermute | solution.py:37
  436.9 3.4 multiply_reduce_fusion
  442.5 3.3 shard_map.397
  449.5 3.6 collective-permute-done.74.cross
  462.0 7.9 %collective-permute-done.71 = bf16[256,1024]{1,0:T(8,128)(2,1)S(1)} collective-permute-done((bf16[256,1024]{1,0:T(8,128)(2,1)}, bf16[256,1024]{1,0:T(8,128)(2,1)S(1)}, u32[]{:S(2)}, u32[]{:S(2)}) %collective-permute-start.71) | collective-permute-done | bytes 524320 | tf_op jit(solution)/shard_map/ppermute | solution.py:33
  471.7 9.8 %shard_map.398 = (bf16[512,256]{1,0:T(8,128)(2,1)S(1)}, f32[1024,256]{1,0:T(8,128)S(1)}, f32[1024,256]{1,0:T(8,128)S(1)}) custom-call(bf16[512,768]{1,0:T(8,128)(2,1)S(1)} %copy-done.16, bf16[1024,768]{1,0:T(8,128)(2,1)S(1)} %pad_maximum_fusion.k_ref.v_ref, bf16[1024,768]{1,0:T(8,128)(2,1)S(1)} %pad_maximum_fusion.k_ref.v_ref, ...), custom_call_target="tpu_custom_call" | custom-call | flops 2684354560 | bytes 6291456 | tf_op jit(solution)/shard_map/pallas_call | solution.py:218
  483.8 5.7 collective-permute-done.77
  489.5 3.2 collective-permute-done.76.refs_10_
  504.6 10.0 %shard_map.399.refs_2_.refs_3_.refs_4_.refs_5_ = bf16[1024,768]{1,0:T(8,128)(2,1)S(1)} custom-call(bf16[512,768]{1,0:T(8,128)(2,1)S(1)} %copy-done.14, bf16[1024,768]{1,0:T(8,128)(2,1)S(1)} %pad_maximum_fusion.k_ref.v_ref, bf16[1024,768]{1,0:T(8,128)(2,1)S(1)} %pad_maximum_fusion.k_ref.v_ref, bf16[512,256]{1,0:T(8,128)(2,1)S(1)} %convolution_convert_fusion.12.g_ref, ...), custom_call_target="tpu_custom_call" | custom-call | flops 2684354560 | bytes 6291456 | tf_op jit(solution)/shard_map/pallas_call | solution.py:218
  525.1 3.5 shard_map.402
  531.8 6.1 collective-permute-done.84.came
  542.1 11.4 %collective-permute-done.86.cross = bf16[2,128,256]{2,1,0:T(8,128)(2,1)S(1)} collective-permute-done((bf16[2,128,256]{2,1,0:T(8,128)(2,1)S(1)}, bf16[2,128,256]{2,1,0:T(8,128)(2,1)S(1)}, u32[]{:S(2)}, u32[]{:S(2)}) %collective-permute-start.86) | collective-permute-done | bytes 131104 | tf_op jit(solution)/shard_map/ppermute | solution.py:33
  559.9 4.9 collective-permute-done.89.refs_2_
  572.2 3.5 collective-permute-done.100.refs_10_
  576.8 4.4 collective-permute-done.101.refs_11_
  583.2 3.6 collective-permute-done.95.refs_3_
  588.6 2.7 collective-permute-done.92
  594.2 6.6 shard_map.405
  601.9 3.8 collective-permute-done.107.refs_3_
  609.4 8.4 %shard_map.406 = (f32[1024,1024]{1,0:T(8,128)}, f32[1024,1]{1,0:T(8,128)}, f32[1,2176]{1,0:T(1,128)}) custom-call(s32[2]{0:T(128)} %pad_add_fusion.1.at, bf16[128,1024]{1,0:T(8,128)(2,1)} %reduce-scatter.15.cloned.1.call-done.refs_0_, bf16[128,1024]{1,0:T(8,128)(2,1)} %copy-done.156, bf16[128,1024]{1,0:T(8,128)(2,1)} %copy-done.144, ...), custom_call_target="tpu_custom_call" | custom-call | tf_op jit(solution)/shard_map/pallas_call | solution.py:389
  618.5 4.3 collective-permute-start.129
  624.6 2.9 collective-permute-start.130
  636.4 5.8 collective-permute-done.117.refs_2_
  642.2 5.5 collective-permute-done.118.refs_3_
  650.7 7.7 %shard_map.407 = (f32[256,3072]{1,0:T(8,128)}, f32[256,1024]{1,0:T(8,128)}, f32[256,1]{1,0:T(8,128)}, f32[256,1]{1,0:T(8,128)}, f32[1,512]{1,0:T(1,128)}, /*index=5*/f32[1,8320]{1,0:T(1,128)}) custom-call(s32[2]{0:T(128)} %pad_add_fusion.1.at, bf16[272,512]{1,0:T(8,128)(2,1)} %reduce-scatter.17.cloned.1.call-done.refs_0_, ...), custom_call_target="tpu_custom_call" | custom-call | tf_op jit(solution)/shard_map/pallas_call | solution.py:389
  669.0 5.7 fusion.3
  674.8 2.9 fusion.1
  689.5 4.4 fusion.5
  (883 shorter events, 285.8 us)
Async XLA Ops:
  7.2 77.9 %all-gather.6.cloned.1.call-start = ((), (), s32[]{:S(2)}) async-start(), calls=%async_computation.6 | async-start | bytes 1310720 | tf_op jit(solution)/shard_map/all_gather | solution.py:582
  8.4 33.4 %collective-permute-start.1 = (bf16[128,1024]{1,0:T(8,128)(2,1)S(1)}, bf16[128,1024]{1,0:T(8,128)(2,1)S(1)}, u32[]{:S(2)}, u32[]{:S(2)}) collective-permute-start(bf16[128,1024]{1,0:T(8,128)(2,1)S(1)} %get-tuple-element.394), channel_id=1, source_target_pairs={{0,8},{4,12},{8,0},{12,4},{1,9},{5,13},{9,1},{13,5},{2,10},{6,14},... | collective-permute-start | bytes 786440 | tf_op jit(solution)/shard_map/ppermute | solution.py:37
  20.2 21.1 %collective-permute-start.7 = (bf16[272,512]{1,0:T(8,128)(2,1)S(1)}, bf16[272,512]{1,0:T(8,128)(2,1)S(1)}, u32[]{:S(2)}, u32[]{:S(2)}) collective-permute-start(bf16[272,512]{1,0:T(8,128)(2,1)S(1)} %get-tuple-element.398.refs_0_), channel_id=1, source_target_pairs={{0,2},{1,3},{2,0},{3,1},{4,6},{5,7},{6,4},{7,5},{8,10},{9,11},{10,... | collective-permute-start | bytes 835592 | tf_op jit(solution)/shard_map/ppermute | solution.py:586
  22.8 18.5 %collective-permute-start.8 = (bf16[272,512]{1,0:T(8,128)(2,1)S(1)}, bf16[272,512]{1,0:T(8,128)(2,1)S(1)}, u32[]{:S(2)}, u32[]{:S(2)}) collective-permute-start(bf16[272,512]{1,0:T(8,128)(2,1)S(1)} %get-tuple-element.398.refs_0_), channel_id=1, source_target_pairs={{0,3},{1,0},{2,1},{3,2},{4,7},{5,4},{6,5},{7,6},{8,11},{9,8},{10,9... | collective-permute-start | bytes 835592 | tf_op jit(solution)/shard_map/ppermute | solution.py:586
  25.2 17.3 %collective-permute-start = (bf16[128,1024]{1,0:T(8,128)(2,1)S(1)}, bf16[128,1024]{1,0:T(8,128)(2,1)}, u32[]{:S(2)}, u32[]{:S(2)}) collective-permute-start(bf16[128,1024]{1,0:T(8,128)(2,1)S(1)} %get-tuple-element.396), channel_id=1, source_target_pairs={{0,8},{4,12},{8,0},{12,4},{1,9},{5,13},{9,1},{13,5},{2,10},{6,14},... | collective-permute-start | bytes 786440 | tf_op jit(solution)/shard_map/ppermute | solution.py:37
  30.1 18.1 %collective-permute-start.9 = (bf16[256,384]{1,0:T(8,128)(2,1)}, bf16[256,384]{1,0:T(8,128)(2,1)S(1)}, u32[]{:S(2)}, u32[]{:S(2)}) collective-permute-start(bf16[256,384]{1,0:T(8,128)(2,1)} %get-tuple-element.190), channel_id=1, source_target_pairs={{0,16},{16,0},{1,17},{17,1},{2,18},{18,2},{3,19},{19,3},{4,20},{20... | collective-permute-start | bytes 589832 | tf_op jit(solution)/shard_map/ppermute | solution.py:29
  41.3 65.6 %all-gather.8.cloned.1.call-start = ((), (), s32[]{:S(2)}) async-start(), calls=%async_computation.7 | async-start | bytes 1310720 | tf_op jit(solution)/shard_map/all_gather | solution.py:582
  44.4 27.8 %collective-permute-start.2 = (bf16[256,1024]{1,0:T(8,128)(2,1)}, bf16[256,1024]{1,0:T(8,128)(2,1)}, u32[]{:S(2)}, u32[]{:S(2)}) collective-permute-start(bf16[256,1024]{1,0:T(8,128)(2,1)} %pad_maximum_fusion.9), channel_id=1, source_target_pairs={{0,16},{16,0},{1,17},{17,1},{2,18},{18,2},{3,19},{19,3},{4,20},{20... | collective-permute-start | bytes 1572872 | tf_op jit(solution)/shard_map/ppermute | solution.py:29
  44.9 25.7 %collective-permute-start.3 = (bf16[256,1024]{1,0:T(8,128)(2,1)}, bf16[256,1024]{1,0:T(8,128)(2,1)}, u32[]{:S(2)}, u32[]{:S(2)}) collective-permute-start(bf16[256,1024]{1,0:T(8,128)(2,1)} %pad_maximum_fusion.9), channel_id=1, source_target_pairs={{0,4},{4,0},{8,12},{12,8},{1,5},{5,1},{9,13},{13,9},{2,6},{6,2},{1... | collective-permute-start | bytes 1572872 | tf_op jit(solution)/shard_map/ppermute | solution.py:33
  64.1 93.4 %all-gather.10.cloned.1.call-start = ((), (), s32[]{:S(2)}) async-start(), calls=%async_computation.8 | async-start | bytes 1392640 | tf_op jit(solution)/shard_map/all_gather | solution.py:582
  64.2 19.6 %collective-permute-start.15 = (bf16[2,128,256]{2,1,0:T(8,128)(2,1)}, bf16[2,128,256]{2,1,0:T(8,128)(2,1)S(1)}, u32[]{:S(2)}, u32[]{:S(2)}) collective-permute-start(bf16[2,128,256]{2,1,0:T(8,128)(2,1)} %get-tuple-element.197.keep), channel_id=1, source_target_pairs={{0,8},{4,12},{8,0},{12,4},{1,9},{5,13},{9,1},{13,5},{2,10},{6,14},... | collective-permute-start | bytes 393224 | tf_op jit(solution)/shard_map/ppermute | solution.py:37
  65.8 18.7 %collective-permute-start.16 = (bf16[2,128,256]{2,1,0:T(8,128)(2,1)}, bf16[2,128,256]{2,1,0:T(8,128)(2,1)S(1)}, u32[]{:S(2)}, u32[]{:S(2)}) collective-permute-start(bf16[2,128,256]{2,1,0:T(8,128)(2,1)} %collective-permute-done.14.came), channel_id=1, source_target_pairs={{0,8},{4,12},{8,0},{12,4},{1,9},{5,13},{9,1},{13,5},{2,10},{6,14},... | collective-permute-start | bytes 393224 | tf_op jit(solution)/shard_map/ppermute | solution.py:37
  102.5 61.7 %all-gather.12.cloned.1.call-start = ((), (), s32[]{:S(2)}) async-start(), calls=%async_computation.9 | async-start | bytes 1310720 | tf_op jit(solution)/shard_map/all_gather | solution.py:582
  102.6 26.3 %collective-permute-start.22 = (bf16[1024,512]{1,0:T(8,128)(2,1)}, bf16[1024,512]{1,0:T(8,128)(2,1)}, u32[]{:S(2)}, u32[]{:S(2)}) collective-permute-start(bf16[1024,512]{1,0:T(8,128)(2,1)} %all-gather.6.cloned.1.call-done), channel_id=1, source_target_pairs={{0,8},{4,12},{8,0},{12,4},{1,9},{5,13},{9,1},{13,5},{2,10},{6,14},... | collective-permute-start | bytes 3145736 | tf_op jit(solution)/shard_map/ppermute | solution.py:37
  111.5 97.7 %all-gather.14.cloned.1.call-start = ((), (), s32[]{:S(2)}) async-start(), calls=%async_computation.10 | async-start | bytes 1310720 | tf_op jit(solution)/shard_map/all_gather | solution.py:582
  111.8 39.1 %collective-permute-start.23 = (bf16[512,1024]{1,0:T(8,128)(2,1)}, bf16[512,1024]{1,0:T(8,128)(2,1)S(1)}, u32[]{:S(2)}, u32[]{:S(2)}) collective-permute-start(bf16[512,1024]{1,0:T(8,128)(2,1)} %all-gather.8.cloned.1.call-done), channel_id=1, source_target_pairs={{0,8},{4,12},{8,0},{12,4},{1,9},{5,13},{9,1},{13,5},{2,10},{6,14},... | collective-permute-start | bytes 3145736 | tf_op jit(solution)/shard_map/ppermute | solution.py:37
  157.5 14.6 %collective-permute-start.28 = (bf16[256,1024]{1,0:T(8,128)(2,1)}, bf16[256,1024]{1,0:T(8,128)(2,1)}, u32[]{:S(2)}, u32[]{:S(2)}) collective-permute-start(bf16[256,1024]{1,0:T(8,128)(2,1)} %add_convert_fusion.20), channel_id=1, source_target_pairs={{0,4},{4,0},{8,12},{12,8},{1,5},{5,1},{9,13},{13,9},{2,6},{6,2},{1... | collective-permute-start | bytes 1572872 | tf_op jit(solution)/shard_map/ppermute | solution.py:33
  163.9 29.6 %collective-permute-start.30 = (bf16[1024,384]{1,0:T(8,128)(2,1)}, bf16[1024,384]{1,0:T(8,128)(2,1)}, u32[]{:S(2)}, u32[]{:S(2)}) collective-permute-start(bf16[1024,384]{1,0:T(8,128)(2,1)} %bitcast.15), channel_id=1, source_target_pairs={{0,8},{4,12},{8,0},{12,4},{1,9},{5,13},{9,1},{13,5},{2,10},{6,14},... | collective-permute-start | bytes 2359304 | tf_op jit(solution)/shard_map/ppermute | solution.py:37
  176.3 15.1 %collective-permute-start.31 = (bf16[256,1024]{1,0:T(8,128)(2,1)}, bf16[256,1024]{1,0:T(8,128)(2,1)}, u32[]{:S(2)}, u32[]{:S(2)}) collective-permute-start(bf16[256,1024]{1,0:T(8,128)(2,1)} %multiply_convert_fusion.5), channel_id=1, source_target_pairs={{0,4},{4,0},{8,12},{12,8},{1,5},{5,1},{9,13},{13,9},{2,6},{6,2},{1... | collective-permute-start | bytes 1572872 | tf_op jit(solution)/shard_map/ppermute | solution.py:33
  176.9 260.0 %reduce-scatter.7.cloned.1.call-start = ((), (), s32[]{:S(2)}) async-start(), calls=%async_computation.11 | async-start | bytes 1310720 | tf_op jit(solution)/shard_map/reduce_scatter | solution.py:784
  177.0 19.9 %collective-permute-start.29 = (bf16[256,1024]{1,0:T(8,128)(2,1)}, bf16[256,1024]{1,0:T(8,128)(2,1)S(1)}, u32[]{:S(2)}, u32[]{:S(2)}) collective-permute-start(bf16[256,1024]{1,0:T(8,128)(2,1)} %multiply_convert_fusion.5), channel_id=1, source_target_pairs={{0,16},{16,0},{1,17},{17,1},{2,18},{18,2},{3,19},{19,3},{4,20},{20... | collective-permute-start | bytes 1572872 | tf_op jit(solution)/shard_map/ppermute | solution.py:29
  177.7 15.2 %collective-permute-start.33 = (bf16[2,128,256]{2,1,0:T(8,128)(2,1)S(1)}, bf16[2,128,256]{2,1,0:T(8,128)(2,1)S(1)}, u32[]{:S(2)}, u32[]{:S(2)}) collective-permute-start(bf16[2,128,256]{2,1,0:T(8,128)(2,1)S(1)} %get-tuple-element.416), channel_id=1, source_target_pairs={{0,4},{4,0},{8,12},{12,8},{1,5},{5,1},{9,13},{13,9},{2,6},{6,2},{1... | collective-permute-start | bytes 393224 | tf_op jit(solution)/shard_map/ppermute | solution.py:33
  191.5 17.7 %collective-permute-start.34 = (bf16[2,128,256]{2,1,0:T(8,128)(2,1)S(1)}, bf16[2,128,256]{2,1,0:T(8,128)(2,1)}, u32[]{:S(2)}, u32[]{:S(2)}) collective-permute-start(bf16[2,128,256]{2,1,0:T(8,128)(2,1)S(1)} %get-tuple-element.220.keep), channel_id=1, source_target_pairs={{0,8},{4,12},{8,0},{12,4},{1,9},{5,13},{9,1},{13,5},{2,10},{6,14},... | collective-permute-start | bytes 393224 | tf_op jit(solution)/shard_map/ppermute | solution.py:37
  192.9 16.3 %collective-permute-start.35 = (bf16[2,128,256]{2,1,0:T(8,128)(2,1)S(1)}, bf16[2,128,256]{2,1,0:T(8,128)(2,1)}, u32[]{:S(2)}, u32[]{:S(2)}) collective-permute-start(bf16[2,128,256]{2,1,0:T(8,128)(2,1)S(1)} %collective-permute-done.33.came), channel_id=1, source_target_pairs={{0,8},{4,12},{8,0},{12,4},{1,9},{5,13},{9,1},{13,5},{2,10},{6,14},... | collective-permute-start | bytes 393224 | tf_op jit(solution)/shard_map/ppermute | solution.py:37
  210.9 26.0 %collective-permute-start.39 = (bf16[1024,512]{1,0:T(8,128)(2,1)S(1)}, bf16[1024,512]{1,0:T(8,128)(2,1)S(1)}, u32[]{:S(2)}, u32[]{:S(2)}) collective-permute-start(bf16[1024,512]{1,0:T(8,128)(2,1)S(1)} %copy-done.110), channel_id=1, source_target_pairs={{0,8},{4,12},{8,0},{12,4},{1,9},{5,13},{9,1},{13,5},{2,10},{6,14},... | collective-permute-start | bytes 3145736 | tf_op jit(solution)/shard_map/ppermute | solution.py:37
  222.1 14.8 %collective-permute-start.37 = (bf16[256,1024]{1,0:T(8,128)(2,1)S(1)}, bf16[256,1024]{1,0:T(8,128)(2,1)S(1)}, u32[]{:S(2)}, u32[]{:S(2)}) collective-permute-start(bf16[256,1024]{1,0:T(8,128)(2,1)S(1)} %slice.345), channel_id=1, source_target_pairs={{0,16},{16,0},{1,17},{17,1},{2,18},{18,2},{3,19},{19,3},{4,20},{20... | collective-permute-start | bytes 1572872 | tf_op jit(solution)/shard_map/ppermute | solution.py:29
  222.9 36.1 %collective-permute-start.41 = (bf16[512,1024]{1,0:T(8,128)(2,1)S(1)}, bf16[512,1024]{1,0:T(8,128)(2,1)S(1)}, u32[]{:S(2)}, u32[]{:S(2)}) collective-permute-start(bf16[512,1024]{1,0:T(8,128)(2,1)S(1)} %copy-done.111), channel_id=1, source_target_pairs={{0,8},{4,12},{8,0},{12,4},{1,9},{5,13},{9,1},{13,5},{2,10},{6,14},... | collective-permute-start | bytes 3145736 | tf_op jit(solution)/shard_map/ppermute | solution.py:37
  240.2 18.7 %collective-permute-start.43 = (bf16[256,1024]{1,0:T(8,128)(2,1)S(1)}, bf16[256,1024]{1,0:T(8,128)(2,1)S(1)}, u32[]{:S(2)}, u32[]{:S(2)}) collective-permute-start(bf16[256,1024]{1,0:T(8,128)(2,1)S(1)} %multiply_convert_fusion.10), channel_id=1, source_target_pairs={{0,4},{4,0},{8,12},{12,8},{1,5},{5,1},{9,13},{13,9},{2,6},{6,2},{1... | collective-permute-start | bytes 1572872 | tf_op jit(solution)/shard_map/ppermute | solution.py:33
  265.8 14.7 %collective-permute-start.42 = (bf16[256,1024]{1,0:T(8,128)(2,1)S(1)}, bf16[256,1024]{1,0:T(8,128)(2,1)S(1)}, u32[]{:S(2)}, u32[]{:S(2)}) collective-permute-start(bf16[256,1024]{1,0:T(8,128)(2,1)S(1)} %slice.347), channel_id=1, source_target_pairs={{0,16},{16,0},{1,17},{17,1},{2,18},{18,2},{3,19},{19,3},{4,20},{20... | collective-permute-start | bytes 1572872 | tf_op jit(solution)/shard_map/ppermute | solution.py:29
  322.4 22.3 %collective-permute-start.56 = (bf16[128,1024]{1,0:T(8,128)(2,1)S(1)}, bf16[128,1024]{1,0:T(8,128)(2,1)S(1)}, u32[]{:S(2)}, u32[]{:S(2)}) collective-permute-start(bf16[128,1024]{1,0:T(8,128)(2,1)S(1)} %slice.354), channel_id=1, source_target_pairs={{0,8},{4,12},{8,0},{12,4},{1,9},{5,13},{9,1},{13,5},{2,10},{6,14},... | collective-permute-start | bytes 786440 | tf_op jit(solution)/shard_map/ppermute | solution.py:37
  324.0 20.7 %collective-permute-start.57 = (bf16[128,1024]{1,0:T(8,128)(2,1)S(1)}, bf16[128,1024]{1,0:T(8,128)(2,1)S(1)}, u32[]{:S(2)}, u32[]{:S(2)}) collective-permute-start(bf16[128,1024]{1,0:T(8,128)(2,1)S(1)} %slice.355), channel_id=1, source_target_pairs={{0,8},{4,12},{8,0},{12,4},{1,9},{5,13},{9,1},{13,5},{2,10},{6,14},... | collective-permute-start | bytes 786440 | tf_op jit(solution)/shard_map/ppermute | solution.py:37
  329.5 29.5 %collective-permute-start.58 = (bf16[512,1024]{1,0:T(8,128)(2,1)S(1)}, bf16[512,1024]{1,0:T(8,128)(2,1)S(1)}, u32[]{:S(2)}, u32[]{:S(2)}) collective-permute-start(bf16[512,1024]{1,0:T(8,128)(2,1)S(1)} %get-tuple-element.251), channel_id=1, source_target_pairs={{0,8},{4,12},{8,0},{12,4},{1,9},{5,13},{9,1},{13,5},{2,10},{6,14},... | collective-permute-start | bytes 3145736 | tf_op jit(solution)/shard_map/ppermute | solution.py:37
  366.5 26.1 %collective-permute-start.63 = (bf16[1024,512]{1,0:T(8,128)(2,1)}, bf16[1024,512]{1,0:T(8,128)(2,1)}, u32[]{:S(2)}, u32[]{:S(2)}) collective-permute-start(bf16[1024,512]{1,0:T(8,128)(2,1)} %get-tuple-element.255), channel_id=1, source_target_pairs={{0,8},{4,12},{8,0},{12,4},{1,9},{5,13},{9,1},{13,5},{2,10},{6,14},... | collective-permute-start | bytes 3145736 | tf_op jit(solution)/shard_map/ppermute | solution.py:37
  382.1 14.7 %collective-permute-start.65 = (bf16[256,1024]{1,0:T(8,128)(2,1)}, bf16[256,1024]{1,0:T(8,128)(2,1)}, u32[]{:S(2)}, u32[]{:S(2)}) collective-permute-start(bf16[256,1024]{1,0:T(8,128)(2,1)} %fusion.88), channel_id=1, source_target_pairs={{0,4},{4,0},{8,12},{12,8},{1,5},{5,1},{9,13},{13,9},{2,6},{6,2},{1... | collective-permute-start | bytes 1572872 | tf_op jit(solution)/shard_map/ppermute | solution.py:33
  384.1 69.0 %reduce-scatter.9.cloned.1.call-start = ((), (), s32[]{:S(2)}) async-start(), calls=%async_computation.12 | async-start | bytes 1310720 | tf_op jit(solution)/shard_map/reduce_scatter | solution.py:784
  410.4 26.5 %collective-permute-start.64 = (bf16[256,1024]{1,0:T(8,128)(2,1)}, bf16[256,1024]{1,0:T(8,128)(2,1)}, u32[]{:S(2)}, u32[]{:S(2)}) collective-permute-start(bf16[256,1024]{1,0:T(8,128)(2,1)} %slice.361), channel_id=1, source_target_pairs={{0,16},{16,0},{1,17},{17,1},{2,18},{18,2},{3,19},{19,3},{4,20},{20... | collective-permute-start | bytes 1572872 | tf_op jit(solution)/shard_map/ppermute | solution.py:29
  410.4 26.5 %collective-permute-start.69 = (bf16[1024,384]{1,0:T(8,128)(2,1)}, bf16[1024,384]{1,0:T(8,128)(2,1)}, u32[]{:S(2)}, u32[]{:S(2)}) collective-permute-start(bf16[1024,384]{1,0:T(8,128)(2,1)} %get-tuple-element.260), channel_id=1, source_target_pairs={{0,8},{4,12},{8,0},{12,4},{1,9},{5,13},{9,1},{13,5},{2,10},{6,14},... | collective-permute-start | bytes 2359304 | tf_op jit(solution)/shard_map/ppermute | solution.py:37
  412.9 24.0 %collective-permute-start.68 = (bf16[256,1024]{1,0:T(8,128)(2,1)}, bf16[256,1024]{1,0:T(8,128)(2,1)}, u32[]{:S(2)}, u32[]{:S(2)}) collective-permute-start(bf16[256,1024]{1,0:T(8,128)(2,1)} %add_convert_fusion.14), channel_id=1, source_target_pairs={{0,4},{4,0},{8,12},{12,8},{1,5},{5,1},{9,13},{13,9},{2,6},{6,2},{1... | collective-permute-start | bytes 1572872 | tf_op jit(solution)/shard_map/ppermute | solution.py:33
  416.0 102.0 %reduce-scatter.11.cloned.1.call-start = ((), (), s32[]{:S(2)}) async-start(), calls=%async_computation.13 | async-start | bytes 1392640 | tf_op jit(solution)/shard_map/reduce_scatter | solution.py:784
  416.1 20.1 %collective-permute-start.70 = (bf16[2,128,512]{2,1,0:T(8,128)(2,1)S(1)}, bf16[2,128,512]{2,1,0:T(8,128)(2,1)S(1)}, u32[]{:S(2)}, u32[]{:S(2)}) collective-permute-start(bf16[2,128,512]{2,1,0:T(8,128)(2,1)S(1)} %bitcast.251), channel_id=1, source_target_pairs={{0,8},{4,12},{8,0},{12,4},{1,9},{5,13},{9,1},{13,5},{2,10},{6,14},... | collective-permute-start | bytes 786440 | tf_op jit(solution)/shard_map/ppermute | solution.py:37
  456.7 98.6 %reduce-scatter.15.cloned.1.call-start = ((), (), s32[]{:S(2)}) async-start(), calls=%async_computation.15 | async-start | bytes 1310720 | tf_op jit(solution)/shard_map/reduce_scatter | solution.py:784
  457.5 35.2 %collective-permute-start.75 = (bf16[512,1024]{1,0:T(8,128)(2,1)}, bf16[512,1024]{1,0:T(8,128)(2,1)S(1)}, u32[]{:S(2)}, u32[]{:S(2)}) collective-permute-start(bf16[512,1024]{1,0:T(8,128)(2,1)} %copy-done.77), channel_id=1, source_target_pairs={{0,8},{4,12},{8,0},{12,4},{1,9},{5,13},{9,1},{13,5},{2,10},{6,14},... | collective-permute-start | bytes 3145736 | tf_op jit(solution)/shard_map/ppermute | solution.py:37
  460.0 29.5 %collective-permute-start.77 = (bf16[128,1024]{1,0:T(8,128)(2,1)S(1)}, bf16[128,1024]{1,0:T(8,128)(2,1)S(1)}, u32[]{:S(2)}, u32[]{:S(2)}) collective-permute-start(bf16[128,1024]{1,0:T(8,128)(2,1)S(1)} %slice.364), channel_id=1, source_target_pairs={{0,8},{4,12},{8,0},{12,4},{1,9},{5,13},{9,1},{13,5},{2,10},{6,14},... | collective-permute-start | bytes 786440 | tf_op jit(solution)/shard_map/ppermute | solution.py:37
  460.6 32.1 %collective-permute-start.76 = (bf16[128,1024]{1,0:T(8,128)(2,1)}, bf16[128,1024]{1,0:T(8,128)(2,1)S(1)}, u32[]{:S(2)}, u32[]{:S(2)}) collective-permute-start(bf16[128,1024]{1,0:T(8,128)(2,1)} %reduce-scatter.7.cloned.1.call-done.refs_8_), channel_id=1, source_target_pairs={{0,8},{4,12},{8,0},{12,4},{1,9},{5,13},{9,1},{13,5},{2,10},{6,14},... | collective-permute-start | bytes 786440 | tf_op jit(solution)/shard_map/ppermute | solution.py:37
  494.8 60.5 %reduce-scatter.13.cloned.1.call-start = ((), (), s32[]{:S(2)}) async-start(), calls=%async_computation.14 | async-start | bytes 1310720 | tf_op jit(solution)/shard_map/reduce_scatter | solution.py:784
  494.9 23.2 %collective-permute-start.78 = (bf16[1024,512]{1,0:T(8,128)(2,1)}, bf16[1024,512]{1,0:T(8,128)(2,1)}, u32[]{:S(2)}, u32[]{:S(2)}) collective-permute-start(bf16[1024,512]{1,0:T(8,128)(2,1)} %copy-done.76), channel_id=1, source_target_pairs={{0,8},{4,12},{8,0},{12,4},{1,9},{5,13},{9,1},{13,5},{2,10},{6,14},... | collective-permute-start | bytes 3145736 | tf_op jit(solution)/shard_map/ppermute | solution.py:37
  496.4 19.4 %collective-permute-start.80 = (bf16[128,1024]{1,0:T(8,128)(2,1)}, bf16[128,1024]{1,0:T(8,128)(2,1)}, u32[]{:S(2)}, u32[]{:S(2)}) collective-permute-start(bf16[128,1024]{1,0:T(8,128)(2,1)} %reduce-scatter.7.cloned.1.call-done.refs_8_), channel_id=1, source_target_pairs={{0,4},{4,0},{8,12},{12,8},{1,5},{5,1},{9,13},{13,9},{2,6},{6,2},{1... | collective-permute-start | bytes 786440 | tf_op jit(solution)/shard_map/ppermute | solution.py:33
  498.0 17.8 %collective-permute-start.79 = (bf16[256,512]{1,0:T(8,128)(2,1)}, bf16[256,512]{1,0:T(8,128)(2,1)}, u32[]{:S(2)}, u32[]{:S(2)}) collective-permute-start(bf16[256,512]{1,0:T(8,128)(2,1)} %reduce-scatter.9.cloned.1.call-done.refs_8_), channel_id=1, source_target_pairs={{0,4},{4,0},{8,12},{12,8},{1,5},{5,1},{9,13},{13,9},{2,6},{6,2},{1... | collective-permute-start | bytes 786440 | tf_op jit(solution)/shard_map/ppermute | solution.py:33
  498.5 17.3 %collective-permute-start.81 = (bf16[128,1024]{1,0:T(8,128)(2,1)}, bf16[128,1024]{1,0:T(8,128)(2,1)}, u32[]{:S(2)}, u32[]{:S(2)}) collective-permute-start(bf16[128,1024]{1,0:T(8,128)(2,1)} %copy-done.141), channel_id=1, source_target_pairs={{0,4},{4,0},{8,12},{12,8},{1,5},{5,1},{9,13},{13,9},{2,6},{6,2},{1... | collective-permute-start | bytes 786440 | tf_op jit(solution)/shard_map/ppermute | solution.py:33
  520.6 102.4 %reduce-scatter.17.cloned.1.call-start = ((), (), s32[]{:S(2)}) async-start(), calls=%async_computation.16 | async-start | bytes 1392640 | tf_op jit(solution)/shard_map/reduce_scatter | solution.py:784
  530.3 23.7 %collective-permute-start.82 = (bf16[1024,384]{1,0:T(8,128)(2,1)S(1)}, bf16[1024,384]{1,0:T(8,128)(2,1)S(1)}, u32[]{:S(2)}, u32[]{:S(2)}) collective-permute-start(bf16[1024,384]{1,0:T(8,128)(2,1)S(1)} %get-tuple-element.293), channel_id=1, source_target_pairs={{0,8},{4,12},{8,0},{12,4},{1,9},{5,13},{9,1},{13,5},{2,10},{6,14},... | collective-permute-start | bytes 2359304 | tf_op jit(solution)/shard_map/ppermute | solution.py:37
  538.0 17.3 %collective-permute-start.87 = (bf16[256,1024]{1,0:T(8,128)(2,1)}, bf16[256,1024]{1,0:T(8,128)(2,1)}, u32[]{:S(2)}, u32[]{:S(2)}) collective-permute-start(bf16[256,1024]{1,0:T(8,128)(2,1)} %add_convert_fusion.13), channel_id=1, source_target_pairs={{0,4},{4,0},{8,12},{12,8},{1,5},{5,1},{9,13},{13,9},{2,6},{6,2},{1... | collective-permute-start | bytes 1572872 | tf_op jit(solution)/shard_map/ppermute | solution.py:33
  539.5 18.2 %collective-permute-start.88 = (bf16[256,1024]{1,0:T(8,128)(2,1)S(1)}, bf16[256,1024]{1,0:T(8,128)(2,1)}, u32[]{:S(2)}, u32[]{:S(2)}) collective-permute-start(bf16[256,1024]{1,0:T(8,128)(2,1)S(1)} %slice.368), channel_id=1, source_target_pairs={{0,16},{16,0},{1,17},{17,1},{2,18},{18,2},{3,19},{19,3},{4,20},{20... | collective-permute-start | bytes 1572872 | tf_op jit(solution)/shard_map/ppermute | solution.py:29
  541.9 28.0 %collective-permute-start.112 = (bf16[128,1024]{1,0:T(8,128)(2,1)}, bf16[128,1024]{1,0:T(8,128)(2,1)}, u32[]{:S(2)}, u32[]{:S(2)}) collective-permute-start(bf16[128,1024]{1,0:T(8,128)(2,1)} %reduce-scatter.7.cloned.1.call-done.refs_8_), channel_id=1, source_target_pairs={{0,16},{16,0},{1,17},{17,1},{2,18},{18,2},{3,19},{19,3},{4,20},{20... | collective-permute-start | bytes 786440 | tf_op jit(solution)/shard_map/ppermute | solution.py:29
  569.7 17.2 %collective-permute-start.102 = (bf16[256,512]{1,0:T(8,128)(2,1)}, bf16[256,512]{1,0:T(8,128)(2,1)S(1)}, u32[]{:S(2)}, u32[]{:S(2)}) collective-permute-start(bf16[256,512]{1,0:T(8,128)(2,1)} %reduce-scatter.9.cloned.1.call-done.refs_8_), channel_id=1, source_target_pairs={{0,16},{16,0},{1,17},{17,1},{2,18},{18,2},{3,19},{19,3},{4,20},{20... | collective-permute-start | bytes 786440 | tf_op jit(solution)/shard_map/ppermute | solution.py:29
  570.5 16.9 %collective-permute-start.103 = (bf16[256,512]{1,0:T(8,128)(2,1)}, bf16[256,512]{1,0:T(8,128)(2,1)S(1)}, u32[]{:S(2)}, u32[]{:S(2)}) collective-permute-start(bf16[256,512]{1,0:T(8,128)(2,1)} %collective-permute-done.79.refs_9_), channel_id=1, source_target_pairs={{0,16},{16,0},{1,17},{17,1},{2,18},{18,2},{3,19},{19,3},{4,20},{20... | collective-permute-start | bytes 786440 | tf_op jit(solution)/shard_map/ppermute | solution.py:29
  570.7 16.1 %collective-permute-start.95 = (bf16[256,512]{1,0:T(8,128)(2,1)}, bf16[256,512]{1,0:T(8,128)(2,1)S(1)}, u32[]{:S(2)}, u32[]{:S(2)}) collective-permute-start(bf16[256,512]{1,0:T(8,128)(2,1)} %copy-done.146), channel_id=1, source_target_pairs={{0,8},{4,12},{8,0},{12,4},{1,9},{5,13},{9,1},{13,5},{2,10},{6,14},... | collective-permute-start | bytes 786440 | tf_op jit(solution)/shard_map/ppermute | solution.py:37
  601.4 21.4 %collective-permute-start.91 = (bf16[2,128,1024]{2,1,0:T(8,128)(2,1)S(1)}, bf16[2,128,1024]{2,1,0:T(8,128)(2,1)S(1)}, u32[]{:S(2)}, u32[]{:S(2)}) collective-permute-start(bf16[2,128,1024]{2,1,0:T(8,128)(2,1)S(1)} %maximum_select_fusion.4), channel_id=1, source_target_pairs={{0,16},{16,0},{1,17},{17,1},{2,18},{18,2},{3,19},{19,3},{4,20},{20... | collective-permute-start | bytes 1572872 | tf_op jit(solution)/shard_map/ppermute | solution.py:29
  606.5 18.1 %collective-permute-start.123 = (bf16[272,512]{1,0:T(8,128)(2,1)S(1)}, bf16[272,512]{1,0:T(8,128)(2,1)}, u32[]{:S(2)}, u32[]{:S(2)}) collective-permute-start(bf16[272,512]{1,0:T(8,128)(2,1)S(1)} %copy-done.129), channel_id=1, source_target_pairs={{0,8},{4,12},{8,0},{12,4},{1,9},{5,13},{9,1},{13,5},{2,10},{6,14},... | collective-permute-start | bytes 835592 | tf_op jit(solution)/shard_map/ppermute | solution.py:37
  608.1 19.4 %collective-permute-start.124 = (bf16[272,512]{1,0:T(8,128)(2,1)}, bf16[272,512]{1,0:T(8,128)(2,1)}, u32[]{:S(2)}, u32[]{:S(2)}) collective-permute-start(bf16[272,512]{1,0:T(8,128)(2,1)} %collective-permute-done.85.refs_9_), channel_id=1, source_target_pairs={{0,8},{4,12},{8,0},{12,4},{1,9},{5,13},{9,1},{13,5},{2,10},{6,14},... | collective-permute-start | bytes 835592 | tf_op jit(solution)/shard_map/ppermute | solution.py:37
  608.6 23.9 %collective-permute-start.93 = (bf16[2,128,1024]{2,1,0:T(8,128)(2,1)S(1)}, bf16[2,128,1024]{2,1,0:T(8,128)(2,1)S(1)}, u32[]{:S(2)}, u32[]{:S(2)}) collective-permute-start(bf16[2,128,1024]{2,1,0:T(8,128)(2,1)S(1)} %maximum_select_fusion.6), channel_id=1, source_target_pairs={{0,16},{16,0},{1,17},{17,1},{2,18},{18,2},{3,19},{19,3},{4,20},{20... | collective-permute-start | bytes 1572872 | tf_op jit(solution)/shard_map/ppermute | solution.py:29
  658.4 22.4 %collective-permute-start.132 = (f32[1,8320]{1,0:T(1,128)}, f32[1,8320]{1,0:T(1,128)S(1)}, u32[]{:S(2)}, u32[]{:S(2)}) collective-permute-start(f32[1,8320]{1,0:T(1,128)} %get-tuple-element.343), channel_id=1, source_target_pairs={{0,2},{1,3},{2,0},{3,1},{4,6},{5,7},{6,4},{7,5},{8,10},{9,11},{10,... | collective-permute-start | bytes 99848 | tf_op jit(solution)/shard_map/ppermute | solution.py:586
  659.1 21.7 %collective-permute-start.133 = (f32[1,8320]{1,0:T(1,128)}, f32[1,8320]{1,0:T(1,128)S(1)}, u32[]{:S(2)}, u32[]{:S(2)}) collective-permute-start(f32[1,8320]{1,0:T(1,128)} %get-tuple-element.343), channel_id=1, source_target_pairs={{0,1},{1,2},{2,3},{3,0},{4,5},{5,6},{6,7},{7,4},{8,9},{9,10},{10,1... | collective-permute-start | bytes 99848 | tf_op jit(solution)/shard_map/ppermute | solution.py:586
  661.2 19.6 %collective-permute-start.134 = (f32[1,8320]{1,0:T(1,128)}, f32[1,8320]{1,0:T(1,128)S(1)}, u32[]{:S(2)}, u32[]{:S(2)}) collective-permute-start(f32[1,8320]{1,0:T(1,128)} %get-tuple-element.343), channel_id=1, source_target_pairs={{0,3},{1,0},{2,1},{3,2},{4,7},{5,4},{6,5},{7,6},{8,11},{9,8},{10,9... | collective-permute-start | bytes 99848 | tf_op jit(solution)/shard_map/ppermute | solution.py:586
  (278 other events, 2078.1 us)
Sparse Core Ops, SparseCore 0:
  41.4 32.2 all-gather.5
  75.8 27.4 all-gather.7
  105.5 29.5 all-gather.9
  136.5 27.4 all-gather.11
  177.0 32.0 all-gather.13
  384.2 31.2 reduce-scatter.6
  418.5 28.0 reduce-scatter.8
  456.8 32.3 reduce-scatter.10
  494.9 31.3 reduce-scatter.14
  529.0 25.7 reduce-scatter.12
  569.8 31.4 reduce-scatter.16
